TPU v7x, 32 devices: a whole 2x2x4 slice. The times are simulated.
32 devices in a mesh: row: 4 (over y, core), gz: 2 (over x), vert: 4 (over z).
Axes of the slice: x: 2, y: 2, z: 4, core: 2. Of those that a mesh axis runs over, the one named last changes fastest.
Arguments:
- distribution: float32 [32, 32, 110592], P('row', 'gz', 'vert'), may hold values from 0 to 10, as said below
- z_order: int32 [48], P('vert'), may hold values from 0 to 47, as said below
- edge_codes: int32 [2, 4], P(None, 'row'), may hold values from 0 to 2, as said below
Outputs:
- new_distribution: float32 [32, 32, 110592], P('row', 'gz', 'vert')
- macroscopic: float32 [8, 32, 32], P(None, 'row', 'gz')
- boundary_flux: float32 [2, 32], P('gz', 'row')
Inputs may be any that keep to these rules, and one draw needn't show every extreme that they name: `z_order`: a permutation of 0 to 47. `edge_codes`: row 0 holds 0 (diffuse wall) or 1 (evaporating film), row 1 holds 0 (diffuse wall) or 2 (outflow); the first column's bottom is film and the last column's top is outflow. `distribution`: every entry is positive.
All inputs are finite; a program needn't handle non-finite values.
Results may differ from a plain program's by a relative error of at most 0.0003.
Values sent between devices are 32-bit elements; how exact they have to be, the bound alone decides.
No kernel may reach another device: no remote copies, remote signals or barrier semaphores. Data moves between devices by JAX's collectives and lax.ppermute only.
A program may use at most 256 MiB of HBM per device.

v0:
```python
import math

import jax
import jax.numpy as jnp
import numpy as np
from jax import lax
from jax.sharding import PartitionSpec as P

NODES = 8
NVR = 48
NVT = 48
NVZ = 48
STEPS = 2


ELEMENT_WIDTH = 4.0
TIME_STEP = 0.001
KNUDSEN = 0.005
VISCOUS_RATIO = 2.0 / 3.0
SAT_DENSITY = 1.5
SPEED_LIMIT = 5.0
HIGHEST_PRECISION = lax.Precision.HIGHEST


def with_halo(cells, sides, width):
    for axis, dim in sides:
        count = lax.axis_size(axis)
        ends = count - 1
        head = lax.slice_in_dim(cells, 0, width, axis=dim)
        tail = lax.slice_in_dim(cells, cells.shape[dim] - width, cells.shape[dim], axis=dim)
        cells = jnp.concatenate(
            [
                lax.ppermute(tail, axis, [(i, (i + 1) % count) for i in range(ends)]),
                cells,
                lax.ppermute(head, axis, [((i + 1) % count, i) for i in range(ends)]),
            ],
            axis=dim,
        )
    return cells


def legendre_pair(position, point_count):
    previous = 1.0
    current = position
    for degree in range(2, point_count + 1):
        previous, current = (
            current,
            ((2 * degree - 1) * position * current - (degree - 1) * previous) / degree,
        )
    slope = point_count * (position * current - previous) / (position * position - 1.0)
    return (current, slope)


def dg_tables(point_count):
    point_list = []
    weight_list = []
    for number in range(point_count):
        position = math.cos(math.pi * (number + 0.75) / (point_count + 0.5))
        for sweep in range(60):
            value, slope = legendre_pair(position, point_count)
            position = position - value / slope
        value, slope = legendre_pair(position, point_count)
        point_list.append(position)
        weight_list.append(2.0 / ((1.0 - position * position) * slope * slope))
    point_list = point_list[::-1]
    weight_list = weight_list[::-1]
    products = []
    for row_number in range(point_count):
        product_value = 1.0
        for other in range(point_count):
            if other != row_number:
                product_value = product_value * (point_list[row_number] - point_list[other])
        products.append(product_value)
    derivative_rows = []
    for row_number in range(point_count):
        entries = []
        for column in range(point_count):
            if column == row_number:
                total_value = 0.0
                for other in range(point_count):
                    if other != row_number:
                        total_value = total_value + 1.0 / (
                            point_list[row_number] - point_list[other]
                        )
                entries.append(total_value)
            else:
                entries.append(
                    products[row_number]
                    / products[column]
                    / (point_list[row_number] - point_list[column])
                )
        derivative_rows.append(entries)
    right_list = []
    left_list = []
    for column in range(point_count):
        right_value = 1.0
        left_value = 1.0
        for other in range(point_count):
            if other != column:
                right_value = right_value * (1.0 - point_list[other])
                left_value = left_value * (-1.0 - point_list[other])
        right_list.append(right_value / products[column])
        left_list.append(left_value / products[column])
    points = np.array(point_list)
    quad_weights = np.array(weight_list)
    derivative = np.array(derivative_rows)
    end_right = np.array(right_list)
    end_left = np.array(left_list)
    return (
        points,
        jnp.asarray(derivative, jnp.float32),
        jnp.asarray(end_right / quad_weights, jnp.float32),
        jnp.asarray(end_left / quad_weights, jnp.float32),
        jnp.asarray(end_right, jnp.float32),
        jnp.asarray(end_left, jnp.float32),
    )


def speed_grid(point_count):
    return -SPEED_LIMIT + (np.arange(point_count) + 0.5) * (2.0 * SPEED_LIMIT / point_count)


def shift_velocity(field_entries, offset, keep_mask):
    padding = jnp.zeros(field_entries.shape[:-1] + (abs(offset),), field_entries.dtype)
    if offset > 0:
        shifted = jnp.concatenate([field_entries[..., offset:], padding], -1)
    else:
        shifted = jnp.concatenate([padding, field_entries[..., :offset]], -1)
    return jnp.where(keep_mask, shifted, 0.0)


def on_device(distribution, z_order, edge_codes):
    local_r, local_z, vdev = distribution.shape
    row_count = local_r // NODES
    col_count = local_z // NODES
    node_count = local_r * local_z
    plane_size = NVR * NVT
    slot_count = vdev // plane_size
    row_index = lax.axis_index("row")
    gz_index = lax.axis_index("gz")
    row_total = lax.axis_size("row")
    gz_total = lax.axis_size("gz")
    points, derivative, lift_right, lift_left, end_right, end_left = dg_tables(NODES)
    weight = (
        2
        * SPEED_LIMIT
        / NVR
        * (2 * SPEED_LIMIT / NVT)
        * (2 * SPEED_LIMIT / NVZ)
        / (2 * math.pi) ** 1.5
    )
    grid_r = speed_grid(NVR)
    grid_t = speed_grid(NVT)
    grid_z = speed_grid(NVZ)
    half_flux = float(
        weight
        * np.sum(np.exp(-(grid_r**2) / 2))
        * np.sum(np.exp(-(grid_t**2) / 2))
        * np.sum(np.maximum(grid_z, 0.0) * np.exp(-(grid_z**2) / 2))
    )
    vel_r = jnp.tile(jnp.asarray(np.repeat(grid_r, NVT), jnp.float32), slot_count)
    vel_t = jnp.tile(jnp.asarray(np.tile(grid_t, NVR), jnp.float32), slot_count)
    slot_speeds = jnp.sum(
        jnp.where(
            z_order[:, None] == jnp.arange(NVZ, dtype=jnp.int32)[None, :],
            jnp.asarray(grid_z, jnp.float32)[None, :],
            0.0,
        ),
        1,
    )
    vel_z = jnp.repeat(slot_speeds, plane_size)
    flat_index = jnp.arange(vdev, dtype=jnp.int32)
    a_index = flat_index // NVT % NVR
    b_index = flat_index % NVT
    speed_sq = vel_r**2 + vel_t**2 + vel_z**2
    maxwell_wall = jnp.exp(-speed_sq / 2)
    element_start = (row_index * row_count).astype(jnp.float32)
    radius = (
        (element_start + jnp.arange(row_count, dtype=jnp.float32))[:, None]
        + (1.0 + jnp.asarray(points, jnp.float32))[None, :] / 2
    ) * ELEMENT_WIDTH
    radius = radius.reshape(local_r)
    code_bottom = jnp.repeat(edge_codes[0], NODES)
    code_top = jnp.repeat(edge_codes[1], NODES)
    down_coef = weight * jnp.maximum(-vel_z, 0.0)
    up_coef = weight * jnp.maximum(vel_z, 0.0)

    def gather_moments(current):
        bottom = jnp.einsum("j,rjv->rv", end_left, current[:, :NODES], precision=HIGHEST_PRECISION)
        top_trace = jnp.einsum(
            "j,rjv->rv", end_right, current[:, local_z - NODES :], precision=HIGHEST_PRECISION
        )
        edge_trace = jnp.where(gz_index == 0, bottom, top_trace)
        first_coef = jnp.where(gz_index == 0, down_coef, up_coef)
        bound_sums = jnp.stack(
            [
                jnp.dot(edge_trace, first_coef, precision=HIGHEST_PRECISION),
                jnp.dot(edge_trace, down_coef, precision=HIGHEST_PRECISION),
            ]
        )
        flat = current.reshape(node_count, vdev)
        moment_basis = jnp.stack(
            [
                jnp.full((vdev,), weight, jnp.float32),
                weight * vel_r,
                weight * vel_t,
                weight * vel_z,
                0.5 * weight * speed_sq,
            ],
            1,
        )
        partials = jnp.dot(
            flat, moment_basis, precision=HIGHEST_PRECISION, preferred_element_type=jnp.float32
        )
        integral_sums_table, bound_sums = lax.psum((partials, bound_sums), "vert")
        particle_concentration = integral_sums_table[:, 0]
        bulk_velocity = integral_sums_table[:, 1:4] / particle_concentration[:, None]
        vapour_warmth = (
            2.0 * integral_sums_table[:, 4] / particle_concentration - jnp.sum(bulk_velocity**2, 1)
        ) / 3.0
        thermal_norm_square = (
            (vel_r[None, :] - bulk_velocity[:, 0:1]) ** 2
            + (vel_t[None, :] - bulk_velocity[:, 1:2]) ** 2
            + (vel_z[None, :] - bulk_velocity[:, 2:3]) ** 2
        )
        weighted = flat * thermal_norm_square
        heat_basis = jnp.stack(
            [
                weight * vel_r,
                weight * vel_t,
                weight * vel_z,
                jnp.full((vdev,), weight, jnp.float32),
            ],
            1,
        )
        heat_parts = jnp.dot(
            weighted, heat_basis, precision=HIGHEST_PRECISION, preferred_element_type=jnp.float32
        )
        heat_local = 0.5 * (heat_parts[:, :3] - bulk_velocity * heat_parts[:, 3:4])
        conduction_integral = lax.psum(heat_local, "vert")
        fluid_observables = (
            particle_concentration,
            bulk_velocity[:, 0],
            bulk_velocity[:, 1],
            bulk_velocity[:, 2],
            vapour_warmth,
            conduction_integral[:, 0],
            conduction_integral[:, 1],
            conduction_integral[:, 2],
        )
        fluid_observables = tuple((entry.reshape(local_r, local_z) for entry in fluid_observables))
        return (fluid_observables, bound_sums)

    def advance(current, fluid_observables, bound_sums):
        (
            particle_concentration,
            drift_outward,
            drift_around,
            drift_lengthwise,
            vapour_warmth,
            conduction_outward,
            conduction_around,
            conduction_lengthwise,
        ) = tuple((entry[:, :, None] for entry in fluid_observables))
        grouped = current.reshape(row_count, NODES, local_z, vdev)
        volume = jnp.einsum("ij,ejzv->eizv", derivative, grouped, precision=HIGHEST_PRECISION)
        trace_hi = jnp.einsum("j,ejzv->ezv", end_right, grouped, precision=HIGHEST_PRECISION)
        trace_lo = jnp.einsum("j,ejzv->ezv", end_left, grouped, precision=HIGHEST_PRECISION)
        mirror = (
            trace_lo[0].reshape(local_z, slot_count, NVR, NVT)[:, :, ::-1, :].reshape(local_z, vdev)
        )
        edge_halo = with_halo(jnp.stack([trace_lo[0], trace_hi[-1]]), (("row", 0),), 1)
        from_left = edge_halo[0]
        from_right = edge_halo[3]
        left_ghost = jnp.where(row_index == 0, mirror, from_left)
        right_ghost = jnp.where(row_index == row_total - 1, trace_hi[-1], from_right)
        plus_side = jnp.concatenate([left_ghost[None], trace_hi], 0)
        minus_side = jnp.concatenate([trace_lo, right_ghost[None]], 0)
        face_values = jnp.where(vel_r > 0, plus_side, minus_side)
        radial = (
            2.0
            / ELEMENT_WIDTH
            * vel_r
            * (
                volume
                + lift_right[None, :, None, None] * (face_values[1:] - trace_hi)[:, None]
                - lift_left[None, :, None, None] * (face_values[:-1] - trace_lo)[:, None]
            )
        )
        radial = radial.reshape(local_r, local_z, vdev)
        grouped = current.reshape(local_r, col_count, NODES, vdev)
        volume = jnp.einsum("ij,rejv->reiv", derivative, grouped, precision=HIGHEST_PRECISION)
        trace_hi = jnp.einsum("j,rejv->rev", end_right, grouped, precision=HIGHEST_PRECISION)
        trace_lo = jnp.einsum("j,rejv->rev", end_left, grouped, precision=HIGHEST_PRECISION)
        edge_halo = with_halo(jnp.stack([trace_lo[:, 0], trace_hi[:, -1]]), (("gz", 0),), 1)
        bottom_density = jnp.where(code_bottom == 1, SAT_DENSITY, bound_sums[0] / half_flux)
        top_density = bound_sums[0] / half_flux
        bottom_ghost = bottom_density[:, None] * maxwell_wall[None, :]
        top_ghost = jnp.where(
            code_top[:, None] == 2, trace_hi[:, -1], top_density[:, None] * maxwell_wall[None, :]
        )
        low_ghost = jnp.where(gz_index == 0, bottom_ghost, edge_halo[0])
        high_ghost = jnp.where(gz_index == gz_total - 1, top_ghost, edge_halo[3])
        plus_side = jnp.concatenate([low_ghost[:, None], trace_hi], 1)
        minus_side = jnp.concatenate([trace_lo, high_ghost[:, None]], 1)
        face_values = jnp.where(vel_z > 0, plus_side, minus_side)
        axial_term = (
            2.0
            / ELEMENT_WIDTH
            * vel_z
            * (
                volume
                + lift_right[None, None, :, None] * (face_values[:, 1:] - trace_hi)[:, :, None]
                - lift_left[None, None, :, None] * (face_values[:, :-1] - trace_lo)[:, :, None]
            )
        )
        axial_term = axial_term.reshape(local_r, local_z, vdev)
        step_r = 2 * SPEED_LIMIT / NVR
        step_t = 2 * SPEED_LIMIT / NVT
        grad_r = (
            shift_velocity(current, NVT, a_index < NVR - 1)
            - shift_velocity(current, -NVT, a_index > 0)
        ) / (2 * step_r)
        grad_t = (
            shift_velocity(current, 1, b_index < NVT - 1) - shift_velocity(current, -1, b_index > 0)
        ) / (2 * step_t)
        rotation = (vel_t * vel_t * grad_r - vel_r * vel_t * grad_t) / radius[:, None, None]
        peculiar_r = vel_r - drift_outward
        peculiar_t = vel_t - drift_around
        peculiar_z = vel_z - drift_lengthwise
        thermal_norm_square = peculiar_r**2 + peculiar_t**2 + peculiar_z**2
        projected_conduction = (
            peculiar_r * conduction_outward
            + peculiar_t * conduction_around
            + peculiar_z * conduction_lengthwise
        )
        gaussian_resting_state = (
            particle_concentration
            * vapour_warmth ** (-1.5)
            * jnp.exp(-thermal_norm_square / (2 * vapour_warmth))
        )
        collision_goal_state = gaussian_resting_state * (
            1.0
            + (1.0 - VISCOUS_RATIO)
            * projected_conduction
            / (5.0 * particle_concentration * vapour_warmth**2)
            * (thermal_norm_square / vapour_warmth - 5.0)
        )
        collide = particle_concentration / KNUDSEN * (collision_goal_state - current)
        return current + TIME_STEP * (collide - radial - axial_term - rotation)

    current = distribution
    for step_index in range(STEPS):
        fluid_observables, bound_sums = gather_moments(current)
        current = advance(current, fluid_observables, bound_sums)
    fluid_observables, bound_sums = gather_moments(current)
    macroscopic = jnp.stack(fluid_observables)
    bottom_row = jnp.where(code_bottom == 1, SAT_DENSITY * half_flux - bound_sums[0], 0.0)
    top_row = jnp.where(code_top == 2, bound_sums[0] - bound_sums[1], 0.0)
    boundary_flux = jnp.where(gz_index == 0, bottom_row, top_row)[None]
    return (current, macroscopic, boundary_flux)


def solution(mesh):
    in_specs = (P("row", "gz", "vert"), P("vert"), P(None, "row"))
    out_specs = (P("row", "gz", "vert"), P(None, "row", "gz"), P("gz", "row"))
    return jax.shard_map(
        on_device, mesh=mesh, in_specs=in_specs, out_specs=out_specs, check_vma=False
    )
```

profile of v0, /device:TPU:4, one launch (start us, length us, event | category | flops | bytes accessed | tf_op | source)
XLA Modules:
  0.0 963.2 jit_solution(16335086213525880315)
XLA Ops:
  0.7 16.1 %fusion.58 = f32[1,8,2,27648]{3,0,2,1:T(1,128)S(1)} fusion(f32[8,1,1,1]{0,1,3,2:T(1,128)} %constant.165, f32[8,16,27648]{2,1,0:T(8,128)} %param.12), kind=kOutput, calls=%fused_computation.74 | convolution fusion | flops 42467328 | bytes 15925280 | tf_op jit(solution)/shard_map/j,rejv->rev/dot_general | solution.py:294
  20.9 20.3 %fusion.150 = f32[1,16,27648]{2,0,1:T(1,128)S(1)} fusion(f32[8,1,1]{0,1,2:T(1,128)S(1)} %copy-done.64, f32[8,16,27648]{2,1,0:T(8,128)S(1)} %copy-done.1), kind=kOutput, calls=%fused_computation.305 | convolution fusion | flops 42467328 | bytes 15925280 | tf_op jit(solution)/shard_map/j,ejzv->ezv/dot_general | solution.py:268
  60.4 20.7 %fusion.148 = f32[1,16,27648]{2,0,1:T(1,128)S(1)} fusion(f32[8,1,1]{0,1,2:T(1,128)S(1)} %copy-done.61, f32[8,16,27648]{2,1,0:T(8,128)S(1)} %copy-done.1), kind=kOutput, calls=%fused_computation.303 | convolution fusion | flops 42467328 | bytes 15925280 | tf_op jit(solution)/shard_map/j,ejzv->ezv/dot_general | solution.py:267
  123.2 13.9 %convolution_bitcast_fusion.4 = f32[128,5]{0,1:T(8,128)S(1)} fusion(f32[27648,5]{0,1:T(8,128)} %stack.24, f32[128,27648]{1,0:T(8,128)} %bitcast.313), kind=kOutput, calls=%fused_computation.170 | convolution fusion | flops 212336640 | bytes 14711296 | tf_op jit(solution)/shard_map/dot_general | solution.py:212
  137.1 12.0 %psum.63 = f32[128,5]{0,1:T(8,128)S(1)} all-reduce(f32[128,5]{0,1:T(8,128)S(1)} %convolution_bitcast_fusion.4), channel_id=1, replica_groups=mesh['row'=4,'gz'=2,'vert'=4] {'vert'}, use_global_device_ids=true, to_apply=%region_1.2 | all-reduce | flops 640 | bytes 5120 | tf_op jit(solution)/shard_map/psum | solution.py:215
  150.2 17.6 %fusion.83 = f32[128,4]{0,1:T(4,128)S(1)} fusion(f32[128,27648]{1,0:T(8,128)} %bitcast.314, f32[128]{0:T(128)S(1)} %get-tuple-element.113, f32[27648]{0:T(1024)} %sub.385, f32[128]{0:T(128)S(1)} %get-tuple-element.112, f32[27648]{0:T(1024)} %sub.380, f32[128]{0:T(128)S(1)} %get-tuple-element.111, f32[27648]{0:T(1024)} %sub.375, f32[27648,1]{0,1:T(1,128)} %broadcast.609, ...), kind=kOutput, calls=%fused_computation.99 | convolution fusion | flops 202051584 | bytes 14933504 | tf_op jit(solution)/shard_map/dot_general | solution.py:236
  203.6 15.9 %fusion.60 = f32[1,8,2,27648]{3,0,2,1:T(1,128)S(1)} fusion(f32[8,1,1,1]{0,1,3,2:T(1,128)} %constant.164, f32[8,16,27648]{2,1,0:T(8,128)} %param.12), kind=kOutput, calls=%fused_computation.76 | convolution fusion | flops 42467328 | bytes 15925280 | tf_op jit(solution)/shard_map/j,rejv->rev/dot_general | solution.py:293
  243.0 18.2 %copy.204 = f32[8,16,27647]{2,0,1:T(8,128)} copy(f32[8,16,27647]{2,1,0:T(8,128)} %get-tuple-element.62) | data formatting | bytes 28310528
  261.2 18.4 %copy.203 = f32[8,16,27647]{2,0,1:T(8,128)} copy(f32[8,16,27647]{2,1,0:T(8,128)} %get-tuple-element.63) | data formatting | bytes 28310528
  279.6 18.6 %copy.206 = f32[8,16,27600]{2,0,1:T(8,128)} copy(f32[8,16,27600]{2,1,0:T(8,128)} %get-tuple-element.60) | data formatting | bytes 28262400
  298.2 18.3 %copy.205 = f32[8,16,27600]{2,0,1:T(8,128)} copy(f32[8,16,27600]{2,1,0:T(8,128)} %get-tuple-element.61) | data formatting | bytes 28262400
  355.1 22.4 %fusion.4 = f32[8,2,8,27648]{3,2,1,0:T(8,128)} fusion(f32[8,8,1,1]{1,0,3,2:T(8,128)S(1)} %copy-done.59, f32[8,16,27648]{2,1,0:T(8,128)} %param.12, f32[8,2,27648]{2,1,0:T(2,128)} %get-tuple-element.71, f32[8]{0:T(128)S(1)} %copy-done.49, f32[8,2,27648]{2,1,0:T(2,128)} %get-tuple-element.70, f32[8]{0:T(128)S(1)} %copy-done.50, f32[27648]{0:T(1024)} %get-tuple-element.86), kind=kOutput, calls=%fused_computation.8 | convolution fusion | flops 357433344 | bytes 31961408 | tf_op jit(solution)/shard_map/ij,rejv->reiv/dot_general | solution.py:292
  377.5 18.3 %copy.96 = f32[8,2,8,27648]{3,0,2,1:T(8,128)} copy(f32[8,2,8,27648]{3,2,1,0:T(8,128)} %fusion.4) | data formatting | bytes 28311552 | tf_op jit(solution)/shard_map/mul | solution.py:308
  403.1 59.3 %fusion.23 = f32[8,16,27648]{2,0,1:T(8,128)} fusion(f32[8,16,27648]{2,0,1:T(8,128)} %bitcast.322, f32[8,8,1]{1,0,2:T(8,128)S(1)} %copy-done.98, f32[8,16,27647]{2,0,1:T(8,128)} %copy.203, f32[8,16,27647]{2,0,1:T(8,128)} %copy.204, f32[8,16,27600]{2,0,1:T(8,128)} %copy.205, f32[8,16,27600]{2,0,1:T(8,128)} %copy.206, f32[8]{0:T(128)S(1)} %copy-done.95, ...), kind=kOutput, calls=%fused_computation.27 | convolution fusion | flops 498991104 | bytes 103359328 | tf_op jit(solution)/shard_map/ij,ejzv->eizv/dot_general | solution.py:266
  462.5 25.6 %fusion.95 = f32[1,8,2,27648]{3,0,2,1:T(1,128)} fusion(f32[8,1,1,1]{0,1,3,2:T(1,128)S(1)} %copy-done.90, f32[8,2,8,27648]{3,0,2,1:T(8,128)} %bitcast.308), kind=kOutput, calls=%fused_computation.111 | convolution fusion | flops 42467328 | bytes 15925280 | tf_op jit(solution)/shard_map/j,rejv->rev/dot_general | solution.py:293
  488.1 18.6 %fusion.93 = f32[1,8,2,27648]{3,0,2,1:T(1,128)} fusion(f32[8,1,1,1]{0,1,3,2:T(1,128)S(1)} %copy-done.89, f32[8,2,8,27648]{3,0,2,1:T(8,128)S(1)} %bitcast.310), kind=kOutput, calls=%fused_computation.109 | convolution fusion | flops 42467328 | bytes 15925280 | tf_op jit(solution)/shard_map/j,rejv->rev/dot_general | solution.py:294
  506.7 13.6 %fusion.163 = f32[1,16,27648]{2,0,1:T(1,128)} fusion(f32[8,16,27648]{2,0,1:T(8,128)S(1)} %copy-done, f32[8,1,1]{0,1,2:T(1,128)S(1)} %copy-done.65), kind=kOutput, calls=%fused_computation.318 | convolution fusion | flops 42467328 | bytes 15925280 | tf_op jit(solution)/shard_map/j,ejzv->ezv/dot_general | solution.py:268
  520.2 18.2 %copy.102 = f32[8,16,27648]{2,1,0:T(8,128)} copy(f32[8,16,27648]{2,0,1:T(8,128)} %fusion.23) | data formatting | bytes 28311552 | tf_op jit(solution)/shard_map/add | solution.py:350
  549.8 12.9 %fusion.104 = f32[1,8,27648]{2,0,1:T(1,128)S(1)} fusion(f32[8,1,1]{0,1,2:T(1,128)S(1)} %copy-done.65, f32[8,8,27648]{2,0,1:T(8,128)} %get-tuple-element.58), kind=kOutput, calls=%fused_computation.120 | convolution fusion | flops 21233664 | bytes 7962656 | tf_op jit(solution)/shard_map/j,rjv->rv/dot_general | solution.py:189
  562.8 13.0 %fusion.102 = f32[1,8,27648]{2,0,1:T(1,128)S(1)} fusion(f32[8,1,1]{0,1,2:T(1,128)S(1)} %copy-done.62, f32[8,8,27648]{2,0,1:T(8,128)} %get-tuple-element.59), kind=kOutput, calls=%fused_computation.118 | convolution fusion | flops 21233664 | bytes 7962656 | tf_op jit(solution)/shard_map/j,rjv->rv/dot_general | solution.py:190
  579.9 23.0 %fusion.154 = (f32[8,16,27600]{2,0,1:T(8,128)}, f32[8,16,27600]{2,0,1:T(8,128)}) fusion(f32[8,16,27648]{2,0,1:T(8,128)} %fusion.23), kind=kLoop, calls=%fused_computation.309 | loop fusion | bytes 56524800 | tf_op jit(solution)/shard_map/slice | solution.py:126
  629.0 12.6 %fusion.162 = f32[128,5]{0,1:T(8,128)S(1)} fusion(f32[128,27648]{1,0:T(8,128)S(1)} %bitcast.320, f32[27648,5]{0,1:T(8,128)} %stack.24), kind=kOutput, calls=%fused_computation.317 | convolution fusion | flops 212336640 | bytes 14711296 | tf_op jit(solution)/shard_map/dot_general | solution.py:212
  651.8 17.6 %fusion.73 = f32[128,4]{0,1:T(4,128)S(1)} fusion(f32[128,27648]{1,0:T(8,128)} %bitcast.317, f32[128]{0:T(128)S(1)} %get-tuple-element.110, f32[128]{0:T(128)S(1)} %get-tuple-element.109, f32[128]{0:T(128)S(1)} %get-tuple-element.108, f32[27648]{0:T(1024)S(1)} %copy-done.25, f32[27648]{0:T(1024)} %sub.380, f32[27648]{0:T(1024)S(1)} %copy-done.29, ...), kind=kOutput, calls=%fused_computation.89 | convolution fusion | flops 202051584 | bytes 14933504 | tf_op jit(solution)/shard_map/dot_general | solution.py:236
  705.7 15.2 %fusion.164 = f32[1,16,27648]{2,0,1:T(1,128)S(1)} fusion(f32[8,16,27648]{2,0,1:T(8,128)} %fusion.23, f32[8,1,1]{0,1,2:T(1,128)S(1)} %copy-done.62), kind=kOutput, calls=%fused_computation.319 | convolution fusion | flops 42467328 | bytes 15925280 | tf_op jit(solution)/shard_map/j,ejzv->ezv/dot_general | solution.py:267
  753.5 30.8 %fusion.5 = f32[8,2,8,27648]{3,2,1,0:T(8,128)} fusion(f32[8,8,1,1]{1,0,3,2:T(8,128)S(1)} %copy-done.60, f32[8,2,8,27648]{3,0,2,1:T(8,128)} %bitcast.309, f32[8,2,27648]{2,1,0:T(2,128)} %get-tuple-element.67, f32[8,2,27648]{2,1,0:T(2,128)} %get-tuple-element.66, f32[8]{0:T(128)S(1)} %copy-done.49, f32[8]{0:T(128)S(1)} %copy-done.50, f32[27648]{0:T(1024)S(1)} %copy-done.11), kind=kOutput, calls=%fused_computation.9 | convolution fusion | flops 357433344 | bytes 31961408 | tf_op jit(solution)/shard_map/ij,rejv->reiv/dot_general | solution.py:292
  784.3 18.3 %copy.115 = f32[8,2,8,27648]{3,0,2,1:T(8,128)} copy(f32[8,2,8,27648]{3,2,1,0:T(8,128)} %fusion.5) | data formatting | bytes 28311552 | tf_op jit(solution)/shard_map/mul | solution.py:308
  808.7 44.1 %fusion.18 = f32[8,16,27648]{2,0,1:T(8,128)} fusion(f32[8,16,27648]{2,0,1:T(8,128)} %fusion.23, f32[8,16,27648]{2,0,1:T(8,128)} %bitcast.321, f32[8,8,1]{1,0,2:T(8,128)S(1)} %copy-done.99, f32[8,16,27647]{2,0,1:T(8,128)} %get-tuple-element.57, f32[8,16,27647]{2,0,1:T(8,128)} %get-tuple-element.56, f32[8,16,27600]{2,0,1:T(8,128)} %get-tuple-element.55, ...), kind=kOutput, calls=%fused_computation.22 | convolution fusion | flops 498991104 | bytes 103359328 | tf_op jit(solution)/shard_map/ij,ejzv->eizv/dot_general | solution.py:266
  852.8 18.5 %copy.117 = f32[8,16,27648]{2,1,0:T(8,128)} copy(f32[8,16,27648]{2,0,1:T(8,128)} %fusion.18) | data formatting | bytes 28311552
  871.3 11.5 %fusion.153 = (f32[8,8,27648]{2,0,1:T(8,128)}, f32[8,8,27648]{2,0,1:T(8,128)}) fusion(f32[8,16,27648]{2,0,1:T(8,128)} %fusion.18), kind=kLoop, calls=%fused_computation.308 | loop fusion | bytes 28311552 | tf_op jit(solution)/shard_map/slice | solution.py:189
  882.8 13.1 %fusion.100 = f32[1,8,27648]{2,0,1:T(1,128)S(1)} fusion(f32[8,1,1]{0,1,2:T(1,128)S(1)} %copy-done.66, f32[8,8,27648]{2,0,1:T(8,128)} %get-tuple-element.52), kind=kOutput, calls=%fused_computation.116 | convolution fusion | flops 21233664 | bytes 7962656 | tf_op jit(solution)/shard_map/j,rjv->rv/dot_general | solution.py:189
  896.0 13.1 %fusion.98 = f32[1,8,27648]{2,0,1:T(1,128)S(1)} fusion(f32[8,1,1]{0,1,2:T(1,128)S(1)} %copy-done.63, f32[8,8,27648]{2,0,1:T(8,128)} %get-tuple-element.53), kind=kOutput, calls=%fused_computation.114 | convolution fusion | flops 21233664 | bytes 7962656 | tf_op jit(solution)/shard_map/j,rjv->rv/dot_general | solution.py:190
  934.5 17.8 %fusion.63 = f32[128,4]{0,1:T(4,128)S(1)} fusion(f32[128,27648]{1,0:T(8,128)} %bitcast.315, f32[128]{0:T(128)S(1)} %get-tuple-element.103, f32[128]{0:T(128)S(1)} %get-tuple-element.107, f32[128]{0:T(128)S(1)} %get-tuple-element.102, f32[27648]{0:T(1024)S(1)} %copy-done.27, f32[27648]{0:T(1024)S(1)} %copy-done.41, f32[27648]{0:T(1024)S(1)} %copy-done.31, ...), kind=kOutput, calls=%fused_computation.79 | convolution fusion | flops 202051584 | bytes 14933504 | tf_op jit(solution)/shard_map/dot_general | solution.py:236
  (393 shorter events, 331.8 us)
Async XLA Ops:
  16.7 36.6 %copy-start.4 = (f32[1,8,2,27648]{3,0,2,1:T(1,128)}, f32[1,8,2,27648]{3,0,2,1:T(1,128)S(1)}, u32[]{:S(2)}) copy-start(f32[1,8,2,27648]{3,0,2,1:T(1,128)S(1)} %fusion.58) | copy-start | bytes 5308420
  19.2 34.1 %copy-start.61 = (f32[8,1,1]{0,1,2:T(1,128)S(1)}, f32[8,1,1]{0,1,2:T(1,128)}, u32[]{:S(2)}) copy-start(f32[8,1,1]{0,1,2:T(1,128)} %constant.162) | copy-start | bytes 100
  19.2 300.3 %collective-permute-start.3 = (f32[1,8,27648]{2,0,1:T(1,128)}, f32[1,8,27648]{2,0,1:T(1,128)}, u32[]{:S(2)}, u32[]{:S(2)}) collective-permute-start(f32[1,8,27648]{2,0,1:T(1,128)} %slice_bitcast_fusion.1), channel_id=1, source_target_pairs={{4,0},{5,1},{6,2},{7,3},{12,8},{13,9},{14,10},{15,11},{20,16},{21,... | collective-permute-start | bytes 2654216 | tf_op jit(solution)/shard_map/ppermute | solution.py:35
  42.7 285.9 %collective-permute-start.1 = (f32[1,16,27648]{2,1,0:T(8,128)}, f32[1,16,27648]{2,1,0:T(8,128)}, u32[]{:S(2)}, u32[]{:S(2)}) collective-permute-start(f32[1,16,27648]{2,1,0:T(8,128)} %copy.216), channel_id=1, source_target_pairs={{8,0},{16,8},{24,16},{9,1},{17,9},{25,17},{10,2},{18,10},{26,18},{... | collective-permute-start | bytes 5308424 | tf_op jit(solution)/shard_map/ppermute | solution.py:35
  298.2 47.4 %copy-start.92 = (f32[8]{0:T(128)S(1)}, f32[8]{0:T(128)}, u32[]{:S(2)}) copy-start(f32[8]{0:T(128)} %broadcast_select_fusion.14) | copy-start | bytes 100
  316.5 35.4 %copy-start.5 = (f32[1,8,2,27648]{3,0,2,1:T(1,128)S(1)}, f32[1,8,2,27648]{3,0,2,1:T(1,128)}, u32[]{:S(2)}) copy-start(f32[1,8,2,27648]{3,0,2,1:T(1,128)} %copy-done.4) | copy-start | bytes 5308420
  316.5 35.4 %copy-start.9 = (f32[1,8,2,27648]{3,0,2,1:T(1,128)S(1)}, f32[1,8,2,27648]{3,0,2,1:T(1,128)}, u32[]{:S(2)}) copy-start(f32[1,8,2,27648]{3,0,2,1:T(1,128)} %copy-done.8) | copy-start | bytes 5308420
  323.0 32.1 %copy-start.49 = (f32[8]{0:T(128)S(1)}, f32[8]{0:T(128)}, u32[]{:S(2)}) copy-start(f32[8]{0:T(128)} %constant.129.clone) | copy-start | bytes 100
  323.0 22.6 %collective-permute-start.2 = (f32[1,8,27648]{2,0,1:T(1,128)S(1)}, f32[1,8,27648]{2,0,1:T(1,128)S(1)}, u32[]{:S(2)}, u32[]{:S(2)}) collective-permute-start(f32[1,8,27648]{2,0,1:T(1,128)S(1)} %get-tuple-element.83), channel_id=1, source_target_pairs={{0,4},{1,5},{2,6},{3,7},{8,12},{9,13},{10,14},{11,15},{16,20},{17,... | collective-permute-start | bytes 2654216 | tf_op jit(solution)/shard_map/ppermute | solution.py:33
  332.4 63.6 %collective-permute-start = (f32[1,16,27648]{2,1,0:T(8,128)}, f32[1,16,27648]{2,1,0:T(8,128)}, u32[]{:S(2)}, u32[]{:S(2)}) collective-permute-start(f32[1,16,27648]{2,1,0:T(8,128)} %get-tuple-element.79), channel_id=1, source_target_pairs={{0,8},{8,16},{16,24},{1,9},{9,17},{17,25},{2,10},{10,18},{18,26},{... | collective-permute-start | bytes 5308424 | tf_op jit(solution)/shard_map/ppermute | solution.py:33
  403.1 59.4 %copy-start.90 = (f32[8,1,1,1]{0,1,3,2:T(1,128)S(1)}, f32[8,1,1,1]{0,1,3,2:T(1,128)}, u32[]{:S(2)}) copy-start(f32[8,1,1,1]{0,1,3,2:T(1,128)} %constant.164) | copy-start | bytes 100
  462.5 44.2 %copy-start.65 = (f32[8,1,1]{0,1,2:T(1,128)S(1)}, f32[8,1,1]{0,1,2:T(1,128)}, u32[]{:S(2)}) copy-start(f32[8,1,1]{0,1,2:T(1,128)} %constant.161) | copy-start | bytes 100
  579.9 49.1 %slice-start.4 = ((s8[14155776]{0:T(1024)(128)(4,1)}), s8[4194304]{0:T(1024)(128)(4,1)S(1)}, s32[]{:S(2)}) async-start(s8[14155776]{0:T(1024)(128)(4,1)} %bitcast.318), calls=%async_computation.4 | async-start | bytes 8388608
  579.9 49.1 %slice-start.5 = ((s8[14155776]{0:T(1024)(128)(4,1)}), s8[4194304]{0:T(1024)(128)(4,1)S(1)}, s32[]{:S(2)}) async-start(s8[14155776]{0:T(1024)(128)(4,1)} %bitcast.318), calls=%async_computation.5 | async-start | bytes 8388608
  613.6 38.1 %copy-start.25 = (f32[27648]{0:T(1024)S(1)}, f32[27648]{0:T(1024)}, u32[]{:S(2)}) copy-start(f32[27648]{0:T(1024)} %sub.385) | copy-start | bytes 331780
  613.7 38.1 %copy-start.29 = (f32[27648]{0:T(1024)S(1)}, f32[27648]{0:T(1024)}, u32[]{:S(2)}) copy-start(f32[27648]{0:T(1024)} %sub.375) | copy-start | bytes 331780
  613.7 38.1 %copy-start.32 = (f32[27648,1]{0,1:T(1,128)S(1)}, f32[27648,1]{0,1:T(1,128)}, u32[]{:S(2)}) copy-start(f32[27648,1]{0,1:T(1,128)} %broadcast.609) | copy-start | bytes 331780
  613.7 38.1 %copy-start.34 = (f32[1,1,12,2304]{3,1,2,0:T(1,128)S(1)}, f32[1,1,12,2304]{3,1,2,0:T(1,128)}, u32[]{:S(2)}) copy-start(f32[1,1,12,2304]{3,1,2,0:T(1,128)} %copy.141) | copy-start | bytes 331780
  613.7 38.1 %copy-start.36 = (f32[1,1,12,2304]{3,1,2,0:T(1,128)S(1)}, f32[1,1,12,2304]{3,1,2,0:T(1,128)}, u32[]{:S(2)}) copy-start(f32[1,1,12,2304]{3,1,2,0:T(1,128)} %copy.142) | copy-start | bytes 331780
  622.0 98.9 %collective-permute-start.7 = (f32[1,8,27648]{2,0,1:T(1,128)}, f32[1,8,27648]{2,0,1:T(1,128)}, u32[]{:S(2)}, u32[]{:S(2)}) collective-permute-start(f32[1,8,27648]{2,0,1:T(1,128)} %slice_bitcast_fusion), channel_id=1, source_target_pairs={{4,0},{5,1},{6,2},{7,3},{12,8},{13,9},{14,10},{15,11},{20,16},{21,... | collective-permute-start | bytes 2654216 | tf_op jit(solution)/shard_map/ppermute | solution.py:35
  627.0 102.5 %collective-permute-start.5 = (f32[1,16,27648]{2,1,0:T(8,128)}, f32[1,16,27648]{2,1,0:T(8,128)}, u32[]{:S(2)}, u32[]{:S(2)}) collective-permute-start(f32[1,16,27648]{2,1,0:T(8,128)} %copy.215), channel_id=1, source_target_pairs={{8,0},{16,8},{24,16},{9,1},{17,9},{25,17},{10,2},{18,10},{26,18},{... | collective-permute-start | bytes 5308424 | tf_op jit(solution)/shard_map/ppermute | solution.py:35
  705.6 41.2 %copy-start.15 = (f32[1,8,2,27648]{3,2,1,0:T(2,128)S(1)}, f32[1,8,2,27648]{3,2,1,0:T(2,128)}, u32[]{:S(2)}) copy-start(f32[1,8,2,27648]{3,2,1,0:T(2,128)} %copy-done.14) | copy-start | bytes 5308420
  705.6 41.2 %copy-start.42 = (pred[27648]{0:T(1024)(128)(4,1)S(1)}, pred[27648]{0:T(1024)(128)(4,1)}, u32[]{:S(2)}) copy-start(pred[27648]{0:T(1024)(128)(4,1)} %broadcast_compare_fusion.2) | copy-start | bytes 82948
  723.9 22.3 %collective-permute-start.6 = (f32[1,8,27648]{2,0,1:T(1,128)S(1)}, f32[1,8,27648]{2,0,1:T(1,128)S(1)}, u32[]{:S(2)}, u32[]{:S(2)}) collective-permute-start(f32[1,8,27648]{2,0,1:T(1,128)S(1)} %get-tuple-element.77), channel_id=1, source_target_pairs={{0,4},{1,5},{2,6},{3,7},{8,12},{9,13},{10,14},{11,15},{16,20},{17,... | collective-permute-start | bytes 2654216 | tf_op jit(solution)/shard_map/ppermute | solution.py:33
  733.3 69.5 %collective-permute-start.4 = (f32[1,16,27648]{2,1,0:T(8,128)}, f32[1,16,27648]{2,1,0:T(8,128)}, u32[]{:S(2)}, u32[]{:S(2)}) collective-permute-start(f32[1,16,27648]{2,1,0:T(8,128)} %get-tuple-element.73), channel_id=1, source_target_pairs={{0,8},{8,16},{16,24},{1,9},{9,17},{17,25},{2,10},{10,18},{18,26},{... | collective-permute-start | bytes 5308424 | tf_op jit(solution)/shard_map/ppermute | solution.py:33
  895.9 38.6 %copy-start.27 = (f32[27648]{0:T(1024)S(1)}, f32[27648]{0:T(1024)}, u32[]{:S(2)}) copy-start(f32[27648]{0:T(1024)} %sub.385) | copy-start | bytes 331780
  895.9 38.5 %copy-start.31 = (f32[27648]{0:T(1024)S(1)}, f32[27648]{0:T(1024)}, u32[]{:S(2)}) copy-start(f32[27648]{0:T(1024)} %sub.375) | copy-start | bytes 331780
  895.9 38.5 %copy-start.33 = (f32[27648,1]{0,1:T(1,128)S(1)}, f32[27648,1]{0,1:T(1,128)}, u32[]{:S(2)}) copy-start(f32[27648,1]{0,1:T(1,128)} %broadcast.609) | copy-start | bytes 331780
  895.9 38.5 %copy-start.35 = (f32[1,1,12,2304]{3,1,2,0:T(1,128)S(1)}, f32[1,1,12,2304]{3,1,2,0:T(1,128)}, u32[]{:S(2)}) copy-start(f32[1,1,12,2304]{3,1,2,0:T(1,128)} %copy.141) | copy-start | bytes 331780
  895.9 38.5 %copy-start.37 = (f32[1,1,12,2304]{3,1,2,0:T(1,128)S(1)}, f32[1,1,12,2304]{3,1,2,0:T(1,128)}, u32[]{:S(2)}) copy-start(f32[1,1,12,2304]{3,1,2,0:T(1,128)} %copy.142) | copy-start | bytes 331780
  895.9 38.5 %copy-start.38 = (f32[1,1,12,2304]{3,1,2,0:T(1,128)S(1)}, f32[1,1,12,2304]{3,1,2,0:T(1,128)}, u32[]{:S(2)}) copy-start(f32[1,1,12,2304]{3,1,2,0:T(1,128)} %copy.143) | copy-start | bytes 331780
  895.9 38.5 %copy-start.41 = (f32[27648]{0:T(1024)S(1)}, f32[27648]{0:T(1024)}, u32[]{:S(2)}) copy-start(f32[27648]{0:T(1024)} %sub.380) | copy-start | bytes 331780
  (84 other events, 1091.7 us)
where the time goes:
time: 973 us; the launch traced here: 963 us
  matrix products  474 us (49%)
  local copies, waits for them, and re-layouts  323 us (33%)
  blocking collectives  58.8 us (6%)
  other arithmetic  58.5 us (6%)
  waiting for transfers between devices  22.3 us (2%)
  starting transfers between devices  22 us (2%)
    dot_general x2, matrix products, advance(): jnp.einsum('ij,ejzv->eizv', derivative, grouped, precision=HIGHEST_PRECIS...  103 us
    unnamed x233, local copies, waits for them, and re-layouts  100 us
    slice x4, local copies, waits for them, and re-layouts, shift_velocity(): shifted = jnp.concatenate([field_entries[..., offset:], padding], -1)  54.8 us
    dot_general x2, matrix products, advance(): jnp.einsum('ij,rejv->reiv', derivative, grouped, precision=HIGHEST_PRECIS...  53.2 us
    dot_general x3, matrix products, gather_moments(): jnp.dot(weighted, heat_basis, precision=HIGHEST_PRECISION, preferred_elem...  52.9 us
    psum x5, blocking collectives, gather_moments(): integral_sums_table, bound_sums = lax.psum((partials, bound_sums), 'vert')  50.1 us
    dot_general x2, matrix products, advance(): jnp.einsum('j,rejv->rev', end_right, grouped, precision=HIGHEST_PRECISION)  41.5 us
    dot_general x3, matrix products, gather_moments(): jnp.dot(flat, moment_basis, precision=HIGHEST_PRECISION, preferred_elemen...  37.6 us
  transfers between devices with their start and end apart: 8, of which 2 were waited for; matrix products, arithmetic and copies ran while one was open for 49% of the time, Pallas kernels for 0%

commit v1 on v0

v1 whole, which is shorter than its diff:
```python
import math

import jax
import jax.numpy as jnp
import ml_dtypes
import numpy as np
from jax import lax
from jax.experimental import pallas as pl
from jax.experimental.pallas import tpu as pltpu
from jax.sharding import PartitionSpec as P

NODES = 8
NVR = 48
NVT = 48
NVZ = 48
STEPS = 2

ELEMENT_WIDTH = 4.0
TIME_STEP = 0.001
KNUDSEN = 0.005
VISCOUS_RATIO = 2.0 / 3.0
SAT_DENSITY = 1.5
SPEED_LIMIT = 5.0

PLANE = NVR * NVT
HALF = PLANE // 2
LOCAL_Z = 2 * NODES
NODE_COUNT = NODES * LOCAL_Z
TILE = 256
WINDOW = 512
GHOST_ROWS = 32
MOMENTS = 16
F32 = jnp.float32
BF16 = jnp.bfloat16
PIECES = [(t, TILE, 0) for t in range(0, 1024, TILE)] + [(1024, 128, 0), (1152, 128, 1)] + [
    (t, TILE, 1) for t in range(1280, PLANE, TILE)
]


def legendre_pair(position, point_count):
    previous = 1.0
    current = position
    for degree in range(2, point_count + 1):
        previous, current = (
            current,
            ((2 * degree - 1) * position * current - (degree - 1) * previous) / degree,
        )
    slope = point_count * (position * current - previous) / (position * position - 1.0)
    return (current, slope)


def dg_tables(point_count):
    point_list = []
    weight_list = []
    for number in range(point_count):
        position = math.cos(math.pi * (number + 0.75) / (point_count + 0.5))
        for sweep in range(60):
            value, slope = legendre_pair(position, point_count)
            position = position - value / slope
        value, slope = legendre_pair(position, point_count)
        point_list.append(position)
        weight_list.append(2.0 / ((1.0 - position * position) * slope * slope))
    point_list = point_list[::-1]
    weight_list = weight_list[::-1]
    points = np.array(point_list)
    derivative = np.zeros((point_count, point_count))
    right = np.zeros(point_count)
    left = np.zeros(point_count)
    products = [
        np.prod([points[i] - points[j] for j in range(point_count) if j != i])
        for i in range(point_count)
    ]
    for i in range(point_count):
        others = [j for j in range(point_count) if j != i]
        derivative[i, i] = sum(1.0 / (points[i] - points[j]) for j in others)
        for j in others:
            derivative[i, j] = products[i] / products[j] / (points[i] - points[j])
        right[i] = np.prod([1.0 - points[j] for j in others]) / products[i]
        left[i] = np.prod([-1.0 - points[j] for j in others]) / products[i]
    return points, np.array(weight_list), derivative, right, left


def speed_grid(point_count):
    return -SPEED_LIMIT + (np.arange(point_count) + 0.5) * (2.0 * SPEED_LIMIT / point_count)


POINTS, QUAD, DERIV, END_R, END_L = dg_tables(NODES)
LIFT_R = END_R / QUAD
LIFT_L = END_L / QUAD
GRID_R = speed_grid(NVR)
GRID_T = speed_grid(NVT)
GRID_Z = speed_grid(NVZ)
STEP_V = 2 * SPEED_LIMIT / NVR
WEIGHT = STEP_V**3 / (2 * math.pi) ** 1.5
HALF_FLUX = float(
    WEIGHT
    * np.sum(np.exp(-(GRID_R**2) / 2))
    * np.sum(np.exp(-(GRID_T**2) / 2))
    * np.sum(np.maximum(GRID_Z, 0.0) * np.exp(-(GRID_Z**2) / 2))
)
SCALE = TIME_STEP * 2.0 / ELEMENT_WIDTH


def transport_tables():
    ident = np.eye(NODES)
    up = DERIV + np.outer(LIFT_L, END_L)
    down = DERIV - np.outer(LIFT_R, END_R)
    zero = np.zeros((NODES, NODES))
    wide = np.eye(LOCAL_Z)
    radial = np.stack([np.kron(down, wide), np.kron(up, wide), np.kron(DERIV, wide)])
    zup = np.block([[up, zero], [-np.outer(LIFT_L, END_R), up]])
    zdown = np.block([[down, np.outer(LIFT_R, END_L)], [zero, down]])
    zout = np.block([[down, np.outer(LIFT_R, END_L)], [zero, DERIV]])
    axial = np.stack([np.kron(ident, zdown), np.kron(ident, zup), np.kron(ident, zout)])
    ghost_r = np.zeros((2, NODE_COUNT, 128))
    ghost_z = np.zeros((2, NODE_COUNT, 128))
    for r in range(NODES):
        for z in range(LOCAL_Z):
            n = r * LOCAL_Z + z
            ghost_r[0, n, z] = -LIFT_R[r]
            ghost_r[1, n, z] = LIFT_L[r]
            if z >= NODES:
                ghost_z[0, n, LOCAL_Z + r] = LIFT_R[z - NODES]
            else:
                ghost_z[1, n, LOCAL_Z + r] = LIFT_L[z]
    trace = np.zeros((2, 2, GHOST_ROWS, NODE_COUNT))
    for side in range(2):
        radial_row = END_R if side == 1 else END_L
        for place in range(2):
            for z in range(LOCAL_Z):
                for r in range(NODES):
                    trace[side, place, z, r * LOCAL_Z + z] = radial_row[r]
            for r in range(NODES):
                for k in range(NODES):
                    if place == 0:
                        trace[side, place, LOCAL_Z + r, r * LOCAL_Z + NODES + k] = END_R[k]
                    else:
                        trace[side, place, LOCAL_Z + r, r * LOCAL_Z + k] = END_L[k]
    return (
        (-SCALE * radial).astype(ml_dtypes.bfloat16),
        (-SCALE * axial).astype(np.float32),
        (SCALE * ghost_r).astype(np.float32),
        (SCALE * ghost_z).astype(np.float32),
        trace.astype(ml_dtypes.bfloat16),
    )


def rotation_table():
    full = np.zeros((PLANE + 2 * TILE, PLANE))
    factor = TIME_STEP / (2 * STEP_V)
    for a in range(NVR):
        for b in range(NVT):
            n = a * NVT + b
            first = factor * GRID_T[b] * GRID_T[b]
            second = factor * GRID_R[a] * GRID_T[b]
            if a + 1 < NVR:
                full[TILE + n + NVT, n] = -first
            if a > 0:
                full[TILE + n - NVT, n] = first
            if b + 1 < NVT:
                full[TILE + n + 1, n] = second
            if b > 0:
                full[TILE + n - 1, n] = -second
    tiles = [full[TILE + t - 128 : TILE + t - 128 + WINDOW, t : t + TILE] for t in range(0, PLANE, TILE)]
    return np.stack(tiles).astype(ml_dtypes.bfloat16)


def mirror_table():
    table = np.zeros((HALF, HALF))
    groups = NVR // 2
    for g in range(groups):
        for b in range(NVT):
            table[(groups - 1 - g) * NVT + b, g * NVT + b] = 1.0
    return table.astype(ml_dtypes.bfloat16)


def plane_rows():
    vr = np.repeat(GRID_R, NVT)
    vt = np.tile(GRID_T, NVR)
    rows = np.zeros((8, PLANE))
    rows[0] = vr
    rows[1] = vt
    rows[2] = np.exp(-(vr**2 + vt**2) / 2)
    return rows.astype(np.float32)


def edge_table():
    table = np.zeros((2, NODE_COUNT, 128))
    for r in range(NODES):
        for k in range(NODES):
            table[0, r * LOCAL_Z + k, r] = END_L[k]
            table[1, r * LOCAL_Z + NODES + k, r] = END_R[k]
    return table.astype(np.float32)


def node_columns():
    table = np.zeros((NODE_COUNT, 128))
    for r in range(NODES):
        table[r * LOCAL_Z : (r + 1) * LOCAL_Z, :] = (1.0 + POINTS[r]) / 2
    return table.astype(np.float32)


RADIAL_M, AXIAL_M, GHOST_R, GHOST_Z, TRACE_M = transport_tables()
ROTATION_M = rotation_table()
MIRROR_M = mirror_table()
ROWS = plane_rows()
EDGE = edge_table()
NODE_POS = node_columns()


def slot_speed(ints, slot):
    return (ints[slot].astype(F32) + 0.5) * (2 * SPEED_LIMIT / NVZ) - SPEED_LIMIT


def macroscopic_of(m):
    rho = m(0)
    inv = 1.0 / rho
    ur, ut, uz = m(1) * inv, m(2) * inv, m(3) * inv
    rr, tt, rt, zz, rz, tz = (m(k) for k in range(4, 10))
    energy = rr + tt + zz
    speed = ur * ur + ut * ut + uz * uz
    temp = (energy * inv - speed) * (1.0 / 3.0)
    tail = 2.0 * rho * speed - energy
    qr = 0.5 * (m(10) - 2.0 * (ur * rr + ut * rt + uz * rz) + ur * tail)
    qt = 0.5 * (m(11) - 2.0 * (ur * rt + ut * tt + uz * tz) + ut * tail)
    qz = 0.5 * (m(12) - 2.0 * (ur * rz + ut * tz + uz * zz) + uz * tail)
    return rho, ur, ut, uz, temp, qr, qt, qz


def add_speed_sums(field, vz, sums):
    one = field * vz
    two = one * vz
    return [
        sums[0] + field,
        sums[1] + one,
        sums[2] + two,
        sums[3] + two * vz,
        sums[4] + field * jnp.abs(vz),
    ]


def finish_moments(sums_ref, rows_ref, table_ref, out_ref):
    lane = lax.broadcasted_iota(jnp.int32, (LOCAL_Z, 128), 1)

    def one_radius(r, carry):
        acc = [jnp.zeros((LOCAL_Z, 128), F32) for _ in range(14)]
        for j in range(PLANE // 128):
            at = pl.ds(j * 128, 128)
            vr = rows_ref[0:1, at]
            vt = rows_ref[1:2, at]
            g0, g1, g2, g3, g4 = (sums_ref[k, r, :, at] for k in range(5))
            a = vr * g0
            b = vt * g0
            aa = vr * a
            bb = vt * b
            c = vr * g1
            d = vt * g1
            perp = aa + bb + g2
            new = [g0, a, b, g1, aa, bb, vr * b, g2, c, d, vr * perp, vt * perp, vr * c + vt * d + g3, g4]
            acc = [x + y for x, y in zip(acc, new)]
        block = jnp.zeros((LOCAL_Z, 128), F32)
        for k in range(14):
            block = jnp.where(lane == k, WEIGHT * jnp.sum(acc[k], axis=1, keepdims=True), block)
        table_ref[pl.ds(pl.multiple_of(r * LOCAL_Z, LOCAL_Z), LOCAL_Z), :] = block
        return carry

    lax.fori_loop(0, NODES, one_radius, 0)
    out_ref[...] = jnp.transpose(table_ref[...])[0:MOMENTS, :]


def send_traces(slot_count, ints, narrow_ref, trace_ref, mirror_ref, right_ref, left_ref, turned_ref, axial_ref, info):
    place = ints[info + 1]
    for s in range(slot_count):
        for first, lanes, side in PIECES:
            got = jnp.dot(
                trace_ref[side, place],
                narrow_ref[s, :, first : first + lanes],
                preferred_element_type=F32,
            )
            if side == 1:
                right_ref[s, :, first - HALF : first - HALF + lanes] = got[0:LOCAL_Z]
            else:
                left_ref[s, :, first : first + lanes] = got[0:LOCAL_Z]
            axial_ref[s, :, first : first + lanes] = got[LOCAL_Z : LOCAL_Z + NODES]

    at_axis = ints[info] == 0

    @pl.when(at_axis)
    def _():
        flat = left_ref[...].reshape(slot_count * LOCAL_Z, HALF).astype(BF16)
        for first in range(0, HALF, 128):
            low = max(0, (HALF - first - 128 - 48) // 128 * 128)
            high = min(HALF, -((first - HALF - 48) // 128) * 128)
            got = jnp.dot(
                flat[:, low:high], mirror_ref[low:high, first : first + 128], preferred_element_type=F32
            )
            turned_ref[:, :, first : first + 128] = got.reshape(slot_count, LOCAL_Z, 128)

    @pl.when(jnp.logical_not(at_axis))
    def _():
        turned_ref[...] = jnp.zeros(turned_ref.shape, F32)


def first_kernel(
    slot_count, info, ints, f_ref, rows_ref, trace_ref, mirror_ref,
    right_ref, left_ref, turned_ref, axial_ref, mom_ref, sums_ref, narrow_ref, table_ref,
):
    step = pl.program_id(0)

    @pl.when(step == 0)
    def _():
        sums_ref[...] = jnp.zeros(sums_ref.shape, F32)

    speeds = [slot_speed(ints, step * slot_count + s) for s in range(slot_count)]

    def one_radius(r, carry):
        for j in range(PLANE // 128):
            at = pl.ds(j * 128, 128)
            sums = [sums_ref[k, r, :, at] for k in range(5)]
            for s in range(slot_count):
                field = f_ref[r, :, pl.ds(s * PLANE + j * 128, 128)]
                sums = add_speed_sums(field, speeds[s], sums)
                narrow_ref[s, pl.ds(pl.multiple_of(r * LOCAL_Z, LOCAL_Z), LOCAL_Z), at] = field.astype(BF16)
            for k in range(5):
                sums_ref[k, r, :, at] = sums[k]
        return carry

    lax.fori_loop(0, NODES, one_radius, 0)
    send_traces(
        slot_count, ints, narrow_ref, trace_ref, mirror_ref, right_ref, left_ref, turned_ref, axial_ref, info
    )

    @pl.when(step == pl.num_programs(0) - 1)
    def _():
        finish_moments(sums_ref, rows_ref, table_ref, mom_ref)


def total_of(parts):
    while len(parts) > 1:
        parts = [parts[k] + parts[k + 1] for k in range(0, len(parts), 2)]
    return parts[0]


def step_kernel(slot_count, info, part_count, last, ints, *refs):
    part_refs, refs = refs[:part_count], refs[part_count:]
    (
        f_ref, in_left_ref, in_turned_ref, in_right_ref, in_axial_ref,
        rows_ref, pos_ref, edge_ref, radial_ref, axial_m_ref, ghost_r_ref, ghost_z_ref, rot_ref,
    ) = refs[:13]
    refs = refs[13:]
    if last:
        (out_ref, mom_ref), refs = refs[:2], refs[2:]
    else:
        (trace_ref, mirror_ref), refs = refs[:2], refs[2:]
        (out_ref, right_ref, left_ref, turned_ref, axial_ref, mom_ref), refs = refs[:6], refs[6:]
    (
        plane_ref, node_ref, wall_ref, slot_ref, sums_ref, work_ref, pad_ref, lhs_ref, ghost_ref, narrow_ref, table_ref,
    ) = refs
    step = pl.program_id(0)
    row = ints[info]
    place = ints[info + 1]
    code_bottom = ints[info + 2]
    code_top = ints[info + 3]
    last_row = ints[info + 4]

    @pl.when(step == 0)
    def _():
        sums_ref[...] = jnp.zeros(sums_ref.shape, F32)
        pad_ref[:, 0:128] = jnp.zeros((NODE_COUNT, 128), BF16)
        pad_ref[:, 128 + PLANE :] = jnp.zeros((NODE_COUNT, 128), BF16)
        total = total_of([p[...] for p in part_refs])
        wide = jnp.concatenate([total, jnp.zeros((128 - MOMENTS, 128), F32)], axis=0)
        table_ref[...] = jnp.transpose(wide)
        rho, ur, ut, uz, temp, qr, qt, qz = macroscopic_of(lambda k: table_ref[:, k : k + 1])
        inv_t = 1.0 / temp
        beta = ((1.0 - VISCOUS_RATIO) / 5.0) / (rho * temp * temp)
        kappa = rho * (TIME_STEP / KNUDSEN)
        peak = kappa * rho * inv_t * jnp.sqrt(inv_t)
        columns = [uz, -0.5 * inv_t, qz * beta, inv_t, peak, 1.0 - kappa, ur, ut, qr * beta, qt * beta]
        for k, column in enumerate(columns):
            node_ref[k] = jnp.broadcast_to(column, (NODE_COUNT, 128))
        radius = ELEMENT_WIDTH * (row.astype(F32) + pos_ref[...])
        node_ref[10] = 1.0 / radius
        net = table_ref[:, 3:4]
        gross = table_ref[:, 13:14]
        to_bottom = 0.5 * (gross - net)
        to_top = 0.5 * (gross + net)
        incident = jnp.sum(edge_ref[0] * to_bottom, axis=0, keepdims=True)
        upward = jnp.sum(edge_ref[1] * to_top, axis=0, keepdims=True)
        bottom = jnp.where(code_bottom == 1, SAT_DENSITY, incident * (1.0 / HALF_FLUX))
        top = jnp.where(code_top == 2, 0.0, upward * (1.0 / HALF_FLUX))
        density = jnp.where(place == 0, bottom, top)
        square = jnp.transpose(jnp.broadcast_to(density, (128, 128)))
        wall_ref[...] = square[0:NODES, :]

        def one_radius(r, carry):
            rows = pl.ds(pl.multiple_of(r * LOCAL_Z, LOCAL_Z), LOCAL_Z)
            n_half, n_inv = node_ref[1, rows, :], node_ref[3, rows, :]
            n_ur, n_ut = node_ref[6, rows, :], node_ref[7, rows, :]
            n_qr, n_qt = node_ref[8, rows, :], node_ref[9, rows, :]
            for j in range(PLANE // 128):
                at = pl.ds(j * 128, 128)
                cr = rows_ref[0:1, at] - n_ur
                ct = rows_ref[1:2, at] - n_ut
                square = cr * cr + ct * ct
                gauss = jnp.exp(square * n_half)
                along = cr * n_qr + ct * n_qt
                reach = square * n_inv - 5.0
                plane_ref[0, rows, at] = gauss
                plane_ref[1, rows, at] = gauss * along
                plane_ref[2, rows, at] = gauss * reach
                plane_ref[3, rows, at] = gauss * along * reach
            return carry

        lax.fori_loop(0, NODES, one_radius, 0)

    speeds = [slot_speed(ints, step * slot_count + s) for s in range(slot_count)]
    kind_minus = jnp.where(row == last_row, 2, 0)
    kind_out = jnp.where(jnp.logical_and(place == 1, code_top == 2), 2, 0)

    for s in range(slot_count):
        vz = speeds[s]
        positive = vz > 0
        cz = vz - node_ref[0]
        lam = node_ref[4] * jnp.exp(cz * cz * node_ref[1])
        alpha = cz * node_ref[2]
        reach = cz * cz * node_ref[3]
        slot_ref[s, 0] = lam * (1.0 + alpha * reach)
        slot_ref[s, 1] = lam * reach
        slot_ref[s, 2] = lam * alpha
        slot_ref[s, 3] = lam

        sign = jnp.where(positive, 1, 0)
        kind = jnp.where(positive, 1, kind_out)
        lhs_ref[0] = (vz * axial_m_ref[kind]).astype(BF16)
        lean = jnp.abs(vz) * ghost_z_ref[sign]
        lhs_ref[1] = (ghost_r_ref[0] + lean).astype(BF16)
        lhs_ref[2] = (ghost_r_ref[1] + lean).astype(BF16)

        own = (place == 0) == positive
        strength = jnp.exp(-0.5 * vz * vz + jnp.zeros((NODES, 128), F32)) * wall_ref[...]
        for j in range(PLANE // 128):
            at = pl.ds(j * 128, 128)
            vr = rows_ref[0:1, at]
            if j * 128 < HALF:
                radial = in_right_ref[s, :, at]
            else:
                back = pl.ds(j * 128 - HALF, 128)
                radial = in_left_ref[s, :, back] + in_turned_ref[s, :, back]
            wall = strength * rows_ref[2:3, at]
            axial = jnp.where(own, wall, in_axial_ref[s, :, at])
            rows = jnp.concatenate([vr * radial, axial, jnp.zeros((8, 128), F32)], axis=0)
            ghost_ref[:, at] = rows.astype(BF16)

        inverse = node_ref[10]
        for j in range(PLANE // 128):
            at = pl.ds(s * PLANE + j * 128, 128)
            field = f_ref[:, :, at].reshape(NODE_COUNT, 128)
            pad_ref[:, 128 + j * 128 : 256 + j * 128] = (field * inverse).astype(BF16)

        lane = lax.broadcasted_iota(jnp.int32, (NODE_COUNT, 128), 1)
        for first, lanes, side in PIECES:
            tile = first // TILE
            inside = first - tile * TILE
            field = f_ref[:, :, s * PLANE + first : s * PLANE + first + lanes].reshape(NODE_COUNT, lanes)
            narrow = field.astype(BF16)
            moved = (field * rows_ref[0:1, first : first + lanes]).astype(BF16)
            start = tile * TILE
            edge = jnp.where(lane < GHOST_ROWS, lhs_ref[1 + side], pad_ref[:, start : start + 128])
            left = jnp.concatenate(
                [radial_ref[1] if side else radial_ref[kind_minus], lhs_ref[0], edge, pad_ref[:, start + 128 : start + WINDOW]],
                axis=1,
            )
            right = jnp.concatenate(
                [
                    moved,
                    narrow,
                    ghost_ref[:, first : first + lanes],
                    rot_ref[tile, GHOST_ROWS:, inside : inside + lanes],
                ],
                axis=0,
            )
            work_ref[s, :, first : first + lanes] = jnp.dot(left, right, preferred_element_type=F32)

    def update(r, carry):
        rows = pl.ds(pl.multiple_of(r * LOCAL_Z, LOCAL_Z), LOCAL_Z)
        keep = node_ref[5, rows, :]
        factor = [[slot_ref[s, k, rows, :] for k in range(4)] for s in range(slot_count)]
        for j in range(PLANE // 128):
            at = pl.ds(j * 128, 128)
            planes = [plane_ref[k, rows, at] for k in range(4)]
            sums = [sums_ref[k, r, :, at] for k in range(5)]
            for s in range(slot_count):
                here = pl.ds(s * PLANE + j * 128, 128)
                new = f_ref[r, :, here] * keep + work_ref[s, rows, at]
                for k in range(4):
                    new = new + planes[k] * factor[s][k]
                out_ref[r, :, here] = new
                sums = add_speed_sums(new, speeds[s], sums)
                if not last:
                    narrow_ref[s, rows, at] = new.astype(BF16)
            for k in range(5):
                sums_ref[k, r, :, at] = sums[k]
        return carry

    lax.fori_loop(0, NODES, update, 0)
    if not last:
        send_traces(
            slot_count, ints, narrow_ref, trace_ref, mirror_ref, right_ref, left_ref, turned_ref, axial_ref, info
        )

    @pl.when(step == pl.num_programs(0) - 1)
    def _():
        finish_moments(sums_ref, rows_ref, table_ref, mom_ref)


def last_kernel(info, part_count, ints, *refs):
    total_ref = total_of([p[...] for p in refs[:part_count]])
    edge_ref, macro_ref, flux_ref = refs[part_count:]
    values = macroscopic_of(lambda k: total_ref[k : k + 1, :])
    for k in range(8):
        macro_ref[k : k + 1, :] = values[k]
    net, gross = total_ref[3:4, :], total_ref[13:14, :]
    to_bottom = jnp.broadcast_to(0.5 * (gross - net), (8, 128))
    to_top = jnp.broadcast_to(0.5 * (gross + net), (8, 128))
    dot = lambda x, y: jnp.dot(x, y, precision=lax.Precision.HIGHEST, preferred_element_type=F32)
    incident = dot(to_bottom, edge_ref[0])
    upward = dot(to_top, edge_ref[1])
    downward = dot(to_bottom, edge_ref[1])
    bottom = jnp.where(ints[info + 2] == 1, SAT_DENSITY * HALF_FLUX - incident, 0.0)
    top = jnp.where(ints[info + 3] == 2, upward - downward, 0.0)
    flux_ref[...] = jnp.where(ints[info + 1] == 0, bottom, top)


def whole(shape):
    return pl.BlockSpec(shape, lambda *a: (0,) * len(shape), pipeline_mode=pl.Buffered(1))


def on_device(distribution, z_order, edge_codes):
    local_r, local_z, vdev = distribution.shape
    assert local_r == NODES and local_z == LOCAL_Z
    slots = vdev // PLANE
    group = math.gcd(slots, 3)
    steps = slots // group
    rows_total = lax.axis_size("row")
    places = lax.axis_size("gz")
    verts = lax.axis_size("vert")
    assert places == 2
    info = slots
    ints = jnp.concatenate(
        [
            z_order,
            jnp.stack(
                [
                    lax.axis_index("row"),
                    lax.axis_index("gz"),
                    edge_codes[0, 0],
                    edge_codes[1, 0],
                    jnp.int32(rows_total - 1),
                ]
            ),
        ]
    )
    rows, pos, edge = jnp.asarray(ROWS), jnp.asarray(NODE_POS), jnp.asarray(EDGE)
    radial_m, axial_m = jnp.asarray(RADIAL_M), jnp.asarray(AXIAL_M)
    ghost_r, ghost_z = jnp.asarray(GHOST_R), jnp.asarray(GHOST_Z)
    trace_m, mirror_m, rot_m = jnp.asarray(TRACE_M), jnp.asarray(MIRROR_M), jnp.asarray(ROTATION_M)

    big = pl.BlockSpec((NODES, LOCAL_Z, group * PLANE), lambda i, n: (0, 0, i))
    radial_spec = pl.BlockSpec((group, LOCAL_Z, HALF), lambda i, n: (i, 0, 0))
    axial_spec = pl.BlockSpec((group, NODES, PLANE), lambda i, n: (i, 0, 0))
    mom_spec = whole((MOMENTS, 128))
    radial_shape = jax.ShapeDtypeStruct((slots, LOCAL_Z, HALF), F32)
    axial_shape = jax.ShapeDtypeStruct((slots, NODES, PLANE), F32)
    mom_shape = jax.ShapeDtypeStruct((MOMENTS, 128), F32)
    big_shape = jax.ShapeDtypeStruct(distribution.shape, F32)
    trace_specs = [radial_spec, radial_spec, radial_spec, axial_spec, mom_spec]
    trace_shapes = [radial_shape, radial_shape, radial_shape, axial_shape, mom_shape]
    sums_scratch = pltpu.VMEM((5, NODES, LOCAL_Z, PLANE), F32)
    narrow_scratch = pltpu.VMEM((group, NODE_COUNT, PLANE), BF16)
    table_scratch = pltpu.VMEM((NODE_COUNT, 128), F32)
    params = pltpu.CompilerParams(vmem_limit_bytes=56 * 1024 * 1024)

    def start(f):
        return pl.pallas_call(
            lambda *a: first_kernel(group, info, *a),
            grid_spec=pltpu.PrefetchScalarGridSpec(
                num_scalar_prefetch=1,
                grid=(steps,),
                in_specs=[big] + [whole(x.shape) for x in (rows, trace_m, mirror_m)],
                out_specs=trace_specs,
                scratch_shapes=[sums_scratch, narrow_scratch, table_scratch],
            ),
            out_shape=trace_shapes,
            compiler_params=params,
            name="moments_and_traces",
        )(ints, f, rows, trace_m, mirror_m)

    def advance(f, parts, left, turned, right, axial, last):
        tables = [rows, pos, edge, radial_m, axial_m, ghost_r, ghost_z, rot_m]
        if not last:
            tables += [trace_m, mirror_m]
        return pl.pallas_call(
            lambda *a: step_kernel(group, info, len(parts), last, *a),
            grid_spec=pltpu.PrefetchScalarGridSpec(
                num_scalar_prefetch=1,
                grid=(steps,),
                in_specs=[mom_spec] * len(parts)
                + [big, radial_spec, radial_spec, radial_spec, axial_spec]
                + [whole(x.shape) for x in tables],
                out_specs=[big] + ([mom_spec] if last else trace_specs),
                scratch_shapes=[
                    pltpu.VMEM((4, NODE_COUNT, PLANE), F32),
                    pltpu.VMEM((11, NODE_COUNT, 128), F32),
                    pltpu.VMEM((NODES, 128), F32),
                    pltpu.VMEM((group, 4, NODE_COUNT, 128), F32),
                    sums_scratch,
                    pltpu.VMEM((group, NODE_COUNT, PLANE), F32),
                    pltpu.VMEM((NODE_COUNT, PLANE + 256), BF16),
                    pltpu.VMEM((3, NODE_COUNT, 128), BF16),
                    pltpu.VMEM((GHOST_ROWS, PLANE), BF16),
                    narrow_scratch,
                    table_scratch,
                ],
            ),
            out_shape=[big_shape] + ([mom_shape] if last else trace_shapes),
            compiler_params=params,
            name="last_step" if last else "step",
        )(ints, *parts, f, left, turned, right, axial, *tables)

    def spread(moments):
        parts = [moments]
        for shift in range(1, verts):
            parts.append(lax.ppermute(moments, "vert", [(i, i ^ shift) for i in range(verts)]))
        return parts

    def halo(right, left, axial):
        from_left = lax.ppermute(right, "row", [(i, i + 1) for i in range(rows_total - 1)])
        from_right = lax.ppermute(left, "row", [(i + 1, i) for i in range(rows_total - 1)])
        from_axial = lax.ppermute(axial, "gz", [(0, 1), (1, 0)])
        return from_left, from_right, from_axial

    right, left, turned, axial, moments = start(distribution)
    current = distribution
    for number in range(STEPS):
        from_left, from_right, from_axial = halo(right, left, axial)
        parts = spread(moments)
        last = number == STEPS - 1
        out = advance(current, parts, from_left, turned, from_right, from_axial, last)
        if last:
            current, moments = out
        else:
            current, right, left, turned, axial, moments = out
    parts = spread(moments)
    macro, flux = pl.pallas_call(
        lambda *a: last_kernel(info, len(parts), *a),
        grid_spec=pltpu.PrefetchScalarGridSpec(
            num_scalar_prefetch=1,
            grid=(1,),
            in_specs=[mom_spec] * len(parts) + [whole(edge.shape)],
            out_specs=[whole((8, 128)), whole((8, 128))],
        ),
        out_shape=[jax.ShapeDtypeStruct((8, 128), F32), jax.ShapeDtypeStruct((8, 128), F32)],
        name="macroscopic",
    )(ints, *parts, edge)
    return (current, macro.reshape(8, local_r, local_z), flux[0:1, 0:local_r])


def solution(mesh):
    in_specs = (P("row", "gz", "vert"), P("vert"), P(None, "row"))
    out_specs = (P("row", "gz", "vert"), P(None, "row", "gz"), P("gz", "row"))
    return jax.shard_map(
        on_device, mesh=mesh, in_specs=in_specs, out_specs=out_specs, check_vma=False
    )
```

time: 973 us -> 151 us (0.16)
  matrix products: 474 us -> 0 us
  local copies, waits for them, and re-layouts: 323 us -> 9.41 us
  Pallas kernels: 0 us -> 79.2 us
  blocking collectives: 58.8 us -> 0 us
  other arithmetic: 58.5 us -> 0 us
  waiting for transfers between devices: 22.3 us -> 34.9 us
    dot_general x30 -> x0, matrix products: 474 us -> none  [the longest x2 103 us: advance(): jnp.einsum('ij,ejzv->eizv', derivative, grouped, precision=HIGHEST_PRECIS...]
    unnamed x233 -> x30, local copies, waits for them, and re-layouts: 100 us -> 3.05 us
    pallas_call x0 -> x4, Pallas kernels: none -> 79.2 us  [the longest x2 62.3 us: advance(): pl.pallas_call(lambda *a: step_kernel(group, info, len(parts), last, *a),...]
    slice x12 -> x2, local copies, waits for them, and re-layouts: 79.7 us -> 2.49 us  [the longest x1 1.31 us: on_device(): edge_codes[1, 0]]
    psum x6 -> x0, blocking collectives: 58.8 us -> none  [the longest x5 50.1 us: gather_moments(): integral_sums_table, bound_sums = lax.psum((partials, bound_sums), 'vert')]
    mul x26 -> x0, local copies, waits for them, and re-layouts: 45.9 us -> none  [the longest x2 36.6 us: advance(): 2.0 / ELEMENT_WIDTH * vel_z]
    select_n x15 -> x0, other arithmetic: 35.4 us -> none  [the longest x2 7.87 us: advance(): face_values = jnp.where(vel_z > 0, plus_side, minus_side)]
    another operation x18 -> x0, local copies, waits for them, and re-layouts: 19.7 us -> none  [the longest x2 9.07 us: advance(): trace_lo[0].reshape(local_z, slot_count, NVR, NVT)[:, :, ::-1, :]]
  transfers between devices with their start and end apart: 8 -> 15, of which waited for: 2 -> 10; matrix products, arithmetic and copies ran while one was open for 49% -> 0% of each run, Pallas kernels for 0% -> 0%
where the time goes in v1:
time: 151 us; the launch traced here: 150 us
  Pallas kernels  79.2 us (52%)
  waiting for transfers between devices  34.9 us (23%)
  starting transfers between devices  25.9 us (17%)
  local copies, waits for them, and re-layouts  9.41 us (6%)
    pallas_call x2, Pallas kernels, advance(): pl.pallas_call(lambda *a: step_kernel(group, info, len(parts), last, *a),...  62.3 us
    ppermute x2, waiting for transfers between devices, halo(): from_axial = lax.ppermute(axial, 'gz', [(0, 1), (1, 0)])  19.1 us
    ppermute x9, waiting for transfers between devices, spread(): lax.ppermute(moments, 'vert', [(i, i ^ shift) for i in range(verts)])  15.8 us
    pallas_call x1, Pallas kernels, start(): pl.pallas_call(lambda *a: first_kernel(group, info, *a), grid_spec=pltpu....  14.5 us
    ppermute x9, starting transfers between devices, spread(): lax.ppermute(moments, 'vert', [(i, i ^ shift) for i in range(verts)])  11.7 us
    ppermute x2, starting transfers between devices, halo(): lax.ppermute(left, 'row', [(i + 1, i) for i in range(rows_total - 1)])  7.28 us
    ppermute x2, starting transfers between devices, halo(): lax.ppermute(right, 'row', [(i, i + 1) for i in range(rows_total - 1)])  3.83 us
    ppermute x2, starting transfers between devices, halo(): from_axial = lax.ppermute(axial, 'gz', [(0, 1), (1, 0)])  3.1 us
  transfers between devices with their start and end apart: 15, of which 10 were waited for; matrix products, arithmetic and copies ran while one was open for 0% of the time, Pallas kernels for 0%

profile of v1, /device:TPU:4, one launch (start us, length us, event | category | flops | bytes accessed | tf_op | source)
XLA Modules:
  0.0 150.2 jit_solution(11161859875369871305)
XLA Ops:
  0.6 1.3 fusion
  1.9 2.5 %concatenate.3.a_0_ = s32[17]{0:T(128)} concatenate(s32[12]{0:T(128)} %param.14, s32[1]{0:T(128)} %bitcast, s32[1]{0:T(128)} %bitcast.1, s32[1]{0:T(128)} %bitcast.2, s32[1]{0:T(128)} %bitcast.3, s32[1]{0:T(128)} %constant.31.clone.1), dimensions={0} | concatenate | bytes 136 | tf_op jit(solution)/shard_map/concatenate | solution.py:550
  4.5 14.5 %moments_and_traces.1 = (f32[12,16,1152]{2,1,0:T(8,128)}, f32[12,16,1152]{2,1,0:T(8,128)}, f32[12,16,1152]{2,1,0:T(8,128)}, f32[12,8,2304]{2,1,0:T(8,128)}, f32[16,128]{1,0:T(8,128)}) custom-call(s32[17]{0:T(128)} %concatenate.3.a_0_, f32[8,16,27648]{2,1,0:T(8,128)} %a_5_.2, f32[8,2304]{1,0:T(8,128)} %constant.32.clone.a_2_.a_10_, ...), custom_call_target="tpu_custom_call" | custom-call | tf_op jit(solution)/shard_map/moments_and_traces/pallas_call | solution.py:585
  18.9 1.9 %collective-permute-start.3 = (f32[12,16,1152]{2,1,0:T(8,128)}, f32[12,16,1152]{2,1,0:T(8,128)S(1)}, u32[]{:S(2)}, u32[]{:S(2)}) collective-permute-start(f32[12,16,1152]{2,1,0:T(8,128)} %get-tuple-element.19), channel_id=1, source_target_pairs={{0,8},{8,16},{16,24},{1,9},{9,17},{17,25},{2,10},{10,18},{18,26},{... | collective-permute-start | bytes 2654216 | tf_op jit(solution)/shard_map/ppermute | solution.py:638
  20.9 3.6 %collective-permute-start.4 = (f32[12,16,1152]{2,1,0:T(8,128)}, f32[12,16,1152]{2,1,0:T(8,128)S(1)}, u32[]{:S(2)}, u32[]{:S(2)}) collective-permute-start(f32[12,16,1152]{2,1,0:T(8,128)} %get-tuple-element.21), channel_id=1, source_target_pairs={{8,0},{16,8},{24,16},{9,1},{17,9},{25,17},{10,2},{18,10},{26,18},{... | collective-permute-start | bytes 2654216 | tf_op jit(solution)/shard_map/ppermute | solution.py:639
  24.5 1.5 %collective-permute-start.5 = (f32[12,8,2304]{2,1,0:T(8,128)}, f32[12,8,2304]{2,1,0:T(8,128)S(1)}, u32[]{:S(2)}, u32[]{:S(2)}) collective-permute-start(f32[12,8,2304]{2,1,0:T(8,128)} %get-tuple-element.22), channel_id=1, source_target_pairs={{0,4},{4,0},{1,5},{5,1},{2,6},{6,2},{3,7},{7,3},{8,12},{12,8},{9,1... | collective-permute-start | bytes 2654216 | tf_op jit(solution)/shard_map/ppermute | solution.py:640
  26.1 3.6 %collective-permute-start.2 = (f32[16,128]{1,0:T(8,128)}, f32[16,128]{1,0:T(8,128)S(1)}, u32[]{:S(2)}, u32[]{:S(2)}) collective-permute-start(f32[16,128]{1,0:T(8,128)} %get-tuple-element.18.a_1_), channel_id=1, source_target_pairs={{0,3},{1,2},{2,1},{3,0},{4,7},{5,6},{6,5},{7,4},{8,11},{9,10},{10,... | collective-permute-start | bytes 24584 | tf_op jit(solution)/shard_map/ppermute | solution.py:634
  29.7 2.1 %collective-permute-done.2.a_4_ = f32[16,128]{1,0:T(8,128)S(1)} collective-permute-done((f32[16,128]{1,0:T(8,128)}, f32[16,128]{1,0:T(8,128)S(1)}, u32[]{:S(2)}, u32[]{:S(2)}) %collective-permute-start.2) | collective-permute-done | bytes 8224 | tf_op jit(solution)/shard_map/ppermute | solution.py:634
  31.7 2.7 %collective-permute-done.1.a_3_ = f32[16,128]{1,0:T(8,128)S(1)} collective-permute-done((f32[16,128]{1,0:T(8,128)}, f32[16,128]{1,0:T(8,128)S(1)}, u32[]{:S(2)}, u32[]{:S(2)}) %collective-permute-start.1) | collective-permute-done | bytes 8224 | tf_op jit(solution)/shard_map/ppermute | solution.py:634
  34.4 1.2 collective-permute-done.a_2_
  35.6 9.6 %collective-permute-done.5.a_9_ = f32[12,8,2304]{2,1,0:T(8,128)S(1)} collective-permute-done((f32[12,8,2304]{2,1,0:T(8,128)}, f32[12,8,2304]{2,1,0:T(8,128)S(1)}, u32[]{:S(2)}, u32[]{:S(2)}) %collective-permute-start.5) | collective-permute-done | bytes 884768 | tf_op jit(solution)/shard_map/ppermute | solution.py:640
  45.2 0.9 copy-done.5
  46.1 32.9 %step.1 = (f32[8,16,27648]{2,1,0:T(8,128)}, f32[12,16,1152]{2,1,0:T(8,128)}, f32[12,16,1152]{2,1,0:T(8,128)}, f32[12,16,1152]{2,1,0:T(8,128)}, f32[12,8,2304]{2,1,0:T(8,128)}, /*index=5*/f32[16,128]{1,0:T(8,128)}) custom-call(s32[17]{0:T(128)} %concatenate.3.a_0_, f32[16,128]{1,0:T(8,128)} %get-tuple-element.18.a_1_, f32[16,128]{1,0:T(8,128)} %copy-done.11, ...), custom_call_target="tpu_custom_call" | custom-call | tf_op jit(solution)/shard_map/step/pallas_call | solution.py:603
  79.0 1.9 %collective-permute-start.9 = (f32[12,16,1152]{2,1,0:T(8,128)}, f32[12,16,1152]{2,1,0:T(8,128)S(1)}, u32[]{:S(2)}, u32[]{:S(2)}) collective-permute-start(f32[12,16,1152]{2,1,0:T(8,128)} %get-tuple-element.25), channel_id=1, source_target_pairs={{0,8},{8,16},{16,24},{1,9},{9,17},{17,25},{2,10},{10,18},{18,26},{... | collective-permute-start | bytes 2654216 | tf_op jit(solution)/shard_map/ppermute | solution.py:638
  80.9 3.6 %collective-permute-start.10 = (f32[12,16,1152]{2,1,0:T(8,128)}, f32[12,16,1152]{2,1,0:T(8,128)S(1)}, u32[]{:S(2)}, u32[]{:S(2)}) collective-permute-start(f32[12,16,1152]{2,1,0:T(8,128)} %get-tuple-element.27), channel_id=1, source_target_pairs={{8,0},{16,8},{24,16},{9,1},{17,9},{25,17},{10,2},{18,10},{26,18},{... | collective-permute-start | bytes 2654216 | tf_op jit(solution)/shard_map/ppermute | solution.py:639
  84.6 1.6 %collective-permute-start.11 = (f32[12,8,2304]{2,1,0:T(8,128)}, f32[12,8,2304]{2,1,0:T(8,128)S(1)}, u32[]{:S(2)}, u32[]{:S(2)}) collective-permute-start(f32[12,8,2304]{2,1,0:T(8,128)} %get-tuple-element.28), channel_id=1, source_target_pairs={{0,4},{4,0},{1,5},{5,1},{2,6},{6,2},{3,7},{7,3},{8,12},{12,8},{9,1... | collective-permute-start | bytes 2654216 | tf_op jit(solution)/shard_map/ppermute | solution.py:640
  86.1 3.6 %collective-permute-start.8 = (f32[16,128]{1,0:T(8,128)}, f32[16,128]{1,0:T(8,128)S(1)}, u32[]{:S(2)}, u32[]{:S(2)}) collective-permute-start(f32[16,128]{1,0:T(8,128)} %get-tuple-element.23.a_1_), channel_id=1, source_target_pairs={{0,3},{1,2},{2,1},{3,0},{4,7},{5,6},{6,5},{7,4},{8,11},{9,10},{10,... | collective-permute-start | bytes 24584 | tf_op jit(solution)/shard_map/ppermute | solution.py:634
  89.8 2.1 %collective-permute-done.8.a_4_ = f32[16,128]{1,0:T(8,128)S(1)} collective-permute-done((f32[16,128]{1,0:T(8,128)}, f32[16,128]{1,0:T(8,128)S(1)}, u32[]{:S(2)}, u32[]{:S(2)}) %collective-permute-start.8) | collective-permute-done | bytes 8224 | tf_op jit(solution)/shard_map/ppermute | solution.py:634
  91.8 2.7 %collective-permute-done.7.a_3_ = f32[16,128]{1,0:T(8,128)S(1)} collective-permute-done((f32[16,128]{1,0:T(8,128)}, f32[16,128]{1,0:T(8,128)S(1)}, u32[]{:S(2)}, u32[]{:S(2)}) %collective-permute-start.7) | collective-permute-done | bytes 8224 | tf_op jit(solution)/shard_map/ppermute | solution.py:634
  94.5 1.2 collective-permute-done.6.a_2_
  95.7 9.5 %collective-permute-done.11.a_9_ = f32[12,8,2304]{2,1,0:T(8,128)S(1)} collective-permute-done((f32[12,8,2304]{2,1,0:T(8,128)}, f32[12,8,2304]{2,1,0:T(8,128)S(1)}, u32[]{:S(2)}, u32[]{:S(2)}) %collective-permute-start.11) | collective-permute-done | bytes 884768 | tf_op jit(solution)/shard_map/ppermute | solution.py:640
  105.3 0.9 copy-done.4
  106.2 29.4 %last_step.1 = (f32[8,16,27648]{2,1,0:T(8,128)}, f32[16,128]{1,0:T(8,128)}) custom-call(s32[17]{0:T(128)} %concatenate.3.a_0_, f32[16,128]{1,0:T(8,128)} %get-tuple-element.23.a_1_, f32[16,128]{1,0:T(8,128)} %copy-done.10, f32[16,128]{1,0:T(8,128)} %copy-done.8, f32[16,128]{1,0:T(8,128)} %copy-done.6, f32[8,16,27648]{2,1,0:T(8,128)} %get-tuple-element.24.a_5_, ...), custom_call_target="tpu_custom_call" | custom-call | tf_op jit(solution)/shard_map/last_step/pallas_call | solution.py:603
  135.6 3.7 %collective-permute-start.14 = (f32[16,128]{1,0:T(8,128)}, f32[16,128]{1,0:T(8,128)S(1)}, u32[]{:S(2)}, u32[]{:S(2)}) collective-permute-start(f32[16,128]{1,0:T(8,128)} %get-tuple-element.30.a_1_), channel_id=1, source_target_pairs={{0,3},{1,2},{2,1},{3,0},{4,7},{5,6},{6,5},{7,4},{8,11},{9,10},{10,... | collective-permute-start | bytes 24584 | tf_op jit(solution)/shard_map/ppermute | solution.py:634
  139.2 0.8 collective-permute-start.12
  140.0 1.3 collective-permute-done.14.a_4_
  141.3 2.7 %collective-permute-done.13.a_3_ = f32[16,128]{1,0:T(8,128)S(1)} collective-permute-done((f32[16,128]{1,0:T(8,128)}, f32[16,128]{1,0:T(8,128)S(1)}, u32[]{:S(2)}, u32[]{:S(2)}) %collective-permute-start.13) | collective-permute-done | bytes 8224 | tf_op jit(solution)/shard_map/ppermute | solution.py:634
  144.0 0.6 copy-done.13
  144.6 0.6 copy-done.14
  145.2 2.5 %macroscopic.1 = (f32[8,128]{1,0:T(8,128)}, f32[8,128]{1,0:T(8,128)}) custom-call(s32[17]{0:T(128)} %concatenate.3.a_0_, f32[16,128]{1,0:T(8,128)} %get-tuple-element.30.a_1_, f32[16,128]{1,0:T(8,128)} %copy-done.14, f32[16,128]{1,0:T(8,128)} %copy-done.13, f32[16,128]{1,0:T(8,128)} %copy-done.12, f32[2,128,128]{2,1,0:T(8,128)} %constant.34.clone.a_12_.a_5_), custom_call_target="tpu_custom_call" | custom-call | tf_op jit(solution)/shard_map/macroscopic/pallas_call | solution.py:655
  147.7 1.2 slice.11
  148.8 1.4 reshape.9
  (36 shorter events, 0.1 us)
Async XLA Ops:
  18.9 16.6 %collective-permute-start.3 = (f32[12,16,1152]{2,1,0:T(8,128)}, f32[12,16,1152]{2,1,0:T(8,128)S(1)}, u32[]{:S(2)}, u32[]{:S(2)}) collective-permute-start(f32[12,16,1152]{2,1,0:T(8,128)} %get-tuple-element.19), channel_id=1, source_target_pairs={{0,8},{8,16},{16,24},{1,9},{9,17},{17,25},{2,10},{10,18},{18,26},{... | collective-permute-start | bytes 2654216 | tf_op jit(solution)/shard_map/ppermute | solution.py:638
  20.9 14.7 %collective-permute-start.4 = (f32[12,16,1152]{2,1,0:T(8,128)}, f32[12,16,1152]{2,1,0:T(8,128)S(1)}, u32[]{:S(2)}, u32[]{:S(2)}) collective-permute-start(f32[12,16,1152]{2,1,0:T(8,128)} %get-tuple-element.21), channel_id=1, source_target_pairs={{8,0},{16,8},{24,16},{9,1},{17,9},{25,17},{10,2},{18,10},{26,18},{... | collective-permute-start | bytes 2654216 | tf_op jit(solution)/shard_map/ppermute | solution.py:639
  24.5 20.7 %collective-permute-start.5 = (f32[12,8,2304]{2,1,0:T(8,128)}, f32[12,8,2304]{2,1,0:T(8,128)S(1)}, u32[]{:S(2)}, u32[]{:S(2)}) collective-permute-start(f32[12,8,2304]{2,1,0:T(8,128)} %get-tuple-element.22), channel_id=1, source_target_pairs={{0,4},{4,0},{1,5},{5,1},{2,6},{6,2},{3,7},{7,3},{8,12},{12,8},{9,1... | collective-permute-start | bytes 2654216 | tf_op jit(solution)/shard_map/ppermute | solution.py:640
  26.1 5.7 %collective-permute-start.2 = (f32[16,128]{1,0:T(8,128)}, f32[16,128]{1,0:T(8,128)S(1)}, u32[]{:S(2)}, u32[]{:S(2)}) collective-permute-start(f32[16,128]{1,0:T(8,128)} %get-tuple-element.18.a_1_), channel_id=1, source_target_pairs={{0,3},{1,2},{2,1},{3,0},{4,7},{5,6},{6,5},{7,4},{8,11},{9,10},{10,... | collective-permute-start | bytes 24584 | tf_op jit(solution)/shard_map/ppermute | solution.py:634
  29.7 4.8 %collective-permute-start.1 = (f32[16,128]{1,0:T(8,128)}, f32[16,128]{1,0:T(8,128)S(1)}, u32[]{:S(2)}, u32[]{:S(2)}) collective-permute-start(f32[16,128]{1,0:T(8,128)} %get-tuple-element.18.a_1_), channel_id=1, source_target_pairs={{0,2},{1,3},{2,0},{3,1},{4,6},{5,7},{6,4},{7,5},{8,10},{9,11},{10,... | collective-permute-start | bytes 24584 | tf_op jit(solution)/shard_map/ppermute | solution.py:634
  31.7 13.4 %copy-start.7 = (f32[16,128]{1,0:T(8,128)}, f32[16,128]{1,0:T(8,128)S(1)}, u32[]{:S(2)}) copy-start(f32[16,128]{1,0:T(8,128)S(1)} %collective-permute-done.2.a_4_) | copy-start | bytes 24580
  31.7 3.9 %collective-permute-start = (f32[16,128]{1,0:T(8,128)}, f32[16,128]{1,0:T(8,128)S(1)}, u32[]{:S(2)}, u32[]{:S(2)}) collective-permute-start(f32[16,128]{1,0:T(8,128)} %get-tuple-element.18.a_1_), channel_id=1, source_target_pairs={{0,1},{1,0},{2,3},{3,2},{4,5},{5,4},{6,7},{7,6},{8,9},{9,8},{10,11... | collective-permute-start | bytes 24584 | tf_op jit(solution)/shard_map/ppermute | solution.py:634
  34.4 10.8 %copy-start.9 = (f32[16,128]{1,0:T(8,128)}, f32[16,128]{1,0:T(8,128)S(1)}, u32[]{:S(2)}) copy-start(f32[16,128]{1,0:T(8,128)S(1)} %collective-permute-done.1.a_3_) | copy-start | bytes 24580
  35.6 9.6 %copy-start.11 = (f32[16,128]{1,0:T(8,128)}, f32[16,128]{1,0:T(8,128)S(1)}, u32[]{:S(2)}) copy-start(f32[16,128]{1,0:T(8,128)S(1)} %collective-permute-done.a_2_) | copy-start | bytes 24580
  35.6 9.6 %copy-start.1 = (f32[12,16,1152]{2,1,0:T(8,128)}, f32[12,16,1152]{2,1,0:T(8,128)S(1)}, u32[]{:S(2)}) copy-start(f32[12,16,1152]{2,1,0:T(8,128)S(1)} %collective-permute-done.3.a_6_) | copy-start | bytes 2654212
  35.6 9.6 %copy-start.3 = (f32[12,16,1152]{2,1,0:T(8,128)}, f32[12,16,1152]{2,1,0:T(8,128)S(1)}, u32[]{:S(2)}) copy-start(f32[12,16,1152]{2,1,0:T(8,128)S(1)} %collective-permute-done.4.a_8_) | copy-start | bytes 2654212
  45.2 0.9 copy-start.5
  79.0 16.7 %collective-permute-start.9 = (f32[12,16,1152]{2,1,0:T(8,128)}, f32[12,16,1152]{2,1,0:T(8,128)S(1)}, u32[]{:S(2)}, u32[]{:S(2)}) collective-permute-start(f32[12,16,1152]{2,1,0:T(8,128)} %get-tuple-element.25), channel_id=1, source_target_pairs={{0,8},{8,16},{16,24},{1,9},{9,17},{17,25},{2,10},{10,18},{18,26},{... | collective-permute-start | bytes 2654216 | tf_op jit(solution)/shard_map/ppermute | solution.py:638
  80.9 14.7 %collective-permute-start.10 = (f32[12,16,1152]{2,1,0:T(8,128)}, f32[12,16,1152]{2,1,0:T(8,128)S(1)}, u32[]{:S(2)}, u32[]{:S(2)}) collective-permute-start(f32[12,16,1152]{2,1,0:T(8,128)} %get-tuple-element.27), channel_id=1, source_target_pairs={{8,0},{16,8},{24,16},{9,1},{17,9},{25,17},{10,2},{18,10},{26,18},{... | collective-permute-start | bytes 2654216 | tf_op jit(solution)/shard_map/ppermute | solution.py:639
  84.6 20.7 %collective-permute-start.11 = (f32[12,8,2304]{2,1,0:T(8,128)}, f32[12,8,2304]{2,1,0:T(8,128)S(1)}, u32[]{:S(2)}, u32[]{:S(2)}) collective-permute-start(f32[12,8,2304]{2,1,0:T(8,128)} %get-tuple-element.28), channel_id=1, source_target_pairs={{0,4},{4,0},{1,5},{5,1},{2,6},{6,2},{3,7},{7,3},{8,12},{12,8},{9,1... | collective-permute-start | bytes 2654216 | tf_op jit(solution)/shard_map/ppermute | solution.py:640
  86.1 5.7 %collective-permute-start.8 = (f32[16,128]{1,0:T(8,128)}, f32[16,128]{1,0:T(8,128)S(1)}, u32[]{:S(2)}, u32[]{:S(2)}) collective-permute-start(f32[16,128]{1,0:T(8,128)} %get-tuple-element.23.a_1_), channel_id=1, source_target_pairs={{0,3},{1,2},{2,1},{3,0},{4,7},{5,6},{6,5},{7,4},{8,11},{9,10},{10,... | collective-permute-start | bytes 24584 | tf_op jit(solution)/shard_map/ppermute | solution.py:634
  89.8 4.8 %collective-permute-start.7 = (f32[16,128]{1,0:T(8,128)}, f32[16,128]{1,0:T(8,128)S(1)}, u32[]{:S(2)}, u32[]{:S(2)}) collective-permute-start(f32[16,128]{1,0:T(8,128)} %get-tuple-element.23.a_1_), channel_id=1, source_target_pairs={{0,2},{1,3},{2,0},{3,1},{4,6},{5,7},{6,4},{7,5},{8,10},{9,11},{10,... | collective-permute-start | bytes 24584 | tf_op jit(solution)/shard_map/ppermute | solution.py:634
  91.8 13.4 %copy-start.6 = (f32[16,128]{1,0:T(8,128)}, f32[16,128]{1,0:T(8,128)S(1)}, u32[]{:S(2)}) copy-start(f32[16,128]{1,0:T(8,128)S(1)} %collective-permute-done.8.a_4_) | copy-start | bytes 24580
  91.8 3.9 %collective-permute-start.6 = (f32[16,128]{1,0:T(8,128)}, f32[16,128]{1,0:T(8,128)S(1)}, u32[]{:S(2)}, u32[]{:S(2)}) collective-permute-start(f32[16,128]{1,0:T(8,128)} %get-tuple-element.23.a_1_), channel_id=1, source_target_pairs={{0,1},{1,0},{2,3},{3,2},{4,5},{5,4},{6,7},{7,6},{8,9},{9,8},{10,11... | collective-permute-start | bytes 24584 | tf_op jit(solution)/shard_map/ppermute | solution.py:634
  94.5 10.7 %copy-start.8 = (f32[16,128]{1,0:T(8,128)}, f32[16,128]{1,0:T(8,128)S(1)}, u32[]{:S(2)}) copy-start(f32[16,128]{1,0:T(8,128)S(1)} %collective-permute-done.7.a_3_) | copy-start | bytes 24580
  95.7 9.6 %copy-start.10 = (f32[16,128]{1,0:T(8,128)}, f32[16,128]{1,0:T(8,128)S(1)}, u32[]{:S(2)}) copy-start(f32[16,128]{1,0:T(8,128)S(1)} %collective-permute-done.6.a_2_) | copy-start | bytes 24580
  95.7 9.6 %copy-start = (f32[12,16,1152]{2,1,0:T(8,128)}, f32[12,16,1152]{2,1,0:T(8,128)S(1)}, u32[]{:S(2)}) copy-start(f32[12,16,1152]{2,1,0:T(8,128)S(1)} %collective-permute-done.9.a_6_) | copy-start | bytes 2654212
  95.7 9.6 %copy-start.2 = (f32[12,16,1152]{2,1,0:T(8,128)}, f32[12,16,1152]{2,1,0:T(8,128)S(1)}, u32[]{:S(2)}) copy-start(f32[12,16,1152]{2,1,0:T(8,128)S(1)} %collective-permute-done.10.a_8_) | copy-start | bytes 2654212
  105.2 1.0 copy-start.4
  135.6 5.7 %collective-permute-start.14 = (f32[16,128]{1,0:T(8,128)}, f32[16,128]{1,0:T(8,128)S(1)}, u32[]{:S(2)}, u32[]{:S(2)}) collective-permute-start(f32[16,128]{1,0:T(8,128)} %get-tuple-element.30.a_1_), channel_id=1, source_target_pairs={{0,3},{1,2},{2,1},{3,0},{4,7},{5,6},{6,5},{7,4},{8,11},{9,10},{10,... | collective-permute-start | bytes 24584 | tf_op jit(solution)/shard_map/ppermute | solution.py:634
  139.2 4.8 %collective-permute-start.13 = (f32[16,128]{1,0:T(8,128)}, f32[16,128]{1,0:T(8,128)S(1)}, u32[]{:S(2)}, u32[]{:S(2)}) collective-permute-start(f32[16,128]{1,0:T(8,128)} %get-tuple-element.30.a_1_), channel_id=1, source_target_pairs={{0,2},{1,3},{2,0},{3,1},{4,6},{5,7},{6,4},{7,5},{8,10},{9,11},{10,... | collective-permute-start | bytes 24584 | tf_op jit(solution)/shard_map/ppermute | solution.py:634
  139.2 4.8 %collective-permute-start.12 = (f32[16,128]{1,0:T(8,128)}, f32[16,128]{1,0:T(8,128)S(1)}, u32[]{:S(2)}, u32[]{:S(2)}) collective-permute-start(f32[16,128]{1,0:T(8,128)} %get-tuple-element.30.a_1_), channel_id=1, source_target_pairs={{0,1},{1,0},{2,3},{3,2},{4,5},{5,4},{6,7},{7,6},{8,9},{9,8},{10,11... | collective-permute-start | bytes 24584 | tf_op jit(solution)/shard_map/ppermute | solution.py:634
  141.3 2.7 %copy-start.12 = (f32[16,128]{1,0:T(8,128)}, f32[16,128]{1,0:T(8,128)S(1)}, u32[]{:S(2)}) copy-start(f32[16,128]{1,0:T(8,128)S(1)} %collective-permute-done.14.a_4_) | copy-start | bytes 24580
  144.0 0.6 copy-start.13
  144.6 0.6 copy-start.14

commit v2 on v1

v2 whole, which is shorter than its diff:
```python
import math

import jax
import jax.numpy as jnp
import ml_dtypes
import numpy as np
from jax import lax
from jax.experimental import pallas as pl
from jax.experimental.pallas import tpu as pltpu
from jax.sharding import PartitionSpec as P

NODES = 8
NVR = 48
NVT = 48
NVZ = 48
STEPS = 2

ELEMENT_WIDTH = 4.0
TIME_STEP = 0.001
KNUDSEN = 0.005
VISCOUS_RATIO = 2.0 / 3.0
SAT_DENSITY = 1.5
SPEED_LIMIT = 5.0

PLANE = NVR * NVT
HALF = PLANE // 2
LOCAL_Z = 2 * NODES
NODE_COUNT = NODES * LOCAL_Z
TILE = 256
WINDOW = 512
GHOST_ROWS = 32
MOMENTS = 16
PARTS_W = 3
F32 = jnp.float32
BF16 = jnp.bfloat16
PIECES = [(t, TILE, 0) for t in range(0, 1024, TILE)] + [(1024, 128, 0), (1152, 128, 1)] + [
    (t, TILE, 1) for t in range(1280, PLANE, TILE)
]


def legendre_pair(position, point_count):
    previous = 1.0
    current = position
    for degree in range(2, point_count + 1):
        previous, current = (
            current,
            ((2 * degree - 1) * position * current - (degree - 1) * previous) / degree,
        )
    slope = point_count * (position * current - previous) / (position * position - 1.0)
    return (current, slope)


def dg_tables(point_count):
    point_list = []
    weight_list = []
    for number in range(point_count):
        position = math.cos(math.pi * (number + 0.75) / (point_count + 0.5))
        for sweep in range(60):
            value, slope = legendre_pair(position, point_count)
            position = position - value / slope
        value, slope = legendre_pair(position, point_count)
        point_list.append(position)
        weight_list.append(2.0 / ((1.0 - position * position) * slope * slope))
    point_list = point_list[::-1]
    weight_list = weight_list[::-1]
    points = np.array(point_list)
    derivative = np.zeros((point_count, point_count))
    right = np.zeros(point_count)
    left = np.zeros(point_count)
    products = [
        np.prod([points[i] - points[j] for j in range(point_count) if j != i])
        for i in range(point_count)
    ]
    for i in range(point_count):
        others = [j for j in range(point_count) if j != i]
        derivative[i, i] = sum(1.0 / (points[i] - points[j]) for j in others)
        for j in others:
            derivative[i, j] = products[i] / products[j] / (points[i] - points[j])
        right[i] = np.prod([1.0 - points[j] for j in others]) / products[i]
        left[i] = np.prod([-1.0 - points[j] for j in others]) / products[i]
    return points, np.array(weight_list), derivative, right, left


def speed_grid(point_count):
    return -SPEED_LIMIT + (np.arange(point_count) + 0.5) * (2.0 * SPEED_LIMIT / point_count)


POINTS, QUAD, DERIV, END_R, END_L = dg_tables(NODES)
LIFT_R = END_R / QUAD
LIFT_L = END_L / QUAD
GRID_R = speed_grid(NVR)
GRID_T = speed_grid(NVT)
GRID_Z = speed_grid(NVZ)
STEP_V = 2 * SPEED_LIMIT / NVR
WEIGHT = STEP_V**3 / (2 * math.pi) ** 1.5
HALF_FLUX = float(
    WEIGHT
    * np.sum(np.exp(-(GRID_R**2) / 2))
    * np.sum(np.exp(-(GRID_T**2) / 2))
    * np.sum(np.maximum(GRID_Z, 0.0) * np.exp(-(GRID_Z**2) / 2))
)
SCALE = TIME_STEP * 2.0 / ELEMENT_WIDTH


def transport_tables():
    ident = np.eye(NODES)
    up = DERIV + np.outer(LIFT_L, END_L)
    down = DERIV - np.outer(LIFT_R, END_R)
    zero = np.zeros((NODES, NODES))
    wide = np.eye(LOCAL_Z)
    radial = np.stack([np.kron(down, wide), np.kron(up, wide), np.kron(DERIV, wide)])
    zup = np.block([[up, zero], [-np.outer(LIFT_L, END_R), up]])
    zdown = np.block([[down, np.outer(LIFT_R, END_L)], [zero, down]])
    zout = np.block([[down, np.outer(LIFT_R, END_L)], [zero, DERIV]])
    axial = np.stack([np.kron(ident, zdown), np.kron(ident, zup), np.kron(ident, zout)])
    ghost_r = np.zeros((2, NODE_COUNT, 128))
    ghost_z = np.zeros((2, NODE_COUNT, 128))
    for r in range(NODES):
        for z in range(LOCAL_Z):
            n = r * LOCAL_Z + z
            ghost_r[0, n, z] = -LIFT_R[r]
            ghost_r[1, n, z] = LIFT_L[r]
            if z >= NODES:
                ghost_z[0, n, LOCAL_Z + r] = LIFT_R[z - NODES]
            else:
                ghost_z[1, n, LOCAL_Z + r] = LIFT_L[z]
    trace = np.zeros((2, 2, GHOST_ROWS, NODE_COUNT))
    for side in range(2):
        radial_row = END_R if side == 1 else END_L
        for place in range(2):
            for z in range(LOCAL_Z):
                for r in range(NODES):
                    trace[side, place, z, r * LOCAL_Z + z] = radial_row[r]
            for r in range(NODES):
                for k in range(NODES):
                    if place == 0:
                        trace[side, place, LOCAL_Z + r, r * LOCAL_Z + NODES + k] = END_R[k]
                    else:
                        trace[side, place, LOCAL_Z + r, r * LOCAL_Z + k] = END_L[k]
    return (
        (-SCALE * radial).astype(ml_dtypes.bfloat16),
        (-SCALE * axial).astype(np.float32),
        (SCALE * ghost_r).astype(np.float32),
        (SCALE * ghost_z).astype(np.float32),
        trace.astype(ml_dtypes.bfloat16),
    )


def rotation_table():
    full = np.zeros((PLANE + 2 * TILE, PLANE))
    factor = TIME_STEP / (2 * STEP_V)
    for a in range(NVR):
        for b in range(NVT):
            n = a * NVT + b
            first = factor * GRID_T[b] * GRID_T[b]
            second = factor * GRID_R[a] * GRID_T[b]
            if a + 1 < NVR:
                full[TILE + n + NVT, n] = -first
            if a > 0:
                full[TILE + n - NVT, n] = first
            if b + 1 < NVT:
                full[TILE + n + 1, n] = second
            if b > 0:
                full[TILE + n - 1, n] = -second
    tiles = [full[TILE + t - 128 : TILE + t - 128 + WINDOW, t : t + TILE] for t in range(0, PLANE, TILE)]
    return np.stack(tiles).astype(ml_dtypes.bfloat16)


def mirror_table():
    table = np.zeros((HALF, HALF))
    groups = NVR // 2
    for g in range(groups):
        for b in range(NVT):
            table[(groups - 1 - g) * NVT + b, g * NVT + b] = 1.0
    return table.astype(ml_dtypes.bfloat16)


def plane_rows():
    vr = np.repeat(GRID_R, NVT)
    vt = np.tile(GRID_T, NVR)
    rows = np.zeros((8, PLANE))
    rows[0] = vr
    rows[1] = vt
    rows[2] = np.exp(-(vr**2 + vt**2) / 2)
    return rows.astype(np.float32)


def weight_table():
    vr = np.repeat(GRID_R, NVT)
    vt = np.tile(GRID_T, NVR)
    square = vr**2 + vt**2
    columns = [np.ones(PLANE), vr, vt, vr**2, vt**2, vr * vt, vr * square, vt * square]
    table = np.zeros((PLANE, 128))
    for k, column in enumerate(columns):
        rest = column.copy()
        for part in range(PARTS_W):
            piece = rest.astype(ml_dtypes.bfloat16).astype(np.float64)
            table[:, k + 8 * part] = piece
            rest = rest - piece
    return table.astype(ml_dtypes.bfloat16)


def edge_table():
    table = np.zeros((2, NODE_COUNT, 128))
    for r in range(NODES):
        for k in range(NODES):
            table[0, r * LOCAL_Z + k, r] = END_L[k]
            table[1, r * LOCAL_Z + NODES + k, r] = END_R[k]
    return table.astype(np.float32)


def node_columns():
    table = np.zeros((NODE_COUNT, 128))
    for r in range(NODES):
        table[r * LOCAL_Z : (r + 1) * LOCAL_Z, :] = (1.0 + POINTS[r]) / 2
    return table.astype(np.float32)


RADIAL_M, AXIAL_M, GHOST_R, GHOST_Z, TRACE_M = transport_tables()
ROTATION_M = rotation_table()
MIRROR_M = mirror_table()
ROWS = plane_rows()
WEIGHT_M = weight_table()
EDGE = edge_table()
NODE_POS = node_columns()


def slot_speed(order, slot):
    return (order[slot].astype(F32) + 0.5) * (2 * SPEED_LIMIT / NVZ) - SPEED_LIMIT


def dot(x, y):
    return jnp.dot(x, y, preferred_element_type=F32)


def split(x):
    high = x.astype(BF16)
    return high, (x - high.astype(F32)).astype(BF16)


def macroscopic_of(m):
    rho = m(0)
    inv = 1.0 / rho
    ur, ut, uz = m(1) * inv, m(2) * inv, m(3) * inv
    rr, tt, rt, zz, rz, tz = (m(k) for k in range(4, 10))
    energy = rr + tt + zz
    speed = ur * ur + ut * ut + uz * uz
    temp = (energy * inv - speed) * (1.0 / 3.0)
    tail = 2.0 * rho * speed - energy
    qr = 0.5 * (m(10) - 2.0 * (ur * rr + ut * rt + uz * rz) + ur * tail)
    qt = 0.5 * (m(11) - 2.0 * (ur * rt + ut * tt + uz * tz) + ut * tail)
    qz = 0.5 * (m(12) - 2.0 * (ur * rz + ut * tz + uz * zz) + uz * tail)
    return rho, ur, ut, uz, temp, qr, qt, qz


def add_speed_sums(sums_ref, sums, vz):
    one = vz * sums
    two = vz * one
    for k, value in enumerate([sums, one, two, vz * two, jnp.abs(vz) * sums]):
        sums_ref[k] += value


def moment_rows(sums_ref):
    lane = lax.broadcasted_iota(jnp.int32, (NODE_COUNT, 128), 1)
    e = []
    for k in range(5):
        x = sums_ref[k]
        e.append(x + pltpu.roll(x, 120, 1) + pltpu.roll(x, 112, 1))
    pick = lambda k, c: e[k][:, c : c + 1]
    columns = [
        pick(0, 0), pick(0, 1), pick(0, 2), pick(1, 0),
        pick(0, 3), pick(0, 4), pick(0, 5), pick(2, 0), pick(1, 1), pick(1, 2),
        pick(0, 6) + pick(2, 1), pick(0, 7) + pick(2, 2), pick(1, 3) + pick(1, 4) + pick(3, 0), pick(4, 0),
    ]
    table = jnp.zeros((NODE_COUNT, 128), F32)
    for k, column in enumerate(columns):
        table = jnp.where(lane == k, WEIGHT * column, table)
    return jnp.transpose(table)[0:MOMENTS, :]


def places_of():
    return lax.axis_index("row"), lax.axis_index("gz")


def send_piece(s, first, lanes, side, place, narrow, trace_ref, right_ref, left_ref, axial_ref):
    got = dot(trace_ref[side, place], narrow)
    if side == 1:
        right_ref[s, :, first - HALF : first - HALF + lanes] = got[0:LOCAL_Z]
    else:
        left_ref[s, :, first : first + lanes] = got[0:LOCAL_Z]
    axial_ref[s, :, first : first + lanes] = got[LOCAL_Z : LOCAL_Z + NODES]


def turn_traces(count, row, mirror_ref, left_ref, turned_ref):
    @pl.when(row == 0)
    def _():
        flat = left_ref[...].reshape(count * LOCAL_Z, HALF).astype(BF16)
        for first in range(0, HALF, 128):
            low = max(0, (HALF - first - 128 - 48) // 128 * 128)
            high = min(HALF, -((first - HALF - 48) // 128) * 128)
            got = dot(flat[:, low:high], mirror_ref[low:high, first : first + 128])
            turned_ref[:, :, first : first + 128] = got.reshape(count, LOCAL_Z, 128)

    @pl.when(row != 0)
    def _():
        turned_ref[...] = jnp.zeros(turned_ref.shape, F32)


def nodes_of(ref, first, lanes):
    return ref[:, :, first : first + lanes].reshape(NODE_COUNT, lanes)


def first_kernel(
    count, order, codes, f_ref, weight_ref, trace_ref, mirror_ref,
    right_ref, left_ref, turned_ref, axial_ref, mom_ref, sums_ref,
):
    step = pl.program_id(0)
    row, place = places_of()

    @pl.when(step == 0)
    def _():
        sums_ref[...] = jnp.zeros(sums_ref.shape, F32)

    for s in range(count):
        sums = jnp.zeros((NODE_COUNT, 128), F32)
        for first, lanes, side in PIECES:
            high, low = split(nodes_of(f_ref, s * PLANE + first, lanes))
            weights = weight_ref[first : first + lanes, :]
            sums = sums + dot(
                jnp.concatenate([high, low], axis=1), jnp.concatenate([weights, weights], axis=0)
            )
            send_piece(s, first, lanes, side, place, high, trace_ref, right_ref, left_ref, axial_ref)
        add_speed_sums(sums_ref, sums, slot_speed(order, step * count + s))
    turn_traces(count, row, mirror_ref, left_ref, turned_ref)

    @pl.when(step == pl.num_programs(0) - 1)
    def _():
        mom_ref[...] = moment_rows(sums_ref)


def inner_kernel(
    count, order, codes, f_ref, rows_ref, pos_ref, weight_ref, radial_ref, axial_m_ref, rot_ref,
    out_ref, mom_ref, sums_ref, inverse_ref, pad_ref, lhs_ref,
):
    step = pl.program_id(0)
    row, place = places_of()

    @pl.when(step == 0)
    def _():
        sums_ref[...] = jnp.zeros(sums_ref.shape, F32)
        pad_ref[:, 0:128] = jnp.zeros((NODE_COUNT, 128), BF16)
        pad_ref[:, 128 + PLANE :] = jnp.zeros((NODE_COUNT, 128), BF16)
        inverse_ref[...] = 1.0 / (ELEMENT_WIDTH * (row.astype(F32) + pos_ref[...]))
        lhs_ref[0, :, 0:128] = radial_ref[jnp.where(row == lax.axis_size("row") - 1, 2, 0)]
        lhs_ref[1, :, 0:128] = radial_ref[1]

    kind_out = jnp.where(jnp.logical_and(place == 1, codes[1, 0] == 2), 2, 0)
    inverse = inverse_ref[...]
    for s in range(count):
        vz = slot_speed(order, step * count + s)
        axial = (vz * axial_m_ref[jnp.where(vz > 0, 1, kind_out)]).astype(BF16)
        lhs_ref[0, :, 128:256] = axial
        lhs_ref[1, :, 128:256] = axial
        for j in range(PLANE // 128):
            field = nodes_of(f_ref, s * PLANE + j * 128, 128)
            pad_ref[:, 128 + j * 128 : 256 + j * 128] = (field * inverse).astype(BF16)
        sums = jnp.zeros((NODE_COUNT, 128), F32)
        for first, lanes, side in PIECES:
            tile = first // TILE
            inside = first - tile * TILE
            start = tile * TILE
            field = nodes_of(f_ref, s * PLANE + first, lanes)
            moved = (field * rows_ref[0:1, first : first + lanes]).astype(BF16)
            left = jnp.concatenate([lhs_ref[side], pad_ref[:, start : start + WINDOW]], axis=1)
            right = jnp.concatenate(
                [moved, field.astype(BF16), rot_ref[tile, :, inside : inside + lanes]], axis=0
            )
            change = dot(left, right).astype(BF16)
            out_ref[:, :, s * PLANE + first : s * PLANE + first + lanes] = change.reshape(
                NODES, LOCAL_Z, lanes
            )
            sums = sums + dot(change, weight_ref[first : first + lanes, :])
        add_speed_sums(sums_ref, sums, vz)

    @pl.when(step == pl.num_programs(0) - 1)
    def _():
        mom_ref[...] = moment_rows(sums_ref)


def total_of(parts):
    while len(parts) > 1:
        parts = [parts[k] + parts[k + 1] for k in range(0, len(parts), 2)]
    return parts[0]


def total_moments(part_refs, base_ref):
    total = total_of([p[...] for p in part_refs])
    return total if base_ref is None else total + base_ref[...]


def prepare_nodes(total, codes, place, rows_ref, edge_ref, table_ref, node_ref, wall_ref, plane_ref):
    wide = jnp.concatenate([total, jnp.zeros((128 - MOMENTS, 128), F32)], axis=0)
    table_ref[...] = jnp.transpose(wide)
    rho, ur, ut, uz, temp, qr, qt, qz = macroscopic_of(lambda k: table_ref[:, k : k + 1])
    inv_t = 1.0 / temp
    beta = ((1.0 - VISCOUS_RATIO) / 5.0) / (rho * temp * temp)
    kappa = rho * (TIME_STEP / KNUDSEN)
    peak = kappa * rho * inv_t * jnp.sqrt(inv_t)
    columns = [uz, -0.5 * inv_t, qz * beta, inv_t, peak, 1.0 - kappa, ur, ut, qr * beta, qt * beta]
    for k, column in enumerate(columns):
        node_ref[k] = jnp.broadcast_to(column, (NODE_COUNT, 128))
    net = table_ref[:, 3:4]
    gross = table_ref[:, 13:14]
    to_bottom = 0.5 * (gross - net)
    to_top = 0.5 * (gross + net)
    incident = jnp.sum(edge_ref[0] * to_bottom, axis=0, keepdims=True)
    upward = jnp.sum(edge_ref[1] * to_top, axis=0, keepdims=True)
    bottom = jnp.where(codes[0, 0] == 1, SAT_DENSITY, incident * (1.0 / HALF_FLUX))
    top = jnp.where(codes[1, 0] == 2, 0.0, upward * (1.0 / HALF_FLUX))
    density = jnp.where(place == 0, bottom, top)
    wall_ref[...] = jnp.transpose(jnp.broadcast_to(density, (128, 128)))[0:NODES, :]

    def one_radius(r, carry):
        rows = pl.ds(pl.multiple_of(r * LOCAL_Z, LOCAL_Z), LOCAL_Z)
        n_half, n_inv = node_ref[1, rows, :], node_ref[3, rows, :]
        n_ur, n_ut = node_ref[6, rows, :], node_ref[7, rows, :]
        n_qr, n_qt = node_ref[8, rows, :], node_ref[9, rows, :]
        for j in range(PLANE // 128):
            at = pl.ds(j * 128, 128)
            cr = rows_ref[0:1, at] - n_ur
            ct = rows_ref[1:2, at] - n_ut
            square = cr * cr + ct * ct
            gauss = jnp.exp(square * n_half)
            along = cr * n_qr + ct * n_qt
            reach = square * n_inv - 5.0
            tilted = gauss * along
            plane_ref[0, rows, at] = gauss
            plane_ref[1, rows, at] = tilted
            plane_ref[2, rows, at] = gauss * reach
            plane_ref[3, rows, at] = tilted * reach
        return carry

    lax.fori_loop(0, NODES, one_radius, 0)


def slot_factors(vz, node_ref):
    cz = vz - node_ref[0]
    lam = node_ref[4] * jnp.exp(cz * cz * node_ref[1])
    alpha = cz * node_ref[2]
    reach = cz * cz * node_ref[3]
    return lam * (1.0 + alpha * reach), lam * reach, lam * alpha, lam


def ghost_lifts(vz, ghost_r_ref, ghost_z_ref, lhs_ref):
    lean = jnp.abs(vz) * ghost_z_ref[jnp.where(vz > 0, 1, 0)]
    lhs_ref[0] = (ghost_r_ref[0] + lean).astype(BF16)
    lhs_ref[1] = (ghost_r_ref[1] + lean).astype(BF16)


def ghost_rows(s, vz, place, in_left_ref, in_turned_ref, in_right_ref, in_axial_ref, rows_ref, wall_ref, ghost_ref):
    own = (place == 0) == (vz > 0)
    strength = jnp.exp(-0.5 * vz * vz + jnp.zeros((NODES, 128), F32)) * wall_ref[...]
    for j in range(PLANE // 128):
        at = pl.ds(j * 128, 128)
        if j * 128 < HALF:
            radial = in_right_ref[s, :, at]
        else:
            back = pl.ds(j * 128 - HALF, 128)
            radial = in_left_ref[s, :, back] + in_turned_ref[s, :, back]
        axial = jnp.where(own, strength * rows_ref[2:3, at], in_axial_ref[s, :, at])
        rows = jnp.concatenate([rows_ref[0:1, at] * radial, axial, jnp.zeros((8, 128), F32)], axis=0)
        ghost_ref[:, at] = rows.astype(BF16)


def outer_kernel(count, part_count, based, last, order, codes, *refs):
    part_refs, refs = refs[:part_count], refs[part_count:]
    base_ref = None
    if based:
        base_ref, refs = refs[0], refs[1:]
    f_ref, inner_ref, in_left_ref, in_turned_ref, in_right_ref, in_axial_ref = refs[:6]
    rows_ref, edge_ref, ghost_r_ref, ghost_z_ref = refs[6:10]
    refs = refs[10:]
    if last:
        out_ref, refs = refs[0], refs[1:]
    else:
        (trace_ref, mirror_ref, out_ref, right_ref, left_ref, turned_ref, axial_ref), refs = refs[:7], refs[7:]
    plane_ref, node_ref, wall_ref, slot_ref, lhs_ref, ghost_ref, table_ref = refs
    step = pl.program_id(0)
    row, place = places_of()

    @pl.when(step == 0)
    def _():
        total = total_moments(part_refs, base_ref)
        prepare_nodes(total, codes, place, rows_ref, edge_ref, table_ref, node_ref, wall_ref, plane_ref)

    for s in range(count):
        vz = slot_speed(order, step * count + s)
        for k, value in enumerate(slot_factors(vz, node_ref)):
            slot_ref[k] = value
        ghost_lifts(vz, ghost_r_ref, ghost_z_ref, lhs_ref)
        ghost_rows(
            s, vz, place, in_left_ref, in_turned_ref, in_right_ref, in_axial_ref, rows_ref, wall_ref, ghost_ref
        )
        for first, lanes, side in PIECES:
            lifted = dot(lhs_ref[side, :, 0:GHOST_ROWS], ghost_ref[:, first : first + lanes])
            pieces = []
            for inside in range(0, lanes, 128):
                here = s * PLANE + first + inside
                at = pl.ds(first + inside, 128)
                new = nodes_of(f_ref, here, 128) * node_ref[5] + nodes_of(inner_ref, here, 128).astype(F32)
                new = new + lifted[:, inside : inside + 128]
                for k in range(4):
                    new = new + plane_ref[k, :, at] * slot_ref[k]
                out_ref[:, :, here : here + 128] = new.reshape(NODES, LOCAL_Z, 128)
                pieces.append(new.astype(BF16))
            if not last:
                narrow = jnp.concatenate(pieces, axis=1) if len(pieces) > 1 else pieces[0]
                send_piece(s, first, lanes, side, place, narrow, trace_ref, right_ref, left_ref, axial_ref)
    if not last:
        turn_traces(count, row, mirror_ref, left_ref, turned_ref)


def moment_kernel(count, part_count, based, order, codes, *refs):
    part_refs, refs = refs[:part_count], refs[part_count:]
    base_ref = None
    if based:
        base_ref, refs = refs[0], refs[1:]
    inner_mom_ref, in_left_ref, in_turned_ref, in_right_ref, in_axial_ref = refs[:5]
    rows_ref, edge_ref, ghost_r_ref, ghost_z_ref, weight_ref = refs[5:10]
    share_ref, kept_ref = refs[10:12]
    plane_ref, node_ref, wall_ref, lhs_ref, ghost_ref, table_ref, sums_ref, plane_sums_ref = refs[12:]
    step = pl.program_id(0)
    row, place = places_of()

    @pl.when(step == 0)
    def _():
        sums_ref[...] = jnp.zeros(sums_ref.shape, F32)
        total = total_moments(part_refs, base_ref)
        kept_ref[...] = total * (1.0 - total[0:1, :] * (TIME_STEP / KNUDSEN))
        prepare_nodes(total, codes, place, rows_ref, edge_ref, table_ref, node_ref, wall_ref, plane_ref)
        for k in range(4):
            high, low = split(plane_ref[k])
            plane_sums_ref[k] = dot(high, weight_ref[...]) + dot(low, weight_ref[...])

    for s in range(count):
        vz = slot_speed(order, step * count + s)
        sums = jnp.zeros((NODE_COUNT, 128), F32)
        for k, value in enumerate(slot_factors(vz, node_ref)):
            sums = sums + plane_sums_ref[k] * value
        ghost_lifts(vz, ghost_r_ref, ghost_z_ref, lhs_ref)
        ghost_rows(
            s, vz, place, in_left_ref, in_turned_ref, in_right_ref, in_axial_ref, rows_ref, wall_ref, ghost_ref
        )
        for side in range(2):
            span = pl.ds(side * HALF, HALF)
            high, low = split(dot(ghost_ref[:, span], weight_ref[span, :]))
            lift = lhs_ref[side, :, 0:GHOST_ROWS]
            sums = sums + dot(lift, high) + dot(lift, low)
        add_speed_sums(sums_ref, sums, vz)

    @pl.when(step == pl.num_programs(0) - 1)
    def _():
        share_ref[...] = moment_rows(sums_ref) + inner_mom_ref[...]


def last_kernel(part_count, codes, *refs):
    total_ref = total_moments(refs[:part_count], refs[part_count])
    edge_ref, macro_ref, flux_ref = refs[part_count + 1 :]
    row, place = places_of()
    values = macroscopic_of(lambda k: total_ref[k : k + 1, :])
    for k in range(8):
        for r in range(NODES):
            macro_ref[k, r : r + 1, :] = values[k][:, r * LOCAL_Z : (r + 1) * LOCAL_Z]
    net, gross = total_ref[3:4, :], total_ref[13:14, :]
    to_bottom = jnp.broadcast_to(0.5 * (gross - net), (8, 128))
    to_top = jnp.broadcast_to(0.5 * (gross + net), (8, 128))
    exact = lambda x, y: jnp.dot(x, y, precision=lax.Precision.HIGHEST, preferred_element_type=F32)
    incident = exact(to_bottom, edge_ref[0])
    upward = exact(to_top, edge_ref[1])
    downward = exact(to_bottom, edge_ref[1])
    bottom = jnp.where(codes[0, 0] == 1, SAT_DENSITY * HALF_FLUX - incident, 0.0)
    top = jnp.where(codes[1, 0] == 2, upward - downward, 0.0)
    flux_ref[...] = jnp.where(place == 0, bottom, top)[0:1, 0:NODES]


def whole(shape):
    return pl.BlockSpec(shape, lambda *a: (0,) * len(shape), pipeline_mode=pl.Buffered(1))


def on_device(distribution, z_order, edge_codes):
    local_r, local_z, vdev = distribution.shape
    assert local_r == NODES and local_z == LOCAL_Z
    slots = vdev // PLANE
    group = math.gcd(slots, 3)
    steps = slots // group
    rows_total = lax.axis_size("row")
    verts = lax.axis_size("vert")
    assert lax.axis_size("gz") == 2
    rows, pos, edge = jnp.asarray(ROWS), jnp.asarray(NODE_POS), jnp.asarray(EDGE)
    radial_m, axial_m = jnp.asarray(RADIAL_M), jnp.asarray(AXIAL_M)
    ghost_r, ghost_z = jnp.asarray(GHOST_R), jnp.asarray(GHOST_Z)
    trace_m, mirror_m, rot_m = jnp.asarray(TRACE_M), jnp.asarray(MIRROR_M), jnp.asarray(ROTATION_M)
    weight_m = jnp.asarray(WEIGHT_M)

    big = pl.BlockSpec((NODES, LOCAL_Z, group * PLANE), lambda i, *n: (0, 0, i))
    radial_spec = pl.BlockSpec((group, LOCAL_Z, HALF), lambda i, *n: (i, 0, 0))
    axial_spec = pl.BlockSpec((group, NODES, PLANE), lambda i, *n: (i, 0, 0))
    mom_spec = whole((MOMENTS, 128))
    radial_shape = jax.ShapeDtypeStruct((slots, LOCAL_Z, HALF), F32)
    axial_shape = jax.ShapeDtypeStruct((slots, NODES, PLANE), F32)
    mom_shape = jax.ShapeDtypeStruct((MOMENTS, 128), F32)
    big_shape = jax.ShapeDtypeStruct(distribution.shape, F32)
    trace_specs = [radial_spec, radial_spec, radial_spec, axial_spec]
    trace_shapes = [radial_shape, radial_shape, radial_shape, axial_shape]
    ghost_specs = [radial_spec, radial_spec, radial_spec, axial_spec]
    square = pltpu.VMEM((NODE_COUNT, 128), F32)
    sums_scratch = pltpu.VMEM((5, NODE_COUNT, 128), F32)
    node_scratch = [
        pltpu.VMEM((4, NODE_COUNT, PLANE), F32),
        pltpu.VMEM((10, NODE_COUNT, 128), F32),
        pltpu.VMEM((NODES, 128), F32),
    ]
    ghost_scratch = [
        pltpu.VMEM((2, NODE_COUNT, 128), BF16),
        pltpu.VMEM((GHOST_ROWS, PLANE), BF16),
        square,
    ]

    def call(body, name, in_specs, out_specs, out_shape, scratch, args):
        return pl.pallas_call(
            body,
            grid_spec=pltpu.PrefetchScalarGridSpec(
                num_scalar_prefetch=2,
                grid=(steps,),
                in_specs=in_specs,
                out_specs=out_specs,
                scratch_shapes=scratch,
            ),
            out_shape=out_shape,
            compiler_params=pltpu.CompilerParams(vmem_limit_bytes=56 * 1024 * 1024),
            name=name,
        )(z_order, edge_codes, *args)

    def all_whole(tables):
        return [whole(x.shape) for x in tables]

    def first(f):
        tables = [weight_m, trace_m, mirror_m]
        return call(
            lambda *a: first_kernel(group, *a), "moments_and_traces", [big] + all_whole(tables),
            trace_specs + [mom_spec], trace_shapes + [mom_shape], [sums_scratch], [f] + tables,
        )

    def inner(f):
        tables = [rows, pos, weight_m, radial_m, axial_m, rot_m]
        scratch = [
            sums_scratch,
            square,
            pltpu.VMEM((NODE_COUNT, PLANE + 256), BF16),
            pltpu.VMEM((2, NODE_COUNT, 256), BF16),
        ]
        return call(
            lambda *a: inner_kernel(group, *a), "inner_increments", [big] + all_whole(tables),
            [big, mom_spec], [jax.ShapeDtypeStruct(f.shape, BF16), mom_shape], scratch, [f] + tables,
        )

    def outer(f, change, ghosts, parts, base, last):
        bases = [] if base is None else [base]
        tables = [rows, edge, ghost_r, ghost_z] + ([] if last else [trace_m, mirror_m])
        return call(
            lambda *a: outer_kernel(group, len(parts), bool(bases), last, *a),
            "last_update" if last else "update",
            [mom_spec] * (len(parts) + len(bases)) + [big, big] + ghost_specs + all_whole(tables),
            [big] + ([] if last else trace_specs),
            [big_shape] + ([] if last else trace_shapes),
            node_scratch + [pltpu.VMEM((4, NODE_COUNT, 128), F32)] + ghost_scratch,
            [*parts, *bases, f, change, *ghosts, *tables],
        )

    def share(change_moments, ghosts, parts, base):
        bases = [] if base is None else [base]
        tables = [rows, edge, ghost_r, ghost_z, weight_m]
        return call(
            lambda *a: moment_kernel(group, len(parts), bool(bases), *a),
            "moment_share",
            [mom_spec] * (len(parts) + len(bases) + 1) + ghost_specs + all_whole(tables),
            [mom_spec, mom_spec],
            [mom_shape, mom_shape],
            node_scratch + ghost_scratch + [sums_scratch, pltpu.VMEM((4, NODE_COUNT, 128), F32)],
            [*parts, *bases, change_moments, *ghosts, *tables],
        )

    def spread(moments):
        parts = [moments]
        for shift in range(1, verts):
            parts.append(lax.ppermute(moments, "vert", [(i, i ^ shift) for i in range(verts)]))
        return parts

    def halo(right, left, turned, axial):
        from_axial = lax.ppermute(axial, "gz", [(0, 1), (1, 0)])
        from_left = lax.ppermute(right, "row", [(i, i + 1) for i in range(rows_total - 1)])
        from_right = lax.ppermute(left, "row", [(i + 1, i) for i in range(rows_total - 1)])
        return from_left, turned, from_right, from_axial

    current = distribution
    *traces, moments = first(current)
    base = None
    for number in range(STEPS):
        last = number == STEPS - 1
        ghosts = halo(*traces)
        parts = spread(moments)
        change, change_moments = inner(current)
        moments, next_base = share(change_moments, ghosts, parts, base)
        current, *traces = outer(current, change, ghosts, parts, base, last)
        base = next_base
    parts = spread(moments)
    macro, flux = pl.pallas_call(
        lambda *a: last_kernel(len(parts), *a),
        grid_spec=pltpu.PrefetchScalarGridSpec(
            num_scalar_prefetch=1,
            grid=(1,),
            in_specs=[mom_spec] * (len(parts) + 1) + [whole(edge.shape)],
            out_specs=[whole((8, NODES, LOCAL_Z)), whole((1, NODES))],
        ),
        out_shape=[
            jax.ShapeDtypeStruct((8, NODES, LOCAL_Z), F32),
            jax.ShapeDtypeStruct((1, NODES), F32),
        ],
        name="macroscopic",
    )(edge_codes, *parts, base, edge)
    return (current, macro, flux)


def solution(mesh):
    in_specs = (P("row", "gz", "vert"), P("vert"), P(None, "row"))
    out_specs = (P("row", "gz", "vert"), P(None, "row", "gz"), P("gz", "row"))
    return jax.shard_map(
        on_device, mesh=mesh, in_specs=in_specs, out_specs=out_specs, check_vma=False
    )
```

time: 151 us -> 177 us (1.17)
  Pallas kernels: 79.2 us -> 141 us
  waiting for transfers between devices: 34.9 us -> 3.6 us
  local copies, waits for them, and re-layouts: 9.41 us -> 4.79 us
    pallas_call x4 -> x8, Pallas kernels: 79.2 us -> 141 us  [the longest x7 138 us: call(): pl.pallas_call(body, grid_spec=pltpu.PrefetchScalarGridSpec(num_scalar_pr...]
    ppermute x2, waiting for transfers between devices: 19.1 us -> 0.01 us  [halo(): from_axial = lax.ppermute(axial, 'gz', [(0, 1), (1, 0)])]
    ppermute x9, waiting for transfers between devices: 15.8 us -> 3.59 us  [spread(): lax.ppermute(moments, 'vert', [(i, i ^ shift) for i in range(verts)])]
    concatenate x1 -> x0, local copies, waits for them, and re-layouts: 2.51 us -> none  [on_device(): jnp.concatenate([z_order, jnp.stack([lax.axis_index('row'), lax.axis_inde...]
    slice x2 -> x0, local copies, waits for them, and re-layouts: 2.49 us -> none  [the longest x1 1.31 us: on_device(): edge_codes[1, 0]]
    unnamed x30 -> x31, local copies, waits for them, and re-layouts: 3.05 us -> 4.79 us
  transfers between devices with their start and end apart: 15 -> 15, of which waited for: 10 -> 2; matrix products, arithmetic and copies ran while one was open for 0% -> 0% of each run, Pallas kernels for 0% -> 47%
where the time goes in v2:
time: 177 us
  Pallas kernels  141 us (80%)
  starting transfers between devices  26.6 us (15%)
  local copies, waits for them, and re-layouts  4.79 us (3%)
  waiting for transfers between devices  3.6 us (2%)
    pallas_call x7, Pallas kernels, call(): pl.pallas_call(body, grid_spec=pltpu.PrefetchScalarGridSpec(num_scalar_pr...  138 us
    ppermute x9, starting transfers between devices, spread(): lax.ppermute(moments, 'vert', [(i, i ^ shift) for i in range(verts)])  13.2 us
    ppermute x2, starting transfers between devices, halo(): lax.ppermute(left, 'row', [(i + 1, i) for i in range(rows_total - 1)])  7.46 us
    unnamed x31, local copies, waits for them, and re-layouts  4.79 us
    ppermute x2, starting transfers between devices, halo(): lax.ppermute(right, 'row', [(i, i + 1) for i in range(rows_total - 1)])  3.83 us
    ppermute x9, waiting for transfers between devices, spread(): lax.ppermute(moments, 'vert', [(i, i ^ shift) for i in range(verts)])  3.59 us
  transfers between devices with their start and end apart: 15, of which 2 were waited for; matrix products, arithmetic and copies ran while one was open for 0% of the time, Pallas kernels for 47%

profile of v2, /device:TPU:4, one launch (start us, length us, event | category | flops | bytes accessed | tf_op | source)
XLA Modules:
  0.0 176.7 jit_solution(2806741381153237140)
XLA Ops:
  0.6 1.3 copy.22.a_1_.a_0_
  1.9 12.0 %moments_and_traces.1 = (f32[12,16,1152]{2,1,0:T(8,128)}, f32[12,16,1152]{2,1,0:T(8,128)}, f32[12,16,1152]{2,1,0:T(8,128)}, f32[12,8,2304]{2,1,0:T(8,128)}, f32[16,128]{1,0:T(8,128)}) custom-call(s32[12]{0:T(128)} %a_0_.14, s32[2,1]{1,0:T(2,128)} %copy.22.a_1_.a_0_, f32[8,16,27648]{2,1,0:T(8,128)} %a_6_.4, ...), custom_call_target="tpu_custom_call" | custom-call | tf_op jit(solution)/shard_map/moments_and_traces/pallas_call | solution.py:630
  13.9 1.9 %collective-permute-start.3 = (f32[12,16,1152]{2,1,0:T(8,128)}, f32[12,16,1152]{2,1,0:T(8,128)S(1)}, u32[]{:S(2)}, u32[]{:S(2)}) collective-permute-start(f32[12,16,1152]{2,1,0:T(8,128)} %get-tuple-element.25), channel_id=1, source_target_pairs={{0,8},{8,16},{16,24},{1,9},{9,17},{17,25},{2,10},{10,18},{18,26},{... | collective-permute-start | bytes 2654216 | tf_op jit(solution)/shard_map/ppermute | solution.py:701
  15.8 3.6 %collective-permute-start.4 = (f32[12,16,1152]{2,1,0:T(8,128)}, f32[12,16,1152]{2,1,0:T(8,128)S(1)}, u32[]{:S(2)}, u32[]{:S(2)}) collective-permute-start(f32[12,16,1152]{2,1,0:T(8,128)} %get-tuple-element.27), channel_id=1, source_target_pairs={{8,0},{16,8},{24,16},{9,1},{17,9},{25,17},{10,2},{18,10},{26,18},{... | collective-permute-start | bytes 2654216 | tf_op jit(solution)/shard_map/ppermute | solution.py:702
  19.5 1.6 collective-permute-start.5
  21.0 3.6 %collective-permute-start.2 = (f32[16,128]{1,0:T(8,128)}, f32[16,128]{1,0:T(8,128)S(1)}, u32[]{:S(2)}, u32[]{:S(2)}) collective-permute-start(f32[16,128]{1,0:T(8,128)} %get-tuple-element.23.a_2_), channel_id=1, source_target_pairs={{0,3},{1,2},{2,1},{3,0},{4,7},{5,6},{6,5},{7,4},{8,11},{9,10},{10,... | collective-permute-start | bytes 24584 | tf_op jit(solution)/shard_map/ppermute | solution.py:696
  24.6 2.1 %collective-permute-done.2.a_5_ = f32[16,128]{1,0:T(8,128)S(1)} collective-permute-done((f32[16,128]{1,0:T(8,128)}, f32[16,128]{1,0:T(8,128)S(1)}, u32[]{:S(2)}, u32[]{:S(2)}) %collective-permute-start.2) | collective-permute-done | bytes 8224 | tf_op jit(solution)/shard_map/ppermute | solution.py:696
  26.7 25.9 %inner_increments.2 = (bf16[8,16,27648]{2,1,0:T(8,128)(2,1)}, f32[16,128]{1,0:T(8,128)}) custom-call(s32[12]{0:T(128)} %a_0_.14, s32[2,1]{1,0:T(2,128)} %copy.22.a_1_.a_0_, f32[8,16,27648]{2,1,0:T(8,128)} %a_6_.4, f32[8,2304]{1,0:T(8,128)} %constant.22.clone.a_3_.a_11_.a_12_.a_13_, f32[128,128]{1,0:T(8,128)} %constant.23.clone.a_4_, ...), custom_call_target="tpu_custom_call" | custom-call | tf_op jit(solution)/shard_map/inner_increments/pallas_call | solution.py:630
  52.7 0.5 copy-done.9
  53.2 0.4 copy-done.3
  53.8 0.3 copy-done.5
  54.1 29.9 %update.1 = (f32[8,16,27648]{2,1,0:T(8,128)}, f32[12,16,1152]{2,1,0:T(8,128)}, f32[12,16,1152]{2,1,0:T(8,128)}, f32[12,16,1152]{2,1,0:T(8,128)}, f32[12,8,2304]{2,1,0:T(8,128)}) custom-call(s32[12]{0:T(128)} %a_0_.14, s32[2,1]{1,0:T(2,128)} %copy.22.a_1_.a_0_, f32[16,128]{1,0:T(8,128)} %get-tuple-element.23.a_2_, f32[16,128]{1,0:T(8,128)} %copy-done.11, ...), custom_call_target="tpu_custom_call" | custom-call | tf_op jit(solution)/shard_map/update/pallas_call | solution.py:630
  84.1 1.9 %collective-permute-start.9 = (f32[12,16,1152]{2,1,0:T(8,128)}, f32[12,16,1152]{2,1,0:T(8,128)S(1)}, u32[]{:S(2)}, u32[]{:S(2)}) collective-permute-start(f32[12,16,1152]{2,1,0:T(8,128)} %get-tuple-element.34), channel_id=1, source_target_pairs={{0,8},{8,16},{16,24},{1,9},{9,17},{17,25},{2,10},{10,18},{18,26},{... | collective-permute-start | bytes 2654216 | tf_op jit(solution)/shard_map/ppermute | solution.py:701
  86.0 3.8 %collective-permute-start.10 = (f32[12,16,1152]{2,1,0:T(8,128)}, f32[12,16,1152]{2,1,0:T(8,128)S(1)}, u32[]{:S(2)}, u32[]{:S(2)}) collective-permute-start(f32[12,16,1152]{2,1,0:T(8,128)} %get-tuple-element.36), channel_id=1, source_target_pairs={{8,0},{16,8},{24,16},{9,1},{17,9},{25,17},{10,2},{18,10},{26,18},{... | collective-permute-start | bytes 2654216 | tf_op jit(solution)/shard_map/ppermute | solution.py:702
  89.8 0.6 collective-permute-start.11
  90.4 12.5 %moment_share.2 = (f32[16,128]{1,0:T(8,128)}, f32[16,128]{1,0:T(8,128)}) custom-call(s32[12]{0:T(128)} %a_0_.14, s32[2,1]{1,0:T(2,128)} %copy.22.a_1_.a_0_, f32[16,128]{1,0:T(8,128)} %get-tuple-element.23.a_2_, f32[16,128]{1,0:T(8,128)} %copy-done.11, f32[16,128]{1,0:T(8,128)} %copy-done.9, f32[16,128]{1,0:T(8,128)} %copy-done.8, ...), custom_call_target="tpu_custom_call" | custom-call | tf_op jit(solution)/shard_map/moment_share/pallas_call | solution.py:630
  103.0 3.7 %collective-permute-start.8 = (f32[16,128]{1,0:T(8,128)}, f32[16,128]{1,0:T(8,128)S(1)}, u32[]{:S(2)}, u32[]{:S(2)}) collective-permute-start(f32[16,128]{1,0:T(8,128)} %get-tuple-element.29.a_2_), channel_id=1, source_target_pairs={{0,3},{1,2},{2,1},{3,0},{4,7},{5,6},{6,5},{7,4},{8,11},{9,10},{10,... | collective-permute-start | bytes 24584 | tf_op jit(solution)/shard_map/ppermute | solution.py:696
  106.6 0.6 collective-permute-start.7
  107.3 1.5 collective-permute-done.8.a_5_
  108.8 0.8 collective-permute-start.6
  109.6 26.0 %inner_increments.3 = (bf16[8,16,27648]{2,1,0:T(8,128)(2,1)}, f32[16,128]{1,0:T(8,128)}) custom-call(s32[12]{0:T(128)} %a_0_.14, s32[2,1]{1,0:T(2,128)} %copy.22.a_1_.a_0_, f32[8,16,27648]{2,1,0:T(8,128)} %get-tuple-element.32.a_2_.a_7_, f32[8,2304]{1,0:T(8,128)} %constant.22.clone.a_3_.a_11_.a_12_.a_13_, f32[128,128]{1,0:T(8,128)} %constant.23.clone.a_4_, ...), custom_call_target="tpu_custom_call" | custom-call | tf_op jit(solution)/shard_map/inner_increments/pallas_call | solution.py:630
  135.7 0.5 copy-done.7
  136.2 0.4 copy-done
  136.6 0.3 copy-done.1
  136.9 0.3 copy-done.2
  137.2 12.6 %moment_share.3 = (f32[16,128]{1,0:T(8,128)}, f32[16,128]{1,0:T(8,128)}) custom-call(s32[12]{0:T(128)} %a_0_.14, s32[2,1]{1,0:T(2,128)} %copy.22.a_1_.a_0_, f32[16,128]{1,0:T(8,128)} %get-tuple-element.29.a_2_, f32[16,128]{1,0:T(8,128)} %copy-done.10, f32[16,128]{1,0:T(8,128)} %copy-done.7, f32[16,128]{1,0:T(8,128)} %copy-done.6, ...), custom_call_target="tpu_custom_call" | custom-call | tf_op jit(solution)/shard_map/moment_share/pallas_call | solution.py:630
  149.7 3.0 %collective-permute-start.14 = (f32[16,128]{1,0:T(8,128)}, f32[16,128]{1,0:T(8,128)S(1)}, u32[]{:S(2)}, u32[]{:S(2)}) collective-permute-start(f32[16,128]{1,0:T(8,128)} %get-tuple-element.39.a_1_), channel_id=1, source_target_pairs={{0,3},{1,2},{2,1},{3,0},{4,7},{5,6},{6,5},{7,4},{8,11},{9,10},{10,... | collective-permute-start | bytes 24584 | tf_op jit(solution)/shard_map/ppermute | solution.py:696
  152.7 0.5 collective-permute-start.13
  153.2 1.0 collective-permute-start.12
  154.2 19.4 %last_update.1 = f32[8,16,27648]{2,1,0:T(8,128)} custom-call(s32[12]{0:T(128)} %a_0_.14, s32[2,1]{1,0:T(2,128)} %copy.22.a_1_.a_0_, f32[16,128]{1,0:T(8,128)} %get-tuple-element.29.a_2_, f32[16,128]{1,0:T(8,128)} %copy-done.10, f32[16,128]{1,0:T(8,128)} %copy-done.7, f32[16,128]{1,0:T(8,128)} %copy-done.6, f32[16,128]{1,0:T(8,128)} %get-tuple-element.30.a_6_, ...), custom_call_target="tpu_custom_call" | custom-call | tf_op jit(solution)/shard_map/last_update/pallas_call | solution.py:630
  173.6 0.5 copy-done.12
  174.2 2.5 %macroscopic.1 = (f32[8,8,16]{2,1,0:T(8,128)}, f32[1,8]{1,0:T(1,128)}) custom-call(s32[2,1]{1,0:T(2,128)} %copy.22.a_1_.a_0_, f32[16,128]{1,0:T(8,128)} %get-tuple-element.39.a_1_, f32[16,128]{1,0:T(8,128)} %copy-done.14, f32[16,128]{1,0:T(8,128)} %copy-done.13, f32[16,128]{1,0:T(8,128)} %copy-done.12, f32[16,128]{1,0:T(8,128)} %get-tuple-element.40.a_5_, ...), custom_call_target="tpu_custom_call" | custom-call | tf_op jit(solution)/shard_map/macroscopic/pallas_call | solution.py:717
  (37 shorter events, 0.4 us)
Async XLA Ops:
  13.9 38.7 %collective-permute-start.3 = (f32[12,16,1152]{2,1,0:T(8,128)}, f32[12,16,1152]{2,1,0:T(8,128)S(1)}, u32[]{:S(2)}, u32[]{:S(2)}) collective-permute-start(f32[12,16,1152]{2,1,0:T(8,128)} %get-tuple-element.25), channel_id=1, source_target_pairs={{0,8},{8,16},{16,24},{1,9},{9,17},{17,25},{2,10},{10,18},{18,26},{... | collective-permute-start | bytes 2654216 | tf_op jit(solution)/shard_map/ppermute | solution.py:701
  15.8 36.8 %collective-permute-start.4 = (f32[12,16,1152]{2,1,0:T(8,128)}, f32[12,16,1152]{2,1,0:T(8,128)S(1)}, u32[]{:S(2)}, u32[]{:S(2)}) collective-permute-start(f32[12,16,1152]{2,1,0:T(8,128)} %get-tuple-element.27), channel_id=1, source_target_pairs={{8,0},{16,8},{24,16},{9,1},{17,9},{25,17},{10,2},{18,10},{26,18},{... | collective-permute-start | bytes 2654216 | tf_op jit(solution)/shard_map/ppermute | solution.py:702
  19.5 33.2 %collective-permute-start.5 = (f32[12,8,2304]{2,1,0:T(8,128)}, f32[12,8,2304]{2,1,0:T(8,128)S(1)}, u32[]{:S(2)}, u32[]{:S(2)}) collective-permute-start(f32[12,8,2304]{2,1,0:T(8,128)} %get-tuple-element.28), channel_id=1, source_target_pairs={{0,4},{4,0},{1,5},{5,1},{2,6},{6,2},{3,7},{7,3},{8,12},{12,8},{9,1... | collective-permute-start | bytes 2654216 | tf_op jit(solution)/shard_map/ppermute | solution.py:700
  21.0 5.7 %collective-permute-start.2 = (f32[16,128]{1,0:T(8,128)}, f32[16,128]{1,0:T(8,128)S(1)}, u32[]{:S(2)}, u32[]{:S(2)}) collective-permute-start(f32[16,128]{1,0:T(8,128)} %get-tuple-element.23.a_2_), channel_id=1, source_target_pairs={{0,3},{1,2},{2,1},{3,0},{4,7},{5,6},{6,5},{7,4},{8,11},{9,10},{10,... | collective-permute-start | bytes 24584 | tf_op jit(solution)/shard_map/ppermute | solution.py:696
  24.6 28.0 %collective-permute-start.1 = (f32[16,128]{1,0:T(8,128)}, f32[16,128]{1,0:T(8,128)S(1)}, u32[]{:S(2)}, u32[]{:S(2)}) collective-permute-start(f32[16,128]{1,0:T(8,128)} %get-tuple-element.23.a_2_), channel_id=1, source_target_pairs={{0,2},{1,3},{2,0},{3,1},{4,6},{5,7},{6,4},{7,5},{8,10},{9,11},{10,... | collective-permute-start | bytes 24584 | tf_op jit(solution)/shard_map/ppermute | solution.py:696
  26.7 25.9 %copy-start.8 = (f32[16,128]{1,0:T(8,128)}, f32[16,128]{1,0:T(8,128)S(1)}, u32[]{:S(2)}) copy-start(f32[16,128]{1,0:T(8,128)S(1)} %collective-permute-done.2.a_5_) | copy-start | bytes 24580
  26.7 25.9 %collective-permute-start = (f32[16,128]{1,0:T(8,128)}, f32[16,128]{1,0:T(8,128)S(1)}, u32[]{:S(2)}, u32[]{:S(2)}) collective-permute-start(f32[16,128]{1,0:T(8,128)} %get-tuple-element.23.a_2_), channel_id=1, source_target_pairs={{0,1},{1,0},{2,3},{3,2},{4,5},{5,4},{6,7},{7,6},{8,9},{9,8},{10,11... | collective-permute-start | bytes 24584 | tf_op jit(solution)/shard_map/ppermute | solution.py:696
  52.6 0.6 copy-start.9
  52.6 0.6 copy-start.11
  52.6 0.9 copy-start.3
  52.6 1.2 copy-start.4
  52.7 1.5 copy-start.5
  84.1 51.6 %collective-permute-start.9 = (f32[12,16,1152]{2,1,0:T(8,128)}, f32[12,16,1152]{2,1,0:T(8,128)S(1)}, u32[]{:S(2)}, u32[]{:S(2)}) collective-permute-start(f32[12,16,1152]{2,1,0:T(8,128)} %get-tuple-element.34), channel_id=1, source_target_pairs={{0,8},{8,16},{16,24},{1,9},{9,17},{17,25},{2,10},{10,18},{18,26},{... | collective-permute-start | bytes 2654216 | tf_op jit(solution)/shard_map/ppermute | solution.py:701
  86.0 49.6 %collective-permute-start.10 = (f32[12,16,1152]{2,1,0:T(8,128)}, f32[12,16,1152]{2,1,0:T(8,128)S(1)}, u32[]{:S(2)}, u32[]{:S(2)}) collective-permute-start(f32[12,16,1152]{2,1,0:T(8,128)} %get-tuple-element.36), channel_id=1, source_target_pairs={{8,0},{16,8},{24,16},{9,1},{17,9},{25,17},{10,2},{18,10},{26,18},{... | collective-permute-start | bytes 2654216 | tf_op jit(solution)/shard_map/ppermute | solution.py:702
  89.8 45.8 %collective-permute-start.11 = (f32[12,8,2304]{2,1,0:T(8,128)}, f32[12,8,2304]{2,1,0:T(8,128)S(1)}, u32[]{:S(2)}, u32[]{:S(2)}) collective-permute-start(f32[12,8,2304]{2,1,0:T(8,128)} %get-tuple-element.37), channel_id=1, source_target_pairs={{0,4},{4,0},{1,5},{5,1},{2,6},{6,2},{3,7},{7,3},{8,12},{12,8},{9,1... | collective-permute-start | bytes 2654216 | tf_op jit(solution)/shard_map/ppermute | solution.py:700
  103.0 5.8 %collective-permute-start.8 = (f32[16,128]{1,0:T(8,128)}, f32[16,128]{1,0:T(8,128)S(1)}, u32[]{:S(2)}, u32[]{:S(2)}) collective-permute-start(f32[16,128]{1,0:T(8,128)} %get-tuple-element.29.a_2_), channel_id=1, source_target_pairs={{0,3},{1,2},{2,1},{3,0},{4,7},{5,6},{6,5},{7,4},{8,11},{9,10},{10,... | collective-permute-start | bytes 24584 | tf_op jit(solution)/shard_map/ppermute | solution.py:696
  106.6 28.9 %collective-permute-start.7 = (f32[16,128]{1,0:T(8,128)}, f32[16,128]{1,0:T(8,128)S(1)}, u32[]{:S(2)}, u32[]{:S(2)}) collective-permute-start(f32[16,128]{1,0:T(8,128)} %get-tuple-element.29.a_2_), channel_id=1, source_target_pairs={{0,2},{1,3},{2,0},{3,1},{4,6},{5,7},{6,4},{7,5},{8,10},{9,11},{10,... | collective-permute-start | bytes 24584 | tf_op jit(solution)/shard_map/ppermute | solution.py:696
  108.8 26.8 %copy-start.6 = (f32[16,128]{1,0:T(8,128)}, f32[16,128]{1,0:T(8,128)S(1)}, u32[]{:S(2)}) copy-start(f32[16,128]{1,0:T(8,128)S(1)} %collective-permute-done.8.a_5_) | copy-start | bytes 24580
  108.8 26.8 %collective-permute-start.6 = (f32[16,128]{1,0:T(8,128)}, f32[16,128]{1,0:T(8,128)S(1)}, u32[]{:S(2)}, u32[]{:S(2)}) collective-permute-start(f32[16,128]{1,0:T(8,128)} %get-tuple-element.29.a_2_), channel_id=1, source_target_pairs={{0,1},{1,0},{2,3},{3,2},{4,5},{5,4},{6,7},{7,6},{8,9},{9,8},{10,11... | collective-permute-start | bytes 24584 | tf_op jit(solution)/shard_map/ppermute | solution.py:696
  135.6 0.6 copy-start.7
  135.6 0.6 copy-start.10
  135.6 1.0 copy-start
  135.7 1.2 copy-start.1
  135.7 1.5 copy-start.2
  149.7 23.9 %collective-permute-start.14 = (f32[16,128]{1,0:T(8,128)}, f32[16,128]{1,0:T(8,128)S(1)}, u32[]{:S(2)}, u32[]{:S(2)}) collective-permute-start(f32[16,128]{1,0:T(8,128)} %get-tuple-element.39.a_1_), channel_id=1, source_target_pairs={{0,3},{1,2},{2,1},{3,0},{4,7},{5,6},{6,5},{7,4},{8,11},{9,10},{10,... | collective-permute-start | bytes 24584 | tf_op jit(solution)/shard_map/ppermute | solution.py:696
  152.7 20.9 %collective-permute-start.13 = (f32[16,128]{1,0:T(8,128)}, f32[16,128]{1,0:T(8,128)S(1)}, u32[]{:S(2)}, u32[]{:S(2)}) collective-permute-start(f32[16,128]{1,0:T(8,128)} %get-tuple-element.39.a_1_), channel_id=1, source_target_pairs={{0,2},{1,3},{2,0},{3,1},{4,6},{5,7},{6,4},{7,5},{8,10},{9,11},{10,... | collective-permute-start | bytes 24584 | tf_op jit(solution)/shard_map/ppermute | solution.py:696
  153.2 20.4 %collective-permute-start.12 = (f32[16,128]{1,0:T(8,128)}, f32[16,128]{1,0:T(8,128)S(1)}, u32[]{:S(2)}, u32[]{:S(2)}) collective-permute-start(f32[16,128]{1,0:T(8,128)} %get-tuple-element.39.a_1_), channel_id=1, source_target_pairs={{0,1},{1,0},{2,3},{3,2},{4,5},{5,4},{6,7},{7,6},{8,9},{9,8},{10,11... | collective-permute-start | bytes 24584 | tf_op jit(solution)/shard_map/ppermute | solution.py:696
  173.6 0.6 copy-start.12
  173.6 0.6 copy-start.13
  173.6 0.6 copy-start.14

commit v3 on v2

--- a/solution.py
+++ b/solution.py
@@ -30,7 +30,6 @@
 WINDOW = 512
 GHOST_ROWS = 32
 MOMENTS = 16
-PARTS_W = 3
 F32 = jnp.float32
 BF16 = jnp.bfloat16
 PIECES = [(t, TILE, 0) for t in range(0, 1024, TILE)] + [(1024, 128, 0), (1152, 128, 1)] + [
@@ -185,21 +184,6 @@
     return rows.astype(np.float32)
 
 
-def weight_table():
-    vr = np.repeat(GRID_R, NVT)
-    vt = np.tile(GRID_T, NVR)
-    square = vr**2 + vt**2
-    columns = [np.ones(PLANE), vr, vt, vr**2, vt**2, vr * vt, vr * square, vt * square]
-    table = np.zeros((PLANE, 128))
-    for k, column in enumerate(columns):
-        rest = column.copy()
-        for part in range(PARTS_W):
-            piece = rest.astype(ml_dtypes.bfloat16).astype(np.float64)
-            table[:, k + 8 * part] = piece
-            rest = rest - piece
-    return table.astype(ml_dtypes.bfloat16)
-
-
 def edge_table():
     table = np.zeros((2, NODE_COUNT, 128))
     for r in range(NODES):
@@ -220,7 +204,6 @@
 ROTATION_M = rotation_table()
 MIRROR_M = mirror_table()
 ROWS = plane_rows()
-WEIGHT_M = weight_table()
 EDGE = edge_table()
 NODE_POS = node_columns()
 
@@ -231,11 +214,6 @@
 
 def dot(x, y):
     return jnp.dot(x, y, preferred_element_type=F32)
-
-
-def split(x):
-    high = x.astype(BF16)
-    return high, (x - high.astype(F32)).astype(BF16)
 
 
 def macroscopic_of(m):
@@ -253,29 +231,49 @@
     return rho, ur, ut, uz, temp, qr, qt, qz
 
 
-def add_speed_sums(sums_ref, sums, vz):
-    one = vz * sums
-    two = vz * one
-    for k, value in enumerate([sums, one, two, vz * two, jnp.abs(vz) * sums]):
-        sums_ref[k] += value
-
-
-def moment_rows(sums_ref):
-    lane = lax.broadcasted_iota(jnp.int32, (NODE_COUNT, 128), 1)
-    e = []
-    for k in range(5):
-        x = sums_ref[k]
-        e.append(x + pltpu.roll(x, 120, 1) + pltpu.roll(x, 112, 1))
-    pick = lambda k, c: e[k][:, c : c + 1]
-    columns = [
-        pick(0, 0), pick(0, 1), pick(0, 2), pick(1, 0),
-        pick(0, 3), pick(0, 4), pick(0, 5), pick(2, 0), pick(1, 1), pick(1, 2),
-        pick(0, 6) + pick(2, 1), pick(0, 7) + pick(2, 2), pick(1, 3) + pick(1, 4) + pick(3, 0), pick(4, 0),
+def add_speed_sums(field, vz, sums):
+    one = field * vz
+    two = one * vz
+    return [
+        sums[0] + field,
+        sums[1] + one,
+        sums[2] + two,
+        sums[3] + two * vz,
+        sums[4] + field * jnp.abs(vz),
     ]
-    table = jnp.zeros((NODE_COUNT, 128), F32)
-    for k, column in enumerate(columns):
-        table = jnp.where(lane == k, WEIGHT * column, table)
-    return jnp.transpose(table)[0:MOMENTS, :]
+
+
+def finish_moments(sums_ref, rows_ref, table_ref, out_ref):
+    lane = lax.broadcasted_iota(jnp.int32, (LOCAL_Z, 128), 1)
+
+    def one_radius(r, carry):
+        acc = [jnp.zeros((LOCAL_Z, 128), F32) for _ in range(14)]
+        for j in range(PLANE // 128):
+            at = pl.ds(j * 128, 128)
+            vr = rows_ref[0:1, at]
+            vt = rows_ref[1:2, at]
+            g0, g1, g2, g3, g4 = (sums_ref[k, r, :, at] for k in range(5))
+            a = vr * g0
+            b = vt * g0
+            aa = vr * a
+            bb = vt * b
+            c = vr * g1
+            d = vt * g1
+            perp = aa + bb + g2
+            new = [g0, a, b, g1, aa, bb, vr * b, g2, c, d, vr * perp, vt * perp, vr * c + vt * d + g3, g4]
+            acc = [x + y for x, y in zip(acc, new)]
+        block = jnp.zeros((LOCAL_Z, 128), F32)
+        for k in range(14):
+            block = jnp.where(lane == k, WEIGHT * jnp.sum(acc[k], axis=1, keepdims=True), block)
+        table_ref[pl.ds(pl.multiple_of(r * LOCAL_Z, LOCAL_Z), LOCAL_Z), :] = block
+        return carry
+
+    lax.fori_loop(0, NODES, one_radius, 0)
+    out_ref[...] = jnp.transpose(table_ref[...])[0:MOMENTS, :]
+
+
+def clear_sums(sums_ref):
+    sums_ref[...] = jnp.zeros(sums_ref.shape, F32)
 
 
 def places_of():
@@ -310,92 +308,98 @@
     return ref[:, :, first : first + lanes].reshape(NODE_COUNT, lanes)
 
 
+def send_traces(count, place, narrow_ref, trace_ref, right_ref, left_ref, axial_ref):
+    for s in range(count):
+        for first, lanes, side in PIECES:
+            narrow = narrow_ref[s, :, first : first + lanes]
+            send_piece(s, first, lanes, side, place, narrow, trace_ref, right_ref, left_ref, axial_ref)
+
+
 def first_kernel(
-    count, order, codes, f_ref, weight_ref, trace_ref, mirror_ref,
-    right_ref, left_ref, turned_ref, axial_ref, mom_ref, sums_ref,
+    count, order, codes, f_ref, rows_ref, trace_ref, mirror_ref,
+    right_ref, left_ref, turned_ref, axial_ref, mom_ref, sums_ref, table_ref,
 ):
     step = pl.program_id(0)
     row, place = places_of()
 
     @pl.when(step == 0)
     def _():
-        sums_ref[...] = jnp.zeros(sums_ref.shape, F32)
-
-    for s in range(count):
-        sums = jnp.zeros((NODE_COUNT, 128), F32)
-        for first, lanes, side in PIECES:
-            high, low = split(nodes_of(f_ref, s * PLANE + first, lanes))
-            weights = weight_ref[first : first + lanes, :]
-            sums = sums + dot(
-                jnp.concatenate([high, low], axis=1), jnp.concatenate([weights, weights], axis=0)
-            )
-            send_piece(s, first, lanes, side, place, high, trace_ref, right_ref, left_ref, axial_ref)
-        add_speed_sums(sums_ref, sums, slot_speed(order, step * count + s))
+        clear_sums(sums_ref)
+
+    speeds = [slot_speed(order, step * count + s) for s in range(count)]
+    for first, lanes, side in PIECES:
+        narrow = [[] for s in range(count)]
+        for inside in range(0, lanes, 128):
+            at = pl.ds(first + inside, 128)
+            column = [[] for s in range(count)]
+            for r in range(NODES):
+                sums = [sums_ref[k, r, :, at] for k in range(5)]
+                for s in range(count):
+                    field = f_ref[r, :, pl.ds(s * PLANE + first + inside, 128)]
+                    sums = add_speed_sums(field, speeds[s], sums)
+                    column[s].append(field.astype(BF16))
+                for k in range(5):
+                    sums_ref[k, r, :, at] = sums[k]
+            for s in range(count):
+                narrow[s].append(jnp.concatenate(column[s], axis=0))
+        for s in range(count):
+            block = jnp.concatenate(narrow[s], axis=1) if len(narrow[s]) > 1 else narrow[s][0]
+            send_piece(s, first, lanes, side, place, block, trace_ref, right_ref, left_ref, axial_ref)
     turn_traces(count, row, mirror_ref, left_ref, turned_ref)
 
     @pl.when(step == pl.num_programs(0) - 1)
     def _():
-        mom_ref[...] = moment_rows(sums_ref)
+        finish_moments(sums_ref, rows_ref, table_ref, mom_ref)
 
 
 def inner_kernel(
-    count, order, codes, f_ref, rows_ref, pos_ref, weight_ref, radial_ref, axial_m_ref, rot_ref,
-    out_ref, mom_ref, sums_ref, inverse_ref, pad_ref, lhs_ref,
+    count, order, codes, f_ref, rows_ref, pos_ref, radial_ref, axial_m_ref, rot_ref,
+    out_ref, inverse_ref, pad_ref, lhs_ref,
 ):
     step = pl.program_id(0)
     row, place = places_of()
 
     @pl.when(step == 0)
     def _():
-        sums_ref[...] = jnp.zeros(sums_ref.shape, F32)
-        pad_ref[:, 0:128] = jnp.zeros((NODE_COUNT, 128), BF16)
-        pad_ref[:, 128 + PLANE :] = jnp.zeros((NODE_COUNT, 128), BF16)
+        pad_ref[:, :, 0:128] = jnp.zeros((count, NODE_COUNT, 128), BF16)
+        pad_ref[:, :, 128 + PLANE :] = jnp.zeros((count, NODE_COUNT, 128), BF16)
         inverse_ref[...] = 1.0 / (ELEMENT_WIDTH * (row.astype(F32) + pos_ref[...]))
-        lhs_ref[0, :, 0:128] = radial_ref[jnp.where(row == lax.axis_size("row") - 1, 2, 0)]
-        lhs_ref[1, :, 0:128] = radial_ref[1]
+        minus = radial_ref[jnp.where(row == lax.axis_size("row") - 1, 2, 0)]
+        for s in range(count):
+            lhs_ref[s, 0, 0:NODE_COUNT] = minus
+            lhs_ref[s, 1, 0:NODE_COUNT] = radial_ref[1]
 
     kind_out = jnp.where(jnp.logical_and(place == 1, codes[1, 0] == 2), 2, 0)
     inverse = inverse_ref[...]
     for s in range(count):
         vz = slot_speed(order, step * count + s)
         axial = (vz * axial_m_ref[jnp.where(vz > 0, 1, kind_out)]).astype(BF16)
-        lhs_ref[0, :, 128:256] = axial
-        lhs_ref[1, :, 128:256] = axial
+        lhs_ref[s, 0, NODE_COUNT:] = axial
+        lhs_ref[s, 1, NODE_COUNT:] = axial
         for j in range(PLANE // 128):
             field = nodes_of(f_ref, s * PLANE + j * 128, 128)
-            pad_ref[:, 128 + j * 128 : 256 + j * 128] = (field * inverse).astype(BF16)
-        sums = jnp.zeros((NODE_COUNT, 128), F32)
+            pad_ref[s, :, 128 + j * 128 : 256 + j * 128] = (field * inverse).astype(BF16)
+
+    for tile in range(PLANE // TILE):
+        start = tile * TILE
+        turned = dot(pad_ref[:, :, start : start + WINDOW].reshape(count * NODE_COUNT, WINDOW), rot_ref[tile])
         for first, lanes, side in PIECES:
-            tile = first // TILE
-            inside = first - tile * TILE
-            start = tile * TILE
-            field = nodes_of(f_ref, s * PLANE + first, lanes)
-            moved = (field * rows_ref[0:1, first : first + lanes]).astype(BF16)
-            left = jnp.concatenate([lhs_ref[side], pad_ref[:, start : start + WINDOW]], axis=1)
-            right = jnp.concatenate(
-                [moved, field.astype(BF16), rot_ref[tile, :, inside : inside + lanes]], axis=0
-            )
-            change = dot(left, right).astype(BF16)
-            out_ref[:, :, s * PLANE + first : s * PLANE + first + lanes] = change.reshape(
-                NODES, LOCAL_Z, lanes
-            )
-            sums = sums + dot(change, weight_ref[first : first + lanes, :])
-        add_speed_sums(sums_ref, sums, vz)
-
-    @pl.when(step == pl.num_programs(0) - 1)
-    def _():
-        mom_ref[...] = moment_rows(sums_ref)
+            if first // TILE != tile:
+                continue
+            vr = rows_ref[0:1, first : first + lanes]
+            inside = first - start
+            for s in range(count):
+                here = s * PLANE + first
+                moved = dot(lhs_ref[s, side], nodes_of(f_ref, here, lanes).astype(BF16))
+                change = turned[s * NODE_COUNT : (s + 1) * NODE_COUNT, inside : inside + lanes]
+                change = change + vr * moved[0:NODE_COUNT] + moved[NODE_COUNT:]
+                out_ref[:, :, here : here + lanes] = change.astype(BF16).reshape(NODES, LOCAL_Z, lanes)
 
 
 def total_of(parts):
     while len(parts) > 1:
         parts = [parts[k] + parts[k + 1] for k in range(0, len(parts), 2)]
     return parts[0]
-
-
-def total_moments(part_refs, base_ref):
-    total = total_of([p[...] for p in part_refs])
-    return total if base_ref is None else total + base_ref[...]
 
 
 def prepare_nodes(total, codes, place, rows_ref, edge_ref, table_ref, node_ref, wall_ref, plane_ref):
@@ -472,100 +476,74 @@
         ghost_ref[:, at] = rows.astype(BF16)
 
 
-def outer_kernel(count, part_count, based, last, order, codes, *refs):
+def outer_kernel(count, part_count, last, order, codes, *refs):
     part_refs, refs = refs[:part_count], refs[part_count:]
-    base_ref = None
-    if based:
-        base_ref, refs = refs[0], refs[1:]
     f_ref, inner_ref, in_left_ref, in_turned_ref, in_right_ref, in_axial_ref = refs[:6]
     rows_ref, edge_ref, ghost_r_ref, ghost_z_ref = refs[6:10]
     refs = refs[10:]
     if last:
-        out_ref, refs = refs[0], refs[1:]
+        (out_ref, mom_ref), refs = refs[:2], refs[2:]
     else:
-        (trace_ref, mirror_ref, out_ref, right_ref, left_ref, turned_ref, axial_ref), refs = refs[:7], refs[7:]
-    plane_ref, node_ref, wall_ref, slot_ref, lhs_ref, ghost_ref, table_ref = refs
+        (trace_ref, mirror_ref, out_ref, right_ref, left_ref, turned_ref, axial_ref, mom_ref), refs = refs[:8], refs[8:]
+        narrow_ref, refs = refs[0], refs[1:]
+    plane_ref, node_ref, wall_ref, slot_ref, work_ref, sums_ref, lhs_ref, ghost_ref, table_ref = refs
     step = pl.program_id(0)
     row, place = places_of()
 
     @pl.when(step == 0)
     def _():
-        total = total_moments(part_refs, base_ref)
+        clear_sums(sums_ref)
+        total = total_of([p[...] for p in part_refs])
         prepare_nodes(total, codes, place, rows_ref, edge_ref, table_ref, node_ref, wall_ref, plane_ref)
 
+    speeds = [slot_speed(order, step * count + s) for s in range(count)]
     for s in range(count):
-        vz = slot_speed(order, step * count + s)
+        vz = speeds[s]
         for k, value in enumerate(slot_factors(vz, node_ref)):
-            slot_ref[k] = value
+            slot_ref[s, k] = value
         ghost_lifts(vz, ghost_r_ref, ghost_z_ref, lhs_ref)
         ghost_rows(
             s, vz, place, in_left_ref, in_turned_ref, in_right_ref, in_axial_ref, rows_ref, wall_ref, ghost_ref
         )
         for first, lanes, side in PIECES:
-            lifted = dot(lhs_ref[side, :, 0:GHOST_ROWS], ghost_ref[:, first : first + lanes])
-            pieces = []
-            for inside in range(0, lanes, 128):
-                here = s * PLANE + first + inside
-                at = pl.ds(first + inside, 128)
-                new = nodes_of(f_ref, here, 128) * node_ref[5] + nodes_of(inner_ref, here, 128).astype(F32)
-                new = new + lifted[:, inside : inside + 128]
+            work_ref[s, :, first : first + lanes] = dot(
+                lhs_ref[side, :, 0:GHOST_ROWS], ghost_ref[:, first : first + lanes]
+            )
+
+    def update(r, carry):
+        rows = pl.ds(pl.multiple_of(r * LOCAL_Z, LOCAL_Z), LOCAL_Z)
+        keep = node_ref[5, rows, :]
+        factor = [[slot_ref[s, k, rows, :] for k in range(4)] for s in range(count)]
+        for j in range(PLANE // 128):
+            at = pl.ds(j * 128, 128)
+            planes = [plane_ref[k, rows, at] for k in range(4)]
+            sums = [sums_ref[k, r, :, at] for k in range(5)]
+            for s in range(count):
+                here = pl.ds(s * PLANE + j * 128, 128)
+                new = f_ref[r, :, here] * keep + work_ref[s, rows, at] + inner_ref[r, :, here].astype(F32)
                 for k in range(4):
-                    new = new + plane_ref[k, :, at] * slot_ref[k]
-                out_ref[:, :, here : here + 128] = new.reshape(NODES, LOCAL_Z, 128)
-                pieces.append(new.astype(BF16))
-            if not last:
-                narrow = jnp.concatenate(pieces, axis=1) if len(pieces) > 1 else pieces[0]
-                send_piece(s, first, lanes, side, place, narrow, trace_ref, right_ref, left_ref, axial_ref)
+                    new = new + planes[k] * factor[s][k]
+                out_ref[r, :, here] = new
+                sums = add_speed_sums(new, speeds[s], sums)
+                if not last:
+                    narrow_ref[s, rows, at] = new.astype(BF16)
+            for k in range(5):
+                sums_ref[k, r, :, at] = sums[k]
+        return carry
+
+    lax.fori_loop(0, NODES, update, 0)
     if not last:
+        send_traces(count, place, narrow_ref, trace_ref, right_ref, left_ref, axial_ref)
         turn_traces(count, row, mirror_ref, left_ref, turned_ref)
-
-
-def moment_kernel(count, part_count, based, order, codes, *refs):
-    part_refs, refs = refs[:part_count], refs[part_count:]
-    base_ref = None
-    if based:
-        base_ref, refs = refs[0], refs[1:]
-    inner_mom_ref, in_left_ref, in_turned_ref, in_right_ref, in_axial_ref = refs[:5]
-    rows_ref, edge_ref, ghost_r_ref, ghost_z_ref, weight_ref = refs[5:10]
-    share_ref, kept_ref = refs[10:12]
-    plane_ref, node_ref, wall_ref, lhs_ref, ghost_ref, table_ref, sums_ref, plane_sums_ref = refs[12:]
-    step = pl.program_id(0)
-    row, place = places_of()
-
-    @pl.when(step == 0)
-    def _():
-        sums_ref[...] = jnp.zeros(sums_ref.shape, F32)
-        total = total_moments(part_refs, base_ref)
-        kept_ref[...] = total * (1.0 - total[0:1, :] * (TIME_STEP / KNUDSEN))
-        prepare_nodes(total, codes, place, rows_ref, edge_ref, table_ref, node_ref, wall_ref, plane_ref)
-        for k in range(4):
-            high, low = split(plane_ref[k])
-            plane_sums_ref[k] = dot(high, weight_ref[...]) + dot(low, weight_ref[...])
-
-    for s in range(count):
-        vz = slot_speed(order, step * count + s)
-        sums = jnp.zeros((NODE_COUNT, 128), F32)
-        for k, value in enumerate(slot_factors(vz, node_ref)):
-            sums = sums + plane_sums_ref[k] * value
-        ghost_lifts(vz, ghost_r_ref, ghost_z_ref, lhs_ref)
-        ghost_rows(
-            s, vz, place, in_left_ref, in_turned_ref, in_right_ref, in_axial_ref, rows_ref, wall_ref, ghost_ref
-        )
-        for side in range(2):
-            span = pl.ds(side * HALF, HALF)
-            high, low = split(dot(ghost_ref[:, span], weight_ref[span, :]))
-            lift = lhs_ref[side, :, 0:GHOST_ROWS]
-            sums = sums + dot(lift, high) + dot(lift, low)
-        add_speed_sums(sums_ref, sums, vz)
 
     @pl.when(step == pl.num_programs(0) - 1)
     def _():
-        share_ref[...] = moment_rows(sums_ref) + inner_mom_ref[...]
+        finish_moments(sums_ref, rows_ref, table_ref, mom_ref)
 
 
 def last_kernel(part_count, codes, *refs):
-    total_ref = total_moments(refs[:part_count], refs[part_count])
-    edge_ref, macro_ref, flux_ref = refs[part_count + 1 :]
+    total_ref = total_of([p[...] for p in refs[:part_count]])
+    edge_ref, macro_ref, flux_ref = refs[part_count:]
     row, place = places_of()
     values = macroscopic_of(lambda k: total_ref[k : k + 1, :])
     for k in range(8):
@@ -600,7 +578,6 @@
     radial_m, axial_m = jnp.asarray(RADIAL_M), jnp.asarray(AXIAL_M)
     ghost_r, ghost_z = jnp.asarray(GHOST_R), jnp.asarray(GHOST_Z)
     trace_m, mirror_m, rot_m = jnp.asarray(TRACE_M), jnp.asarray(MIRROR_M), jnp.asarray(ROTATION_M)
-    weight_m = jnp.asarray(WEIGHT_M)
 
     big = pl.BlockSpec((NODES, LOCAL_Z, group * PLANE), lambda i, *n: (0, 0, i))
     radial_spec = pl.BlockSpec((group, LOCAL_Z, HALF), lambda i, *n: (i, 0, 0))
@@ -614,7 +591,8 @@
     trace_shapes = [radial_shape, radial_shape, radial_shape, axial_shape]
     ghost_specs = [radial_spec, radial_spec, radial_spec, axial_spec]
     square = pltpu.VMEM((NODE_COUNT, 128), F32)
-    sums_scratch = pltpu.VMEM((5, NODE_COUNT, 128), F32)
+    sums_scratch = pltpu.VMEM((5, NODES, LOCAL_Z, PLANE), F32)
+    narrow_scratch = pltpu.VMEM((group, NODE_COUNT, PLANE), BF16)
     node_scratch = [
         pltpu.VMEM((4, NODE_COUNT, PLANE), F32),
         pltpu.VMEM((10, NODE_COUNT, 128), F32),
@@ -645,49 +623,39 @@
         return [whole(x.shape) for x in tables]
 
     def first(f):
-        tables = [weight_m, trace_m, mirror_m]
+        tables = [rows, trace_m, mirror_m]
         return call(
             lambda *a: first_kernel(group, *a), "moments_and_traces", [big] + all_whole(tables),
-            trace_specs + [mom_spec], trace_shapes + [mom_shape], [sums_scratch], [f] + tables,
+            trace_specs + [mom_spec], trace_shapes + [mom_shape], [sums_scratch, square], [f] + tables,
         )
 
     def inner(f):
-        tables = [rows, pos, weight_m, radial_m, axial_m, rot_m]
+        tables = [rows, pos, radial_m, axial_m, rot_m]
         scratch = [
-            sums_scratch,
             square,
-            pltpu.VMEM((NODE_COUNT, PLANE + 256), BF16),
-            pltpu.VMEM((2, NODE_COUNT, 256), BF16),
+            pltpu.VMEM((group, NODE_COUNT, PLANE + 256), BF16),
+            pltpu.VMEM((group, 2, 2 * NODE_COUNT, 128), BF16),
         ]
         return call(
             lambda *a: inner_kernel(group, *a), "inner_increments", [big] + all_whole(tables),
-            [big, mom_spec], [jax.ShapeDtypeStruct(f.shape, BF16), mom_shape], scratch, [f] + tables,
-        )
-
-    def outer(f, change, ghosts, parts, base, last):
-        bases = [] if base is None else [base]
+            [big], [jax.ShapeDtypeStruct(f.shape, BF16)], scratch, [f] + tables,
+        )[0]
+
+    def outer(f, change, ghosts, parts, last):
         tables = [rows, edge, ghost_r, ghost_z] + ([] if last else [trace_m, mirror_m])
+        scratch = node_scratch + [
+            pltpu.VMEM((group, 4, NODE_COUNT, 128), F32),
+            pltpu.VMEM((group, NODE_COUNT, PLANE), F32),
+            sums_scratch,
+        ]
         return call(
-            lambda *a: outer_kernel(group, len(parts), bool(bases), last, *a),
+            lambda *a: outer_kernel(group, len(parts), last, *a),
             "last_update" if last else "update",
-            [mom_spec] * (len(parts) + len(bases)) + [big, big] + ghost_specs + all_whole(tables),
-            [big] + ([] if last else trace_specs),
-            [big_shape] + ([] if last else trace_shapes),
-            node_scratch + [pltpu.VMEM((4, NODE_COUNT, 128), F32)] + ghost_scratch,
-            [*parts, *bases, f, change, *ghosts, *tables],
-        )
-
-    def share(change_moments, ghosts, parts, base):
-        bases = [] if base is None else [base]
-        tables = [rows, edge, ghost_r, ghost_z, weight_m]
-        return call(
-            lambda *a: moment_kernel(group, len(parts), bool(bases), *a),
-            "moment_share",
-            [mom_spec] * (len(parts) + len(bases) + 1) + ghost_specs + all_whole(tables),
-            [mom_spec, mom_spec],
-            [mom_shape, mom_shape],
-            node_scratch + ghost_scratch + [sums_scratch, pltpu.VMEM((4, NODE_COUNT, 128), F32)],
-            [*parts, *bases, change_moments, *ghosts, *tables],
+            [mom_spec] * len(parts) + [big, big] + ghost_specs + all_whole(tables),
+            [big] + ([] if last else trace_specs) + [mom_spec],
+            [big_shape] + ([] if last else trace_shapes) + [mom_shape],
+            ([] if last else [narrow_scratch]) + scratch + ghost_scratch,
+            [*parts, f, change, *ghosts, *tables],
         )
 
     def spread(moments):
@@ -704,22 +672,19 @@
 
     current = distribution
     *traces, moments = first(current)
-    base = None
     for number in range(STEPS):
         last = number == STEPS - 1
         ghosts = halo(*traces)
         parts = spread(moments)
-        change, change_moments = inner(current)
-        moments, next_base = share(change_moments, ghosts, parts, base)
-        current, *traces = outer(current, change, ghosts, parts, base, last)
-        base = next_base
+        change = inner(current)
+        current, *traces, moments = outer(current, change, ghosts, parts, last)
     parts = spread(moments)
     macro, flux = pl.pallas_call(
         lambda *a: last_kernel(len(parts), *a),
         grid_spec=pltpu.PrefetchScalarGridSpec(
             num_scalar_prefetch=1,
             grid=(1,),
-            in_specs=[mom_spec] * (len(parts) + 1) + [whole(edge.shape)],
+            in_specs=[mom_spec] * len(parts) + [whole(edge.shape)],
             out_specs=[whole((8, NODES, LOCAL_Z)), whole((1, NODES))],
         ),
         out_shape=[
@@ -727,7 +692,7 @@
             jax.ShapeDtypeStruct((1, NODES), F32),
         ],
         name="macroscopic",
-    )(edge_codes, *parts, base, edge)
+    )(edge_codes, *parts, edge)
     return (current, macro, flux)
 
 

time: 177 us -> 139 us (0.79)
  Pallas kernels: 141 us -> 98.3 us
  waiting for transfers between devices: 3.6 us -> 6.96 us
    pallas_call x7 -> x5, Pallas kernels: 138 us -> 95.8 us  [call(): pl.pallas_call(body, grid_spec=pltpu.PrefetchScalarGridSpec(num_scalar_pr...]
    ppermute x9, waiting for transfers between devices: 3.59 us -> 6.95 us  [spread(): lax.ppermute(moments, 'vert', [(i, i ^ shift) for i in range(verts)])]
  transfers between devices with their start and end apart: 15 -> 15, of which waited for: 2 -> 4; matrix products, arithmetic and copies ran while one was open for 0% -> 0% of each run, Pallas kernels for 47% -> 20%
where the time goes in v3:
time: 139 us; the launch traced here: 138 us
  Pallas kernels  98.3 us (71%)
  starting transfers between devices  26.5 us (19%)
  waiting for transfers between devices  6.96 us (5%)
  local copies, waits for them, and re-layouts  5.42 us (4%)
    pallas_call x5, Pallas kernels, call(): pl.pallas_call(body, grid_spec=pltpu.PrefetchScalarGridSpec(num_scalar_pr...  95.8 us
    ppermute x9, starting transfers between devices, spread(): lax.ppermute(moments, 'vert', [(i, i ^ shift) for i in range(verts)])  12.9 us
    ppermute x2, starting transfers between devices, halo(): lax.ppermute(left, 'row', [(i + 1, i) for i in range(rows_total - 1)])  7.46 us
    ppermute x9, waiting for transfers between devices, spread(): lax.ppermute(moments, 'vert', [(i, i ^ shift) for i in range(verts)])  6.95 us
    unnamed x31, local copies, waits for them, and re-layouts  5.42 us
    ppermute x2, starting transfers between devices, halo(): lax.ppermute(right, 'row', [(i, i + 1) for i in range(rows_total - 1)])  3.83 us
  transfers between devices with their start and end apart: 15, of which 4 were waited for; matrix products, arithmetic and copies ran while one was open for 0% of the time, Pallas kernels for 20%

profile of v3, /device:TPU:4, one launch (start us, length us, event | category | flops | bytes accessed | tf_op | source)
XLA Modules:
  0.0 138.0 jit_solution(16535608554901638938)
XLA Ops:
  0.6 1.3 copy.20.a_1_.a_0_
  1.9 13.9 %moments_and_traces.1 = (f32[12,16,1152]{2,1,0:T(8,128)}, f32[12,16,1152]{2,1,0:T(8,128)}, f32[12,16,1152]{2,1,0:T(8,128)}, f32[12,8,2304]{2,1,0:T(8,128)}, f32[16,128]{1,0:T(8,128)}) custom-call(s32[12]{0:T(128)} %a_0_.10, s32[2,1]{1,0:T(2,128)} %copy.20.a_1_.a_0_, f32[8,16,27648]{2,1,0:T(8,128)} %a_6_.3, f32[8,2304]{1,0:T(8,128)} %constant.20.clone.a_3_.a_12_, ...), custom_call_target="tpu_custom_call" | custom-call | tf_op jit(solution)/shard_map/moments_and_traces/pallas_call | solution.py:608
  15.9 1.9 %collective-permute-start.3 = (f32[12,16,1152]{2,1,0:T(8,128)}, f32[12,16,1152]{2,1,0:T(8,128)S(1)}, u32[]{:S(2)}, u32[]{:S(2)}) collective-permute-start(f32[12,16,1152]{2,1,0:T(8,128)} %get-tuple-element.19), channel_id=1, source_target_pairs={{0,8},{8,16},{16,24},{1,9},{9,17},{17,25},{2,10},{10,18},{18,26},{... | collective-permute-start | bytes 2654216 | tf_op jit(solution)/shard_map/ppermute | solution.py:669
  17.8 3.6 %collective-permute-start.4 = (f32[12,16,1152]{2,1,0:T(8,128)}, f32[12,16,1152]{2,1,0:T(8,128)S(1)}, u32[]{:S(2)}, u32[]{:S(2)}) collective-permute-start(f32[12,16,1152]{2,1,0:T(8,128)} %get-tuple-element.21), channel_id=1, source_target_pairs={{8,0},{16,8},{24,16},{9,1},{17,9},{25,17},{10,2},{18,10},{26,18},{... | collective-permute-start | bytes 2654216 | tf_op jit(solution)/shard_map/ppermute | solution.py:670
  21.4 1.5 %collective-permute-start.5 = (f32[12,8,2304]{2,1,0:T(8,128)}, f32[12,8,2304]{2,1,0:T(8,128)S(1)}, u32[]{:S(2)}, u32[]{:S(2)}) collective-permute-start(f32[12,8,2304]{2,1,0:T(8,128)} %get-tuple-element.22), channel_id=1, source_target_pairs={{0,4},{4,0},{1,5},{5,1},{2,6},{6,2},{3,7},{7,3},{8,12},{12,8},{9,1... | collective-permute-start | bytes 2654216 | tf_op jit(solution)/shard_map/ppermute | solution.py:668
  23.0 3.6 %collective-permute-start.2 = (f32[16,128]{1,0:T(8,128)}, f32[16,128]{1,0:T(8,128)S(1)}, u32[]{:S(2)}, u32[]{:S(2)}) collective-permute-start(f32[16,128]{1,0:T(8,128)} %get-tuple-element.18.a_2_), channel_id=1, source_target_pairs={{0,3},{1,2},{2,1},{3,0},{4,7},{5,6},{6,5},{7,4},{8,11},{9,10},{10,... | collective-permute-start | bytes 24584 | tf_op jit(solution)/shard_map/ppermute | solution.py:664
  26.6 2.1 %collective-permute-done.2.a_5_ = f32[16,128]{1,0:T(8,128)S(1)} collective-permute-done((f32[16,128]{1,0:T(8,128)}, f32[16,128]{1,0:T(8,128)S(1)}, u32[]{:S(2)}, u32[]{:S(2)}) %collective-permute-start.2) | collective-permute-done | bytes 8224 | tf_op jit(solution)/shard_map/ppermute | solution.py:664
  28.6 13.8 %inner_increments.2.a_7_ = bf16[8,16,27648]{2,1,0:T(8,128)(2,1)} custom-call(s32[12]{0:T(128)} %a_0_.10, s32[2,1]{1,0:T(2,128)} %copy.20.a_1_.a_0_, f32[8,16,27648]{2,1,0:T(8,128)} %a_6_.3, f32[8,2304]{1,0:T(8,128)} %constant.20.clone.a_3_.a_12_, f32[128,128]{1,0:T(8,128)} %constant.21.clone.a_4_, bf16[3,128,128]{2,1,0:T(8,128)(2,1)} %constant.23.clone.a_5_, ...), custom_call_target="tpu_custom_call" | custom-call | tf_op jit(solution)/shard_map/inner_increments/pallas_call | solution.py:608
  42.6 0.5 copy-done.9
  43.1 0.4 copy-done
  43.7 0.3 copy-done.2
  44.0 28.8 %update.1 = (f32[8,16,27648]{2,1,0:T(8,128)}, f32[12,16,1152]{2,1,0:T(8,128)}, f32[12,16,1152]{2,1,0:T(8,128)}, f32[12,16,1152]{2,1,0:T(8,128)}, f32[12,8,2304]{2,1,0:T(8,128)}, /*index=5*/f32[16,128]{1,0:T(8,128)}) custom-call(s32[12]{0:T(128)} %a_0_.10, s32[2,1]{1,0:T(2,128)} %copy.20.a_1_.a_0_, f32[16,128]{1,0:T(8,128)} %get-tuple-element.18.a_2_, ...), custom_call_target="tpu_custom_call" | custom-call | tf_op jit(solution)/shard_map/update/pallas_call | solution.py:608
  72.8 1.9 %collective-permute-start.9 = (f32[12,16,1152]{2,1,0:T(8,128)}, f32[12,16,1152]{2,1,0:T(8,128)S(1)}, u32[]{:S(2)}, u32[]{:S(2)}) collective-permute-start(f32[12,16,1152]{2,1,0:T(8,128)} %get-tuple-element.25), channel_id=1, source_target_pairs={{0,8},{8,16},{16,24},{1,9},{9,17},{17,25},{2,10},{10,18},{18,26},{... | collective-permute-start | bytes 2654216 | tf_op jit(solution)/shard_map/ppermute | solution.py:669
  74.7 3.8 %collective-permute-start.10 = (f32[12,16,1152]{2,1,0:T(8,128)}, f32[12,16,1152]{2,1,0:T(8,128)S(1)}, u32[]{:S(2)}, u32[]{:S(2)}) collective-permute-start(f32[12,16,1152]{2,1,0:T(8,128)} %get-tuple-element.27), channel_id=1, source_target_pairs={{8,0},{16,8},{24,16},{9,1},{17,9},{25,17},{10,2},{18,10},{26,18},{... | collective-permute-start | bytes 2654216 | tf_op jit(solution)/shard_map/ppermute | solution.py:670
  78.5 0.7 collective-permute-start.11
  79.2 3.5 %collective-permute-start.8 = (f32[16,128]{1,0:T(8,128)}, f32[16,128]{1,0:T(8,128)S(1)}, u32[]{:S(2)}, u32[]{:S(2)}) collective-permute-start(f32[16,128]{1,0:T(8,128)} %get-tuple-element.23.a_2_), channel_id=1, source_target_pairs={{0,3},{1,2},{2,1},{3,0},{4,7},{5,6},{6,5},{7,4},{8,11},{9,10},{10,... | collective-permute-start | bytes 24584 | tf_op jit(solution)/shard_map/ppermute | solution.py:664
  82.7 0.6 collective-permute-start.7
  83.3 1.6 %collective-permute-done.8.a_5_ = f32[16,128]{1,0:T(8,128)S(1)} collective-permute-done((f32[16,128]{1,0:T(8,128)}, f32[16,128]{1,0:T(8,128)S(1)}, u32[]{:S(2)}, u32[]{:S(2)}) %collective-permute-start.8) | collective-permute-done | bytes 8224 | tf_op jit(solution)/shard_map/ppermute | solution.py:664
  84.9 0.8 collective-permute-start.6
  85.7 13.9 %inner_increments.3.a_7_ = bf16[8,16,27648]{2,1,0:T(8,128)(2,1)} custom-call(s32[12]{0:T(128)} %a_0_.10, s32[2,1]{1,0:T(2,128)} %copy.20.a_1_.a_0_, f32[8,16,27648]{2,1,0:T(8,128)} %get-tuple-element.24.a_2_.a_6_, f32[8,2304]{1,0:T(8,128)} %constant.20.clone.a_3_.a_12_, f32[128,128]{1,0:T(8,128)} %constant.21.clone.a_4_, ...), custom_call_target="tpu_custom_call" | custom-call | tf_op jit(solution)/shard_map/inner_increments/pallas_call | solution.py:608
  99.7 0.5 copy-done.8
  100.2 0.4 copy-done.3
  100.8 0.3 copy-done.5
  101.1 25.4 %last_update.1 = (f32[8,16,27648]{2,1,0:T(8,128)}, f32[16,128]{1,0:T(8,128)}) custom-call(s32[12]{0:T(128)} %a_0_.10, s32[2,1]{1,0:T(2,128)} %copy.20.a_1_.a_0_, f32[16,128]{1,0:T(8,128)} %get-tuple-element.23.a_2_, f32[16,128]{1,0:T(8,128)} %copy-done.10, f32[16,128]{1,0:T(8,128)} %copy-done.8, f32[16,128]{1,0:T(8,128)} %copy-done.6, ...), custom_call_target="tpu_custom_call" | custom-call | tf_op jit(solution)/shard_map/last_update/pallas_call | solution.py:608
  126.6 3.0 %collective-permute-start.14 = (f32[16,128]{1,0:T(8,128)}, f32[16,128]{1,0:T(8,128)S(1)}, u32[]{:S(2)}, u32[]{:S(2)}) collective-permute-start(f32[16,128]{1,0:T(8,128)} %get-tuple-element.30.a_1_), channel_id=1, source_target_pairs={{0,3},{1,2},{2,1},{3,0},{4,7},{5,6},{6,5},{7,4},{8,11},{9,10},{10,... | collective-permute-start | bytes 24584 | tf_op jit(solution)/shard_map/ppermute | solution.py:664
  129.6 0.5 collective-permute-start.13
  130.0 1.0 collective-permute-start.12
  131.0 1.3 collective-permute-done.14.a_4_
  132.3 2.0 %collective-permute-done.13.a_3_ = f32[16,128]{1,0:T(8,128)S(1)} collective-permute-done((f32[16,128]{1,0:T(8,128)}, f32[16,128]{1,0:T(8,128)S(1)}, u32[]{:S(2)}, u32[]{:S(2)}) %collective-permute-start.13) | collective-permute-done | bytes 8224 | tf_op jit(solution)/shard_map/ppermute | solution.py:664
  134.3 0.6 copy-done.13
  134.9 0.6 copy-done.14
  135.5 2.5 %macroscopic.1 = (f32[8,8,16]{2,1,0:T(8,128)}, f32[1,8]{1,0:T(1,128)}) custom-call(s32[2,1]{1,0:T(2,128)} %copy.20.a_1_.a_0_, f32[16,128]{1,0:T(8,128)} %get-tuple-element.30.a_1_, f32[16,128]{1,0:T(8,128)} %copy-done.14, f32[16,128]{1,0:T(8,128)} %copy-done.13, f32[16,128]{1,0:T(8,128)} %copy-done.12, f32[2,128,128]{2,1,0:T(8,128)} %constant.22.clone.a_13_.a_5_), custom_call_target="tpu_custom_call" | custom-call | tf_op jit(solution)/shard_map/macroscopic/pallas_call | solution.py:682
  (35 shorter events, 0.6 us)
Async XLA Ops:
  15.9 26.6 %collective-permute-start.3 = (f32[12,16,1152]{2,1,0:T(8,128)}, f32[12,16,1152]{2,1,0:T(8,128)S(1)}, u32[]{:S(2)}, u32[]{:S(2)}) collective-permute-start(f32[12,16,1152]{2,1,0:T(8,128)} %get-tuple-element.19), channel_id=1, source_target_pairs={{0,8},{8,16},{16,24},{1,9},{9,17},{17,25},{2,10},{10,18},{18,26},{... | collective-permute-start | bytes 2654216 | tf_op jit(solution)/shard_map/ppermute | solution.py:669
  17.8 24.7 %collective-permute-start.4 = (f32[12,16,1152]{2,1,0:T(8,128)}, f32[12,16,1152]{2,1,0:T(8,128)S(1)}, u32[]{:S(2)}, u32[]{:S(2)}) collective-permute-start(f32[12,16,1152]{2,1,0:T(8,128)} %get-tuple-element.21), channel_id=1, source_target_pairs={{8,0},{16,8},{24,16},{9,1},{17,9},{25,17},{10,2},{18,10},{26,18},{... | collective-permute-start | bytes 2654216 | tf_op jit(solution)/shard_map/ppermute | solution.py:670
  21.4 21.1 %collective-permute-start.5 = (f32[12,8,2304]{2,1,0:T(8,128)}, f32[12,8,2304]{2,1,0:T(8,128)S(1)}, u32[]{:S(2)}, u32[]{:S(2)}) collective-permute-start(f32[12,8,2304]{2,1,0:T(8,128)} %get-tuple-element.22), channel_id=1, source_target_pairs={{0,4},{4,0},{1,5},{5,1},{2,6},{6,2},{3,7},{7,3},{8,12},{12,8},{9,1... | collective-permute-start | bytes 2654216 | tf_op jit(solution)/shard_map/ppermute | solution.py:668
  23.0 5.7 %collective-permute-start.2 = (f32[16,128]{1,0:T(8,128)}, f32[16,128]{1,0:T(8,128)S(1)}, u32[]{:S(2)}, u32[]{:S(2)}) collective-permute-start(f32[16,128]{1,0:T(8,128)} %get-tuple-element.18.a_2_), channel_id=1, source_target_pairs={{0,3},{1,2},{2,1},{3,0},{4,7},{5,6},{6,5},{7,4},{8,11},{9,10},{10,... | collective-permute-start | bytes 24584 | tf_op jit(solution)/shard_map/ppermute | solution.py:664
  26.6 15.9 %collective-permute-start.1 = (f32[16,128]{1,0:T(8,128)}, f32[16,128]{1,0:T(8,128)S(1)}, u32[]{:S(2)}, u32[]{:S(2)}) collective-permute-start(f32[16,128]{1,0:T(8,128)} %get-tuple-element.18.a_2_), channel_id=1, source_target_pairs={{0,2},{1,3},{2,0},{3,1},{4,6},{5,7},{6,4},{7,5},{8,10},{9,11},{10,... | collective-permute-start | bytes 24584 | tf_op jit(solution)/shard_map/ppermute | solution.py:664
  28.6 13.8 %copy-start.7 = (f32[16,128]{1,0:T(8,128)}, f32[16,128]{1,0:T(8,128)S(1)}, u32[]{:S(2)}) copy-start(f32[16,128]{1,0:T(8,128)S(1)} %collective-permute-done.2.a_5_) | copy-start | bytes 24580
  28.6 13.8 %collective-permute-start = (f32[16,128]{1,0:T(8,128)}, f32[16,128]{1,0:T(8,128)S(1)}, u32[]{:S(2)}, u32[]{:S(2)}) collective-permute-start(f32[16,128]{1,0:T(8,128)} %get-tuple-element.18.a_2_), channel_id=1, source_target_pairs={{0,1},{1,0},{2,3},{3,2},{4,5},{5,4},{6,7},{7,6},{8,9},{9,8},{10,11... | collective-permute-start | bytes 24584 | tf_op jit(solution)/shard_map/ppermute | solution.py:664
  42.5 0.6 copy-start.9
  42.5 0.6 copy-start.11
  42.5 1.0 copy-start
  42.5 1.2 copy-start.1
  42.5 1.5 %copy-start.2 = (f32[12,8,2304]{2,1,0:T(8,128)}, f32[12,8,2304]{2,1,0:T(8,128)S(1)}, u32[]{:S(2)}) copy-start(f32[12,8,2304]{2,1,0:T(8,128)S(1)} %collective-permute-done.5.a_11_) | copy-start | bytes 2654212
  72.8 26.8 %collective-permute-start.9 = (f32[12,16,1152]{2,1,0:T(8,128)}, f32[12,16,1152]{2,1,0:T(8,128)S(1)}, u32[]{:S(2)}, u32[]{:S(2)}) collective-permute-start(f32[12,16,1152]{2,1,0:T(8,128)} %get-tuple-element.25), channel_id=1, source_target_pairs={{0,8},{8,16},{16,24},{1,9},{9,17},{17,25},{2,10},{10,18},{18,26},{... | collective-permute-start | bytes 2654216 | tf_op jit(solution)/shard_map/ppermute | solution.py:669
  74.7 24.9 %collective-permute-start.10 = (f32[12,16,1152]{2,1,0:T(8,128)}, f32[12,16,1152]{2,1,0:T(8,128)S(1)}, u32[]{:S(2)}, u32[]{:S(2)}) collective-permute-start(f32[12,16,1152]{2,1,0:T(8,128)} %get-tuple-element.27), channel_id=1, source_target_pairs={{8,0},{16,8},{24,16},{9,1},{17,9},{25,17},{10,2},{18,10},{26,18},{... | collective-permute-start | bytes 2654216 | tf_op jit(solution)/shard_map/ppermute | solution.py:670
  78.5 21.1 %collective-permute-start.11 = (f32[12,8,2304]{2,1,0:T(8,128)}, f32[12,8,2304]{2,1,0:T(8,128)S(1)}, u32[]{:S(2)}, u32[]{:S(2)}) collective-permute-start(f32[12,8,2304]{2,1,0:T(8,128)} %get-tuple-element.28), channel_id=1, source_target_pairs={{0,4},{4,0},{1,5},{5,1},{2,6},{6,2},{3,7},{7,3},{8,12},{12,8},{9,1... | collective-permute-start | bytes 2654216 | tf_op jit(solution)/shard_map/ppermute | solution.py:668
  79.2 5.7 %collective-permute-start.8 = (f32[16,128]{1,0:T(8,128)}, f32[16,128]{1,0:T(8,128)S(1)}, u32[]{:S(2)}, u32[]{:S(2)}) collective-permute-start(f32[16,128]{1,0:T(8,128)} %get-tuple-element.23.a_2_), channel_id=1, source_target_pairs={{0,3},{1,2},{2,1},{3,0},{4,7},{5,6},{6,5},{7,4},{8,11},{9,10},{10,... | collective-permute-start | bytes 24584 | tf_op jit(solution)/shard_map/ppermute | solution.py:664
  82.7 16.8 %collective-permute-start.7 = (f32[16,128]{1,0:T(8,128)}, f32[16,128]{1,0:T(8,128)S(1)}, u32[]{:S(2)}, u32[]{:S(2)}) collective-permute-start(f32[16,128]{1,0:T(8,128)} %get-tuple-element.23.a_2_), channel_id=1, source_target_pairs={{0,2},{1,3},{2,0},{3,1},{4,6},{5,7},{6,4},{7,5},{8,10},{9,11},{10,... | collective-permute-start | bytes 24584 | tf_op jit(solution)/shard_map/ppermute | solution.py:664
  84.9 14.7 %copy-start.6 = (f32[16,128]{1,0:T(8,128)}, f32[16,128]{1,0:T(8,128)S(1)}, u32[]{:S(2)}) copy-start(f32[16,128]{1,0:T(8,128)S(1)} %collective-permute-done.8.a_5_) | copy-start | bytes 24580
  84.9 14.7 %collective-permute-start.6 = (f32[16,128]{1,0:T(8,128)}, f32[16,128]{1,0:T(8,128)S(1)}, u32[]{:S(2)}, u32[]{:S(2)}) collective-permute-start(f32[16,128]{1,0:T(8,128)} %get-tuple-element.23.a_2_), channel_id=1, source_target_pairs={{0,1},{1,0},{2,3},{3,2},{4,5},{5,4},{6,7},{7,6},{8,9},{9,8},{10,11... | collective-permute-start | bytes 24584 | tf_op jit(solution)/shard_map/ppermute | solution.py:664
  99.6 0.6 copy-start.8
  99.6 0.6 copy-start.10
  99.6 1.0 copy-start.3
  99.6 1.2 copy-start.4
  99.6 1.5 %copy-start.5 = (f32[12,8,2304]{2,1,0:T(8,128)}, f32[12,8,2304]{2,1,0:T(8,128)S(1)}, u32[]{:S(2)}) copy-start(f32[12,8,2304]{2,1,0:T(8,128)S(1)} %collective-permute-done.11.a_11_) | copy-start | bytes 2654212
  126.6 5.7 %collective-permute-start.14 = (f32[16,128]{1,0:T(8,128)}, f32[16,128]{1,0:T(8,128)S(1)}, u32[]{:S(2)}, u32[]{:S(2)}) collective-permute-start(f32[16,128]{1,0:T(8,128)} %get-tuple-element.30.a_1_), channel_id=1, source_target_pairs={{0,3},{1,2},{2,1},{3,0},{4,7},{5,6},{6,5},{7,4},{8,11},{9,10},{10,... | collective-permute-start | bytes 24584 | tf_op jit(solution)/shard_map/ppermute | solution.py:664
  129.6 4.8 %collective-permute-start.13 = (f32[16,128]{1,0:T(8,128)}, f32[16,128]{1,0:T(8,128)S(1)}, u32[]{:S(2)}, u32[]{:S(2)}) collective-permute-start(f32[16,128]{1,0:T(8,128)} %get-tuple-element.30.a_1_), channel_id=1, source_target_pairs={{0,2},{1,3},{2,0},{3,1},{4,6},{5,7},{6,4},{7,5},{8,10},{9,11},{10,... | collective-permute-start | bytes 24584 | tf_op jit(solution)/shard_map/ppermute | solution.py:664
  130.0 4.3 %collective-permute-start.12 = (f32[16,128]{1,0:T(8,128)}, f32[16,128]{1,0:T(8,128)S(1)}, u32[]{:S(2)}, u32[]{:S(2)}) collective-permute-start(f32[16,128]{1,0:T(8,128)} %get-tuple-element.30.a_1_), channel_id=1, source_target_pairs={{0,1},{1,0},{2,3},{3,2},{4,5},{5,4},{6,7},{7,6},{8,9},{9,8},{10,11... | collective-permute-start | bytes 24584 | tf_op jit(solution)/shard_map/ppermute | solution.py:664
  132.3 2.0 %copy-start.12 = (f32[16,128]{1,0:T(8,128)}, f32[16,128]{1,0:T(8,128)S(1)}, u32[]{:S(2)}) copy-start(f32[16,128]{1,0:T(8,128)S(1)} %collective-permute-done.14.a_4_) | copy-start | bytes 24580
  134.3 0.6 copy-start.13
  134.9 0.6 copy-start.14

commit v4 on v3

--- a/solution.py
+++ b/solution.py
@@ -27,6 +27,8 @@
 LOCAL_Z = 2 * NODES
 NODE_COUNT = NODES * LOCAL_Z
 TILE = 256
+CHUNK = 384
+CHUNKS = PLANE // CHUNK
 WINDOW = 512
 GHOST_ROWS = 32
 MOMENTS = 16
@@ -243,35 +245,38 @@
     ]
 
 
-def finish_moments(sums_ref, rows_ref, table_ref, out_ref):
+def add_moments(acc, vr, vt, sums):
+    g0, g1, g2, g3, g4 = sums
+    a = vr * g0
+    b = vt * g0
+    aa = vr * a
+    bb = vt * b
+    c = vr * g1
+    d = vt * g1
+    perp = aa + bb + g2
+    new = [g0, a, b, g1, aa, bb, vr * b, g2, c, d, vr * perp, vt * perp, vr * c + vt * d + g3, g4]
+    return new if acc is None else [x + y for x, y in zip(acc, new)]
+
+
+def finish_moments(sums_ref, table_ref, out_ref):
     lane = lax.broadcasted_iota(jnp.int32, (LOCAL_Z, 128), 1)
 
     def one_radius(r, carry):
-        acc = [jnp.zeros((LOCAL_Z, 128), F32) for _ in range(14)]
-        for j in range(PLANE // 128):
-            at = pl.ds(j * 128, 128)
-            vr = rows_ref[0:1, at]
-            vt = rows_ref[1:2, at]
-            g0, g1, g2, g3, g4 = (sums_ref[k, r, :, at] for k in range(5))
-            a = vr * g0
-            b = vt * g0
-            aa = vr * a
-            bb = vt * b
-            c = vr * g1
-            d = vt * g1
-            perp = aa + bb + g2
-            new = [g0, a, b, g1, aa, bb, vr * b, g2, c, d, vr * perp, vt * perp, vr * c + vt * d + g3, g4]
-            acc = [x + y for x, y in zip(acc, new)]
+        rows = radius_rows(r)
         block = jnp.zeros((LOCAL_Z, 128), F32)
         for k in range(14):
-            block = jnp.where(lane == k, WEIGHT * jnp.sum(acc[k], axis=1, keepdims=True), block)
-        table_ref[pl.ds(pl.multiple_of(r * LOCAL_Z, LOCAL_Z), LOCAL_Z), :] = block
+            block = jnp.where(lane == k, WEIGHT * jnp.sum(sums_ref[k, rows, :], axis=1, keepdims=True), block)
+        table_ref[rows, :] = block
         return carry
 
     lax.fori_loop(0, NODES, one_radius, 0)
     out_ref[...] = jnp.transpose(table_ref[...])[0:MOMENTS, :]
 
 
+def radius_rows(r):
+    return pl.ds(pl.multiple_of(r * LOCAL_Z, LOCAL_Z), LOCAL_Z)
+
+
 def clear_sums(sums_ref):
     sums_ref[...] = jnp.zeros(sums_ref.shape, F32)
 
@@ -280,23 +285,29 @@
     return lax.axis_index("row"), lax.axis_index("gz")
 
 
-def send_piece(s, first, lanes, side, place, narrow, trace_ref, right_ref, left_ref, axial_ref):
-    got = dot(trace_ref[side, place], narrow)
-    if side == 1:
-        right_ref[s, :, first - HALF : first - HALF + lanes] = got[0:LOCAL_Z]
-    else:
-        left_ref[s, :, first : first + lanes] = got[0:LOCAL_Z]
-    axial_ref[s, :, first : first + lanes] = got[LOCAL_Z : LOCAL_Z + NODES]
-
-
-def turn_traces(count, row, mirror_ref, left_ref, turned_ref):
+def send_traces(count, step, place, narrow_ref, trace_ref, right_ref, left_ref, axial_ref, mirrored_ref):
+    for side in range(2):
+
+        @pl.when((step >= CHUNKS // 2) == (side == 1))
+        def _():
+            for s in range(count):
+                got = dot(trace_ref[side, place], narrow_ref[s])
+                axial_ref[s] = got[LOCAL_Z : LOCAL_Z + NODES]
+                if side == 1:
+                    right_ref[s] = got[0:LOCAL_Z]
+                else:
+                    left_ref[s] = got[0:LOCAL_Z]
+                    at = pl.ds(pl.multiple_of(step * CHUNK, CHUNK), CHUNK)
+                    mirrored_ref[s * LOCAL_Z : (s + 1) * LOCAL_Z, at] = got[0:LOCAL_Z].astype(BF16)
+
+
+def turn_traces(count, row, mirror_ref, mirrored_ref, turned_ref):
     @pl.when(row == 0)
     def _():
-        flat = left_ref[...].reshape(count * LOCAL_Z, HALF).astype(BF16)
         for first in range(0, HALF, 128):
             low = max(0, (HALF - first - 128 - 48) // 128 * 128)
             high = min(HALF, -((first - HALF - 48) // 128) * 128)
-            got = dot(flat[:, low:high], mirror_ref[low:high, first : first + 128])
+            got = dot(mirrored_ref[:, low:high], mirror_ref[low:high, first : first + 128])
             turned_ref[:, :, first : first + 128] = got.reshape(count, LOCAL_Z, 128)
 
     @pl.when(row != 0)
@@ -304,21 +315,12 @@
         turned_ref[...] = jnp.zeros(turned_ref.shape, F32)
 
 
-def nodes_of(ref, first, lanes):
-    return ref[:, :, first : first + lanes].reshape(NODE_COUNT, lanes)
-
-
-def send_traces(count, place, narrow_ref, trace_ref, right_ref, left_ref, axial_ref):
-    for s in range(count):
-        for first, lanes, side in PIECES:
-            narrow = narrow_ref[s, :, first : first + lanes]
-            send_piece(s, first, lanes, side, place, narrow, trace_ref, right_ref, left_ref, axial_ref)
-
-
-def first_kernel(
-    count, order, codes, f_ref, rows_ref, trace_ref, mirror_ref,
-    right_ref, left_ref, turned_ref, axial_ref, mom_ref, sums_ref, table_ref,
-):
+def first_kernel(count, order, codes, *refs):
+    f_refs, refs = refs[:count], refs[count:]
+    (
+        rows_ref, trace_ref, mirror_ref, right_ref, left_ref, turned_ref, axial_ref, mom_ref,
+        sums_ref, narrow_ref, mirrored_ref, table_ref,
+    ) = refs
     step = pl.program_id(0)
     row, place = places_of()
 
@@ -326,36 +328,41 @@
     def _():
         clear_sums(sums_ref)
 
-    speeds = [slot_speed(order, step * count + s) for s in range(count)]
-    for first, lanes, side in PIECES:
-        narrow = [[] for s in range(count)]
-        for inside in range(0, lanes, 128):
-            at = pl.ds(first + inside, 128)
-            column = [[] for s in range(count)]
-            for r in range(NODES):
-                sums = [sums_ref[k, r, :, at] for k in range(5)]
-                for s in range(count):
-                    field = f_ref[r, :, pl.ds(s * PLANE + first + inside, 128)]
-                    sums = add_speed_sums(field, speeds[s], sums)
-                    column[s].append(field.astype(BF16))
-                for k in range(5):
-                    sums_ref[k, r, :, at] = sums[k]
+    speeds = [slot_speed(order, s) for s in range(count)]
+
+    def one_radius(r, carry):
+        rows = radius_rows(r)
+        acc = None
+        for j in range(0, CHUNK, 128):
+            at = pl.ds(j, 128)
+            sums = [jnp.zeros((LOCAL_Z, 128), F32) for _ in range(5)]
             for s in range(count):
-                narrow[s].append(jnp.concatenate(column[s], axis=0))
-        for s in range(count):
-            block = jnp.concatenate(narrow[s], axis=1) if len(narrow[s]) > 1 else narrow[s][0]
-            send_piece(s, first, lanes, side, place, block, trace_ref, right_ref, left_ref, axial_ref)
-    turn_traces(count, row, mirror_ref, left_ref, turned_ref)
-
-    @pl.when(step == pl.num_programs(0) - 1)
+                field = f_refs[s][r, :, at]
+                sums = add_speed_sums(field, speeds[s], sums)
+                narrow_ref[s, rows, at] = field.astype(BF16)
+            acc = add_moments(acc, rows_ref[0:1, at], rows_ref[1:2, at], sums)
+        for k in range(14):
+            sums_ref[k, rows, :] += acc[k]
+        return carry
+
+    lax.fori_loop(0, NODES, one_radius, 0)
+    send_traces(count, step, place, narrow_ref, trace_ref, right_ref, left_ref, axial_ref, mirrored_ref)
+
+    @pl.when(step == CHUNKS - 1)
     def _():
-        finish_moments(sums_ref, rows_ref, table_ref, mom_ref)
+        turn_traces(count, row, mirror_ref, mirrored_ref, turned_ref)
+        finish_moments(sums_ref, table_ref, mom_ref)
 
 
 def inner_kernel(
-    count, order, codes, f_ref, rows_ref, pos_ref, radial_ref, axial_m_ref, rot_ref,
+    count, split, order, codes, f_ref, rows_ref, pos_ref, radial_ref, axial_m_ref, rot_ref,
     out_ref, inverse_ref, pad_ref, lhs_ref,
 ):
+    def nodes_of(s, first, lanes):
+        if split:
+            return f_ref[s, :, :, first : first + lanes].reshape(NODE_COUNT, lanes)
+        return f_ref[:, :, s * PLANE + first : s * PLANE + first + lanes].reshape(NODE_COUNT, lanes)
+
     step = pl.program_id(0)
     row, place = places_of()
 
@@ -377,7 +384,7 @@
         lhs_ref[s, 0, NODE_COUNT:] = axial
         lhs_ref[s, 1, NODE_COUNT:] = axial
         for j in range(PLANE // 128):
-            field = nodes_of(f_ref, s * PLANE + j * 128, 128)
+            field = nodes_of(s, j * 128, 128)
             pad_ref[s, :, 128 + j * 128 : 256 + j * 128] = (field * inverse).astype(BF16)
 
     for tile in range(PLANE // TILE):
@@ -389,20 +396,20 @@
             vr = rows_ref[0:1, first : first + lanes]
             inside = first - start
             for s in range(count):
-                here = s * PLANE + first
-                moved = dot(lhs_ref[s, side], nodes_of(f_ref, here, lanes).astype(BF16))
+                moved = dot(lhs_ref[s, side], nodes_of(s, first, lanes).astype(BF16))
                 change = turned[s * NODE_COUNT : (s + 1) * NODE_COUNT, inside : inside + lanes]
                 change = change + vr * moved[0:NODE_COUNT] + moved[NODE_COUNT:]
-                out_ref[:, :, here : here + lanes] = change.astype(BF16).reshape(NODES, LOCAL_Z, lanes)
-
-
-def total_of(parts):
+                out_ref[s, :, :, first : first + lanes] = change.astype(BF16).reshape(NODES, LOCAL_Z, lanes)
+
+
+def total_of(parts_ref):
+    parts = [parts_ref[k : k + MOMENTS, :] for k in range(0, parts_ref.shape[0], MOMENTS)]
     while len(parts) > 1:
         parts = [parts[k] + parts[k + 1] for k in range(0, len(parts), 2)]
     return parts[0]
 
 
-def prepare_nodes(total, codes, place, rows_ref, edge_ref, table_ref, node_ref, wall_ref, plane_ref):
+def prepare_nodes(total, codes, place, edge_ref, table_ref, node_ref, wall_ref):
     wide = jnp.concatenate([total, jnp.zeros((128 - MOMENTS, 128), F32)], axis=0)
     table_ref[...] = jnp.transpose(wide)
     rho, ur, ut, uz, temp, qr, qt, qz = macroscopic_of(lambda k: table_ref[:, k : k + 1])
@@ -424,126 +431,128 @@
     density = jnp.where(place == 0, bottom, top)
     wall_ref[...] = jnp.transpose(jnp.broadcast_to(density, (128, 128)))[0:NODES, :]
 
-    def one_radius(r, carry):
-        rows = pl.ds(pl.multiple_of(r * LOCAL_Z, LOCAL_Z), LOCAL_Z)
-        n_half, n_inv = node_ref[1, rows, :], node_ref[3, rows, :]
-        n_ur, n_ut = node_ref[6, rows, :], node_ref[7, rows, :]
-        n_qr, n_qt = node_ref[8, rows, :], node_ref[9, rows, :]
-        for j in range(PLANE // 128):
-            at = pl.ds(j * 128, 128)
-            cr = rows_ref[0:1, at] - n_ur
-            ct = rows_ref[1:2, at] - n_ut
-            square = cr * cr + ct * ct
-            gauss = jnp.exp(square * n_half)
-            along = cr * n_qr + ct * n_qt
-            reach = square * n_inv - 5.0
-            tilted = gauss * along
-            plane_ref[0, rows, at] = gauss
-            plane_ref[1, rows, at] = tilted
-            plane_ref[2, rows, at] = gauss * reach
-            plane_ref[3, rows, at] = tilted * reach
-        return carry
-
-    lax.fori_loop(0, NODES, one_radius, 0)
-
 
 def slot_factors(vz, node_ref):
     cz = vz - node_ref[0]
-    lam = node_ref[4] * jnp.exp(cz * cz * node_ref[1])
-    alpha = cz * node_ref[2]
-    reach = cz * cz * node_ref[3]
-    return lam * (1.0 + alpha * reach), lam * reach, lam * alpha, lam
-
-
-def ghost_lifts(vz, ghost_r_ref, ghost_z_ref, lhs_ref):
+    square = cz * cz
+    return node_ref[4] * jnp.exp(square * node_ref[1]), cz * node_ref[2], square * node_ref[3] - 5.0
+
+
+def ghost_lifts(vz, ghost_r_ref, ghost_z_ref, lhs_ref, s):
     lean = jnp.abs(vz) * ghost_z_ref[jnp.where(vz > 0, 1, 0)]
-    lhs_ref[0] = (ghost_r_ref[0] + lean).astype(BF16)
-    lhs_ref[1] = (ghost_r_ref[1] + lean).astype(BF16)
-
-
-def ghost_rows(s, vz, place, in_left_ref, in_turned_ref, in_right_ref, in_axial_ref, rows_ref, wall_ref, ghost_ref):
-    own = (place == 0) == (vz > 0)
-    strength = jnp.exp(-0.5 * vz * vz + jnp.zeros((NODES, 128), F32)) * wall_ref[...]
-    for j in range(PLANE // 128):
-        at = pl.ds(j * 128, 128)
-        if j * 128 < HALF:
-            radial = in_right_ref[s, :, at]
-        else:
-            back = pl.ds(j * 128 - HALF, 128)
-            radial = in_left_ref[s, :, back] + in_turned_ref[s, :, back]
-        axial = jnp.where(own, strength * rows_ref[2:3, at], in_axial_ref[s, :, at])
-        rows = jnp.concatenate([rows_ref[0:1, at] * radial, axial, jnp.zeros((8, 128), F32)], axis=0)
-        ghost_ref[:, at] = rows.astype(BF16)
-
-
-def outer_kernel(count, part_count, last, order, codes, *refs):
-    part_refs, refs = refs[:part_count], refs[part_count:]
-    f_ref, inner_ref, in_left_ref, in_turned_ref, in_right_ref, in_axial_ref = refs[:6]
-    rows_ref, edge_ref, ghost_r_ref, ghost_z_ref = refs[6:10]
-    refs = refs[10:]
+    lhs_ref[s, 0] = (ghost_r_ref[0] + lean).astype(BF16)
+    lhs_ref[s, 1] = (ghost_r_ref[1] + lean).astype(BF16)
+
+
+def outer_kernel(count, split, last, order, codes, parts_ref, *refs):
+    if split:
+        f_ref, refs = refs[0], refs[1:]
+        field_of = lambda s, r, at: f_ref[s, r, :, at]
+    else:
+        f_refs, refs = refs[:count], refs[count:]
+        field_of = lambda s, r, at: f_refs[s][r, :, at]
+    inner_ref, in_left_ref, in_turned_ref, in_right_ref, in_axial_ref = refs[:5]
+    rows_ref, edge_ref, ghost_r_ref, ghost_z_ref = refs[5:9]
+    refs = refs[9:]
     if last:
-        (out_ref, mom_ref), refs = refs[:2], refs[2:]
+        (out_hbm, mom_ref, out_buf, out_sem), refs = refs[:4], refs[4:]
     else:
         (trace_ref, mirror_ref, out_ref, right_ref, left_ref, turned_ref, axial_ref, mom_ref), refs = refs[:8], refs[8:]
-        narrow_ref, refs = refs[0], refs[1:]
-    plane_ref, node_ref, wall_ref, slot_ref, work_ref, sums_ref, lhs_ref, ghost_ref, table_ref = refs
+        (narrow_ref, mirrored_ref), refs = refs[:2], refs[2:]
+    node_ref, wall_ref, slot_ref, work_ref, sums_ref, lhs_ref, ghost_ref, table_ref = refs
     step = pl.program_id(0)
     row, place = places_of()
+    speeds = [slot_speed(order, s) for s in range(count)]
 
     @pl.when(step == 0)
     def _():
         clear_sums(sums_ref)
-        total = total_of([p[...] for p in part_refs])
-        prepare_nodes(total, codes, place, rows_ref, edge_ref, table_ref, node_ref, wall_ref, plane_ref)
-
-    speeds = [slot_speed(order, step * count + s) for s in range(count)]
+        prepare_nodes(total_of(parts_ref), codes, place, edge_ref, table_ref, node_ref, wall_ref)
+        for s in range(count):
+            for k, value in enumerate(slot_factors(speeds[s], node_ref)):
+                slot_ref[s, k] = value
+            ghost_lifts(speeds[s], ghost_r_ref, ghost_z_ref, lhs_ref, s)
+
+    side = jnp.where(step >= CHUNKS // 2, 1, 0)
+    inward = step < CHUNKS // 2
     for s in range(count):
         vz = speeds[s]
-        for k, value in enumerate(slot_factors(vz, node_ref)):
-            slot_ref[s, k] = value
-        ghost_lifts(vz, ghost_r_ref, ghost_z_ref, lhs_ref)
-        ghost_rows(
-            s, vz, place, in_left_ref, in_turned_ref, in_right_ref, in_axial_ref, rows_ref, wall_ref, ghost_ref
-        )
-        for first, lanes, side in PIECES:
-            work_ref[s, :, first : first + lanes] = dot(
-                lhs_ref[side, :, 0:GHOST_ROWS], ghost_ref[:, first : first + lanes]
-            )
+        own = (place == 0) == (vz > 0)
+        strength = jnp.exp(-0.5 * vz * vz + jnp.zeros((NODES, 128), F32)) * wall_ref[...]
+        for j in range(0, CHUNK, 128):
+            at = pl.ds(j, 128)
+            radial = jnp.where(inward, in_right_ref[s, :, at], in_left_ref[s, :, at] + in_turned_ref[s, :, at])
+            axial = jnp.where(own, strength * rows_ref[2:3, at], in_axial_ref[s, :, at])
+            rows = jnp.concatenate([rows_ref[0:1, at] * radial, axial, jnp.zeros((8, 128), F32)], axis=0)
+            ghost_ref[s, :, at] = rows.astype(BF16)
+        work_ref[s] = dot(lhs_ref[s, side, :, 0:GHOST_ROWS], ghost_ref[s])
+
+    def copy_out(s, chunk):
+        at = pl.ds(pl.multiple_of(s * PLANE + chunk * CHUNK, CHUNK), CHUNK)
+        slot = lax.rem(chunk, 2)
+        return pltpu.make_async_copy(out_buf.at[slot, s], out_hbm.at[:, :, at], out_sem.at[slot, s])
+
+    if last:
+
+        @pl.when(step >= 2)
+        def _():
+            for s in range(count):
+                copy_out(s, step - 2).wait()
+
+        buffer = lax.rem(step, 2)
 
     def update(r, carry):
-        rows = pl.ds(pl.multiple_of(r * LOCAL_Z, LOCAL_Z), LOCAL_Z)
-        keep = node_ref[5, rows, :]
-        factor = [[slot_ref[s, k, rows, :] for k in range(4)] for s in range(count)]
-        for j in range(PLANE // 128):
-            at = pl.ds(j * 128, 128)
-            planes = [plane_ref[k, rows, at] for k in range(4)]
-            sums = [sums_ref[k, r, :, at] for k in range(5)]
+        rows = radius_rows(r)
+        acc = None
+        for j in range(0, CHUNK, 128):
+            at = pl.ds(j, 128)
+            vr, vt = rows_ref[0:1, at], rows_ref[1:2, at]
+            cr = vr - node_ref[6, rows, :]
+            ct = vt - node_ref[7, rows, :]
+            square = cr * cr + ct * ct
+            gauss = jnp.exp(square * node_ref[1, rows, :])
+            along = cr * node_ref[8, rows, :] + ct * node_ref[9, rows, :]
+            reach = square * node_ref[3, rows, :]
+            keep = node_ref[5, rows, :]
+            sums = [jnp.zeros((LOCAL_Z, 128), F32) for _ in range(5)]
             for s in range(count):
-                here = pl.ds(s * PLANE + j * 128, 128)
-                new = f_ref[r, :, here] * keep + work_ref[s, rows, at] + inner_ref[r, :, here].astype(F32)
-                for k in range(4):
-                    new = new + planes[k] * factor[s][k]
-                out_ref[r, :, here] = new
+                new = field_of(s, r, at) * keep + work_ref[s, rows, at] + inner_ref[s, r, :, at].astype(F32)
+                bend = (along + slot_ref[s, 1, rows, :]) * (reach + slot_ref[s, 2, rows, :]) + 1.0
+                new = new + (gauss * slot_ref[s, 0, rows, :]) * bend
+                if last:
+                    out_buf[buffer, s, r, :, at] = new
+                else:
+                    out_ref[s, r, :, at] = new
+                    narrow_ref[s, rows, at] = new.astype(BF16)
                 sums = add_speed_sums(new, speeds[s], sums)
-                if not last:
-                    narrow_ref[s, rows, at] = new.astype(BF16)
-            for k in range(5):
-                sums_ref[k, r, :, at] = sums[k]
+            acc = add_moments(acc, vr, vt, sums)
+        for k in range(14):
+            sums_ref[k, rows, :] += acc[k]
         return carry
 
     lax.fori_loop(0, NODES, update, 0)
-    if not last:
-        send_traces(count, place, narrow_ref, trace_ref, right_ref, left_ref, axial_ref)
-        turn_traces(count, row, mirror_ref, left_ref, turned_ref)
-
-    @pl.when(step == pl.num_programs(0) - 1)
+    if last:
+        for s in range(count):
+            copy_out(s, step).start()
+
+        @pl.when(step == CHUNKS - 1)
+        def _():
+            for s in range(count):
+                copy_out(s, step - 1).wait()
+                copy_out(s, step).wait()
+
+    else:
+        send_traces(count, step, place, narrow_ref, trace_ref, right_ref, left_ref, axial_ref, mirrored_ref)
+
+    @pl.when(step == CHUNKS - 1)
     def _():
-        finish_moments(sums_ref, rows_ref, table_ref, mom_ref)
-
-
-def last_kernel(part_count, codes, *refs):
-    total_ref = total_of([p[...] for p in refs[:part_count]])
-    edge_ref, macro_ref, flux_ref = refs[part_count:]
+        if not last:
+            turn_traces(count, row, mirror_ref, mirrored_ref, turned_ref)
+        finish_moments(sums_ref, table_ref, mom_ref)
+
+
+def last_kernel(codes, parts_ref, edge_ref, macro_ref, flux_ref):
+    total_ref = total_of(parts_ref)
     row, place = places_of()
     values = macroscopic_of(lambda k: total_ref[k : k + 1, :])
     for k in range(8):
@@ -579,37 +588,39 @@
     ghost_r, ghost_z = jnp.asarray(GHOST_R), jnp.asarray(GHOST_Z)
     trace_m, mirror_m, rot_m = jnp.asarray(TRACE_M), jnp.asarray(MIRROR_M), jnp.asarray(ROTATION_M)
 
-    big = pl.BlockSpec((NODES, LOCAL_Z, group * PLANE), lambda i, *n: (0, 0, i))
-    radial_spec = pl.BlockSpec((group, LOCAL_Z, HALF), lambda i, *n: (i, 0, 0))
-    axial_spec = pl.BlockSpec((group, NODES, PLANE), lambda i, *n: (i, 0, 0))
+    everything = verts * MOMENTS
+    slab = pl.BlockSpec((NODES, LOCAL_Z, group * PLANE), lambda i, *n: (0, 0, i))
+    slot_slab = pl.BlockSpec((group, NODES, LOCAL_Z, PLANE), lambda i, *n: (i, 0, 0, 0))
+    chunk_specs = [
+        pl.BlockSpec((NODES, LOCAL_Z, CHUNK), lambda i, *n, s=s: (0, 0, s * CHUNKS + i)) for s in range(slots)
+    ]
+    slot_chunk = pl.BlockSpec((slots, NODES, LOCAL_Z, CHUNK), lambda i, *n: (0, 0, 0, i))
+    half = CHUNKS // 2
+    outward_spec = pl.BlockSpec((slots, LOCAL_Z, CHUNK), lambda i, *n: (0, 0, jnp.maximum(i - half, 0)))
+    inward_spec = pl.BlockSpec((slots, LOCAL_Z, CHUNK), lambda i, *n: (0, 0, jnp.minimum(i, half - 1)))
+    axial_spec = pl.BlockSpec((slots, NODES, CHUNK), lambda i, *n: (0, 0, i))
+    rows_spec = pl.BlockSpec((8, CHUNK), lambda i, *n: (0, i))
     mom_spec = whole((MOMENTS, 128))
     radial_shape = jax.ShapeDtypeStruct((slots, LOCAL_Z, HALF), F32)
     axial_shape = jax.ShapeDtypeStruct((slots, NODES, PLANE), F32)
     mom_shape = jax.ShapeDtypeStruct((MOMENTS, 128), F32)
-    big_shape = jax.ShapeDtypeStruct(distribution.shape, F32)
-    trace_specs = [radial_spec, radial_spec, radial_spec, axial_spec]
+    inner_shape = (slots, NODES, LOCAL_Z, PLANE)
+    trace_specs = [outward_spec, inward_spec, whole(radial_shape.shape), axial_spec]
     trace_shapes = [radial_shape, radial_shape, radial_shape, axial_shape]
-    ghost_specs = [radial_spec, radial_spec, radial_spec, axial_spec]
+    ghost_specs = [outward_spec, outward_spec, inward_spec, axial_spec]
     square = pltpu.VMEM((NODE_COUNT, 128), F32)
-    sums_scratch = pltpu.VMEM((5, NODES, LOCAL_Z, PLANE), F32)
-    narrow_scratch = pltpu.VMEM((group, NODE_COUNT, PLANE), BF16)
-    node_scratch = [
-        pltpu.VMEM((4, NODE_COUNT, PLANE), F32),
-        pltpu.VMEM((10, NODE_COUNT, 128), F32),
-        pltpu.VMEM((NODES, 128), F32),
+    sums_scratch = pltpu.VMEM((14, NODE_COUNT, 128), F32)
+    trace_scratch = [
+        pltpu.VMEM((slots, NODE_COUNT, CHUNK), BF16),
+        pltpu.VMEM((slots * LOCAL_Z, HALF), BF16),
     ]
-    ghost_scratch = [
-        pltpu.VMEM((2, NODE_COUNT, 128), BF16),
-        pltpu.VMEM((GHOST_ROWS, PLANE), BF16),
-        square,
-    ]
-
-    def call(body, name, in_specs, out_specs, out_shape, scratch, args):
+
+    def call(body, name, grid, in_specs, out_specs, out_shape, scratch, args):
         return pl.pallas_call(
             body,
             grid_spec=pltpu.PrefetchScalarGridSpec(
                 num_scalar_prefetch=2,
-                grid=(steps,),
+                grid=(grid,),
                 in_specs=in_specs,
                 out_specs=out_specs,
                 scratch_shapes=scratch,
@@ -623,13 +634,15 @@
         return [whole(x.shape) for x in tables]
 
     def first(f):
-        tables = [rows, trace_m, mirror_m]
         return call(
-            lambda *a: first_kernel(group, *a), "moments_and_traces", [big] + all_whole(tables),
-            trace_specs + [mom_spec], trace_shapes + [mom_shape], [sums_scratch, square], [f] + tables,
+            lambda *a: first_kernel(slots, *a), "moments_and_traces", CHUNKS,
+            chunk_specs + [rows_spec] + all_whole([trace_m, mirror_m]),
+            trace_specs + [mom_spec], trace_shapes + [mom_shape],
+            [sums_scratch] + trace_scratch + [square],
+            [f] * slots + [rows, trace_m, mirror_m],
         )
 
-    def inner(f):
+    def inner(f, split):
         tables = [rows, pos, radial_m, axial_m, rot_m]
         scratch = [
             square,
@@ -637,32 +650,49 @@
             pltpu.VMEM((group, 2, 2 * NODE_COUNT, 128), BF16),
         ]
         return call(
-            lambda *a: inner_kernel(group, *a), "inner_increments", [big] + all_whole(tables),
-            [big], [jax.ShapeDtypeStruct(f.shape, BF16)], scratch, [f] + tables,
+            lambda *a: inner_kernel(group, split, *a), "inner_increments", steps,
+            [slot_slab if split else slab] + all_whole(tables),
+            [slot_slab], [jax.ShapeDtypeStruct(inner_shape, BF16)], scratch, [f] + tables,
         )[0]
 
-    def outer(f, change, ghosts, parts, last):
-        tables = [rows, edge, ghost_r, ghost_z] + ([] if last else [trace_m, mirror_m])
-        scratch = node_scratch + [
-            pltpu.VMEM((group, 4, NODE_COUNT, 128), F32),
-            pltpu.VMEM((group, NODE_COUNT, PLANE), F32),
+    def outer(f, split, change, ghosts, parts, last):
+        more = [] if last else [trace_m, mirror_m]
+        if last:
+            outs = [pl.BlockSpec(memory_space=pl.ANY)]
+            out_shapes = [jax.ShapeDtypeStruct(distribution.shape, F32)]
+            scratch = [
+                pltpu.VMEM((2, slots, NODES, LOCAL_Z, CHUNK), F32),
+                pltpu.SemaphoreType.DMA((2, slots)),
+            ]
+        else:
+            outs = [slot_chunk] + trace_specs
+            out_shapes = [jax.ShapeDtypeStruct(inner_shape, F32)] + trace_shapes
+            scratch = trace_scratch
+        scratch = scratch + [
+            pltpu.VMEM((10, NODE_COUNT, 128), F32),
+            pltpu.VMEM((NODES, 128), F32),
+            pltpu.VMEM((slots, 3, NODE_COUNT, 128), F32),
+            pltpu.VMEM((slots, NODE_COUNT, CHUNK), F32),
             sums_scratch,
+            pltpu.VMEM((slots, 2, NODE_COUNT, 128), BF16),
+            pltpu.VMEM((slots, GHOST_ROWS, CHUNK), BF16),
+            square,
         ]
         return call(
-            lambda *a: outer_kernel(group, len(parts), last, *a),
+            lambda *a: outer_kernel(slots, split, last, *a),
             "last_update" if last else "update",
-            [mom_spec] * len(parts) + [big, big] + ghost_specs + all_whole(tables),
-            [big] + ([] if last else trace_specs) + [mom_spec],
-            [big_shape] + ([] if last else trace_shapes) + [mom_shape],
-            ([] if last else [narrow_scratch]) + scratch + ghost_scratch,
-            [*parts, f, change, *ghosts, *tables],
+            CHUNKS,
+            [whole((everything, 128))]
+            + ([slot_chunk] if split else chunk_specs)
+            + [slot_chunk] + ghost_specs + [rows_spec] + all_whole([edge, ghost_r, ghost_z] + more),
+            outs + [mom_spec],
+            out_shapes + [mom_shape],
+            scratch,
+            [parts] + [f] * (1 if split else slots) + [change, *ghosts, rows, edge, ghost_r, ghost_z] + more,
         )
 
     def spread(moments):
-        parts = [moments]
-        for shift in range(1, verts):
-            parts.append(lax.ppermute(moments, "vert", [(i, i ^ shift) for i in range(verts)]))
-        return parts
+        return lax.all_gather(moments, "vert", tiled=True)
 
     def halo(right, left, turned, axial):
         from_axial = lax.ppermute(axial, "gz", [(0, 1), (1, 0)])
@@ -676,15 +706,15 @@
         last = number == STEPS - 1
         ghosts = halo(*traces)
         parts = spread(moments)
-        change = inner(current)
-        current, *traces, moments = outer(current, change, ghosts, parts, last)
+        change = inner(current, number > 0)
+        current, *traces, moments = outer(current, number > 0, change, ghosts, parts, last)
     parts = spread(moments)
     macro, flux = pl.pallas_call(
-        lambda *a: last_kernel(len(parts), *a),
+        last_kernel,
         grid_spec=pltpu.PrefetchScalarGridSpec(
             num_scalar_prefetch=1,
             grid=(1,),
-            in_specs=[mom_spec] * len(parts) + [whole(edge.shape)],
+            in_specs=[whole((everything, 128)), whole(edge.shape)],
             out_specs=[whole((8, NODES, LOCAL_Z)), whole((1, NODES))],
         ),
         out_shape=[
@@ -692,7 +722,7 @@
             jax.ShapeDtypeStruct((1, NODES), F32),
         ],
         name="macroscopic",
-    )(edge_codes, *parts, edge)
+    )(edge_codes, parts, edge)
     return (current, macro, flux)
 
 

time: 139 us -> 161 us (1.16)
  blocking collectives: 0 us -> 42.9 us
  starting transfers between devices: 26.5 us -> 13.3 us
  waiting for transfers between devices: 6.96 us -> 0.02 us
    all_gather x0 -> x3, blocking collectives: none -> 42.9 us  [spread(): return lax.all_gather(moments, 'vert', tiled=True)]
    ppermute x9 -> x0, starting transfers between devices: 12.9 us -> none  [spread(): lax.ppermute(moments, 'vert', [(i, i ^ shift) for i in range(verts)])]
    ppermute x9 -> x0, waiting for transfers between devices: 6.95 us -> none  [spread(): lax.ppermute(moments, 'vert', [(i, i ^ shift) for i in range(verts)])]
    unnamed x31 -> x17, local copies, waits for them, and re-layouts: 5.42 us -> 4.18 us
  transfers between devices with their start and end apart: 15 -> 6, of which waited for: 4 -> 0; matrix products, arithmetic and copies ran while one was open for 0% -> 0% of each run, Pallas kernels for 20% -> 17%
where the time goes in v4:
time: 161 us; the launch traced here: 160 us
  Pallas kernels  99.2 us (62%)
  blocking collectives  42.9 us (27%)
  starting transfers between devices  13.3 us (8%)
  local copies, waits for them, and re-layouts  4.18 us (3%)
    pallas_call x5, Pallas kernels, call(): pl.pallas_call(body, grid_spec=pltpu.PrefetchScalarGridSpec(num_scalar_pr...  96.7 us
    all_gather x3, blocking collectives, spread(): return lax.all_gather(moments, 'vert', tiled=True)  42.9 us
    ppermute x2, starting transfers between devices, halo(): lax.ppermute(left, 'row', [(i + 1, i) for i in range(rows_total - 1)])  7.28 us
    unnamed x17, local copies, waits for them, and re-layouts  4.18 us
    ppermute x2, starting transfers between devices, halo(): lax.ppermute(right, 'row', [(i, i + 1) for i in range(rows_total - 1)])  3.84 us
  transfers between devices with their start and end apart: 6, of which 0 were waited for; matrix products, arithmetic and copies ran while one was open for 0% of the time, Pallas kernels for 17%

profile of v4, /device:TPU:4, one launch (start us, length us, event | category | flops | bytes accessed | tf_op | source)
XLA Modules:
  0.0 160.3 jit_solution(16372427146947663361)
XLA Ops:
  0.6 1.3 copy.20.a_1_.codes
  1.9 15.4 %moments_and_traces.1 = (f32[12,16,1152]{2,1,0:T(8,128)}, f32[12,16,1152]{2,1,0:T(8,128)}, f32[12,16,1152]{2,1,0:T(8,128)}, f32[12,8,2304]{2,1,0:T(8,128)}, f32[16,128]{1,0:T(8,128)}) custom-call(s32[12]{0:T(128)} %a_0_.9, s32[2,1]{1,0:T(2,128)} %copy.20.a_1_.codes, f32[8,16,27648]{2,1,0:T(8,128)} %a_14_.2, f32[8,16,27648]{2,1,0:T(8,128)} %a_14_.2, ...), custom_call_target="tpu_custom_call" | custom-call | tf_op jit(solution)/shard_map/moments_and_traces/pallas_call | solution.py:619
  17.3 1.9 %collective-permute-start = (f32[12,16,1152]{2,1,0:T(8,128)}, f32[12,16,1152]{2,1,0:T(8,128)S(1)}, u32[]{:S(2)}, u32[]{:S(2)}) collective-permute-start(f32[12,16,1152]{2,1,0:T(8,128)} %get-tuple-element.19), channel_id=1, source_target_pairs={{0,8},{8,16},{16,24},{1,9},{9,17},{17,25},{2,10},{10,18},{18,26},{... | collective-permute-start | bytes 2654216 | tf_op jit(solution)/shard_map/ppermute | solution.py:699
  19.3 3.6 %collective-permute-start.1 = (f32[12,16,1152]{2,1,0:T(8,128)}, f32[12,16,1152]{2,1,0:T(8,128)S(1)}, u32[]{:S(2)}, u32[]{:S(2)}) collective-permute-start(f32[12,16,1152]{2,1,0:T(8,128)} %get-tuple-element.21), channel_id=1, source_target_pairs={{8,0},{16,8},{24,16},{9,1},{17,9},{25,17},{10,2},{18,10},{26,18},{... | collective-permute-start | bytes 2654216 | tf_op jit(solution)/shard_map/ppermute | solution.py:700
  22.9 0.0 copy-start.7
  22.9 1.6 collective-permute-start.2
  24.5 13.8 %inner_increments.2.a_15_ = bf16[12,8,16,2304]{3,2,1,0:T(8,128)(2,1)} custom-call(s32[12]{0:T(128)} %a_0_.9, s32[2,1]{1,0:T(2,128)} %copy.20.a_1_.codes, f32[8,16,27648]{2,1,0:T(8,128)} %a_14_.2, f32[8,2304]{1,0:T(8,128)} %constant.20.clone.a_14_.a_3_.a_20_.a_9_, f32[128,128]{1,0:T(8,128)} %constant.21.clone.a_4_, bf16[3,128,128]{2,1,0:T(8,128)(2,1)} %constant.23.clone.a_5_, ...), custom_call_target="tpu_custom_call" | custom-call | tf_op jit(solution)/shard_map/inner_increments/pallas_call | solution.py:619
  38.3 0.0 copy-done.7
  38.3 14.1 %all_gather.9.a_2_ = f32[64,128]{1,0:T(8,128)} all-gather(f32[16,128]{1,0:T(8,128)S(1)} %copy-done.7), channel_id=1, replica_groups=mesh['row'=4,'gz'=2,'vert'=4] {'vert'}, dimensions={0}, use_global_device_ids=true | all-gather | bytes 40960 | tf_op jit(solution)/shard_map/all_gather | solution.py:695
  52.4 0.0 collective-permute-done.a_16_
  52.4 0.0 collective-permute-done.1.a_18_
  52.4 0.0 copy-start.1
  52.4 0.0 collective-permute-done.2.a_19_
  52.4 0.0 copy-start.2
  52.4 0.9 copy-done
  53.3 0.3 copy-done.1
  53.6 0.3 copy-done.2
  53.8 28.8 %update.1 = (f32[12,8,16,2304]{3,2,1,0:T(8,128)}, f32[12,16,1152]{2,1,0:T(8,128)}, f32[12,16,1152]{2,1,0:T(8,128)}, f32[12,16,1152]{2,1,0:T(8,128)}, f32[12,8,2304]{2,1,0:T(8,128)}, /*index=5*/f32[16,128]{1,0:T(8,128)}) custom-call(s32[12]{0:T(128)} %a_0_.9, s32[2,1]{1,0:T(2,128)} %copy.20.a_1_.codes, f32[64,128]{1,0:T(8,128)} %all_gather.9.a_2_, ...), custom_call_target="tpu_custom_call" | custom-call | tf_op jit(solution)/shard_map/update/pallas_call | solution.py:619
  82.6 1.9 %collective-permute-start.3 = (f32[12,16,1152]{2,1,0:T(8,128)}, f32[12,16,1152]{2,1,0:T(8,128)S(1)}, u32[]{:S(2)}, u32[]{:S(2)}) collective-permute-start(f32[12,16,1152]{2,1,0:T(8,128)} %get-tuple-element.25), channel_id=1, source_target_pairs={{0,8},{8,16},{16,24},{1,9},{9,17},{17,25},{2,10},{10,18},{18,26},{... | collective-permute-start | bytes 2654216 | tf_op jit(solution)/shard_map/ppermute | solution.py:699
  84.5 3.6 %collective-permute-start.4 = (f32[12,16,1152]{2,1,0:T(8,128)}, f32[12,16,1152]{2,1,0:T(8,128)S(1)}, u32[]{:S(2)}, u32[]{:S(2)}) collective-permute-start(f32[12,16,1152]{2,1,0:T(8,128)} %get-tuple-element.27), channel_id=1, source_target_pairs={{8,0},{16,8},{24,16},{9,1},{17,9},{25,17},{10,2},{18,10},{26,18},{... | collective-permute-start | bytes 2654216 | tf_op jit(solution)/shard_map/ppermute | solution.py:700
  88.2 0.6 collective-permute-start.5
  88.8 14.0 %inner_increments.3.a_4_ = bf16[12,8,16,2304]{3,2,1,0:T(8,128)(2,1)} custom-call(s32[12]{0:T(128)} %a_0_.9, s32[2,1]{1,0:T(2,128)} %copy.20.a_1_.codes, f32[12,8,16,2304]{3,2,1,0:T(8,128)} %get-tuple-element.24.a_2_.a_3_, f32[8,2304]{1,0:T(8,128)} %constant.20.clone.a_14_.a_3_.a_20_.a_9_, f32[128,128]{1,0:T(8,128)} %constant.21.clone.a_4_, ...), custom_call_target="tpu_custom_call" | custom-call | tf_op jit(solution)/shard_map/inner_increments/pallas_call | solution.py:619
  102.7 14.0 %all_gather.10.a_2_ = f32[64,128]{1,0:T(8,128)} all-gather(f32[16,128]{1,0:T(8,128)S(1)} %copy-done.6), channel_id=1, replica_groups=mesh['row'=4,'gz'=2,'vert'=4] {'vert'}, dimensions={0}, use_global_device_ids=true | all-gather | bytes 40960 | tf_op jit(solution)/shard_map/all_gather | solution.py:695
  116.7 0.0 collective-permute-done.3.a_5_
  116.7 0.0 collective-permute-done.4.a_7_
  116.7 0.0 collective-permute-done.5.a_8_
  116.8 0.9 copy-done.3
  117.6 0.3 copy-done.4
  118.0 0.2 copy-done.5
  118.2 24.8 %last_update.1 = (f32[8,16,27648]{2,1,0:T(8,128)}, f32[16,128]{1,0:T(8,128)}) custom-call(s32[12]{0:T(128)} %a_0_.9, s32[2,1]{1,0:T(2,128)} %copy.20.a_1_.codes, f32[64,128]{1,0:T(8,128)} %all_gather.10.a_2_, f32[12,8,16,2304]{3,2,1,0:T(8,128)} %get-tuple-element.24.a_2_.a_3_, bf16[12,8,16,2304]{3,2,1,0:T(8,128)(2,1)} %inner_increments.3.a_4_, ...), custom_call_target="tpu_custom_call" | custom-call | tf_op jit(solution)/shard_map/last_update/pallas_call | solution.py:619
  143.0 14.9 %all_gather.11.parts_ref = f32[64,128]{1,0:T(8,128)} all-gather(f32[16,128]{1,0:T(8,128)} %get-tuple-element.30), channel_id=1, replica_groups=mesh['row'=4,'gz'=2,'vert'=4] {'vert'}, dimensions={0}, use_global_device_ids=true | all-gather | bytes 40960 | tf_op jit(solution)/shard_map/all_gather | solution.py:695
  157.9 2.4 %macroscopic.1 = (f32[8,8,16]{2,1,0:T(8,128)}, f32[1,8]{1,0:T(1,128)}) custom-call(s32[2,1]{1,0:T(2,128)} %copy.20.a_1_.codes, f32[64,128]{1,0:T(8,128)} %all_gather.11.parts_ref, f32[2,128,128]{2,1,0:T(8,128)} %constant.22.clone.a_21_.a_10_.edge_ref), custom_call_target="tpu_custom_call" | custom-call | tf_op jit(solution)/shard_map/macroscopic/pallas_call | solution.py:712
  (6 shorter events, 0.0 us)
Async XLA Ops:
  17.3 35.0 %collective-permute-start = (f32[12,16,1152]{2,1,0:T(8,128)}, f32[12,16,1152]{2,1,0:T(8,128)S(1)}, u32[]{:S(2)}, u32[]{:S(2)}) collective-permute-start(f32[12,16,1152]{2,1,0:T(8,128)} %get-tuple-element.19), channel_id=1, source_target_pairs={{0,8},{8,16},{16,24},{1,9},{9,17},{17,25},{2,10},{10,18},{18,26},{... | collective-permute-start | bytes 2654216 | tf_op jit(solution)/shard_map/ppermute | solution.py:699
  19.3 33.1 %collective-permute-start.1 = (f32[12,16,1152]{2,1,0:T(8,128)}, f32[12,16,1152]{2,1,0:T(8,128)S(1)}, u32[]{:S(2)}, u32[]{:S(2)}) collective-permute-start(f32[12,16,1152]{2,1,0:T(8,128)} %get-tuple-element.21), channel_id=1, source_target_pairs={{8,0},{16,8},{24,16},{9,1},{17,9},{25,17},{10,2},{18,10},{26,18},{... | collective-permute-start | bytes 2654216 | tf_op jit(solution)/shard_map/ppermute | solution.py:700
  22.9 15.4 %copy-start.7 = (f32[16,128]{1,0:T(8,128)S(1)}, f32[16,128]{1,0:T(8,128)}, u32[]{:S(2)}) copy-start(f32[16,128]{1,0:T(8,128)} %get-tuple-element.18) | copy-start | bytes 24580
  22.9 29.5 %collective-permute-start.2 = (f32[12,8,2304]{2,1,0:T(8,128)}, f32[12,8,2304]{2,1,0:T(8,128)S(1)}, u32[]{:S(2)}, u32[]{:S(2)}) collective-permute-start(f32[12,8,2304]{2,1,0:T(8,128)} %get-tuple-element.22), channel_id=1, source_target_pairs={{0,4},{4,0},{1,5},{5,1},{2,6},{6,2},{3,7},{7,3},{8,12},{12,8},{9,1... | collective-permute-start | bytes 2654216 | tf_op jit(solution)/shard_map/ppermute | solution.py:698
  52.4 0.9 copy-start
  52.4 1.2 copy-start.1
  52.4 1.4 copy-start.2
  82.6 34.1 %collective-permute-start.3 = (f32[12,16,1152]{2,1,0:T(8,128)}, f32[12,16,1152]{2,1,0:T(8,128)S(1)}, u32[]{:S(2)}, u32[]{:S(2)}) collective-permute-start(f32[12,16,1152]{2,1,0:T(8,128)} %get-tuple-element.25), channel_id=1, source_target_pairs={{0,8},{8,16},{16,24},{1,9},{9,17},{17,25},{2,10},{10,18},{18,26},{... | collective-permute-start | bytes 2654216 | tf_op jit(solution)/shard_map/ppermute | solution.py:699
  84.5 32.2 %collective-permute-start.4 = (f32[12,16,1152]{2,1,0:T(8,128)}, f32[12,16,1152]{2,1,0:T(8,128)S(1)}, u32[]{:S(2)}, u32[]{:S(2)}) collective-permute-start(f32[12,16,1152]{2,1,0:T(8,128)} %get-tuple-element.27), channel_id=1, source_target_pairs={{8,0},{16,8},{24,16},{9,1},{17,9},{25,17},{10,2},{18,10},{26,18},{... | collective-permute-start | bytes 2654216 | tf_op jit(solution)/shard_map/ppermute | solution.py:700
  88.2 28.6 %collective-permute-start.5 = (f32[12,8,2304]{2,1,0:T(8,128)}, f32[12,8,2304]{2,1,0:T(8,128)S(1)}, u32[]{:S(2)}, u32[]{:S(2)}) collective-permute-start(f32[12,8,2304]{2,1,0:T(8,128)} %get-tuple-element.28), channel_id=1, source_target_pairs={{0,4},{4,0},{1,5},{5,1},{2,6},{6,2},{3,7},{7,3},{8,12},{12,8},{9,1... | collective-permute-start | bytes 2654216 | tf_op jit(solution)/shard_map/ppermute | solution.py:698
  88.8 14.0 %copy-start.6 = (f32[16,128]{1,0:T(8,128)S(1)}, f32[16,128]{1,0:T(8,128)}, u32[]{:S(2)}) copy-start(f32[16,128]{1,0:T(8,128)} %get-tuple-element.23) | copy-start | bytes 24580
  116.7 0.9 copy-start.3
  116.7 1.3 copy-start.4
  116.7 1.5 copy-start.5

commit v5 on v4

--- a/solution.py
+++ b/solution.py
@@ -32,6 +32,7 @@
 WINDOW = 512
 GHOST_ROWS = 32
 MOMENTS = 16
+PARTS_W = 3
 F32 = jnp.float32
 BF16 = jnp.bfloat16
 PIECES = [(t, TILE, 0) for t in range(0, 1024, TILE)] + [(1024, 128, 0), (1152, 128, 1)] + [
@@ -186,6 +187,21 @@
     return rows.astype(np.float32)
 
 
+def weight_table():
+    vr = np.repeat(GRID_R, NVT)
+    vt = np.tile(GRID_T, NVR)
+    square = vr**2 + vt**2
+    columns = [np.ones(PLANE), vr, vt, vr**2, vt**2, vr * vt, vr * square, vt * square]
+    table = np.zeros((PLANE, 128))
+    for k, column in enumerate(columns):
+        rest = column.copy()
+        for part in range(PARTS_W):
+            piece = rest.astype(ml_dtypes.bfloat16).astype(np.float64)
+            table[:, k + 8 * part] = piece
+            rest = rest - piece
+    return table.astype(ml_dtypes.bfloat16)
+
+
 def edge_table():
     table = np.zeros((2, NODE_COUNT, 128))
     for r in range(NODES):
@@ -206,6 +222,7 @@
 ROTATION_M = rotation_table()
 MIRROR_M = mirror_table()
 ROWS = plane_rows()
+WEIGHT_M = weight_table()
 EDGE = edge_table()
 NODE_POS = node_columns()
 
@@ -216,6 +233,11 @@
 
 def dot(x, y):
     return jnp.dot(x, y, preferred_element_type=F32)
+
+
+def split(x):
+    high = x.astype(BF16)
+    return high, (x - high.astype(F32)).astype(BF16)
 
 
 def macroscopic_of(m):
@@ -233,52 +255,37 @@
     return rho, ur, ut, uz, temp, qr, qt, qz
 
 
-def add_speed_sums(field, vz, sums):
-    one = field * vz
-    two = one * vz
-    return [
-        sums[0] + field,
-        sums[1] + one,
-        sums[2] + two,
-        sums[3] + two * vz,
-        sums[4] + field * jnp.abs(vz),
+def add_speed_sums(sums_ref, sums, vz):
+    one = vz * sums
+    two = vz * one
+    for k, value in enumerate([sums, one, two, vz * two, jnp.abs(vz) * sums]):
+        sums_ref[k] += value
+
+
+def moment_rows(sums_ref):
+    lane = lax.broadcasted_iota(jnp.int32, (NODE_COUNT, 128), 1)
+    e = []
+    for k in range(5):
+        x = sums_ref[k]
+        e.append(x + pltpu.roll(x, 120, 1) + pltpu.roll(x, 112, 1))
+    pick = lambda k, c: e[k][:, c : c + 1]
+    columns = [
+        pick(0, 0), pick(0, 1), pick(0, 2), pick(1, 0),
+        pick(0, 3), pick(0, 4), pick(0, 5), pick(2, 0), pick(1, 1), pick(1, 2),
+        pick(0, 6) + pick(2, 1), pick(0, 7) + pick(2, 2), pick(1, 3) + pick(1, 4) + pick(3, 0), pick(4, 0),
     ]
-
-
-def add_moments(acc, vr, vt, sums):
-    g0, g1, g2, g3, g4 = sums
-    a = vr * g0
-    b = vt * g0
-    aa = vr * a
-    bb = vt * b
-    c = vr * g1
-    d = vt * g1
-    perp = aa + bb + g2
-    new = [g0, a, b, g1, aa, bb, vr * b, g2, c, d, vr * perp, vt * perp, vr * c + vt * d + g3, g4]
-    return new if acc is None else [x + y for x, y in zip(acc, new)]
-
-
-def finish_moments(sums_ref, table_ref, out_ref):
-    lane = lax.broadcasted_iota(jnp.int32, (LOCAL_Z, 128), 1)
-
-    def one_radius(r, carry):
-        rows = radius_rows(r)
-        block = jnp.zeros((LOCAL_Z, 128), F32)
-        for k in range(14):
-            block = jnp.where(lane == k, WEIGHT * jnp.sum(sums_ref[k, rows, :], axis=1, keepdims=True), block)
-        table_ref[rows, :] = block
-        return carry
-
-    lax.fori_loop(0, NODES, one_radius, 0)
-    out_ref[...] = jnp.transpose(table_ref[...])[0:MOMENTS, :]
+    table = jnp.zeros((NODE_COUNT, 128), F32)
+    for k, column in enumerate(columns):
+        table = jnp.where(lane == k, WEIGHT * column, table)
+    return jnp.transpose(table)[0:MOMENTS, :]
 
 
 def radius_rows(r):
     return pl.ds(pl.multiple_of(r * LOCAL_Z, LOCAL_Z), LOCAL_Z)
 
 
-def clear_sums(sums_ref):
-    sums_ref[...] = jnp.zeros(sums_ref.shape, F32)
+def clear(ref):
+    ref[...] = jnp.zeros(ref.shape, ref.dtype)
 
 
 def places_of():
@@ -318,56 +325,58 @@
 def first_kernel(count, order, codes, *refs):
     f_refs, refs = refs[:count], refs[count:]
     (
-        rows_ref, trace_ref, mirror_ref, right_ref, left_ref, turned_ref, axial_ref, mom_ref,
-        sums_ref, narrow_ref, mirrored_ref, table_ref,
+        weight_ref, trace_ref, mirror_ref, right_ref, left_ref, turned_ref, axial_ref, mom_ref,
+        sums_ref, slot_sums_ref, narrow_ref, mirrored_ref, low_ref,
     ) = refs
     step = pl.program_id(0)
     row, place = places_of()
 
     @pl.when(step == 0)
     def _():
-        clear_sums(sums_ref)
-
-    speeds = [slot_speed(order, s) for s in range(count)]
+        clear(slot_sums_ref)
 
     def one_radius(r, carry):
         rows = radius_rows(r)
-        acc = None
         for j in range(0, CHUNK, 128):
             at = pl.ds(j, 128)
-            sums = [jnp.zeros((LOCAL_Z, 128), F32) for _ in range(5)]
             for s in range(count):
-                field = f_refs[s][r, :, at]
-                sums = add_speed_sums(field, speeds[s], sums)
-                narrow_ref[s, rows, at] = field.astype(BF16)
-            acc = add_moments(acc, rows_ref[0:1, at], rows_ref[1:2, at], sums)
-        for k in range(14):
-            sums_ref[k, rows, :] += acc[k]
+                high, low = split(f_refs[s][r, :, at])
+                narrow_ref[s, rows, at] = high
+                low_ref[s, rows, at] = low
         return carry
 
     lax.fori_loop(0, NODES, one_radius, 0)
     send_traces(count, step, place, narrow_ref, trace_ref, right_ref, left_ref, axial_ref, mirrored_ref)
+    every = (count * NODE_COUNT, CHUNK)
+    found = dot(narrow_ref[...].reshape(every), weight_ref[...]) + dot(low_ref[...].reshape(every), weight_ref[...])
+    slot_sums_ref[...] += found.reshape(count, NODE_COUNT, 128)
 
     @pl.when(step == CHUNKS - 1)
     def _():
         turn_traces(count, row, mirror_ref, mirrored_ref, turned_ref)
-        finish_moments(sums_ref, table_ref, mom_ref)
+        clear(sums_ref)
+        for s in range(count):
+            add_speed_sums(sums_ref, slot_sums_ref[s], slot_speed(order, s))
+        mom_ref[...] = moment_rows(sums_ref)
 
 
 def inner_kernel(
-    count, split, order, codes, f_ref, rows_ref, pos_ref, radial_ref, axial_m_ref, rot_ref,
-    out_ref, inverse_ref, pad_ref, lhs_ref,
+    count, slotted, order, codes, f_ref, rows_ref, pos_ref, weight_ref, radial_ref, axial_m_ref, rot_ref,
+    out_ref, mom_ref, sums_ref, slot_sums_ref, inverse_ref, pad_ref, lhs_ref,
 ):
     def nodes_of(s, first, lanes):
-        if split:
+        if slotted:
             return f_ref[s, :, :, first : first + lanes].reshape(NODE_COUNT, lanes)
         return f_ref[:, :, s * PLANE + first : s * PLANE + first + lanes].reshape(NODE_COUNT, lanes)
 
     step = pl.program_id(0)
     row, place = places_of()
 
+    clear(slot_sums_ref)
+
     @pl.when(step == 0)
     def _():
+        clear(sums_ref)
         pad_ref[:, :, 0:128] = jnp.zeros((count, NODE_COUNT, 128), BF16)
         pad_ref[:, :, 128 + PLANE :] = jnp.zeros((count, NODE_COUNT, 128), BF16)
         inverse_ref[...] = 1.0 / (ELEMENT_WIDTH * (row.astype(F32) + pos_ref[...]))
@@ -395,18 +404,29 @@
                 continue
             vr = rows_ref[0:1, first : first + lanes]
             inside = first - start
+            changes = []
             for s in range(count):
                 moved = dot(lhs_ref[s, side], nodes_of(s, first, lanes).astype(BF16))
                 change = turned[s * NODE_COUNT : (s + 1) * NODE_COUNT, inside : inside + lanes]
                 change = change + vr * moved[0:NODE_COUNT] + moved[NODE_COUNT:]
-                out_ref[s, :, :, first : first + lanes] = change.astype(BF16).reshape(NODES, LOCAL_Z, lanes)
-
-
-def total_of(parts_ref):
-    parts = [parts_ref[k : k + MOMENTS, :] for k in range(0, parts_ref.shape[0], MOMENTS)]
+                changes.append(change.astype(BF16))
+                out_ref[s, :, :, first : first + lanes] = changes[s].reshape(NODES, LOCAL_Z, lanes)
+            found = dot(jnp.concatenate(changes, axis=0), weight_ref[first : first + lanes, :])
+            slot_sums_ref[...] += found.reshape(count, NODE_COUNT, 128)
+
+    for s in range(count):
+        add_speed_sums(sums_ref, slot_sums_ref[s], slot_speed(order, step * count + s))
+
+    @pl.when(step == pl.num_programs(0) - 1)
+    def _():
+        mom_ref[...] = moment_rows(sums_ref)
+
+
+def total_of(part_refs, base_ref):
+    parts = [p[...] for p in part_refs]
     while len(parts) > 1:
         parts = [parts[k] + parts[k + 1] for k in range(0, len(parts), 2)]
-    return parts[0]
+    return parts[0] if base_ref is None else parts[0] + base_ref[...]
 
 
 def prepare_nodes(total, codes, place, edge_ref, table_ref, node_ref, wall_ref):
@@ -444,30 +464,41 @@
     lhs_ref[s, 1] = (ghost_r_ref[1] + lean).astype(BF16)
 
 
-def outer_kernel(count, split, last, order, codes, parts_ref, *refs):
-    if split:
+def outer_kernel(count, part_count, slotted, last, order, codes, *refs):
+    part_refs, refs = refs[:part_count], refs[part_count:]
+    base_ref = None
+    if slotted:
+        base_ref, refs = refs[0], refs[1:]
+    inner_mom_ref, refs = refs[0], refs[1:]
+    if slotted:
         f_ref, refs = refs[0], refs[1:]
         field_of = lambda s, r, at: f_ref[s, r, :, at]
     else:
         f_refs, refs = refs[:count], refs[count:]
         field_of = lambda s, r, at: f_refs[s][r, :, at]
     inner_ref, in_left_ref, in_turned_ref, in_right_ref, in_axial_ref = refs[:5]
-    rows_ref, edge_ref, ghost_r_ref, ghost_z_ref = refs[5:9]
-    refs = refs[9:]
+    rows_ref, weight_ref, edge_ref, ghost_r_ref, ghost_z_ref = refs[5:10]
+    refs = refs[10:]
     if last:
-        (out_hbm, mom_ref, out_buf, out_sem), refs = refs[:4], refs[4:]
+        (out_hbm, share_ref, kept_ref, out_buf, out_sem), refs = refs[:5], refs[5:]
     else:
-        (trace_ref, mirror_ref, out_ref, right_ref, left_ref, turned_ref, axial_ref, mom_ref), refs = refs[:8], refs[8:]
-        (narrow_ref, mirrored_ref), refs = refs[:2], refs[2:]
-    node_ref, wall_ref, slot_ref, work_ref, sums_ref, lhs_ref, ghost_ref, table_ref = refs
+        (trace_ref, mirror_ref, out_ref, right_ref, left_ref, turned_ref, axial_ref), refs = refs[:7], refs[7:]
+        (share_ref, kept_ref, narrow_ref, mirrored_ref), refs = refs[:4], refs[4:]
+    (
+        node_ref, wall_ref, slot_ref, work_ref, sums_ref, lhs_ref, ghost_ref, table_ref,
+        plane_ref, plane_sums_ref, ghost_sums_ref,
+    ) = refs
     step = pl.program_id(0)
     row, place = places_of()
     speeds = [slot_speed(order, s) for s in range(count)]
 
     @pl.when(step == 0)
     def _():
-        clear_sums(sums_ref)
-        prepare_nodes(total_of(parts_ref), codes, place, edge_ref, table_ref, node_ref, wall_ref)
+        clear(plane_sums_ref)
+        clear(ghost_sums_ref)
+        total = total_of(part_refs, base_ref)
+        kept_ref[...] = total * (1.0 - total[0:1, :] * (TIME_STEP / KNUDSEN))
+        prepare_nodes(total, codes, place, edge_ref, table_ref, node_ref, wall_ref)
         for s in range(count):
             for k, value in enumerate(slot_factors(speeds[s], node_ref)):
                 slot_ref[s, k] = value
@@ -486,6 +517,7 @@
             rows = jnp.concatenate([rows_ref[0:1, at] * radial, axial, jnp.zeros((8, 128), F32)], axis=0)
             ghost_ref[s, :, at] = rows.astype(BF16)
         work_ref[s] = dot(lhs_ref[s, side, :, 0:GHOST_ROWS], ghost_ref[s])
+    ghost_sums_ref[side] += dot(ghost_ref[...].reshape(count * GHOST_ROWS, CHUNK), weight_ref[...])
 
     def copy_out(s, chunk):
         at = pl.ds(pl.multiple_of(s * PLANE + chunk * CHUNK, CHUNK), CHUNK)
@@ -503,18 +535,20 @@
 
     def update(r, carry):
         rows = radius_rows(r)
-        acc = None
         for j in range(0, CHUNK, 128):
             at = pl.ds(j, 128)
-            vr, vt = rows_ref[0:1, at], rows_ref[1:2, at]
-            cr = vr - node_ref[6, rows, :]
-            ct = vt - node_ref[7, rows, :]
+            cr = rows_ref[0:1, at] - node_ref[6, rows, :]
+            ct = rows_ref[1:2, at] - node_ref[7, rows, :]
             square = cr * cr + ct * ct
             gauss = jnp.exp(square * node_ref[1, rows, :])
             along = cr * node_ref[8, rows, :] + ct * node_ref[9, rows, :]
             reach = square * node_ref[3, rows, :]
             keep = node_ref[5, rows, :]
-            sums = [jnp.zeros((LOCAL_Z, 128), F32) for _ in range(5)]
+            tilted = gauss * along
+            for k, plane in enumerate([gauss, tilted, gauss * reach, tilted * reach]):
+                high, low = split(plane)
+                plane_ref[k, rows, at] = high
+                plane_ref[4 + k, rows, at] = low
             for s in range(count):
                 new = field_of(s, r, at) * keep + work_ref[s, rows, at] + inner_ref[s, r, :, at].astype(F32)
                 bend = (along + slot_ref[s, 1, rows, :]) * (reach + slot_ref[s, 2, rows, :]) + 1.0
@@ -524,10 +558,6 @@
                 else:
                     out_ref[s, r, :, at] = new
                     narrow_ref[s, rows, at] = new.astype(BF16)
-                sums = add_speed_sums(new, speeds[s], sums)
-            acc = add_moments(acc, vr, vt, sums)
-        for k in range(14):
-            sums_ref[k, rows, :] += acc[k]
         return carry
 
     lax.fori_loop(0, NODES, update, 0)
@@ -544,15 +574,29 @@
     else:
         send_traces(count, step, place, narrow_ref, trace_ref, right_ref, left_ref, axial_ref, mirrored_ref)
 
+    found = dot(plane_ref[...].reshape(8 * NODE_COUNT, CHUNK), weight_ref[...]).reshape(8, NODE_COUNT, 128)
+    plane_sums_ref[...] += found[0:4] + found[4:8]
+
     @pl.when(step == CHUNKS - 1)
     def _():
         if not last:
             turn_traces(count, row, mirror_ref, mirrored_ref, turned_ref)
-        finish_moments(sums_ref, table_ref, mom_ref)
-
-
-def last_kernel(codes, parts_ref, edge_ref, macro_ref, flux_ref):
-    total_ref = total_of(parts_ref)
+        clear(sums_ref)
+        for s in range(count):
+            peak, heat, reach = (slot_ref[s, k] for k in range(3))
+            sums = plane_sums_ref[0] * (1.0 + heat * reach) + plane_sums_ref[1] * reach
+            sums = peak * (sums + plane_sums_ref[2] * heat + plane_sums_ref[3])
+            for edge_side in range(2):
+                lift = lhs_ref[s, edge_side, :, 0:GHOST_ROWS]
+                high, low = split(ghost_sums_ref[edge_side, s * GHOST_ROWS : (s + 1) * GHOST_ROWS, :])
+                sums = sums + dot(lift, high) + dot(lift, low)
+            add_speed_sums(sums_ref, sums, speeds[s])
+        share_ref[...] = moment_rows(sums_ref) + inner_mom_ref[...]
+
+
+def last_kernel(part_count, codes, *refs):
+    total_ref = total_of(refs[:part_count], refs[part_count])
+    edge_ref, macro_ref, flux_ref = refs[part_count + 1 :]
     row, place = places_of()
     values = macroscopic_of(lambda k: total_ref[k : k + 1, :])
     for k in range(8):
@@ -588,7 +632,7 @@
     ghost_r, ghost_z = jnp.asarray(GHOST_R), jnp.asarray(GHOST_Z)
     trace_m, mirror_m, rot_m = jnp.asarray(TRACE_M), jnp.asarray(MIRROR_M), jnp.asarray(ROTATION_M)
 
-    everything = verts * MOMENTS
+    weight_m = jnp.asarray(WEIGHT_M)
     slab = pl.BlockSpec((NODES, LOCAL_Z, group * PLANE), lambda i, *n: (0, 0, i))
     slot_slab = pl.BlockSpec((group, NODES, LOCAL_Z, PLANE), lambda i, *n: (i, 0, 0, 0))
     chunk_specs = [
@@ -600,6 +644,7 @@
     inward_spec = pl.BlockSpec((slots, LOCAL_Z, CHUNK), lambda i, *n: (0, 0, jnp.minimum(i, half - 1)))
     axial_spec = pl.BlockSpec((slots, NODES, CHUNK), lambda i, *n: (0, 0, i))
     rows_spec = pl.BlockSpec((8, CHUNK), lambda i, *n: (0, i))
+    weight_spec = pl.BlockSpec((CHUNK, 128), lambda i, *n: (i, 0))
     mom_spec = whole((MOMENTS, 128))
     radial_shape = jax.ShapeDtypeStruct((slots, LOCAL_Z, HALF), F32)
     axial_shape = jax.ShapeDtypeStruct((slots, NODES, PLANE), F32)
@@ -609,7 +654,7 @@
     trace_shapes = [radial_shape, radial_shape, radial_shape, axial_shape]
     ghost_specs = [outward_spec, outward_spec, inward_spec, axial_spec]
     square = pltpu.VMEM((NODE_COUNT, 128), F32)
-    sums_scratch = pltpu.VMEM((14, NODE_COUNT, 128), F32)
+    sums_scratch = pltpu.VMEM((5, NODE_COUNT, 128), F32)
     trace_scratch = [
         pltpu.VMEM((slots, NODE_COUNT, CHUNK), BF16),
         pltpu.VMEM((slots * LOCAL_Z, HALF), BF16),
@@ -636,15 +681,17 @@
     def first(f):
         return call(
             lambda *a: first_kernel(slots, *a), "moments_and_traces", CHUNKS,
-            chunk_specs + [rows_spec] + all_whole([trace_m, mirror_m]),
+            chunk_specs + [weight_spec] + all_whole([trace_m, mirror_m]),
             trace_specs + [mom_spec], trace_shapes + [mom_shape],
-            [sums_scratch] + trace_scratch + [square],
-            [f] * slots + [rows, trace_m, mirror_m],
+            [sums_scratch, pltpu.VMEM((slots, NODE_COUNT, 128), F32)] + trace_scratch + trace_scratch[:1],
+            [f] * slots + [weight_m, trace_m, mirror_m],
         )
 
     def inner(f, split):
-        tables = [rows, pos, radial_m, axial_m, rot_m]
+        tables = [rows, pos, weight_m, radial_m, axial_m, rot_m]
         scratch = [
+            sums_scratch,
+            pltpu.VMEM((group, NODE_COUNT, 128), F32),
             square,
             pltpu.VMEM((group, NODE_COUNT, PLANE + 256), BF16),
             pltpu.VMEM((group, 2, 2 * NODE_COUNT, 128), BF16),
@@ -652,10 +699,11 @@
         return call(
             lambda *a: inner_kernel(group, split, *a), "inner_increments", steps,
             [slot_slab if split else slab] + all_whole(tables),
-            [slot_slab], [jax.ShapeDtypeStruct(inner_shape, BF16)], scratch, [f] + tables,
-        )[0]
-
-    def outer(f, split, change, ghosts, parts, last):
+            [slot_slab, mom_spec], [jax.ShapeDtypeStruct(inner_shape, BF16), mom_shape], scratch, [f] + tables,
+        )
+
+    def outer(f, base, change, change_moments, ghosts, parts, last):
+        split = base is not None
         more = [] if last else [trace_m, mirror_m]
         if last:
             outs = [pl.BlockSpec(memory_space=pl.ANY)]
@@ -677,22 +725,29 @@
             pltpu.VMEM((slots, 2, NODE_COUNT, 128), BF16),
             pltpu.VMEM((slots, GHOST_ROWS, CHUNK), BF16),
             square,
+            pltpu.VMEM((8, NODE_COUNT, CHUNK), BF16),
+            pltpu.VMEM((4, NODE_COUNT, 128), F32),
+            pltpu.VMEM((2, slots * GHOST_ROWS, 128), F32),
         ]
         return call(
-            lambda *a: outer_kernel(slots, split, last, *a),
+            lambda *a: outer_kernel(slots, len(parts), split, last, *a),
             "last_update" if last else "update",
             CHUNKS,
-            [whole((everything, 128))]
+            [mom_spec] * (len(parts) + (2 if split else 1))
             + ([slot_chunk] if split else chunk_specs)
-            + [slot_chunk] + ghost_specs + [rows_spec] + all_whole([edge, ghost_r, ghost_z] + more),
-            outs + [mom_spec],
-            out_shapes + [mom_shape],
+            + [slot_chunk] + ghost_specs + [rows_spec, weight_spec] + all_whole([edge, ghost_r, ghost_z] + more),
+            outs + [mom_spec, mom_spec],
+            out_shapes + [mom_shape, mom_shape],
             scratch,
-            [parts] + [f] * (1 if split else slots) + [change, *ghosts, rows, edge, ghost_r, ghost_z] + more,
+            [*parts] + ([base] if split else []) + [change_moments] + [f] * (1 if split else slots)
+            + [change, *ghosts, rows, weight_m, edge, ghost_r, ghost_z] + more,
         )
 
     def spread(moments):
-        return lax.all_gather(moments, "vert", tiled=True)
+        parts = [moments]
+        for shift in range(1, verts):
+            parts.append(lax.ppermute(moments, "vert", [(i, i ^ shift) for i in range(verts)]))
+        return parts
 
     def halo(right, left, turned, axial):
         from_axial = lax.ppermute(axial, "gz", [(0, 1), (1, 0)])
@@ -702,19 +757,20 @@
 
     current = distribution
     *traces, moments = first(current)
+    base = None
     for number in range(STEPS):
         last = number == STEPS - 1
         ghosts = halo(*traces)
         parts = spread(moments)
-        change = inner(current, number > 0)
-        current, *traces, moments = outer(current, number > 0, change, ghosts, parts, last)
+        change, change_moments = inner(current, number > 0)
+        current, *traces, moments, base = outer(current, base, change, change_moments, ghosts, parts, last)
     parts = spread(moments)
     macro, flux = pl.pallas_call(
-        last_kernel,
+        lambda *a: last_kernel(len(parts), *a),
         grid_spec=pltpu.PrefetchScalarGridSpec(
             num_scalar_prefetch=1,
             grid=(1,),
-            in_specs=[whole((everything, 128)), whole(edge.shape)],
+            in_specs=[mom_spec] * (len(parts) + 1) + [whole(edge.shape)],
             out_specs=[whole((8, NODES, LOCAL_Z)), whole((1, NODES))],
         ),
         out_shape=[
@@ -722,7 +778,7 @@
             jax.ShapeDtypeStruct((1, NODES), F32),
         ],
         name="macroscopic",
-    )(edge_codes, parts, edge)
+    )(edge_codes, *parts, base, edge)
     return (current, macro, flux)
 
 

time: 161 us -> 148 us (0.919)
  blocking collectives: 42.9 us -> 0 us
  starting transfers between devices: 13.3 us -> 26.5 us
  Pallas kernels: 99.2 us -> 109 us
  waiting for transfers between devices: 0.02 us -> 6.97 us
    all_gather x3 -> x0, blocking collectives: 42.9 us -> none  [spread(): return lax.all_gather(moments, 'vert', tiled=True)]
    ppermute x0 -> x9, starting transfers between devices: none -> 13 us  [spread(): lax.ppermute(moments, 'vert', [(i, i ^ shift) for i in range(verts)])]
    pallas_call x5, Pallas kernels: 96.7 us -> 106 us  [call(): pl.pallas_call(body, grid_spec=pltpu.PrefetchScalarGridSpec(num_scalar_pr...]
    ppermute x0 -> x9, waiting for transfers between devices: none -> 6.96 us  [spread(): lax.ppermute(moments, 'vert', [(i, i ^ shift) for i in range(verts)])]
    unnamed x17 -> x31, local copies, waits for them, and re-layouts: 4.18 us -> 4.8 us
  transfers between devices with their start and end apart: 6 -> 15, of which waited for: 0 -> 4; matrix products, arithmetic and copies ran while one was open for 0% -> 0% of each run, Pallas kernels for 17% -> 27%
where the time goes in v5:
time: 148 us
  Pallas kernels  109 us (74%)
  starting transfers between devices  26.5 us (18%)
  waiting for transfers between devices  6.97 us (5%)
  local copies, waits for them, and re-layouts  4.8 us (3%)
    pallas_call x5, Pallas kernels, call(): pl.pallas_call(body, grid_spec=pltpu.PrefetchScalarGridSpec(num_scalar_pr...  106 us
    ppermute x9, starting transfers between devices, spread(): lax.ppermute(moments, 'vert', [(i, i ^ shift) for i in range(verts)])  13 us
    ppermute x2, starting transfers between devices, halo(): lax.ppermute(left, 'row', [(i + 1, i) for i in range(rows_total - 1)])  7.46 us
    ppermute x9, waiting for transfers between devices, spread(): lax.ppermute(moments, 'vert', [(i, i ^ shift) for i in range(verts)])  6.96 us
    unnamed x31, local copies, waits for them, and re-layouts  4.8 us
    ppermute x2, starting transfers between devices, halo(): lax.ppermute(right, 'row', [(i, i + 1) for i in range(rows_total - 1)])  3.84 us
  transfers between devices with their start and end apart: 15, of which 4 were waited for; matrix products, arithmetic and copies ran while one was open for 0% of the time, Pallas kernels for 27%

profile of v5, /device:TPU:4, one launch (start us, length us, event | category | flops | bytes accessed | tf_op | source)
XLA Modules:
  0.0 148.1 jit_solution(12166953492500680283)
XLA Ops:
  0.6 1.3 copy.21.a_1_.a_0_
  1.9 16.0 %moments_and_traces.1 = (f32[12,16,1152]{2,1,0:T(8,128)}, f32[12,16,1152]{2,1,0:T(8,128)}, f32[12,16,1152]{2,1,0:T(8,128)}, f32[12,8,2304]{2,1,0:T(8,128)}, f32[16,128]{1,0:T(8,128)}) custom-call(s32[12]{0:T(128)} %a_0_.10, s32[2,1]{1,0:T(2,128)} %copy.21.a_1_.a_0_, f32[8,16,27648]{2,1,0:T(8,128)} %a_18_.2, f32[8,16,27648]{2,1,0:T(8,128)} %a_18_.2, ...), custom_call_target="tpu_custom_call" | custom-call | tf_op jit(solution)/shard_map/moments_and_traces/pallas_call | solution.py:664
  17.9 1.9 %collective-permute-start.3 = (f32[12,16,1152]{2,1,0:T(8,128)}, f32[12,16,1152]{2,1,0:T(8,128)S(1)}, u32[]{:S(2)}, u32[]{:S(2)}) collective-permute-start(f32[12,16,1152]{2,1,0:T(8,128)} %get-tuple-element.27), channel_id=1, source_target_pairs={{0,8},{8,16},{16,24},{1,9},{9,17},{17,25},{2,10},{10,18},{18,26},{... | collective-permute-start | bytes 2654216 | tf_op jit(solution)/shard_map/ppermute | solution.py:754
  19.8 3.6 %collective-permute-start.4 = (f32[12,16,1152]{2,1,0:T(8,128)}, f32[12,16,1152]{2,1,0:T(8,128)S(1)}, u32[]{:S(2)}, u32[]{:S(2)}) collective-permute-start(f32[12,16,1152]{2,1,0:T(8,128)} %get-tuple-element.29), channel_id=1, source_target_pairs={{8,0},{16,8},{24,16},{9,1},{17,9},{25,17},{10,2},{18,10},{26,18},{... | collective-permute-start | bytes 2654216 | tf_op jit(solution)/shard_map/ppermute | solution.py:755
  23.4 1.6 %collective-permute-start.5 = (f32[12,8,2304]{2,1,0:T(8,128)}, f32[12,8,2304]{2,1,0:T(8,128)S(1)}, u32[]{:S(2)}, u32[]{:S(2)}) collective-permute-start(f32[12,8,2304]{2,1,0:T(8,128)} %get-tuple-element.30), channel_id=1, source_target_pairs={{0,4},{4,0},{1,5},{5,1},{2,6},{6,2},{3,7},{7,3},{8,12},{12,8},{9,1... | collective-permute-start | bytes 2654216 | tf_op jit(solution)/shard_map/ppermute | solution.py:753
  25.0 3.6 %collective-permute-start.2 = (f32[16,128]{1,0:T(8,128)}, f32[16,128]{1,0:T(8,128)S(1)}, u32[]{:S(2)}, u32[]{:S(2)}) collective-permute-start(f32[16,128]{1,0:T(8,128)} %get-tuple-element.24.a_2_), channel_id=1, source_target_pairs={{0,3},{1,2},{2,1},{3,0},{4,7},{5,6},{6,5},{7,4},{8,11},{9,10},{10,... | collective-permute-start | bytes 24584 | tf_op jit(solution)/shard_map/ppermute | solution.py:749
  28.6 2.1 %collective-permute-done.2.a_5_ = f32[16,128]{1,0:T(8,128)S(1)} collective-permute-done((f32[16,128]{1,0:T(8,128)}, f32[16,128]{1,0:T(8,128)S(1)}, u32[]{:S(2)}, u32[]{:S(2)}) %collective-permute-start.2) | collective-permute-done | bytes 8224 | tf_op jit(solution)/shard_map/ppermute | solution.py:749
  30.7 19.9 %inner_increments.2 = (bf16[12,8,16,2304]{3,2,1,0:T(8,128)(2,1)}, f32[16,128]{1,0:T(8,128)}) custom-call(s32[12]{0:T(128)} %a_0_.10, s32[2,1]{1,0:T(2,128)} %copy.21.a_1_.a_0_, f32[8,16,27648]{2,1,0:T(8,128)} %a_18_.2, f32[8,2304]{1,0:T(8,128)} %constant.22.clone.a_3_.a_24_.a_14_, f32[128,128]{1,0:T(8,128)} %constant.23.clone.a_4_, ...), custom_call_target="tpu_custom_call" | custom-call | tf_op jit(solution)/shard_map/inner_increments/pallas_call | solution.py:664
  50.7 0.5 copy-done.9
  51.2 0.4 copy-done
  51.9 0.3 copy-done.2
  52.2 27.2 %update.1 = (f32[12,8,16,2304]{3,2,1,0:T(8,128)}, f32[12,16,1152]{2,1,0:T(8,128)}, f32[12,16,1152]{2,1,0:T(8,128)}, f32[12,16,1152]{2,1,0:T(8,128)}, f32[12,8,23...) custom-call(s32[12]{0:T(128)} %a_0_.10, s32[2,1]{1,0:T(2,128)} %copy.21.a_1_.a_0_, ...), custom_call_target="tpu_custom_call" | custom-call | tf_op jit(solution)/shard_map/update/pallas_call | solution.py:664
  79.4 1.9 %collective-permute-start.9 = (f32[12,16,1152]{2,1,0:T(8,128)}, f32[12,16,1152]{2,1,0:T(8,128)S(1)}, u32[]{:S(2)}, u32[]{:S(2)}) collective-permute-start(f32[12,16,1152]{2,1,0:T(8,128)} %get-tuple-element.36), channel_id=1, source_target_pairs={{0,8},{8,16},{16,24},{1,9},{9,17},{17,25},{2,10},{10,18},{18,26},{... | collective-permute-start | bytes 2654216 | tf_op jit(solution)/shard_map/ppermute | solution.py:754
  81.3 3.8 %collective-permute-start.10 = (f32[12,16,1152]{2,1,0:T(8,128)}, f32[12,16,1152]{2,1,0:T(8,128)S(1)}, u32[]{:S(2)}, u32[]{:S(2)}) collective-permute-start(f32[12,16,1152]{2,1,0:T(8,128)} %get-tuple-element.38), channel_id=1, source_target_pairs={{8,0},{16,8},{24,16},{9,1},{17,9},{25,17},{10,2},{18,10},{26,18},{... | collective-permute-start | bytes 2654216 | tf_op jit(solution)/shard_map/ppermute | solution.py:755
  85.1 0.6 collective-permute-start.11
  85.7 3.6 %collective-permute-start.8 = (f32[16,128]{1,0:T(8,128)}, f32[16,128]{1,0:T(8,128)S(1)}, u32[]{:S(2)}, u32[]{:S(2)}) collective-permute-start(f32[16,128]{1,0:T(8,128)} %get-tuple-element.31.a_2_), channel_id=1, source_target_pairs={{0,3},{1,2},{2,1},{3,0},{4,7},{5,6},{6,5},{7,4},{8,11},{9,10},{10,... | collective-permute-start | bytes 24584 | tf_op jit(solution)/shard_map/ppermute | solution.py:749
  89.3 0.6 collective-permute-start.7
  89.9 1.6 %collective-permute-done.8.a_5_ = f32[16,128]{1,0:T(8,128)S(1)} collective-permute-done((f32[16,128]{1,0:T(8,128)}, f32[16,128]{1,0:T(8,128)S(1)}, u32[]{:S(2)}, u32[]{:S(2)}) %collective-permute-start.8) | collective-permute-done | bytes 8224 | tf_op jit(solution)/shard_map/ppermute | solution.py:749
  91.5 0.8 collective-permute-start.6
  92.3 20.0 %inner_increments.3 = (bf16[12,8,16,2304]{3,2,1,0:T(8,128)(2,1)}, f32[16,128]{1,0:T(8,128)}) custom-call(s32[12]{0:T(128)} %a_0_.10, s32[2,1]{1,0:T(2,128)} %copy.21.a_1_.a_0_, f32[12,8,16,2304]{3,2,1,0:T(8,128)} %get-tuple-element.33.a_2_.a_8_, f32[8,2304]{1,0:T(8,128)} %constant.22.clone.a_3_.a_24_.a_14_, f32[128,128]{1,0:T(8,128)} %constant.23.clone.a_4_, ...), custom_call_target="tpu_custom_call" | custom-call | tf_op jit(solution)/shard_map/inner_increments/pallas_call | solution.py:664
  112.4 0.5 copy-done.7
  112.9 0.4 copy-done.3
  113.3 0.3 copy-done.4
  113.5 0.3 copy-done.5
  113.8 23.4 %last_update.1 = (f32[8,16,27648]{2,1,0:T(8,128)}, f32[16,128]{1,0:T(8,128)}, f32[16,128]{1,0:T(8,128)}) custom-call(s32[12]{0:T(128)} %a_0_.10, s32[2,1]{1,0:T(2,128)} %copy.21.a_1_.a_0_, f32[16,128]{1,0:T(8,128)} %get-tuple-element.31.a_2_, f32[16,128]{1,0:T(8,128)} %copy-done.10, f32[16,128]{1,0:T(8,128)} %copy-done.7, f32[16,128]{1,0:T(8,128)} %copy-done.6, ...), custom_call_target="tpu_custom_call" | custom-call | tf_op jit(solution)/shard_map/last_update/pallas_call | solution.py:664
  137.2 3.0 %collective-permute-start.14 = (f32[16,128]{1,0:T(8,128)}, f32[16,128]{1,0:T(8,128)S(1)}, u32[]{:S(2)}, u32[]{:S(2)}) collective-permute-start(f32[16,128]{1,0:T(8,128)} %get-tuple-element.41.a_1_), channel_id=1, source_target_pairs={{0,3},{1,2},{2,1},{3,0},{4,7},{5,6},{6,5},{7,4},{8,11},{9,10},{10,... | collective-permute-start | bytes 24584 | tf_op jit(solution)/shard_map/ppermute | solution.py:749
  140.2 0.5 collective-permute-start.13
  140.7 1.0 collective-permute-start.12
  141.7 1.3 collective-permute-done.14.a_4_
  143.0 2.0 %collective-permute-done.13.a_3_ = f32[16,128]{1,0:T(8,128)S(1)} collective-permute-done((f32[16,128]{1,0:T(8,128)}, f32[16,128]{1,0:T(8,128)S(1)}, u32[]{:S(2)}, u32[]{:S(2)}) %collective-permute-start.13) | collective-permute-done | bytes 8224 | tf_op jit(solution)/shard_map/ppermute | solution.py:749
  145.0 0.6 copy-done.13
  145.6 2.5 %macroscopic.1 = (f32[8,8,16]{2,1,0:T(8,128)}, f32[1,8]{1,0:T(1,128)}) custom-call(s32[2,1]{1,0:T(2,128)} %copy.21.a_1_.a_0_, f32[16,128]{1,0:T(8,128)} %get-tuple-element.41.a_1_, f32[16,128]{1,0:T(8,128)} %copy-done.14, f32[16,128]{1,0:T(8,128)} %copy-done.13, f32[16,128]{1,0:T(8,128)} %copy-done.12, f32[16,128]{1,0:T(8,128)} %get-tuple-element.42.a_5_, ...), custom_call_target="tpu_custom_call" | custom-call | tf_op jit(solution)/shard_map/macroscopic/pallas_call | solution.py:768
  (35 shorter events, 0.4 us)
Async XLA Ops:
  17.9 32.8 %collective-permute-start.3 = (f32[12,16,1152]{2,1,0:T(8,128)}, f32[12,16,1152]{2,1,0:T(8,128)S(1)}, u32[]{:S(2)}, u32[]{:S(2)}) collective-permute-start(f32[12,16,1152]{2,1,0:T(8,128)} %get-tuple-element.27), channel_id=1, source_target_pairs={{0,8},{8,16},{16,24},{1,9},{9,17},{17,25},{2,10},{10,18},{18,26},{... | collective-permute-start | bytes 2654216 | tf_op jit(solution)/shard_map/ppermute | solution.py:754
  19.8 30.9 %collective-permute-start.4 = (f32[12,16,1152]{2,1,0:T(8,128)}, f32[12,16,1152]{2,1,0:T(8,128)S(1)}, u32[]{:S(2)}, u32[]{:S(2)}) collective-permute-start(f32[12,16,1152]{2,1,0:T(8,128)} %get-tuple-element.29), channel_id=1, source_target_pairs={{8,0},{16,8},{24,16},{9,1},{17,9},{25,17},{10,2},{18,10},{26,18},{... | collective-permute-start | bytes 2654216 | tf_op jit(solution)/shard_map/ppermute | solution.py:755
  23.4 27.3 %collective-permute-start.5 = (f32[12,8,2304]{2,1,0:T(8,128)}, f32[12,8,2304]{2,1,0:T(8,128)S(1)}, u32[]{:S(2)}, u32[]{:S(2)}) collective-permute-start(f32[12,8,2304]{2,1,0:T(8,128)} %get-tuple-element.30), channel_id=1, source_target_pairs={{0,4},{4,0},{1,5},{5,1},{2,6},{6,2},{3,7},{7,3},{8,12},{12,8},{9,1... | collective-permute-start | bytes 2654216 | tf_op jit(solution)/shard_map/ppermute | solution.py:753
  25.0 5.7 %collective-permute-start.2 = (f32[16,128]{1,0:T(8,128)}, f32[16,128]{1,0:T(8,128)S(1)}, u32[]{:S(2)}, u32[]{:S(2)}) collective-permute-start(f32[16,128]{1,0:T(8,128)} %get-tuple-element.24.a_2_), channel_id=1, source_target_pairs={{0,3},{1,2},{2,1},{3,0},{4,7},{5,6},{6,5},{7,4},{8,11},{9,10},{10,... | collective-permute-start | bytes 24584 | tf_op jit(solution)/shard_map/ppermute | solution.py:749
  28.6 22.0 %collective-permute-start.1 = (f32[16,128]{1,0:T(8,128)}, f32[16,128]{1,0:T(8,128)S(1)}, u32[]{:S(2)}, u32[]{:S(2)}) collective-permute-start(f32[16,128]{1,0:T(8,128)} %get-tuple-element.24.a_2_), channel_id=1, source_target_pairs={{0,2},{1,3},{2,0},{3,1},{4,6},{5,7},{6,4},{7,5},{8,10},{9,11},{10,... | collective-permute-start | bytes 24584 | tf_op jit(solution)/shard_map/ppermute | solution.py:749
  30.7 20.0 %copy-start.8 = (f32[16,128]{1,0:T(8,128)}, f32[16,128]{1,0:T(8,128)S(1)}, u32[]{:S(2)}) copy-start(f32[16,128]{1,0:T(8,128)S(1)} %collective-permute-done.2.a_5_) | copy-start | bytes 24580
  30.7 20.0 %collective-permute-start = (f32[16,128]{1,0:T(8,128)}, f32[16,128]{1,0:T(8,128)S(1)}, u32[]{:S(2)}, u32[]{:S(2)}) collective-permute-start(f32[16,128]{1,0:T(8,128)} %get-tuple-element.24.a_2_), channel_id=1, source_target_pairs={{0,1},{1,0},{2,3},{3,2},{4,5},{5,4},{6,7},{7,6},{8,9},{9,8},{10,11... | collective-permute-start | bytes 24584 | tf_op jit(solution)/shard_map/ppermute | solution.py:749
  50.6 0.6 copy-start.9
  50.6 0.6 copy-start.11
  50.7 1.0 copy-start
  50.7 1.2 copy-start.1
  50.7 1.5 copy-start.2
  79.4 32.9 %collective-permute-start.9 = (f32[12,16,1152]{2,1,0:T(8,128)}, f32[12,16,1152]{2,1,0:T(8,128)S(1)}, u32[]{:S(2)}, u32[]{:S(2)}) collective-permute-start(f32[12,16,1152]{2,1,0:T(8,128)} %get-tuple-element.36), channel_id=1, source_target_pairs={{0,8},{8,16},{16,24},{1,9},{9,17},{17,25},{2,10},{10,18},{18,26},{... | collective-permute-start | bytes 2654216 | tf_op jit(solution)/shard_map/ppermute | solution.py:754
  81.3 31.0 %collective-permute-start.10 = (f32[12,16,1152]{2,1,0:T(8,128)}, f32[12,16,1152]{2,1,0:T(8,128)S(1)}, u32[]{:S(2)}, u32[]{:S(2)}) collective-permute-start(f32[12,16,1152]{2,1,0:T(8,128)} %get-tuple-element.38), channel_id=1, source_target_pairs={{8,0},{16,8},{24,16},{9,1},{17,9},{25,17},{10,2},{18,10},{26,18},{... | collective-permute-start | bytes 2654216 | tf_op jit(solution)/shard_map/ppermute | solution.py:755
  85.1 27.2 %collective-permute-start.11 = (f32[12,8,2304]{2,1,0:T(8,128)}, f32[12,8,2304]{2,1,0:T(8,128)S(1)}, u32[]{:S(2)}, u32[]{:S(2)}) collective-permute-start(f32[12,8,2304]{2,1,0:T(8,128)} %get-tuple-element.39), channel_id=1, source_target_pairs={{0,4},{4,0},{1,5},{5,1},{2,6},{6,2},{3,7},{7,3},{8,12},{12,8},{9,1... | collective-permute-start | bytes 2654216 | tf_op jit(solution)/shard_map/ppermute | solution.py:753
  85.7 5.7 %collective-permute-start.8 = (f32[16,128]{1,0:T(8,128)}, f32[16,128]{1,0:T(8,128)S(1)}, u32[]{:S(2)}, u32[]{:S(2)}) collective-permute-start(f32[16,128]{1,0:T(8,128)} %get-tuple-element.31.a_2_), channel_id=1, source_target_pairs={{0,3},{1,2},{2,1},{3,0},{4,7},{5,6},{6,5},{7,4},{8,11},{9,10},{10,... | collective-permute-start | bytes 24584 | tf_op jit(solution)/shard_map/ppermute | solution.py:749
  89.3 22.9 %collective-permute-start.7 = (f32[16,128]{1,0:T(8,128)}, f32[16,128]{1,0:T(8,128)S(1)}, u32[]{:S(2)}, u32[]{:S(2)}) collective-permute-start(f32[16,128]{1,0:T(8,128)} %get-tuple-element.31.a_2_), channel_id=1, source_target_pairs={{0,2},{1,3},{2,0},{3,1},{4,6},{5,7},{6,4},{7,5},{8,10},{9,11},{10,... | collective-permute-start | bytes 24584 | tf_op jit(solution)/shard_map/ppermute | solution.py:749
  91.5 20.8 %copy-start.6 = (f32[16,128]{1,0:T(8,128)}, f32[16,128]{1,0:T(8,128)S(1)}, u32[]{:S(2)}) copy-start(f32[16,128]{1,0:T(8,128)S(1)} %collective-permute-done.8.a_5_) | copy-start | bytes 24580
  91.5 20.8 %collective-permute-start.6 = (f32[16,128]{1,0:T(8,128)}, f32[16,128]{1,0:T(8,128)S(1)}, u32[]{:S(2)}, u32[]{:S(2)}) collective-permute-start(f32[16,128]{1,0:T(8,128)} %get-tuple-element.31.a_2_), channel_id=1, source_target_pairs={{0,1},{1,0},{2,3},{3,2},{4,5},{5,4},{6,7},{7,6},{8,9},{9,8},{10,11... | collective-permute-start | bytes 24584 | tf_op jit(solution)/shard_map/ppermute | solution.py:749
  112.3 0.6 copy-start.7
  112.3 0.6 copy-start.10
  112.3 1.0 copy-start.3
  112.3 1.2 copy-start.4
  112.3 1.5 %copy-start.5 = (f32[12,8,2304]{2,1,0:T(8,128)}, f32[12,8,2304]{2,1,0:T(8,128)S(1)}, u32[]{:S(2)}) copy-start(f32[12,8,2304]{2,1,0:T(8,128)S(1)} %collective-permute-done.11.a_13_) | copy-start | bytes 2654212
  137.2 5.7 %collective-permute-start.14 = (f32[16,128]{1,0:T(8,128)}, f32[16,128]{1,0:T(8,128)S(1)}, u32[]{:S(2)}, u32[]{:S(2)}) collective-permute-start(f32[16,128]{1,0:T(8,128)} %get-tuple-element.41.a_1_), channel_id=1, source_target_pairs={{0,3},{1,2},{2,1},{3,0},{4,7},{5,6},{6,5},{7,4},{8,11},{9,10},{10,... | collective-permute-start | bytes 24584 | tf_op jit(solution)/shard_map/ppermute | solution.py:749
  140.2 4.8 %collective-permute-start.13 = (f32[16,128]{1,0:T(8,128)}, f32[16,128]{1,0:T(8,128)S(1)}, u32[]{:S(2)}, u32[]{:S(2)}) collective-permute-start(f32[16,128]{1,0:T(8,128)} %get-tuple-element.41.a_1_), channel_id=1, source_target_pairs={{0,2},{1,3},{2,0},{3,1},{4,6},{5,7},{6,4},{7,5},{8,10},{9,11},{10,... | collective-permute-start | bytes 24584 | tf_op jit(solution)/shard_map/ppermute | solution.py:749
  140.7 4.3 %collective-permute-start.12 = (f32[16,128]{1,0:T(8,128)}, f32[16,128]{1,0:T(8,128)S(1)}, u32[]{:S(2)}, u32[]{:S(2)}) collective-permute-start(f32[16,128]{1,0:T(8,128)} %get-tuple-element.41.a_1_), channel_id=1, source_target_pairs={{0,1},{1,0},{2,3},{3,2},{4,5},{5,4},{6,7},{7,6},{8,9},{9,8},{10,11... | collective-permute-start | bytes 24584 | tf_op jit(solution)/shard_map/ppermute | solution.py:749
  142.9 2.0 %copy-start.12 = (f32[16,128]{1,0:T(8,128)}, f32[16,128]{1,0:T(8,128)S(1)}, u32[]{:S(2)}) copy-start(f32[16,128]{1,0:T(8,128)S(1)} %collective-permute-done.14.a_4_) | copy-start | bytes 24580
  145.0 0.6 copy-start.13
  145.0 0.6 copy-start.14

commit v6 on v3

--- a/solution.py
+++ b/solution.py
@@ -308,44 +308,33 @@
     return ref[:, :, first : first + lanes].reshape(NODE_COUNT, lanes)
 
 
-def send_traces(count, place, narrow_ref, trace_ref, right_ref, left_ref, axial_ref):
+def trace_kernel(
+    count, order, codes, f_ref, trace_ref, mirror_ref, right_ref, left_ref, turned_ref, axial_ref
+):
+    row, place = places_of()
     for s in range(count):
         for first, lanes, side in PIECES:
-            narrow = narrow_ref[s, :, first : first + lanes]
+            narrow = nodes_of(f_ref, s * PLANE + first, lanes).astype(BF16)
             send_piece(s, first, lanes, side, place, narrow, trace_ref, right_ref, left_ref, axial_ref)
-
-
-def first_kernel(
-    count, order, codes, f_ref, rows_ref, trace_ref, mirror_ref,
-    right_ref, left_ref, turned_ref, axial_ref, mom_ref, sums_ref, table_ref,
-):
+    turn_traces(count, row, mirror_ref, left_ref, turned_ref)
+
+
+def moment_kernel(count, order, codes, f_ref, rows_ref, mom_ref, sums_ref, table_ref):
     step = pl.program_id(0)
-    row, place = places_of()
 
     @pl.when(step == 0)
     def _():
         clear_sums(sums_ref)
 
     speeds = [slot_speed(order, step * count + s) for s in range(count)]
-    for first, lanes, side in PIECES:
-        narrow = [[] for s in range(count)]
-        for inside in range(0, lanes, 128):
-            at = pl.ds(first + inside, 128)
-            column = [[] for s in range(count)]
-            for r in range(NODES):
-                sums = [sums_ref[k, r, :, at] for k in range(5)]
-                for s in range(count):
-                    field = f_ref[r, :, pl.ds(s * PLANE + first + inside, 128)]
-                    sums = add_speed_sums(field, speeds[s], sums)
-                    column[s].append(field.astype(BF16))
-                for k in range(5):
-                    sums_ref[k, r, :, at] = sums[k]
+    for j in range(0, PLANE, 128):
+        at = pl.ds(j, 128)
+        for r in range(NODES):
+            sums = [sums_ref[k, r, :, at] for k in range(5)]
             for s in range(count):
-                narrow[s].append(jnp.concatenate(column[s], axis=0))
-        for s in range(count):
-            block = jnp.concatenate(narrow[s], axis=1) if len(narrow[s]) > 1 else narrow[s][0]
-            send_piece(s, first, lanes, side, place, block, trace_ref, right_ref, left_ref, axial_ref)
-    turn_traces(count, row, mirror_ref, left_ref, turned_ref)
+                sums = add_speed_sums(f_ref[r, :, pl.ds(s * PLANE + j, 128)], speeds[s], sums)
+            for k in range(5):
+                sums_ref[k, r, :, at] = sums[k]
 
     @pl.when(step == pl.num_programs(0) - 1)
     def _():
@@ -366,16 +355,16 @@
         inverse_ref[...] = 1.0 / (ELEMENT_WIDTH * (row.astype(F32) + pos_ref[...]))
         minus = radial_ref[jnp.where(row == lax.axis_size("row") - 1, 2, 0)]
         for s in range(count):
-            lhs_ref[s, 0, 0:NODE_COUNT] = minus
-            lhs_ref[s, 1, 0:NODE_COUNT] = radial_ref[1]
+            lhs_ref[s, 0, :, 0:NODE_COUNT] = minus
+            lhs_ref[s, 1, :, 0:NODE_COUNT] = radial_ref[1]
 
     kind_out = jnp.where(jnp.logical_and(place == 1, codes[1, 0] == 2), 2, 0)
     inverse = inverse_ref[...]
     for s in range(count):
         vz = slot_speed(order, step * count + s)
         axial = (vz * axial_m_ref[jnp.where(vz > 0, 1, kind_out)]).astype(BF16)
-        lhs_ref[s, 0, NODE_COUNT:] = axial
-        lhs_ref[s, 1, NODE_COUNT:] = axial
+        lhs_ref[s, 0, :, NODE_COUNT:] = axial
+        lhs_ref[s, 1, :, NODE_COUNT:] = axial
         for j in range(PLANE // 128):
             field = nodes_of(f_ref, s * PLANE + j * 128, 128)
             pad_ref[s, :, 128 + j * 128 : 256 + j * 128] = (field * inverse).astype(BF16)
@@ -390,9 +379,10 @@
             inside = first - start
             for s in range(count):
                 here = s * PLANE + first
-                moved = dot(lhs_ref[s, side], nodes_of(f_ref, here, lanes).astype(BF16))
+                field = nodes_of(f_ref, here, lanes)
+                both = jnp.concatenate([(field * vr).astype(BF16), field.astype(BF16)], axis=0)
                 change = turned[s * NODE_COUNT : (s + 1) * NODE_COUNT, inside : inside + lanes]
-                change = change + vr * moved[0:NODE_COUNT] + moved[NODE_COUNT:]
+                change = change + dot(lhs_ref[s, side], both)
                 out_ref[:, :, here : here + lanes] = change.astype(BF16).reshape(NODES, LOCAL_Z, lanes)
 
 
@@ -436,12 +426,9 @@
             square = cr * cr + ct * ct
             gauss = jnp.exp(square * n_half)
             along = cr * n_qr + ct * n_qt
-            reach = square * n_inv - 5.0
-            tilted = gauss * along
             plane_ref[0, rows, at] = gauss
-            plane_ref[1, rows, at] = tilted
-            plane_ref[2, rows, at] = gauss * reach
-            plane_ref[3, rows, at] = tilted * reach
+            plane_ref[1, rows, at] = along
+            plane_ref[2, rows, at] = square * n_inv
         return carry
 
     lax.fori_loop(0, NODES, one_radius, 0)
@@ -449,10 +436,8 @@
 
 def slot_factors(vz, node_ref):
     cz = vz - node_ref[0]
-    lam = node_ref[4] * jnp.exp(cz * cz * node_ref[1])
-    alpha = cz * node_ref[2]
-    reach = cz * cz * node_ref[3]
-    return lam * (1.0 + alpha * reach), lam * reach, lam * alpha, lam
+    square = cz * cz
+    return node_ref[4] * jnp.exp(square * node_ref[1]), cz * node_ref[2], square * node_ref[3] - 5.0
 
 
 def ghost_lifts(vz, ghost_r_ref, ghost_z_ref, lhs_ref):
@@ -476,69 +461,46 @@
         ghost_ref[:, at] = rows.astype(BF16)
 
 
-def outer_kernel(count, part_count, last, order, codes, *refs):
+def outer_kernel(part_count, last, order, codes, *refs):
     part_refs, refs = refs[:part_count], refs[part_count:]
     f_ref, inner_ref, in_left_ref, in_turned_ref, in_right_ref, in_axial_ref = refs[:6]
     rows_ref, edge_ref, ghost_r_ref, ghost_z_ref = refs[6:10]
     refs = refs[10:]
     if last:
-        (out_ref, mom_ref), refs = refs[:2], refs[2:]
+        out_ref, refs = refs[0], refs[1:]
     else:
-        (trace_ref, mirror_ref, out_ref, right_ref, left_ref, turned_ref, axial_ref, mom_ref), refs = refs[:8], refs[8:]
-        narrow_ref, refs = refs[0], refs[1:]
-    plane_ref, node_ref, wall_ref, slot_ref, work_ref, sums_ref, lhs_ref, ghost_ref, table_ref = refs
+        (trace_ref, mirror_ref, out_ref, right_ref, left_ref, turned_ref, axial_ref), refs = refs[:7], refs[7:]
+    plane_ref, node_ref, wall_ref, slot_ref, lhs_ref, ghost_ref, table_ref = refs
     step = pl.program_id(0)
     row, place = places_of()
 
     @pl.when(step == 0)
     def _():
-        clear_sums(sums_ref)
         total = total_of([p[...] for p in part_refs])
         prepare_nodes(total, codes, place, rows_ref, edge_ref, table_ref, node_ref, wall_ref, plane_ref)
 
-    speeds = [slot_speed(order, step * count + s) for s in range(count)]
-    for s in range(count):
-        vz = speeds[s]
-        for k, value in enumerate(slot_factors(vz, node_ref)):
-            slot_ref[s, k] = value
-        ghost_lifts(vz, ghost_r_ref, ghost_z_ref, lhs_ref)
-        ghost_rows(
-            s, vz, place, in_left_ref, in_turned_ref, in_right_ref, in_axial_ref, rows_ref, wall_ref, ghost_ref
-        )
-        for first, lanes, side in PIECES:
-            work_ref[s, :, first : first + lanes] = dot(
-                lhs_ref[side, :, 0:GHOST_ROWS], ghost_ref[:, first : first + lanes]
-            )
-
-    def update(r, carry):
-        rows = pl.ds(pl.multiple_of(r * LOCAL_Z, LOCAL_Z), LOCAL_Z)
-        keep = node_ref[5, rows, :]
-        factor = [[slot_ref[s, k, rows, :] for k in range(4)] for s in range(count)]
-        for j in range(PLANE // 128):
-            at = pl.ds(j * 128, 128)
-            planes = [plane_ref[k, rows, at] for k in range(4)]
-            sums = [sums_ref[k, r, :, at] for k in range(5)]
-            for s in range(count):
-                here = pl.ds(s * PLANE + j * 128, 128)
-                new = f_ref[r, :, here] * keep + work_ref[s, rows, at] + inner_ref[r, :, here].astype(F32)
-                for k in range(4):
-                    new = new + planes[k] * factor[s][k]
-                out_ref[r, :, here] = new
-                sums = add_speed_sums(new, speeds[s], sums)
-                if not last:
-                    narrow_ref[s, rows, at] = new.astype(BF16)
-            for k in range(5):
-                sums_ref[k, r, :, at] = sums[k]
-        return carry
-
-    lax.fori_loop(0, NODES, update, 0)
+    vz = slot_speed(order, step)
+    for k, value in enumerate(slot_factors(vz, node_ref)):
+        slot_ref[k] = value
+    ghost_lifts(vz, ghost_r_ref, ghost_z_ref, lhs_ref)
+    ghost_rows(0, vz, place, in_left_ref, in_turned_ref, in_right_ref, in_axial_ref, rows_ref, wall_ref, ghost_ref)
+    for first, lanes, side in PIECES:
+        lifted = dot(lhs_ref[side, :, 0:GHOST_ROWS], ghost_ref[:, first : first + lanes])
+        pieces = []
+        for inside in range(0, lanes, 128):
+            here = first + inside
+            at = pl.ds(here, 128)
+            new = nodes_of(f_ref, here, 128) * node_ref[5] + nodes_of(inner_ref, here, 128).astype(F32)
+            new = new + lifted[:, inside : inside + 128]
+            bend = (plane_ref[1, :, at] + slot_ref[1]) * (plane_ref[2, :, at] + slot_ref[2]) + 1.0
+            new = new + (plane_ref[0, :, at] * slot_ref[0]) * bend
+            out_ref[:, :, here : here + 128] = new.reshape(NODES, LOCAL_Z, 128)
+            pieces.append(new.astype(BF16))
+        if not last:
+            narrow = jnp.concatenate(pieces, axis=1) if len(pieces) > 1 else pieces[0]
+            send_piece(0, first, lanes, side, place, narrow, trace_ref, right_ref, left_ref, axial_ref)
     if not last:
-        send_traces(count, place, narrow_ref, trace_ref, right_ref, left_ref, axial_ref)
-        turn_traces(count, row, mirror_ref, left_ref, turned_ref)
-
-    @pl.when(step == pl.num_programs(0) - 1)
-    def _():
-        finish_moments(sums_ref, rows_ref, table_ref, mom_ref)
+        turn_traces(1, row, mirror_ref, left_ref, turned_ref)
 
 
 def last_kernel(part_count, codes, *refs):
@@ -570,7 +532,6 @@
     assert local_r == NODES and local_z == LOCAL_Z
     slots = vdev // PLANE
     group = math.gcd(slots, 3)
-    steps = slots // group
     rows_total = lax.axis_size("row")
     verts = lax.axis_size("vert")
     assert lax.axis_size("gz") == 2
@@ -579,54 +540,54 @@
     ghost_r, ghost_z = jnp.asarray(GHOST_R), jnp.asarray(GHOST_Z)
     trace_m, mirror_m, rot_m = jnp.asarray(TRACE_M), jnp.asarray(MIRROR_M), jnp.asarray(ROTATION_M)
 
-    big = pl.BlockSpec((NODES, LOCAL_Z, group * PLANE), lambda i, *n: (0, 0, i))
-    radial_spec = pl.BlockSpec((group, LOCAL_Z, HALF), lambda i, *n: (i, 0, 0))
-    axial_spec = pl.BlockSpec((group, NODES, PLANE), lambda i, *n: (i, 0, 0))
+    def slab(count):
+        return pl.BlockSpec((NODES, LOCAL_Z, count * PLANE), lambda i, *n: (0, 0, i))
+
+    def radial_spec(count):
+        return pl.BlockSpec((count, LOCAL_Z, HALF), lambda i, *n: (i, 0, 0))
+
+    def axial_spec(count):
+        return pl.BlockSpec((count, NODES, PLANE), lambda i, *n: (i, 0, 0))
+
+    def trace_specs(count):
+        return [radial_spec(count), radial_spec(count), radial_spec(count), axial_spec(count)]
+
     mom_spec = whole((MOMENTS, 128))
     radial_shape = jax.ShapeDtypeStruct((slots, LOCAL_Z, HALF), F32)
     axial_shape = jax.ShapeDtypeStruct((slots, NODES, PLANE), F32)
     mom_shape = jax.ShapeDtypeStruct((MOMENTS, 128), F32)
     big_shape = jax.ShapeDtypeStruct(distribution.shape, F32)
-    trace_specs = [radial_spec, radial_spec, radial_spec, axial_spec]
     trace_shapes = [radial_shape, radial_shape, radial_shape, axial_shape]
-    ghost_specs = [radial_spec, radial_spec, radial_spec, axial_spec]
     square = pltpu.VMEM((NODE_COUNT, 128), F32)
-    sums_scratch = pltpu.VMEM((5, NODES, LOCAL_Z, PLANE), F32)
-    narrow_scratch = pltpu.VMEM((group, NODE_COUNT, PLANE), BF16)
-    node_scratch = [
-        pltpu.VMEM((4, NODE_COUNT, PLANE), F32),
-        pltpu.VMEM((10, NODE_COUNT, 128), F32),
-        pltpu.VMEM((NODES, 128), F32),
-    ]
-    ghost_scratch = [
-        pltpu.VMEM((2, NODE_COUNT, 128), BF16),
-        pltpu.VMEM((GHOST_ROWS, PLANE), BF16),
-        square,
-    ]
-
-    def call(body, name, in_specs, out_specs, out_shape, scratch, args):
+
+    def call(body, name, count, limit, in_specs, out_specs, out_shape, scratch, args):
         return pl.pallas_call(
             body,
             grid_spec=pltpu.PrefetchScalarGridSpec(
                 num_scalar_prefetch=2,
-                grid=(steps,),
+                grid=(slots // count,),
                 in_specs=in_specs,
                 out_specs=out_specs,
                 scratch_shapes=scratch,
             ),
             out_shape=out_shape,
-            compiler_params=pltpu.CompilerParams(vmem_limit_bytes=56 * 1024 * 1024),
+            compiler_params=pltpu.CompilerParams(vmem_limit_bytes=limit * 1024 * 1024),
             name=name,
         )(z_order, edge_codes, *args)
 
     def all_whole(tables):
         return [whole(x.shape) for x in tables]
 
-    def first(f):
-        tables = [rows, trace_m, mirror_m]
+    def traces_of(f):
         return call(
-            lambda *a: first_kernel(group, *a), "moments_and_traces", [big] + all_whole(tables),
-            trace_specs + [mom_spec], trace_shapes + [mom_shape], [sums_scratch, square], [f] + tables,
+            lambda *a: trace_kernel(group, *a), "traces", group, 20, [slab(group)] + all_whole([trace_m, mirror_m]),
+            trace_specs(group), trace_shapes, [], [f, trace_m, mirror_m],
+        )
+
+    def moments_of(f):
+        return call(
+            lambda *a: moment_kernel(group, *a), "moments", group, 20, [slab(group)] + all_whole([rows]),
+            mom_spec, mom_shape, [pltpu.VMEM((5, NODES, LOCAL_Z, PLANE), F32), square], [f, rows],
         )
 
     def inner(f):
@@ -634,29 +595,34 @@
         scratch = [
             square,
             pltpu.VMEM((group, NODE_COUNT, PLANE + 256), BF16),
-            pltpu.VMEM((group, 2, 2 * NODE_COUNT, 128), BF16),
+            pltpu.VMEM((group, 2, NODE_COUNT, 2 * NODE_COUNT), BF16),
         ]
         return call(
-            lambda *a: inner_kernel(group, *a), "inner_increments", [big] + all_whole(tables),
-            [big], [jax.ShapeDtypeStruct(f.shape, BF16)], scratch, [f] + tables,
-        )[0]
+            lambda *a: inner_kernel(group, *a), "inner_increments", group, 22, [slab(group)] + all_whole(tables),
+            slab(group), jax.ShapeDtypeStruct(f.shape, BF16), scratch, [f] + tables,
+        )
 
     def outer(f, change, ghosts, parts, last):
         tables = [rows, edge, ghost_r, ghost_z] + ([] if last else [trace_m, mirror_m])
-        scratch = node_scratch + [
-            pltpu.VMEM((group, 4, NODE_COUNT, 128), F32),
-            pltpu.VMEM((group, NODE_COUNT, PLANE), F32),
-            sums_scratch,
+        scratch = [
+            pltpu.VMEM((3, NODE_COUNT, PLANE), F32),
+            pltpu.VMEM((10, NODE_COUNT, 128), F32),
+            pltpu.VMEM((NODES, 128), F32),
+            pltpu.VMEM((3, NODE_COUNT, 128), F32),
+            pltpu.VMEM((2, NODE_COUNT, 128), BF16),
+            pltpu.VMEM((GHOST_ROWS, PLANE), BF16),
+            square,
         ]
-        return call(
-            lambda *a: outer_kernel(group, len(parts), last, *a),
-            "last_update" if last else "update",
-            [mom_spec] * len(parts) + [big, big] + ghost_specs + all_whole(tables),
-            [big] + ([] if last else trace_specs) + [mom_spec],
-            [big_shape] + ([] if last else trace_shapes) + [mom_shape],
-            ([] if last else [narrow_scratch]) + scratch + ghost_scratch,
+        out = call(
+            lambda *a: outer_kernel(len(parts), last, *a),
+            "last_update" if last else "update", 1, 20,
+            [mom_spec] * len(parts) + [slab(1), slab(1)] + trace_specs(1) + all_whole(tables),
+            [slab(1)] + ([] if last else trace_specs(1)),
+            [big_shape] + ([] if last else trace_shapes),
+            scratch,
             [*parts, f, change, *ghosts, *tables],
         )
+        return out[0], out[1:]
 
     def spread(moments):
         parts = [moments]
@@ -671,14 +637,13 @@
         return from_left, turned, from_right, from_axial
 
     current = distribution
-    *traces, moments = first(current)
+    traces = traces_of(current)
     for number in range(STEPS):
-        last = number == STEPS - 1
         ghosts = halo(*traces)
-        parts = spread(moments)
+        parts = spread(moments_of(current))
         change = inner(current)
-        current, *traces, moments = outer(current, change, ghosts, parts, last)
-    parts = spread(moments)
+        current, traces = outer(current, change, ghosts, parts, number == STEPS - 1)
+    parts = spread(moments_of(current))
     macro, flux = pl.pallas_call(
         lambda *a: last_kernel(len(parts), *a),
         grid_spec=pltpu.PrefetchScalarGridSpec(

time: 139 us -> 140 us (level)
  local copies, waits for them, and re-layouts: 5.42 us -> 17.3 us
  Pallas kernels: 98.3 us -> 87.7 us
    unnamed x31 -> x59, local copies, waits for them, and re-layouts: 5.42 us -> 17.3 us
    pallas_call x5 -> x8, Pallas kernels: 95.8 us -> 85.3 us  [call(): pl.pallas_call(body, grid_spec=pltpu.PrefetchScalarGridSpec(num_scalar_pr...]
  transfers between devices with their start and end apart: 15 -> 15, of which waited for: 4 -> 4; matrix products, arithmetic and copies ran while one was open for 0% -> 0% of each run, Pallas kernels for 20% -> 24%
where the time goes in v6:
time: 140 us; the launch traced here: 139 us
  Pallas kernels  87.7 us (63%)
  starting transfers between devices  26.9 us (19%)
  local copies, waits for them, and re-layouts  17.3 us (12%)
  waiting for transfers between devices  6.28 us (4%)
    pallas_call x8, Pallas kernels, call(): pl.pallas_call(body, grid_spec=pltpu.PrefetchScalarGridSpec(num_scalar_pr...  85.3 us
    unnamed x59, local copies, waits for them, and re-layouts  17.3 us
    ppermute x9, starting transfers between devices, spread(): lax.ppermute(moments, 'vert', [(i, i ^ shift) for i in range(verts)])  13.2 us
    ppermute x2, starting transfers between devices, halo(): lax.ppermute(left, 'row', [(i + 1, i) for i in range(rows_total - 1)])  7.46 us
    ppermute x9, waiting for transfers between devices, spread(): lax.ppermute(moments, 'vert', [(i, i ^ shift) for i in range(verts)])  6.26 us
    ppermute x2, starting transfers between devices, halo(): lax.ppermute(right, 'row', [(i, i + 1) for i in range(rows_total - 1)])  3.97 us
  transfers between devices with their start and end apart: 15, of which 4 were waited for; matrix products, arithmetic and copies ran while one was open for 0% of the time, Pallas kernels for 24%

profile of v6, /device:TPU:4, one launch (start us, length us, event | category | flops | bytes accessed | tf_op | source)
XLA Modules:
  0.0 139.1 jit_solution(2168085386002262937)
XLA Ops:
  0.6 0.7 copy.22.a_1_.a_0_
  1.4 5.0 %copy-done = f32[8,16,27648]{2,1,0:T(8,128)S(1)} copy-done((f32[8,16,27648]{2,1,0:T(8,128)S(1)}, f32[8,16,27648]{2,1,0:T(8,128)}, u32[]{:S(2)}) %copy-start) | copy-done | bytes 14155800
  6.4 1.7 %copy-done.2 = bf16[1152,1152]{1,0:T(8,128)(2,1)S(1)} copy-done((bf16[1152,1152]{1,0:T(8,128)(2,1)S(1)}, bf16[1152,1152]{1,0:T(8,128)(2,1)}, u32[]{:S(2)}) %copy-start.2) | copy-done | bytes 2654232
  8.1 0.8 copy-done.16
  8.9 0.7 copy-done.19
  9.6 3.2 %traces.1 = (f32[12,16,1152]{2,1,0:T(8,128)S(1)}, f32[12,16,1152]{2,1,0:T(8,128)S(1)}, f32[12,16,1152]{2,1,0:T(8,128)S(1)}, f32[12,8,2304]{2,1,0:T(8,128)S(1)}) custom-call(s32[12]{0:T(128)S(1)} %copy-done.19, s32[2,1]{1,0:T(2,128)S(1)} %copy.22.a_1_.a_0_, f32[8,16,27648]{2,1,0:T(8,128)S(1)} %copy-done, bf16[2,2,32,128]{3,2,1,0:T(8,128)(2,1)S(1)} %copy-done.16, ...), custom_call_target="tpu_custom_call" | custom-call | tf_op jit(solution)/shard_map/traces/pallas_call | solution.py:564
  12.8 2.1 %collective-permute-start.3 = (f32[12,16,1152]{2,1,0:T(8,128)S(1)}, f32[12,16,1152]{2,1,0:T(8,128)S(1)}, u32[]{:S(2)}, u32[]{:S(2)}) collective-permute-start(f32[12,16,1152]{2,1,0:T(8,128)S(1)} %get-tuple-element.14), channel_id=1, source_target_pairs={{0,8},{8,16},{16,24},{1,9},{9,17},{17,25},{2,10},{10,18},{18,26},{... | collective-permute-start | bytes 2654216 | tf_op jit(solution)/shard_map/ppermute | solution.py:635
  14.8 3.6 %collective-permute-start.4 = (f32[12,16,1152]{2,1,0:T(8,128)S(1)}, f32[12,16,1152]{2,1,0:T(8,128)S(1)}, u32[]{:S(2)}, u32[]{:S(2)}) collective-permute-start(f32[12,16,1152]{2,1,0:T(8,128)S(1)} %get-tuple-element.16), channel_id=1, source_target_pairs={{8,0},{16,8},{24,16},{9,1},{17,9},{25,17},{10,2},{18,10},{26,18},{... | collective-permute-start | bytes 2654216 | tf_op jit(solution)/shard_map/ppermute | solution.py:636
  18.6 1.6 %collective-permute-start.5 = (f32[12,8,2304]{2,1,0:T(8,128)S(1)}, f32[12,8,2304]{2,1,0:T(8,128)S(1)}, u32[]{:S(2)}, u32[]{:S(2)}) collective-permute-start(f32[12,8,2304]{2,1,0:T(8,128)S(1)} %get-tuple-element.17), channel_id=1, source_target_pairs={{0,4},{4,0},{1,5},{5,1},{2,6},{6,2},{3,7},{7,3},{8,12},{12,8},{9,1... | collective-permute-start | bytes 2654216 | tf_op jit(solution)/shard_map/ppermute | solution.py:634
  20.1 8.1 %moments.3.a_2_ = f32[16,128]{1,0:T(8,128)S(1)} custom-call(s32[12]{0:T(128)S(1)} %copy-done.19, s32[2,1]{1,0:T(2,128)S(1)} %copy.22.a_1_.a_0_, f32[8,16,27648]{2,1,0:T(8,128)S(1)} %copy-done, f32[8,2304]{1,0:T(8,128)S(1)} %copy-done.6), custom_call_target="tpu_custom_call" | custom-call | tf_op jit(solution)/shard_map/moments/pallas_call | solution.py:564
  28.3 3.7 %collective-permute-start.2 = (f32[16,128]{1,0:T(8,128)S(1)}, f32[16,128]{1,0:T(8,128)S(1)}, u32[]{:S(2)}, u32[]{:S(2)}) collective-permute-start(f32[16,128]{1,0:T(8,128)S(1)} %moments.3.a_2_), channel_id=1, source_target_pairs={{0,3},{1,2},{2,1},{3,0},{4,7},{5,6},{6,5},{7,4},{8,11},{9,10},{10,... | collective-permute-start | bytes 24584 | tf_op jit(solution)/shard_map/ppermute | solution.py:630
  32.0 1.8 %collective-permute-done.2.a_5_ = f32[16,128]{1,0:T(8,128)S(1)} collective-permute-done((f32[16,128]{1,0:T(8,128)S(1)}, f32[16,128]{1,0:T(8,128)S(1)}, u32[]{:S(2)}, u32[]{:S(2)}) %collective-permute-start.2) | collective-permute-done | bytes 8224 | tf_op jit(solution)/shard_map/ppermute | solution.py:630
  33.9 8.6 %inner_increments.2.a_7_ = bf16[8,16,27648]{2,1,0:T(8,128)(2,1)S(1)} custom-call(s32[12]{0:T(128)S(1)} %copy-done.20, s32[2,1]{1,0:T(2,128)S(1)} %copy.22.a_1_.a_0_, f32[8,16,27648]{2,1,0:T(8,128)S(1)} %bitcast.1, f32[8,2304]{1,0:T(8,128)S(1)} %copy-done.6, f32[128,128]{1,0:T(8,128)S(1)} %copy-done.15, bf16[3,128,128]{2,1,0:T(8,128)(2,1)S(1)} %copy-done.13, ...), custom_call_target="tpu_custom_call" | custom-call | tf_op jit(solution)/shard_map/inner_increments/pallas_call | solution.py:564
  42.6 0.9 copy-done.8
  43.5 1.2 copy-done.9
  44.7 26.4 %update.1 = (f32[8,16,27648]{2,1,0:T(8,128)S(1)}, f32[12,16,1152]{2,1,0:T(8,128)S(1)}, f32[12,16,1152]{2,1,0:T(8,128)S(1)}, f32[12,16,1152]{2,1,0:T(8,128)S(1)}, f32[12,8,2304]{2,1,0:T(8,128)S(1)}) custom-call(s32[12]{0:T(128)S(1)} %copy-done.20, s32[2,1]{1,0:T(2,128)S(1)} %copy.22.a_1_.a_0_, f32[16,128]{1,0:T(8,128)S(1)} %moments.3.a_2_, ...), custom_call_target="tpu_custom_call" | custom-call | tf_op jit(solution)/shard_map/update/pallas_call | solution.py:564
  71.1 1.9 %collective-permute-start.9 = (f32[12,16,1152]{2,1,0:T(8,128)S(1)}, f32[12,16,1152]{2,1,0:T(8,128)S(1)}, u32[]{:S(2)}, u32[]{:S(2)}) collective-permute-start(f32[12,16,1152]{2,1,0:T(8,128)S(1)} %get-tuple-element.19), channel_id=1, source_target_pairs={{0,8},{8,16},{16,24},{1,9},{9,17},{17,25},{2,10},{10,18},{18,26},{... | collective-permute-start | bytes 2654216 | tf_op jit(solution)/shard_map/ppermute | solution.py:635
  73.0 3.8 %collective-permute-start.10 = (f32[12,16,1152]{2,1,0:T(8,128)S(1)}, f32[12,16,1152]{2,1,0:T(8,128)S(1)}, u32[]{:S(2)}, u32[]{:S(2)}) collective-permute-start(f32[12,16,1152]{2,1,0:T(8,128)S(1)} %get-tuple-element.21), channel_id=1, source_target_pairs={{8,0},{16,8},{24,16},{9,1},{17,9},{25,17},{10,2},{18,10},{26,18},{... | collective-permute-start | bytes 2654216 | tf_op jit(solution)/shard_map/ppermute | solution.py:636
  76.8 0.6 collective-permute-start.11
  77.5 8.1 %moments.4.a_2_ = f32[16,128]{1,0:T(8,128)S(1)} custom-call(s32[12]{0:T(128)S(1)} %copy-done.20, s32[2,1]{1,0:T(2,128)S(1)} %copy.22.a_1_.a_0_, f32[8,16,27648]{2,1,0:T(8,128)S(1)} %get-tuple-element.18.a_2_.a_6_, f32[8,2304]{1,0:T(8,128)S(1)} %copy-done.6), custom_call_target="tpu_custom_call" | custom-call | tf_op jit(solution)/shard_map/moments/pallas_call | solution.py:564
  85.6 3.7 %collective-permute-start.8 = (f32[16,128]{1,0:T(8,128)S(1)}, f32[16,128]{1,0:T(8,128)S(1)}, u32[]{:S(2)}, u32[]{:S(2)}) collective-permute-start(f32[16,128]{1,0:T(8,128)S(1)} %moments.4.a_2_), channel_id=1, source_target_pairs={{0,3},{1,2},{2,1},{3,0},{4,7},{5,6},{6,5},{7,4},{8,11},{9,10},{10,... | collective-permute-start | bytes 24584 | tf_op jit(solution)/shard_map/ppermute | solution.py:630
  89.9 1.3 collective-permute-done.8.a_5_
  91.2 0.8 collective-permute-start.6
  92.0 8.8 %inner_increments.3.a_7_ = bf16[8,16,27648]{2,1,0:T(8,128)(2,1)S(1)} custom-call(s32[12]{0:T(128)S(1)} %copy-done.20, s32[2,1]{1,0:T(2,128)S(1)} %copy.22.a_1_.a_0_, f32[8,16,27648]{2,1,0:T(8,128)S(1)} %get-tuple-element.18.a_2_.a_6_, f32[8,2304]{1,0:T(8,128)S(1)} %copy-done.6, f32[128,128]{1,0:T(8,128)S(1)} %copy-done.15, ...), custom_call_target="tpu_custom_call" | custom-call | tf_op jit(solution)/shard_map/inner_increments/pallas_call | solution.py:564
  100.9 13.9 %last_update.1.a_2_ = f32[8,16,27648]{2,1,0:T(8,128)} custom-call(s32[12]{0:T(128)S(1)} %copy-done.20, s32[2,1]{1,0:T(2,128)S(1)} %copy.22.a_1_.a_0_, f32[16,128]{1,0:T(8,128)S(1)} %moments.4.a_2_, f32[16,128]{1,0:T(8,128)S(1)} %collective-permute-done.6.a_3_, f32[16,128]{1,0:T(8,128)S(1)} %collective-permute-done.7.a_4_, ...), custom_call_target="tpu_custom_call" | custom-call | tf_op jit(solution)/shard_map/last_update/pallas_call | solution.py:564
  114.8 5.0 %copy-done.1 = f32[8,16,27648]{2,1,0:T(8,128)S(1)} copy-done((f32[8,16,27648]{2,1,0:T(8,128)S(1)}, f32[8,16,27648]{2,1,0:T(8,128)}, u32[]{:S(2)}) %copy-start.1) | copy-done | bytes 14155800
  119.8 8.1 %moments.5.a_1_ = f32[16,128]{1,0:T(8,128)S(1)} custom-call(s32[12]{0:T(128)S(1)} %copy-done.20, s32[2,1]{1,0:T(2,128)S(1)} %copy.22.a_1_.a_0_, f32[8,16,27648]{2,1,0:T(8,128)S(1)} %copy-done.1, f32[8,2304]{1,0:T(8,128)S(1)} %copy-done.6), custom_call_target="tpu_custom_call" | custom-call | tf_op jit(solution)/shard_map/moments/pallas_call | solution.py:564
  127.9 3.0 %collective-permute-start.14 = (f32[16,128]{1,0:T(8,128)S(1)}, f32[16,128]{1,0:T(8,128)S(1)}, u32[]{:S(2)}, u32[]{:S(2)}) collective-permute-start(f32[16,128]{1,0:T(8,128)S(1)} %moments.5.a_1_), channel_id=1, source_target_pairs={{0,3},{1,2},{2,1},{3,0},{4,7},{5,6},{6,5},{7,4},{8,11},{9,10},{10,... | collective-permute-start | bytes 24584 | tf_op jit(solution)/shard_map/ppermute | solution.py:630
  131.3 1.0 collective-permute-start.12
  132.4 1.1 collective-permute-done.14.a_4_
  133.4 2.0 %collective-permute-done.13.a_3_ = f32[16,128]{1,0:T(8,128)S(1)} collective-permute-done((f32[16,128]{1,0:T(8,128)S(1)}, f32[16,128]{1,0:T(8,128)S(1)}, u32[]{:S(2)}, u32[]{:S(2)}) %collective-permute-start.13) | collective-permute-done | bytes 8224 | tf_op jit(solution)/shard_map/ppermute | solution.py:630
  136.7 2.5 %macroscopic.1 = (f32[8,8,16]{2,1,0:T(8,128)}, f32[1,8]{1,0:T(1,128)}) custom-call(s32[2,1]{1,0:T(2,128)} %copy-done.18, f32[16,128]{1,0:T(8,128)} %copy-done.21, f32[16,128]{1,0:T(8,128)} %copy-done.24, f32[16,128]{1,0:T(8,128)} %copy-done.23, f32[16,128]{1,0:T(8,128)} %copy-done.22, f32[2,128,128]{2,1,0:T(8,128)} %constant.22.clone.a_13_.a_5_), custom_call_target="tpu_custom_call" | custom-call | tf_op jit(solution)/shard_map/macroscopic/pallas_call | solution.py:647
  (67 shorter events, 2.4 us)
Async XLA Ops:
  9.6 105.2 %copy-start.18 = (s32[2,1]{1,0:T(2,128)}, s32[2,1]{1,0:T(2,128)S(1)}, u32[]{:S(2)}) copy-start(s32[2,1]{1,0:T(2,128)S(1)} %copy.22.a_1_.a_0_) | copy-start | bytes 28
  9.6 24.3 %slice-start = ((s8[14155776]{0:T(1024)(128)(4,1)}), s8[4194304]{0:T(1024)(128)(4,1)S(1)}, s32[]{:S(2)}) async-start(s8[14155776]{0:T(1024)(128)(4,1)} %bitcast), calls=%async_computation | async-start | bytes 8388608
  9.6 24.3 %slice-start.1 = ((s8[14155776]{0:T(1024)(128)(4,1)}), s8[4194304]{0:T(1024)(128)(4,1)S(1)}, s32[]{:S(2)}) async-start(s8[14155776]{0:T(1024)(128)(4,1)} %bitcast), calls=%async_computation.1 | async-start | bytes 8388608
  9.6 24.3 %slice-start.2 = ((s8[14155776]{0:T(1024)(128)(4,1)}), s8[4194304]{0:T(1024)(128)(4,1)S(1)}, s32[]{:S(2)}) async-start(s8[14155776]{0:T(1024)(128)(4,1)} %bitcast), calls=%async_computation.2 | async-start | bytes 8388608
  12.8 29.8 %collective-permute-start.3 = (f32[12,16,1152]{2,1,0:T(8,128)S(1)}, f32[12,16,1152]{2,1,0:T(8,128)S(1)}, u32[]{:S(2)}, u32[]{:S(2)}) collective-permute-start(f32[12,16,1152]{2,1,0:T(8,128)S(1)} %get-tuple-element.14), channel_id=1, source_target_pairs={{0,8},{8,16},{16,24},{1,9},{9,17},{17,25},{2,10},{10,18},{18,26},{... | collective-permute-start | bytes 2654216 | tf_op jit(solution)/shard_map/ppermute | solution.py:635
  14.8 27.7 %collective-permute-start.4 = (f32[12,16,1152]{2,1,0:T(8,128)S(1)}, f32[12,16,1152]{2,1,0:T(8,128)S(1)}, u32[]{:S(2)}, u32[]{:S(2)}) collective-permute-start(f32[12,16,1152]{2,1,0:T(8,128)S(1)} %get-tuple-element.16), channel_id=1, source_target_pairs={{8,0},{16,8},{24,16},{9,1},{17,9},{25,17},{10,2},{18,10},{26,18},{... | collective-permute-start | bytes 2654216 | tf_op jit(solution)/shard_map/ppermute | solution.py:636
  18.5 15.4 %slice-start.3 = ((s8[14155776]{0:T(1024)(128)(4,1)}), s8[1572864]{0:T(1024)(128)(4,1)S(1)}, s32[]{:S(2)}) async-start(s8[14155776]{0:T(1024)(128)(4,1)} %bitcast), calls=%async_computation.3 | async-start | bytes 3145728
  18.5 15.4 %copy-start.4 = (bf16[9,512,256]{2,1,0:T(8,128)(2,1)S(1)}, bf16[9,512,256]{2,1,0:T(8,128)(2,1)}, u32[]{:S(2)}) copy-start(bf16[9,512,256]{2,1,0:T(8,128)(2,1)} %constant.29.clone.a_7_) | copy-start | bytes 7077892
  18.5 15.4 %copy-start.10 = (f32[3,128,128]{2,1,0:T(8,128)S(1)}, f32[3,128,128]{2,1,0:T(8,128)}, u32[]{:S(2)}) copy-start(f32[3,128,128]{2,1,0:T(8,128)} %constant.24.clone.a_6_) | copy-start | bytes 589828
  18.5 15.4 %copy-start.13 = (bf16[3,128,128]{2,1,0:T(8,128)(2,1)S(1)}, bf16[3,128,128]{2,1,0:T(8,128)(2,1)}, u32[]{:S(2)}) copy-start(bf16[3,128,128]{2,1,0:T(8,128)(2,1)} %constant.23.clone.a_5_) | copy-start | bytes 294916
  18.5 15.4 %copy-start.15 = (f32[128,128]{1,0:T(8,128)S(1)}, f32[128,128]{1,0:T(8,128)}, u32[]{:S(2)}) copy-start(f32[128,128]{1,0:T(8,128)} %constant.21.clone.a_4_) | copy-start | bytes 196612
  18.5 15.4 %copy-start.20 = (s32[12]{0:T(128)S(1)}, s32[12]{0:T(128)}, u32[]{:S(2)}) copy-start(s32[12]{0:T(128)} %a_0_.16) | copy-start | bytes 148
  18.6 24.0 %collective-permute-start.5 = (f32[12,8,2304]{2,1,0:T(8,128)S(1)}, f32[12,8,2304]{2,1,0:T(8,128)S(1)}, u32[]{:S(2)}, u32[]{:S(2)}) collective-permute-start(f32[12,8,2304]{2,1,0:T(8,128)S(1)} %get-tuple-element.17), channel_id=1, source_target_pairs={{0,4},{4,0},{1,5},{5,1},{2,6},{6,2},{3,7},{7,3},{8,12},{12,8},{9,1... | collective-permute-start | bytes 2654216 | tf_op jit(solution)/shard_map/ppermute | solution.py:634
  28.2 15.2 %copy-start.3 = (bf16[1152,1152]{1,0:T(8,128)(2,1)S(1)}, bf16[1152,1152]{1,0:T(8,128)(2,1)}, u32[]{:S(2)}) copy-start(bf16[1152,1152]{1,0:T(8,128)(2,1)} %constant.28.clone.a_4_.a_17_) | copy-start | bytes 7962628
  28.3 15.2 %copy-start.7 = (f32[2,128,128]{2,1,0:T(8,128)S(1)}, f32[2,128,128]{2,1,0:T(8,128)}, u32[]{:S(2)}) copy-start(f32[2,128,128]{2,1,0:T(8,128)} %constant.22.clone.a_13_.a_5_) | copy-start | bytes 393220
  28.3 15.2 %copy-start.11 = (f32[2,128,128]{2,1,0:T(8,128)S(1)}, f32[2,128,128]{2,1,0:T(8,128)}, u32[]{:S(2)}) copy-start(f32[2,128,128]{2,1,0:T(8,128)} %constant.26.clone.a_15_) | copy-start | bytes 393220
  28.3 15.2 %copy-start.12 = (f32[2,128,128]{2,1,0:T(8,128)S(1)}, f32[2,128,128]{2,1,0:T(8,128)}, u32[]{:S(2)}) copy-start(f32[2,128,128]{2,1,0:T(8,128)} %constant.25.clone.a_14_) | copy-start | bytes 393220
  28.3 15.2 %copy-start.17 = (bf16[2,2,32,128]{3,2,1,0:T(8,128)(2,1)S(1)}, bf16[2,2,32,128]{3,2,1,0:T(8,128)(2,1)}, u32[]{:S(2)}) copy-start(bf16[2,2,32,128]{3,2,1,0:T(8,128)(2,1)} %constant.27.clone.a_3_.a_16_) | copy-start | bytes 98308
  28.3 5.5 %collective-permute-start.2 = (f32[16,128]{1,0:T(8,128)S(1)}, f32[16,128]{1,0:T(8,128)S(1)}, u32[]{:S(2)}, u32[]{:S(2)}) collective-permute-start(f32[16,128]{1,0:T(8,128)S(1)} %moments.3.a_2_), channel_id=1, source_target_pairs={{0,3},{1,2},{2,1},{3,0},{4,7},{5,6},{6,5},{7,4},{8,11},{9,10},{10,... | collective-permute-start | bytes 24584 | tf_op jit(solution)/shard_map/ppermute | solution.py:630
  32.0 10.5 %collective-permute-start.1 = (f32[16,128]{1,0:T(8,128)S(1)}, f32[16,128]{1,0:T(8,128)S(1)}, u32[]{:S(2)}, u32[]{:S(2)}) collective-permute-start(f32[16,128]{1,0:T(8,128)S(1)} %moments.3.a_2_), channel_id=1, source_target_pairs={{0,2},{1,3},{2,0},{3,1},{4,6},{5,7},{6,4},{7,5},{8,10},{9,11},{10,... | collective-permute-start | bytes 24584 | tf_op jit(solution)/shard_map/ppermute | solution.py:630
  33.8 8.7 %collective-permute-start = (f32[16,128]{1,0:T(8,128)S(1)}, f32[16,128]{1,0:T(8,128)S(1)}, u32[]{:S(2)}, u32[]{:S(2)}) collective-permute-start(f32[16,128]{1,0:T(8,128)S(1)} %moments.3.a_2_), channel_id=1, source_target_pairs={{0,1},{1,0},{2,3},{3,2},{4,5},{5,4},{6,7},{7,6},{8,9},{9,8},{10,11... | collective-permute-start | bytes 24584 | tf_op jit(solution)/shard_map/ppermute | solution.py:630
  71.1 29.8 %collective-permute-start.9 = (f32[12,16,1152]{2,1,0:T(8,128)S(1)}, f32[12,16,1152]{2,1,0:T(8,128)S(1)}, u32[]{:S(2)}, u32[]{:S(2)}) collective-permute-start(f32[12,16,1152]{2,1,0:T(8,128)S(1)} %get-tuple-element.19), channel_id=1, source_target_pairs={{0,8},{8,16},{16,24},{1,9},{9,17},{17,25},{2,10},{10,18},{18,26},{... | collective-permute-start | bytes 2654216 | tf_op jit(solution)/shard_map/ppermute | solution.py:635
  73.0 27.9 %collective-permute-start.10 = (f32[12,16,1152]{2,1,0:T(8,128)S(1)}, f32[12,16,1152]{2,1,0:T(8,128)S(1)}, u32[]{:S(2)}, u32[]{:S(2)}) collective-permute-start(f32[12,16,1152]{2,1,0:T(8,128)S(1)} %get-tuple-element.21), channel_id=1, source_target_pairs={{8,0},{16,8},{24,16},{9,1},{17,9},{25,17},{10,2},{18,10},{26,18},{... | collective-permute-start | bytes 2654216 | tf_op jit(solution)/shard_map/ppermute | solution.py:636
  76.8 24.1 %collective-permute-start.11 = (f32[12,8,2304]{2,1,0:T(8,128)S(1)}, f32[12,8,2304]{2,1,0:T(8,128)S(1)}, u32[]{:S(2)}, u32[]{:S(2)}) collective-permute-start(f32[12,8,2304]{2,1,0:T(8,128)S(1)} %get-tuple-element.22), channel_id=1, source_target_pairs={{0,4},{4,0},{1,5},{5,1},{2,6},{6,2},{3,7},{7,3},{8,12},{12,8},{9,1... | collective-permute-start | bytes 2654216 | tf_op jit(solution)/shard_map/ppermute | solution.py:634
  77.5 14.5 %copy-start.5 = (bf16[9,512,256]{2,1,0:T(8,128)(2,1)S(1)}, bf16[9,512,256]{2,1,0:T(8,128)(2,1)}, u32[]{:S(2)}) copy-start(bf16[9,512,256]{2,1,0:T(8,128)(2,1)} %constant.29.clone.a_7_) | copy-start | bytes 7077892
  77.5 14.5 %copy-start.14 = (bf16[3,128,128]{2,1,0:T(8,128)(2,1)S(1)}, bf16[3,128,128]{2,1,0:T(8,128)(2,1)}, u32[]{:S(2)}) copy-start(bf16[3,128,128]{2,1,0:T(8,128)(2,1)} %constant.23.clone.a_5_) | copy-start | bytes 294916
  85.6 5.6 %collective-permute-start.8 = (f32[16,128]{1,0:T(8,128)S(1)}, f32[16,128]{1,0:T(8,128)S(1)}, u32[]{:S(2)}, u32[]{:S(2)}) collective-permute-start(f32[16,128]{1,0:T(8,128)S(1)} %moments.4.a_2_), channel_id=1, source_target_pairs={{0,3},{1,2},{2,1},{3,0},{4,7},{5,6},{6,5},{7,4},{8,11},{9,10},{10,... | collective-permute-start | bytes 24584 | tf_op jit(solution)/shard_map/ppermute | solution.py:630
  89.2 11.6 %collective-permute-start.7 = (f32[16,128]{1,0:T(8,128)S(1)}, f32[16,128]{1,0:T(8,128)S(1)}, u32[]{:S(2)}, u32[]{:S(2)}) collective-permute-start(f32[16,128]{1,0:T(8,128)S(1)} %moments.4.a_2_), channel_id=1, source_target_pairs={{0,2},{1,3},{2,0},{3,1},{4,6},{5,7},{6,4},{7,5},{8,10},{9,11},{10,... | collective-permute-start | bytes 24584 | tf_op jit(solution)/shard_map/ppermute | solution.py:630
  91.2 9.7 %collective-permute-start.6 = (f32[16,128]{1,0:T(8,128)S(1)}, f32[16,128]{1,0:T(8,128)S(1)}, u32[]{:S(2)}, u32[]{:S(2)}) collective-permute-start(f32[16,128]{1,0:T(8,128)S(1)} %moments.4.a_2_), channel_id=1, source_target_pairs={{0,1},{1,0},{2,3},{3,2},{4,5},{5,4},{6,7},{7,6},{8,9},{9,8},{10,11... | collective-permute-start | bytes 24584 | tf_op jit(solution)/shard_map/ppermute | solution.py:630
  127.9 5.5 %collective-permute-start.14 = (f32[16,128]{1,0:T(8,128)S(1)}, f32[16,128]{1,0:T(8,128)S(1)}, u32[]{:S(2)}, u32[]{:S(2)}) collective-permute-start(f32[16,128]{1,0:T(8,128)S(1)} %moments.5.a_1_), channel_id=1, source_target_pairs={{0,3},{1,2},{2,1},{3,0},{4,7},{5,6},{6,5},{7,4},{8,11},{9,10},{10,... | collective-permute-start | bytes 24584 | tf_op jit(solution)/shard_map/ppermute | solution.py:630
  130.9 4.5 %collective-permute-start.13 = (f32[16,128]{1,0:T(8,128)S(1)}, f32[16,128]{1,0:T(8,128)S(1)}, u32[]{:S(2)}, u32[]{:S(2)}) collective-permute-start(f32[16,128]{1,0:T(8,128)S(1)} %moments.5.a_1_), channel_id=1, source_target_pairs={{0,2},{1,3},{2,0},{3,1},{4,6},{5,7},{6,4},{7,5},{8,10},{9,11},{10,... | collective-permute-start | bytes 24584 | tf_op jit(solution)/shard_map/ppermute | solution.py:630
  131.3 4.1 %collective-permute-start.12 = (f32[16,128]{1,0:T(8,128)S(1)}, f32[16,128]{1,0:T(8,128)S(1)}, u32[]{:S(2)}, u32[]{:S(2)}) collective-permute-start(f32[16,128]{1,0:T(8,128)S(1)} %moments.5.a_1_), channel_id=1, source_target_pairs={{0,1},{1,0},{2,3},{3,2},{4,5},{5,4},{6,7},{7,6},{8,9},{9,8},{10,11... | collective-permute-start | bytes 24584 | tf_op jit(solution)/shard_map/ppermute | solution.py:630
  (12 other events, 36.6 us)

commit v7 on v6

--- a/solution.py
+++ b/solution.py
@@ -24,6 +24,8 @@
 
 PLANE = NVR * NVT
 HALF = PLANE // 2
+THIRD = HALF // 3
+BOTTOM, TOP = 0, 1
 LOCAL_Z = 2 * NODES
 NODE_COUNT = NODES * LOCAL_Z
 TILE = 256
@@ -166,8 +168,8 @@
 
 
 def mirror_table():
-    table = np.zeros((HALF, HALF))
-    groups = NVR // 2
+    table = np.zeros((THIRD, THIRD))
+    groups = THIRD // NVT
     for g in range(groups):
         for b in range(NVT):
             table[(groups - 1 - g) * NVT + b, g * NVT + b] = 1.0
@@ -292,12 +294,11 @@
 def turn_traces(count, row, mirror_ref, left_ref, turned_ref):
     @pl.when(row == 0)
     def _():
-        flat = left_ref[...].reshape(count * LOCAL_Z, HALF).astype(BF16)
-        for first in range(0, HALF, 128):
-            low = max(0, (HALF - first - 128 - 48) // 128 * 128)
-            high = min(HALF, -((first - HALF - 48) // 128) * 128)
-            got = dot(flat[:, low:high], mirror_ref[low:high, first : first + 128])
-            turned_ref[:, :, first : first + 128] = got.reshape(count, LOCAL_Z, 128)
+        for part in range(3):
+            start = (2 - part) * THIRD
+            flat = left_ref[:, :, start : start + THIRD].reshape(count * LOCAL_Z, THIRD).astype(BF16)
+            got = dot(flat, mirror_ref[...])
+            turned_ref[:, :, part * THIRD : (part + 1) * THIRD] = got.reshape(count, LOCAL_Z, THIRD)
 
     @pl.when(row != 0)
     def _():
@@ -358,7 +359,7 @@
             lhs_ref[s, 0, :, 0:NODE_COUNT] = minus
             lhs_ref[s, 1, :, 0:NODE_COUNT] = radial_ref[1]
 
-    kind_out = jnp.where(jnp.logical_and(place == 1, codes[1, 0] == 2), 2, 0)
+    kind_out = jnp.where(jnp.logical_and(place == 1, codes[0, TOP] == 2), 2, 0)
     inverse = inverse_ref[...]
     for s in range(count):
         vz = slot_speed(order, step * count + s)
@@ -409,8 +410,8 @@
     to_top = 0.5 * (gross + net)
     incident = jnp.sum(edge_ref[0] * to_bottom, axis=0, keepdims=True)
     upward = jnp.sum(edge_ref[1] * to_top, axis=0, keepdims=True)
-    bottom = jnp.where(codes[0, 0] == 1, SAT_DENSITY, incident * (1.0 / HALF_FLUX))
-    top = jnp.where(codes[1, 0] == 2, 0.0, upward * (1.0 / HALF_FLUX))
+    bottom = jnp.where(codes[0, BOTTOM] == 1, SAT_DENSITY, incident * (1.0 / HALF_FLUX))
+    top = jnp.where(codes[0, TOP] == 2, 0.0, upward * (1.0 / HALF_FLUX))
     density = jnp.where(place == 0, bottom, top)
     wall_ref[...] = jnp.transpose(jnp.broadcast_to(density, (128, 128)))[0:NODES, :]
 
@@ -461,16 +462,11 @@
         ghost_ref[:, at] = rows.astype(BF16)
 
 
-def outer_kernel(part_count, last, order, codes, *refs):
+def outer_kernel(count, part_count, order, codes, *refs):
     part_refs, refs = refs[:part_count], refs[part_count:]
     f_ref, inner_ref, in_left_ref, in_turned_ref, in_right_ref, in_axial_ref = refs[:6]
-    rows_ref, edge_ref, ghost_r_ref, ghost_z_ref = refs[6:10]
-    refs = refs[10:]
-    if last:
-        out_ref, refs = refs[0], refs[1:]
-    else:
-        (trace_ref, mirror_ref, out_ref, right_ref, left_ref, turned_ref, axial_ref), refs = refs[:7], refs[7:]
-    plane_ref, node_ref, wall_ref, slot_ref, lhs_ref, ghost_ref, table_ref = refs
+    rows_ref, edge_ref, ghost_r_ref, ghost_z_ref, out_ref = refs[6:11]
+    plane_ref, node_ref, wall_ref, slot_ref, work_ref, lhs_ref, ghost_ref, table_ref = refs[11:]
     step = pl.program_id(0)
     row, place = places_of()
 
@@ -479,28 +475,34 @@
         total = total_of([p[...] for p in part_refs])
         prepare_nodes(total, codes, place, rows_ref, edge_ref, table_ref, node_ref, wall_ref, plane_ref)
 
-    vz = slot_speed(order, step)
-    for k, value in enumerate(slot_factors(vz, node_ref)):
-        slot_ref[k] = value
-    ghost_lifts(vz, ghost_r_ref, ghost_z_ref, lhs_ref)
-    ghost_rows(0, vz, place, in_left_ref, in_turned_ref, in_right_ref, in_axial_ref, rows_ref, wall_ref, ghost_ref)
-    for first, lanes, side in PIECES:
-        lifted = dot(lhs_ref[side, :, 0:GHOST_ROWS], ghost_ref[:, first : first + lanes])
-        pieces = []
-        for inside in range(0, lanes, 128):
-            here = first + inside
-            at = pl.ds(here, 128)
-            new = nodes_of(f_ref, here, 128) * node_ref[5] + nodes_of(inner_ref, here, 128).astype(F32)
-            new = new + lifted[:, inside : inside + 128]
-            bend = (plane_ref[1, :, at] + slot_ref[1]) * (plane_ref[2, :, at] + slot_ref[2]) + 1.0
-            new = new + (plane_ref[0, :, at] * slot_ref[0]) * bend
-            out_ref[:, :, here : here + 128] = new.reshape(NODES, LOCAL_Z, 128)
-            pieces.append(new.astype(BF16))
-        if not last:
-            narrow = jnp.concatenate(pieces, axis=1) if len(pieces) > 1 else pieces[0]
-            send_piece(0, first, lanes, side, place, narrow, trace_ref, right_ref, left_ref, axial_ref)
-    if not last:
-        turn_traces(1, row, mirror_ref, left_ref, turned_ref)
+    for s in range(count):
+        vz = slot_speed(order, step * count + s)
+        for k, value in enumerate(slot_factors(vz, node_ref)):
+            slot_ref[s, k] = value
+        ghost_lifts(vz, ghost_r_ref, ghost_z_ref, lhs_ref)
+        ghost_rows(
+            s, vz, place, in_left_ref, in_turned_ref, in_right_ref, in_axial_ref, rows_ref, wall_ref, ghost_ref
+        )
+        for first, lanes, side in PIECES:
+            work_ref[s, :, first : first + lanes] = dot(
+                lhs_ref[side, :, 0:GHOST_ROWS], ghost_ref[:, first : first + lanes]
+            )
+
+    def update(r, carry):
+        rows = pl.ds(pl.multiple_of(r * LOCAL_Z, LOCAL_Z), LOCAL_Z)
+        keep = node_ref[5, rows, :]
+        factor = [[slot_ref[s, k, rows, :] for k in range(3)] for s in range(count)]
+        for j in range(PLANE // 128):
+            at = pl.ds(j * 128, 128)
+            gauss, along, reach = (plane_ref[k, rows, at] for k in range(3))
+            for s in range(count):
+                here = pl.ds(s * PLANE + j * 128, 128)
+                new = f_ref[r, :, here] * keep + work_ref[s, rows, at] + inner_ref[r, :, here].astype(F32)
+                bend = (along + factor[s][1]) * (reach + factor[s][2]) + 1.0
+                out_ref[r, :, here] = new + (gauss * factor[s][0]) * bend
+        return carry
+
+    lax.fori_loop(0, NODES, update, 0)
 
 
 def last_kernel(part_count, codes, *refs):
@@ -518,8 +520,8 @@
     incident = exact(to_bottom, edge_ref[0])
     upward = exact(to_top, edge_ref[1])
     downward = exact(to_bottom, edge_ref[1])
-    bottom = jnp.where(codes[0, 0] == 1, SAT_DENSITY * HALF_FLUX - incident, 0.0)
-    top = jnp.where(codes[1, 0] == 2, upward - downward, 0.0)
+    bottom = jnp.where(codes[0, BOTTOM] == 1, SAT_DENSITY * HALF_FLUX - incident, 0.0)
+    top = jnp.where(codes[0, TOP] == 2, upward - downward, 0.0)
     flux_ref[...] = jnp.where(place == 0, bottom, top)[0:1, 0:NODES]
 
 
@@ -535,6 +537,7 @@
     rows_total = lax.axis_size("row")
     verts = lax.axis_size("vert")
     assert lax.axis_size("gz") == 2
+    codes = edge_codes.T
     rows, pos, edge = jnp.asarray(ROWS), jnp.asarray(NODE_POS), jnp.asarray(EDGE)
     radial_m, axial_m = jnp.asarray(RADIAL_M), jnp.asarray(AXIAL_M)
     ghost_r, ghost_z = jnp.asarray(GHOST_R), jnp.asarray(GHOST_Z)
@@ -573,24 +576,24 @@
             out_shape=out_shape,
             compiler_params=pltpu.CompilerParams(vmem_limit_bytes=limit * 1024 * 1024),
             name=name,
-        )(z_order, edge_codes, *args)
+        )(z_order, codes, *args)
 
     def all_whole(tables):
         return [whole(x.shape) for x in tables]
 
-    def traces_of(f):
+    def traces_of(f, limit):
         return call(
-            lambda *a: trace_kernel(group, *a), "traces", group, 20, [slab(group)] + all_whole([trace_m, mirror_m]),
+            lambda *a: trace_kernel(group, *a), "traces", group, limit, [slab(group)] + all_whole([trace_m, mirror_m]),
             trace_specs(group), trace_shapes, [], [f, trace_m, mirror_m],
         )
 
-    def moments_of(f):
+    def moments_of(f, limit):
         return call(
-            lambda *a: moment_kernel(group, *a), "moments", group, 20, [slab(group)] + all_whole([rows]),
+            lambda *a: moment_kernel(group, *a), "moments", group, limit, [slab(group)] + all_whole([rows]),
             mom_spec, mom_shape, [pltpu.VMEM((5, NODES, LOCAL_Z, PLANE), F32), square], [f, rows],
         )
 
-    def inner(f):
+    def inner(f, limit):
         tables = [rows, pos, radial_m, axial_m, rot_m]
         scratch = [
             square,
@@ -598,31 +601,28 @@
             pltpu.VMEM((group, 2, NODE_COUNT, 2 * NODE_COUNT), BF16),
         ]
         return call(
-            lambda *a: inner_kernel(group, *a), "inner_increments", group, 22, [slab(group)] + all_whole(tables),
+            lambda *a: inner_kernel(group, *a), "inner_increments", group, limit, [slab(group)] + all_whole(tables),
             slab(group), jax.ShapeDtypeStruct(f.shape, BF16), scratch, [f] + tables,
         )
 
-    def outer(f, change, ghosts, parts, last):
-        tables = [rows, edge, ghost_r, ghost_z] + ([] if last else [trace_m, mirror_m])
+    def outer(f, change, ghosts, parts, limit):
+        count = math.gcd(slots, 2)
+        tables = [rows, edge, ghost_r, ghost_z]
         scratch = [
             pltpu.VMEM((3, NODE_COUNT, PLANE), F32),
             pltpu.VMEM((10, NODE_COUNT, 128), F32),
             pltpu.VMEM((NODES, 128), F32),
-            pltpu.VMEM((3, NODE_COUNT, 128), F32),
+            pltpu.VMEM((count, 3, NODE_COUNT, 128), F32),
+            pltpu.VMEM((count, NODE_COUNT, PLANE), F32),
             pltpu.VMEM((2, NODE_COUNT, 128), BF16),
             pltpu.VMEM((GHOST_ROWS, PLANE), BF16),
             square,
         ]
-        out = call(
-            lambda *a: outer_kernel(len(parts), last, *a),
-            "last_update" if last else "update", 1, 20,
-            [mom_spec] * len(parts) + [slab(1), slab(1)] + trace_specs(1) + all_whole(tables),
-            [slab(1)] + ([] if last else trace_specs(1)),
-            [big_shape] + ([] if last else trace_shapes),
-            scratch,
-            [*parts, f, change, *ghosts, *tables],
+        return call(
+            lambda *a: outer_kernel(count, len(parts), *a), "update", count, limit,
+            [mom_spec] * len(parts) + [slab(count), slab(count)] + trace_specs(count) + all_whole(tables),
+            slab(count), big_shape, scratch, [*parts, f, change, *ghosts, *tables],
         )
-        return out[0], out[1:]
 
     def spread(moments):
         parts = [moments]
@@ -637,13 +637,13 @@
         return from_left, turned, from_right, from_axial
 
     current = distribution
-    traces = traces_of(current)
     for number in range(STEPS):
-        ghosts = halo(*traces)
-        parts = spread(moments_of(current))
-        change = inner(current)
-        current, traces = outer(current, change, ghosts, parts, number == STEPS - 1)
-    parts = spread(moments_of(current))
+        first, last = number == 0, number == STEPS - 1
+        ghosts = halo(*traces_of(current, 56 if first else 12))
+        parts = spread(moments_of(current, 56 if first else 18))
+        change = inner(current, 44 if first else 20)
+        current = outer(current, change, ghosts, parts, 32 if last else 20)
+    parts = spread(moments_of(current, 56))
     macro, flux = pl.pallas_call(
         lambda *a: last_kernel(len(parts), *a),
         grid_spec=pltpu.PrefetchScalarGridSpec(
@@ -657,7 +657,7 @@
             jax.ShapeDtypeStruct((1, NODES), F32),
         ],
         name="macroscopic",
-    )(edge_codes, *parts, edge)
+    )(codes, *parts, edge)
     return (current, macro, flux)
 
 

time: 140 us -> 134 us (0.957)
  local copies, waits for them, and re-layouts: 17.3 us -> 4.06 us
  Pallas kernels: 87.7 us -> 95.1 us
    unnamed x59 -> x40, local copies, waits for them, and re-layouts: 17.3 us -> 4.06 us
    pallas_call x8 -> x9, Pallas kernels: 85.3 us -> 92.6 us  [call(): pl.pallas_call(body, grid_spec=pltpu.PrefetchScalarGridSpec(num_scalar_pr...]
  transfers between devices with their start and end apart: 15 -> 15, of which waited for: 4 -> 4; matrix products, arithmetic and copies ran while one was open for 0% -> 0% of each run, Pallas kernels for 24% -> 28%
where the time goes in v7:
time: 134 us; the launch traced here: 133 us
  Pallas kernels  95.1 us (71%)
  starting transfers between devices  26.6 us (20%)
  waiting for transfers between devices  6.6 us (5%)
  local copies, waits for them, and re-layouts  4.06 us (3%)
    pallas_call x9, Pallas kernels, call(): pl.pallas_call(body, grid_spec=pltpu.PrefetchScalarGridSpec(num_scalar_pr...  92.6 us
    ppermute x9, starting transfers between devices, spread(): lax.ppermute(moments, 'vert', [(i, i ^ shift) for i in range(verts)])  13.2 us
    ppermute x2, starting transfers between devices, halo(): lax.ppermute(left, 'row', [(i + 1, i) for i in range(rows_total - 1)])  7.47 us
    ppermute x9, waiting for transfers between devices, spread(): lax.ppermute(moments, 'vert', [(i, i ^ shift) for i in range(verts)])  6.58 us
    unnamed x40, local copies, waits for them, and re-layouts  4.06 us
    ppermute x2, starting transfers between devices, halo(): lax.ppermute(right, 'row', [(i, i + 1) for i in range(rows_total - 1)])  3.83 us
  transfers between devices with their start and end apart: 15, of which 4 were waited for; matrix products, arithmetic and copies ran while one was open for 0% of the time, Pallas kernels for 28%

profile of v7, /device:TPU:4, one launch (start us, length us, event | category | flops | bytes accessed | tf_op | source)
XLA Modules:
  0.0 133.3 jit_solution(6189901547406035596)
XLA Ops:
  0.6 0.0 copy-start.3
  0.7 8.4 %traces.2 = (f32[12,16,1152]{2,1,0:T(8,128)}, f32[12,16,1152]{2,1,0:T(8,128)}, f32[12,16,1152]{2,1,0:T(8,128)}, f32[12,8,2304]{2,1,0:T(8,128)}) custom-call(s32[12]{0:T(128)} %a_0_.17, s32[1,2]{1,0:T(1,128)} %bitcast.1, f32[8,16,27648]{2,1,0:T(8,128)} %a_6_.3, bf16[2,2,32,128]{3,2,1,0:T(8,128)(2,1)} %constant.27.clone.a_3_, bf16[384,384]{1,0:T(8,128)(2,1)} %constant.28.clone.a_4_), custom_call_target="tpu_custom_call" | custom-call | tf_op jit(solution)/shard_map/traces/pallas_call | solution.py:567
  9.1 1.9 %collective-permute-start.3 = (f32[12,16,1152]{2,1,0:T(8,128)}, f32[12,16,1152]{2,1,0:T(8,128)}, u32[]{:S(2)}, u32[]{:S(2)}) collective-permute-start(f32[12,16,1152]{2,1,0:T(8,128)} %get-tuple-element.13), channel_id=1, source_target_pairs={{0,8},{8,16},{16,24},{1,9},{9,17},{17,25},{2,10},{10,18},{18,26},{... | collective-permute-start | bytes 2654216 | tf_op jit(solution)/shard_map/ppermute | solution.py:635
  11.0 3.6 %collective-permute-start.4 = (f32[12,16,1152]{2,1,0:T(8,128)}, f32[12,16,1152]{2,1,0:T(8,128)}, u32[]{:S(2)}, u32[]{:S(2)}) collective-permute-start(f32[12,16,1152]{2,1,0:T(8,128)} %get-tuple-element.15), channel_id=1, source_target_pairs={{8,0},{16,8},{24,16},{9,1},{17,9},{25,17},{10,2},{18,10},{26,18},{... | collective-permute-start | bytes 2654216 | tf_op jit(solution)/shard_map/ppermute | solution.py:636
  14.6 1.6 %collective-permute-start.5 = (f32[12,8,2304]{2,1,0:T(8,128)}, f32[12,8,2304]{2,1,0:T(8,128)}, u32[]{:S(2)}, u32[]{:S(2)}) collective-permute-start(f32[12,8,2304]{2,1,0:T(8,128)} %get-tuple-element.16), channel_id=1, source_target_pairs={{0,4},{4,0},{1,5},{5,1},{2,6},{6,2},{3,7},{7,3},{8,12},{12,8},{9,1... | collective-permute-start | bytes 2654216 | tf_op jit(solution)/shard_map/ppermute | solution.py:634
  16.2 11.2 %moments.3.a_2_ = f32[16,128]{1,0:T(8,128)} custom-call(s32[12]{0:T(128)} %a_0_.17, s32[1,2]{1,0:T(1,128)} %bitcast.2, f32[8,16,27648]{2,1,0:T(8,128)} %a_6_.3, f32[8,2304]{1,0:T(8,128)} %constant.20.clone.a_3_.a_12_), custom_call_target="tpu_custom_call" | custom-call | tf_op jit(solution)/shard_map/moments/pallas_call | solution.py:567
  27.4 3.6 %collective-permute-start.2 = (f32[16,128]{1,0:T(8,128)}, f32[16,128]{1,0:T(8,128)S(1)}, u32[]{:S(2)}, u32[]{:S(2)}) collective-permute-start(f32[16,128]{1,0:T(8,128)} %moments.3.a_2_), channel_id=1, source_target_pairs={{0,3},{1,2},{2,1},{3,0},{4,7},{5,6},{6,5},{7,4},{8,11},{9,10},{10,... | collective-permute-start | bytes 24584 | tf_op jit(solution)/shard_map/ppermute | solution.py:630
  31.0 2.1 %collective-permute-done.2.a_5_ = f32[16,128]{1,0:T(8,128)S(1)} collective-permute-done((f32[16,128]{1,0:T(8,128)}, f32[16,128]{1,0:T(8,128)S(1)}, u32[]{:S(2)}, u32[]{:S(2)}) %collective-permute-start.2) | collective-permute-done | bytes 8224 | tf_op jit(solution)/shard_map/ppermute | solution.py:630
  33.2 1.7 %copy-done.1 = bf16[9,512,256]{2,1,0:T(8,128)(2,1)S(1)} copy-done((bf16[9,512,256]{2,1,0:T(8,128)(2,1)S(1)}, bf16[9,512,256]{2,1,0:T(8,128)(2,1)}, u32[]{:S(2)}) %copy-start.1) | copy-done | bytes 2359320
  34.8 9.9 %inner_increments.2.a_7_ = bf16[8,16,27648]{2,1,0:T(8,128)(2,1)S(1)} custom-call(s32[12]{0:T(128)S(1)} %copy-done.15, s32[1,2]{1,0:T(1,128)S(1)} %bitcast.5, f32[8,16,27648]{2,1,0:T(8,128)} %a_6_.3, f32[8,2304]{1,0:T(8,128)S(1)} %copy-done.3, f32[128,128]{1,0:T(8,128)S(1)} %copy-done.11, bf16[3,128,128]{2,1,0:T(8,128)(2,1)S(1)} %copy-done.10, ...), custom_call_target="tpu_custom_call" | custom-call | tf_op jit(solution)/shard_map/inner_increments/pallas_call | solution.py:567
  44.8 1.2 copy-done.6
  46.0 14.8 %update.2.a_2_.a_6_ = f32[8,16,27648]{2,1,0:T(8,128)S(1)} custom-call(s32[12]{0:T(128)S(1)} %copy-done.15, s32[1,2]{1,0:T(1,128)S(1)} %bitcast.6, f32[16,128]{1,0:T(8,128)S(1)} %copy-done.16, f32[16,128]{1,0:T(8,128)S(1)} %collective-permute-done.a_3_, f32[16,128]{1,0:T(8,128)S(1)} %collective-permute-done.1.a_4_, ...), custom_call_target="tpu_custom_call" | custom-call | tf_op jit(solution)/shard_map/update/pallas_call | solution.py:567
  60.9 3.2 %traces.3 = (f32[12,16,1152]{2,1,0:T(8,128)S(1)}, f32[12,16,1152]{2,1,0:T(8,128)S(1)}, f32[12,16,1152]{2,1,0:T(8,128)S(1)}, f32[12,8,2304]{2,1,0:T(8,128)S(1)}) custom-call(s32[12]{0:T(128)S(1)} %copy-done.15, s32[1,2]{1,0:T(1,128)S(1)} %bitcast.7, f32[8,16,27648]{2,1,0:T(8,128)S(1)} %update.2.a_2_.a_6_, bf16[2,2,32,128]{3,2,1,0:T(8,128)(2,1)S(1)} %copy-done.13, ...), custom_call_target="tpu_custom_call" | custom-call | tf_op jit(solution)/shard_map/traces/pallas_call | solution.py:567
  64.1 1.9 %collective-permute-start.9 = (f32[12,16,1152]{2,1,0:T(8,128)S(1)}, f32[12,16,1152]{2,1,0:T(8,128)S(1)}, u32[]{:S(2)}, u32[]{:S(2)}) collective-permute-start(f32[12,16,1152]{2,1,0:T(8,128)S(1)} %get-tuple-element.17), channel_id=1, source_target_pairs={{0,8},{8,16},{16,24},{1,9},{9,17},{17,25},{2,10},{10,18},{18,26},{... | collective-permute-start | bytes 2654216 | tf_op jit(solution)/shard_map/ppermute | solution.py:635
  66.0 3.8 %collective-permute-start.10 = (f32[12,16,1152]{2,1,0:T(8,128)S(1)}, f32[12,16,1152]{2,1,0:T(8,128)S(1)}, u32[]{:S(2)}, u32[]{:S(2)}) collective-permute-start(f32[12,16,1152]{2,1,0:T(8,128)S(1)} %get-tuple-element.19), channel_id=1, source_target_pairs={{8,0},{16,8},{24,16},{9,1},{17,9},{25,17},{10,2},{18,10},{26,18},{... | collective-permute-start | bytes 2654216 | tf_op jit(solution)/shard_map/ppermute | solution.py:636
  69.9 0.6 collective-permute-start.11
  70.5 8.1 %moments.4.a_2_ = f32[16,128]{1,0:T(8,128)S(1)} custom-call(s32[12]{0:T(128)S(1)} %copy-done.15, s32[1,2]{1,0:T(1,128)S(1)} %bitcast.8, f32[8,16,27648]{2,1,0:T(8,128)S(1)} %update.2.a_2_.a_6_, f32[8,2304]{1,0:T(8,128)S(1)} %copy-done.3), custom_call_target="tpu_custom_call" | custom-call | tf_op jit(solution)/shard_map/moments/pallas_call | solution.py:567
  78.6 3.7 %collective-permute-start.8 = (f32[16,128]{1,0:T(8,128)S(1)}, f32[16,128]{1,0:T(8,128)S(1)}, u32[]{:S(2)}, u32[]{:S(2)}) collective-permute-start(f32[16,128]{1,0:T(8,128)S(1)} %moments.4.a_2_), channel_id=1, source_target_pairs={{0,3},{1,2},{2,1},{3,0},{4,7},{5,6},{6,5},{7,4},{8,11},{9,10},{10,... | collective-permute-start | bytes 24584 | tf_op jit(solution)/shard_map/ppermute | solution.py:630
  82.2 0.6 collective-permute-start.7
  82.9 1.2 collective-permute-done.8.a_5_
  84.1 0.9 collective-permute-start.6
  85.0 8.6 %inner_increments.3.a_7_ = bf16[8,16,27648]{2,1,0:T(8,128)(2,1)S(1)} custom-call(s32[12]{0:T(128)S(1)} %copy-done.15, s32[1,2]{1,0:T(1,128)S(1)} %bitcast.9, f32[8,16,27648]{2,1,0:T(8,128)S(1)} %update.2.a_2_.a_6_, f32[8,2304]{1,0:T(8,128)S(1)} %copy-done.3, f32[128,128]{1,0:T(8,128)S(1)} %copy-done.12, bf16[3,128,128]{2,1,0:T(8,128)(2,1)S(1)} %copy-done.10, ...), custom_call_target="tpu_custom_call" | custom-call | tf_op jit(solution)/shard_map/inner_increments/pallas_call | solution.py:567
  93.6 17.3 %update.3.a_2_ = f32[8,16,27648]{2,1,0:T(8,128)} custom-call(s32[12]{0:T(128)S(1)} %copy-done.15, s32[1,2]{1,0:T(1,128)S(1)} %bitcast.10, f32[16,128]{1,0:T(8,128)S(1)} %moments.4.a_2_, f32[16,128]{1,0:T(8,128)S(1)} %collective-permute-done.6.a_3_, f32[16,128]{1,0:T(8,128)S(1)} %collective-permute-done.7.a_4_, f32[16,128]{1,0:T(8,128)S(1)} %collective-permute-done.8.a_5_, ...), custom_call_target="tpu_custom_call" | custom-call | tf_op jit(solution)/shard_map/update/pallas_call | solution.py:567
  110.9 11.1 %moments.5.a_1_ = f32[16,128]{1,0:T(8,128)} custom-call(s32[12]{0:T(128)} %a_0_.17, s32[1,2]{1,0:T(1,128)} %bitcast.3, f32[8,16,27648]{2,1,0:T(8,128)} %update.3.a_2_, f32[8,2304]{1,0:T(8,128)} %constant.20.clone.a_3_.a_12_), custom_call_target="tpu_custom_call" | custom-call | tf_op jit(solution)/shard_map/moments/pallas_call | solution.py:567
  122.0 2.9 %collective-permute-start.14 = (f32[16,128]{1,0:T(8,128)}, f32[16,128]{1,0:T(8,128)S(1)}, u32[]{:S(2)}, u32[]{:S(2)}) collective-permute-start(f32[16,128]{1,0:T(8,128)} %moments.5.a_1_), channel_id=1, source_target_pairs={{0,3},{1,2},{2,1},{3,0},{4,7},{5,6},{6,5},{7,4},{8,11},{9,10},{10,... | collective-permute-start | bytes 24584 | tf_op jit(solution)/shard_map/ppermute | solution.py:630
  125.0 0.4 collective-permute-start.13
  125.3 1.1 collective-permute-start.12
  126.4 1.3 collective-permute-done.14.a_4_
  127.7 2.0 %collective-permute-done.13.a_3_ = f32[16,128]{1,0:T(8,128)S(1)} collective-permute-done((f32[16,128]{1,0:T(8,128)}, f32[16,128]{1,0:T(8,128)S(1)}, u32[]{:S(2)}, u32[]{:S(2)}) %collective-permute-start.13) | collective-permute-done | bytes 8224 | tf_op jit(solution)/shard_map/ppermute | solution.py:630
  129.7 0.6 copy-done.18
  130.3 0.6 copy-done.19
  130.9 2.4 %macroscopic.1 = (f32[8,8,16]{2,1,0:T(8,128)}, f32[1,8]{1,0:T(1,128)}) custom-call(s32[1,2]{1,0:T(1,128)} %bitcast.4, f32[16,128]{1,0:T(8,128)} %moments.5.a_1_, f32[16,128]{1,0:T(8,128)} %copy-done.19, f32[16,128]{1,0:T(8,128)} %copy-done.18, f32[16,128]{1,0:T(8,128)} %copy-done.17, f32[2,128,128]{2,1,0:T(8,128)} %constant.22.clone.a_13_.a_5_), custom_call_target="tpu_custom_call" | custom-call | tf_op jit(solution)/shard_map/macroscopic/pallas_call | solution.py:647
  (48 shorter events, 0.1 us)
Async XLA Ops:
  0.6 32.5 %copy-start.3 = (f32[8,2304]{1,0:T(8,128)S(1)}, f32[8,2304]{1,0:T(8,128)}, u32[]{:S(2)}) copy-start(f32[8,2304]{1,0:T(8,128)} %constant.20.clone.a_3_.a_12_) | copy-start | bytes 221188
  0.6 32.5 %copy-start.7 = (f32[3,128,128]{2,1,0:T(8,128)S(1)}, f32[3,128,128]{2,1,0:T(8,128)}, u32[]{:S(2)}) copy-start(f32[3,128,128]{2,1,0:T(8,128)} %constant.24.clone.a_6_) | copy-start | bytes 589828
  0.7 32.5 %copy-start.10 = (bf16[3,128,128]{2,1,0:T(8,128)(2,1)S(1)}, bf16[3,128,128]{2,1,0:T(8,128)(2,1)}, u32[]{:S(2)}) copy-start(bf16[3,128,128]{2,1,0:T(8,128)(2,1)} %constant.23.clone.a_5_) | copy-start | bytes 294916
  0.7 32.4 %copy-start.11 = (f32[128,128]{1,0:T(8,128)S(1)}, f32[128,128]{1,0:T(8,128)}, u32[]{:S(2)}) copy-start(f32[128,128]{1,0:T(8,128)} %constant.21.clone.a_4_) | copy-start | bytes 196612
  0.7 32.4 %copy-start.14 = (s32[2,1]{0,1:T(1,128)S(1)}, s32[2,1]{0,1:T(1,128)}, u32[]{:S(2)}) copy-start(s32[2,1]{0,1:T(1,128)} %param.15) | copy-start | bytes 28
  0.7 32.4 %copy-start.15 = (s32[12]{0:T(128)S(1)}, s32[12]{0:T(128)}, u32[]{:S(2)}) copy-start(s32[12]{0:T(128)} %a_0_.17) | copy-start | bytes 148
  9.1 35.7 %collective-permute-start.3 = (f32[12,16,1152]{2,1,0:T(8,128)}, f32[12,16,1152]{2,1,0:T(8,128)}, u32[]{:S(2)}, u32[]{:S(2)}) collective-permute-start(f32[12,16,1152]{2,1,0:T(8,128)} %get-tuple-element.13), channel_id=1, source_target_pairs={{0,8},{8,16},{16,24},{1,9},{9,17},{17,25},{2,10},{10,18},{18,26},{... | collective-permute-start | bytes 2654216 | tf_op jit(solution)/shard_map/ppermute | solution.py:635
  11.0 33.8 %collective-permute-start.4 = (f32[12,16,1152]{2,1,0:T(8,128)}, f32[12,16,1152]{2,1,0:T(8,128)}, u32[]{:S(2)}, u32[]{:S(2)}) collective-permute-start(f32[12,16,1152]{2,1,0:T(8,128)} %get-tuple-element.15), channel_id=1, source_target_pairs={{8,0},{16,8},{24,16},{9,1},{17,9},{25,17},{10,2},{18,10},{26,18},{... | collective-permute-start | bytes 2654216 | tf_op jit(solution)/shard_map/ppermute | solution.py:636
  14.6 30.2 %collective-permute-start.5 = (f32[12,8,2304]{2,1,0:T(8,128)}, f32[12,8,2304]{2,1,0:T(8,128)}, u32[]{:S(2)}, u32[]{:S(2)}) collective-permute-start(f32[12,8,2304]{2,1,0:T(8,128)} %get-tuple-element.16), channel_id=1, source_target_pairs={{0,4},{4,0},{1,5},{5,1},{2,6},{6,2},{3,7},{7,3},{8,12},{12,8},{9,1... | collective-permute-start | bytes 2654216 | tf_op jit(solution)/shard_map/ppermute | solution.py:634
  16.2 28.6 %copy-start.4 = (f32[2,128,128]{2,1,0:T(8,128)S(1)}, f32[2,128,128]{2,1,0:T(8,128)}, u32[]{:S(2)}) copy-start(f32[2,128,128]{2,1,0:T(8,128)} %constant.22.clone.a_13_.a_5_) | copy-start | bytes 393220
  16.2 28.6 %copy-start.8 = (f32[2,128,128]{2,1,0:T(8,128)S(1)}, f32[2,128,128]{2,1,0:T(8,128)}, u32[]{:S(2)}) copy-start(f32[2,128,128]{2,1,0:T(8,128)} %constant.26.clone.a_15_) | copy-start | bytes 393220
  16.2 28.6 %copy-start.9 = (f32[2,128,128]{2,1,0:T(8,128)S(1)}, f32[2,128,128]{2,1,0:T(8,128)}, u32[]{:S(2)}) copy-start(f32[2,128,128]{2,1,0:T(8,128)} %constant.25.clone.a_14_) | copy-start | bytes 393220
  27.4 5.7 %collective-permute-start.2 = (f32[16,128]{1,0:T(8,128)}, f32[16,128]{1,0:T(8,128)S(1)}, u32[]{:S(2)}, u32[]{:S(2)}) collective-permute-start(f32[16,128]{1,0:T(8,128)} %moments.3.a_2_), channel_id=1, source_target_pairs={{0,3},{1,2},{2,1},{3,0},{4,7},{5,6},{6,5},{7,4},{8,11},{9,10},{10,... | collective-permute-start | bytes 24584 | tf_op jit(solution)/shard_map/ppermute | solution.py:630
  31.0 13.7 %collective-permute-start.1 = (f32[16,128]{1,0:T(8,128)}, f32[16,128]{1,0:T(8,128)S(1)}, u32[]{:S(2)}, u32[]{:S(2)}) collective-permute-start(f32[16,128]{1,0:T(8,128)} %moments.3.a_2_), channel_id=1, source_target_pairs={{0,2},{1,3},{2,0},{3,1},{4,6},{5,7},{6,4},{7,5},{8,10},{9,11},{10,... | collective-permute-start | bytes 24584 | tf_op jit(solution)/shard_map/ppermute | solution.py:630
  33.1 11.7 %collective-permute-start = (f32[16,128]{1,0:T(8,128)}, f32[16,128]{1,0:T(8,128)S(1)}, u32[]{:S(2)}, u32[]{:S(2)}) collective-permute-start(f32[16,128]{1,0:T(8,128)} %moments.3.a_2_), channel_id=1, source_target_pairs={{0,1},{1,0},{2,3},{3,2},{4,5},{5,4},{6,7},{7,6},{8,9},{9,8},{10,11... | collective-permute-start | bytes 24584 | tf_op jit(solution)/shard_map/ppermute | solution.py:630
  33.1 1.7 %copy-start.1 = (bf16[9,512,256]{2,1,0:T(8,128)(2,1)S(1)}, bf16[9,512,256]{2,1,0:T(8,128)(2,1)}, u32[]{:S(2)}) copy-start(bf16[9,512,256]{2,1,0:T(8,128)(2,1)} %constant.29.clone.a_7_) | copy-start | bytes 7077892
  34.8 10.0 %copy-start.16 = (f32[16,128]{1,0:T(8,128)S(1)}, f32[16,128]{1,0:T(8,128)}, u32[]{:S(2)}) copy-start(f32[16,128]{1,0:T(8,128)} %moments.3.a_2_) | copy-start | bytes 24580
  46.0 14.9 %copy-start.5 = (bf16[384,384]{1,0:T(8,128)(2,1)S(1)}, bf16[384,384]{1,0:T(8,128)(2,1)}, u32[]{:S(2)}) copy-start(bf16[384,384]{1,0:T(8,128)(2,1)} %constant.28.clone.a_4_) | copy-start | bytes 884740
  46.0 14.9 %copy-start.13 = (bf16[2,2,32,128]{3,2,1,0:T(8,128)(2,1)S(1)}, bf16[2,2,32,128]{3,2,1,0:T(8,128)(2,1)}, u32[]{:S(2)}) copy-start(bf16[2,2,32,128]{3,2,1,0:T(8,128)(2,1)} %constant.27.clone.a_3_) | copy-start | bytes 98308
  60.9 24.1 %copy-start = (f32[8,16,27648]{2,1,0:T(8,128)}, f32[8,16,27648]{2,1,0:T(8,128)S(1)}, u32[]{:S(2)}) copy-start(f32[8,16,27648]{2,1,0:T(8,128)S(1)} %update.2.a_2_.a_6_) | copy-start | bytes 42467332
  60.9 24.1 %copy-start.2 = (bf16[9,512,256]{2,1,0:T(8,128)(2,1)S(1)}, bf16[9,512,256]{2,1,0:T(8,128)(2,1)}, u32[]{:S(2)}) copy-start(bf16[9,512,256]{2,1,0:T(8,128)(2,1)} %constant.29.clone.a_7_) | copy-start | bytes 7077892
  60.9 24.1 %copy-start.12 = (f32[128,128]{1,0:T(8,128)S(1)}, f32[128,128]{1,0:T(8,128)}, u32[]{:S(2)}) copy-start(f32[128,128]{1,0:T(8,128)} %constant.21.clone.a_4_) | copy-start | bytes 196612
  64.1 29.5 %collective-permute-start.9 = (f32[12,16,1152]{2,1,0:T(8,128)S(1)}, f32[12,16,1152]{2,1,0:T(8,128)S(1)}, u32[]{:S(2)}, u32[]{:S(2)}) collective-permute-start(f32[12,16,1152]{2,1,0:T(8,128)S(1)} %get-tuple-element.17), channel_id=1, source_target_pairs={{0,8},{8,16},{16,24},{1,9},{9,17},{17,25},{2,10},{10,18},{18,26},{... | collective-permute-start | bytes 2654216 | tf_op jit(solution)/shard_map/ppermute | solution.py:635
  66.0 27.6 %collective-permute-start.10 = (f32[12,16,1152]{2,1,0:T(8,128)S(1)}, f32[12,16,1152]{2,1,0:T(8,128)S(1)}, u32[]{:S(2)}, u32[]{:S(2)}) collective-permute-start(f32[12,16,1152]{2,1,0:T(8,128)S(1)} %get-tuple-element.19), channel_id=1, source_target_pairs={{8,0},{16,8},{24,16},{9,1},{17,9},{25,17},{10,2},{18,10},{26,18},{... | collective-permute-start | bytes 2654216 | tf_op jit(solution)/shard_map/ppermute | solution.py:636
  69.9 23.8 %collective-permute-start.11 = (f32[12,8,2304]{2,1,0:T(8,128)S(1)}, f32[12,8,2304]{2,1,0:T(8,128)S(1)}, u32[]{:S(2)}, u32[]{:S(2)}) collective-permute-start(f32[12,8,2304]{2,1,0:T(8,128)S(1)} %get-tuple-element.20), channel_id=1, source_target_pairs={{0,4},{4,0},{1,5},{5,1},{2,6},{6,2},{3,7},{7,3},{8,12},{12,8},{9,1... | collective-permute-start | bytes 2654216 | tf_op jit(solution)/shard_map/ppermute | solution.py:634
  78.6 5.5 %collective-permute-start.8 = (f32[16,128]{1,0:T(8,128)S(1)}, f32[16,128]{1,0:T(8,128)S(1)}, u32[]{:S(2)}, u32[]{:S(2)}) collective-permute-start(f32[16,128]{1,0:T(8,128)S(1)} %moments.4.a_2_), channel_id=1, source_target_pairs={{0,3},{1,2},{2,1},{3,0},{4,7},{5,6},{6,5},{7,4},{8,11},{9,10},{10,... | collective-permute-start | bytes 24584 | tf_op jit(solution)/shard_map/ppermute | solution.py:630
  82.2 11.3 %collective-permute-start.7 = (f32[16,128]{1,0:T(8,128)S(1)}, f32[16,128]{1,0:T(8,128)S(1)}, u32[]{:S(2)}, u32[]{:S(2)}) collective-permute-start(f32[16,128]{1,0:T(8,128)S(1)} %moments.4.a_2_), channel_id=1, source_target_pairs={{0,2},{1,3},{2,0},{3,1},{4,6},{5,7},{6,4},{7,5},{8,10},{9,11},{10,... | collective-permute-start | bytes 24584 | tf_op jit(solution)/shard_map/ppermute | solution.py:630
  84.1 9.5 %collective-permute-start.6 = (f32[16,128]{1,0:T(8,128)S(1)}, f32[16,128]{1,0:T(8,128)S(1)}, u32[]{:S(2)}, u32[]{:S(2)}) collective-permute-start(f32[16,128]{1,0:T(8,128)S(1)} %moments.4.a_2_), channel_id=1, source_target_pairs={{0,1},{1,0},{2,3},{3,2},{4,5},{5,4},{6,7},{7,6},{8,9},{9,8},{10,11... | collective-permute-start | bytes 24584 | tf_op jit(solution)/shard_map/ppermute | solution.py:630
  122.0 5.7 %collective-permute-start.14 = (f32[16,128]{1,0:T(8,128)}, f32[16,128]{1,0:T(8,128)S(1)}, u32[]{:S(2)}, u32[]{:S(2)}) collective-permute-start(f32[16,128]{1,0:T(8,128)} %moments.5.a_1_), channel_id=1, source_target_pairs={{0,3},{1,2},{2,1},{3,0},{4,7},{5,6},{6,5},{7,4},{8,11},{9,10},{10,... | collective-permute-start | bytes 24584 | tf_op jit(solution)/shard_map/ppermute | solution.py:630
  125.0 4.8 %collective-permute-start.13 = (f32[16,128]{1,0:T(8,128)}, f32[16,128]{1,0:T(8,128)S(1)}, u32[]{:S(2)}, u32[]{:S(2)}) collective-permute-start(f32[16,128]{1,0:T(8,128)} %moments.5.a_1_), channel_id=1, source_target_pairs={{0,2},{1,3},{2,0},{3,1},{4,6},{5,7},{6,4},{7,5},{8,10},{9,11},{10,... | collective-permute-start | bytes 24584 | tf_op jit(solution)/shard_map/ppermute | solution.py:630
  125.3 4.4 %collective-permute-start.12 = (f32[16,128]{1,0:T(8,128)}, f32[16,128]{1,0:T(8,128)S(1)}, u32[]{:S(2)}, u32[]{:S(2)}) collective-permute-start(f32[16,128]{1,0:T(8,128)} %moments.5.a_1_), channel_id=1, source_target_pairs={{0,1},{1,0},{2,3},{3,2},{4,5},{5,4},{6,7},{7,6},{8,9},{9,8},{10,11... | collective-permute-start | bytes 24584 | tf_op jit(solution)/shard_map/ppermute | solution.py:630
  127.7 2.0 %copy-start.17 = (f32[16,128]{1,0:T(8,128)}, f32[16,128]{1,0:T(8,128)S(1)}, u32[]{:S(2)}) copy-start(f32[16,128]{1,0:T(8,128)S(1)} %collective-permute-done.14.a_4_) | copy-start | bytes 24580
  (3 other events, 2.3 us)

commit v8 on v7

--- a/solution.py
+++ b/solution.py
@@ -187,11 +187,11 @@
 
 
 def edge_table():
-    table = np.zeros((2, NODE_COUNT, 128))
+    table = np.zeros((2, NODES, NODE_COUNT))
     for r in range(NODES):
         for k in range(NODES):
-            table[0, r * LOCAL_Z + k, r] = END_L[k]
-            table[1, r * LOCAL_Z + NODES + k, r] = END_R[k]
+            table[0, r, r * LOCAL_Z + k] = END_L[k]
+            table[1, r, r * LOCAL_Z + NODES + k] = END_R[k]
     return table.astype(np.float32)
 
 
@@ -393,27 +393,30 @@
     return parts[0]
 
 
+def edge_sums(total, edge_ref):
+    net, gross = total[3:4, :], total[13:14, :]
+    down, up = 0.5 * (gross - net), 0.5 * (gross + net)
+    pairs = ((0, down), (1, up), (1, down))
+    return tuple(jnp.sum(edge_ref[k] * row, axis=1, keepdims=True) for k, row in pairs)
+
+
 def prepare_nodes(total, codes, place, rows_ref, edge_ref, table_ref, node_ref, wall_ref, plane_ref):
-    wide = jnp.concatenate([total, jnp.zeros((128 - MOMENTS, 128), F32)], axis=0)
-    table_ref[...] = jnp.transpose(wide)
-    rho, ur, ut, uz, temp, qr, qt, qz = macroscopic_of(lambda k: table_ref[:, k : k + 1])
+    rho, ur, ut, uz, temp, qr, qt, qz = macroscopic_of(lambda k: total[k : k + 1, :])
     inv_t = 1.0 / temp
     beta = ((1.0 - VISCOUS_RATIO) / 5.0) / (rho * temp * temp)
     kappa = rho * (TIME_STEP / KNUDSEN)
     peak = kappa * rho * inv_t * jnp.sqrt(inv_t)
-    columns = [uz, -0.5 * inv_t, qz * beta, inv_t, peak, 1.0 - kappa, ur, ut, qr * beta, qt * beta]
-    for k, column in enumerate(columns):
-        node_ref[k] = jnp.broadcast_to(column, (NODE_COUNT, 128))
-    net = table_ref[:, 3:4]
-    gross = table_ref[:, 13:14]
-    to_bottom = 0.5 * (gross - net)
-    to_top = 0.5 * (gross + net)
-    incident = jnp.sum(edge_ref[0] * to_bottom, axis=0, keepdims=True)
-    upward = jnp.sum(edge_ref[1] * to_top, axis=0, keepdims=True)
+    values = [uz, -0.5 * inv_t, qz * beta, inv_t, peak, 1.0 - kappa, ur, ut, qr * beta, qt * beta]
+    clear_sums(table_ref)
+    for k, value in enumerate(values):
+        table_ref[k : k + 1, :] = value
+    table_ref[...] = jnp.transpose(table_ref[...])
+    for k in range(len(values)):
+        node_ref[k] = jnp.broadcast_to(table_ref[:, k : k + 1], (NODE_COUNT, 128))
+    incident, upward, downward = edge_sums(total, edge_ref)
     bottom = jnp.where(codes[0, BOTTOM] == 1, SAT_DENSITY, incident * (1.0 / HALF_FLUX))
     top = jnp.where(codes[0, TOP] == 2, 0.0, upward * (1.0 / HALF_FLUX))
-    density = jnp.where(place == 0, bottom, top)
-    wall_ref[...] = jnp.transpose(jnp.broadcast_to(density, (128, 128)))[0:NODES, :]
+    wall_ref[...] = jnp.broadcast_to(jnp.where(place == 0, bottom, top), (NODES, 128))
 
     def one_radius(r, carry):
         rows = pl.ds(pl.multiple_of(r * LOCAL_Z, LOCAL_Z), LOCAL_Z)
@@ -462,21 +465,27 @@
         ghost_ref[:, at] = rows.astype(BF16)
 
 
-def outer_kernel(count, part_count, order, codes, *refs):
+def outer_kernel(count, part_count, last, order, codes, *refs):
     part_refs, refs = refs[:part_count], refs[part_count:]
-    f_ref, inner_ref, in_left_ref, in_turned_ref, in_right_ref, in_axial_ref = refs[:6]
+    f_ref, inner_ref, in_axial_ref, in_left_ref, in_turned_ref, in_right_ref = refs[:6]
     rows_ref, edge_ref, ghost_r_ref, ghost_z_ref, out_ref = refs[6:11]
-    plane_ref, node_ref, wall_ref, slot_ref, work_ref, lhs_ref, ghost_ref, table_ref = refs[11:]
+    refs = refs[11:]
+    if last:
+        (mom_ref, sums_ref), refs = refs[:2], refs[2:]
+    plane_ref, node_ref, wall_ref, slot_ref, work_ref, lhs_ref, ghost_ref, table_ref = refs
     step = pl.program_id(0)
     row, place = places_of()
 
     @pl.when(step == 0)
     def _():
+        if last:
+            clear_sums(sums_ref)
         total = total_of([p[...] for p in part_refs])
         prepare_nodes(total, codes, place, rows_ref, edge_ref, table_ref, node_ref, wall_ref, plane_ref)
 
+    speeds = [slot_speed(order, step * count + s) for s in range(count)]
     for s in range(count):
-        vz = slot_speed(order, step * count + s)
+        vz = speeds[s]
         for k, value in enumerate(slot_factors(vz, node_ref)):
             slot_ref[s, k] = value
         ghost_lifts(vz, ghost_r_ref, ghost_z_ref, lhs_ref)
@@ -495,14 +504,27 @@
         for j in range(PLANE // 128):
             at = pl.ds(j * 128, 128)
             gauss, along, reach = (plane_ref[k, rows, at] for k in range(3))
+            if last:
+                sums = [sums_ref[k, r, :, at] for k in range(5)]
             for s in range(count):
                 here = pl.ds(s * PLANE + j * 128, 128)
                 new = f_ref[r, :, here] * keep + work_ref[s, rows, at] + inner_ref[r, :, here].astype(F32)
                 bend = (along + factor[s][1]) * (reach + factor[s][2]) + 1.0
-                out_ref[r, :, here] = new + (gauss * factor[s][0]) * bend
+                new = new + (gauss * factor[s][0]) * bend
+                out_ref[r, :, here] = new
+                if last:
+                    sums = add_speed_sums(new, speeds[s], sums)
+            if last:
+                for k in range(5):
+                    sums_ref[k, r, :, at] = sums[k]
         return carry
 
     lax.fori_loop(0, NODES, update, 0)
+    if last:
+
+        @pl.when(step == pl.num_programs(0) - 1)
+        def _():
+            finish_moments(sums_ref, rows_ref, table_ref, mom_ref)
 
 
 def last_kernel(part_count, codes, *refs):
@@ -513,16 +535,12 @@
     for k in range(8):
         for r in range(NODES):
             macro_ref[k, r : r + 1, :] = values[k][:, r * LOCAL_Z : (r + 1) * LOCAL_Z]
-    net, gross = total_ref[3:4, :], total_ref[13:14, :]
-    to_bottom = jnp.broadcast_to(0.5 * (gross - net), (8, 128))
-    to_top = jnp.broadcast_to(0.5 * (gross + net), (8, 128))
-    exact = lambda x, y: jnp.dot(x, y, precision=lax.Precision.HIGHEST, preferred_element_type=F32)
-    incident = exact(to_bottom, edge_ref[0])
-    upward = exact(to_top, edge_ref[1])
-    downward = exact(to_bottom, edge_ref[1])
+    incident, upward, downward = edge_sums(total_ref, edge_ref)
     bottom = jnp.where(codes[0, BOTTOM] == 1, SAT_DENSITY * HALF_FLUX - incident, 0.0)
     top = jnp.where(codes[0, TOP] == 2, upward - downward, 0.0)
-    flux_ref[...] = jnp.where(place == 0, bottom, top)[0:1, 0:NODES]
+    square = jnp.broadcast_to(jnp.where(place == 0, bottom, top), (NODES, 128))
+    same = lax.broadcasted_iota(jnp.int32, (NODES, 128), 0) == lax.broadcasted_iota(jnp.int32, (NODES, 128), 1)
+    flux_ref[...] = jnp.sum(jnp.where(same, square, 0.0), axis=0, keepdims=True)[:, 0:NODES]
 
 
 def whole(shape):
@@ -605,7 +623,7 @@
             slab(group), jax.ShapeDtypeStruct(f.shape, BF16), scratch, [f] + tables,
         )
 
-    def outer(f, change, ghosts, parts, limit):
+    def outer(f, change, ghosts, parts, last, limit):
         count = math.gcd(slots, 2)
         tables = [rows, edge, ghost_r, ghost_z]
         scratch = [
@@ -619,9 +637,12 @@
             square,
         ]
         return call(
-            lambda *a: outer_kernel(count, len(parts), *a), "update", count, limit,
-            [mom_spec] * len(parts) + [slab(count), slab(count)] + trace_specs(count) + all_whole(tables),
-            slab(count), big_shape, scratch, [*parts, f, change, *ghosts, *tables],
+            lambda *a: outer_kernel(count, len(parts), last, *a), "last_update" if last else "update", count, limit,
+            [mom_spec] * len(parts) + [slab(count), slab(count), axial_spec(count)] + [radial_spec(count)] * 3
+            + all_whole(tables),
+            [slab(count)] + ([mom_spec] if last else []), [big_shape] + ([mom_shape] if last else []),
+            ([pltpu.VMEM((5, NODES, LOCAL_Z, PLANE), F32)] if last else []) + scratch,
+            [*parts, f, change, *ghosts, *tables],
         )
 
     def spread(moments):
@@ -634,16 +655,16 @@
         from_axial = lax.ppermute(axial, "gz", [(0, 1), (1, 0)])
         from_left = lax.ppermute(right, "row", [(i, i + 1) for i in range(rows_total - 1)])
         from_right = lax.ppermute(left, "row", [(i + 1, i) for i in range(rows_total - 1)])
-        return from_left, turned, from_right, from_axial
+        return from_axial, from_left, turned, from_right
 
     current = distribution
     for number in range(STEPS):
-        first, last = number == 0, number == STEPS - 1
-        ghosts = halo(*traces_of(current, 56 if first else 12))
-        parts = spread(moments_of(current, 56 if first else 18))
-        change = inner(current, 44 if first else 20)
-        current = outer(current, change, ghosts, parts, 32 if last else 20)
-    parts = spread(moments_of(current, 56))
+        last = number == STEPS - 1
+        ghosts = halo(*traces_of(current, 12))
+        parts = spread(moments_of(current, 18))
+        change = inner(current, 20)
+        current, *moments = outer(current, change, ghosts, parts, last, 28 if last else 20)
+    parts = spread(moments[0])
     macro, flux = pl.pallas_call(
         lambda *a: last_kernel(len(parts), *a),
         grid_spec=pltpu.PrefetchScalarGridSpec(

time: 134 us -> 132 us (0.985)
  Pallas kernels: 95.1 us -> 76.3 us
  local copies, waits for them, and re-layouts: 4.06 us -> 21.4 us
    pallas_call x9 -> x8, Pallas kernels: 92.6 us -> 74.1 us  [call(): pl.pallas_call(body, grid_spec=pltpu.PrefetchScalarGridSpec(num_scalar_pr...]
    unnamed x40 -> x62, local copies, waits for them, and re-layouts: 4.06 us -> 21.4 us
  transfers between devices with their start and end apart: 15 -> 15, of which waited for: 4 -> 4; matrix products, arithmetic and copies ran while one was open for 0% -> 0% of each run, Pallas kernels for 28% -> 25%
where the time goes in v8:
time: 132 us
  Pallas kernels  76.3 us (58%)
  starting transfers between devices  27 us (20%)
  local copies, waits for them, and re-layouts  21.4 us (16%)
  waiting for transfers between devices  6.15 us (5%)
    pallas_call x8, Pallas kernels, call(): pl.pallas_call(body, grid_spec=pltpu.PrefetchScalarGridSpec(num_scalar_pr...  74.1 us
    unnamed x62, local copies, waits for them, and re-layouts  21.4 us
    ppermute x9, starting transfers between devices, spread(): lax.ppermute(moments, 'vert', [(i, i ^ shift) for i in range(verts)])  13.3 us
    ppermute x2, starting transfers between devices, halo(): lax.ppermute(left, 'row', [(i + 1, i) for i in range(rows_total - 1)])  7.46 us
    ppermute x9, waiting for transfers between devices, spread(): lax.ppermute(moments, 'vert', [(i, i ^ shift) for i in range(verts)])  6.13 us
    ppermute x2, starting transfers between devices, halo(): lax.ppermute(right, 'row', [(i, i + 1) for i in range(rows_total - 1)])  3.82 us
  transfers between devices with their start and end apart: 15, of which 4 were waited for; matrix products, arithmetic and copies ran while one was open for 0% of the time, Pallas kernels for 25%

profile of v8, /device:TPU:4, one launch (start us, length us, event | category | flops | bytes accessed | tf_op | source)
XLA Modules:
  0.0 131.8 jit_solution(3493811144928448817)
XLA Ops:
  0.7 5.0 %copy-done.2 = f32[8,16,27648]{2,1,0:T(8,128)S(1)} copy-done((f32[8,16,27648]{2,1,0:T(8,128)S(1)}, f32[8,16,27648]{2,1,0:T(8,128)}, u32[]{:S(2)}) %copy-start.2) | copy-done | bytes 14155800
  5.7 1.0 copy-done.7
  8.7 3.2 %traces.2 = (f32[12,16,1152]{2,1,0:T(8,128)S(1)}, f32[12,16,1152]{2,1,0:T(8,128)S(1)}, f32[12,16,1152]{2,1,0:T(8,128)S(1)}, f32[12,8,2304]{2,1,0:T(8,128)S(1)}) custom-call(s32[12]{0:T(128)S(1)} %copy-done.25, s32[1,2]{1,0:T(1,128)S(1)} %bitcast.2, f32[8,16,27648]{2,1,0:T(8,128)S(1)} %copy-done.2, bf16[2,2,32,128]{3,2,1,0:T(8,128)(2,1)S(1)} %copy-done.20, ...), custom_call_target="tpu_custom_call" | custom-call | tf_op jit(solution)/shard_map/traces/pallas_call | solution.py:585
  11.9 1.6 %collective-permute-start.3 = (f32[12,8,2304]{2,1,0:T(8,128)S(1)}, f32[12,8,2304]{2,1,0:T(8,128)S(1)}, u32[]{:S(2)}, u32[]{:S(2)}) collective-permute-start(f32[12,8,2304]{2,1,0:T(8,128)S(1)} %get-tuple-element.15), channel_id=1, source_target_pairs={{0,4},{4,0},{1,5},{5,1},{2,6},{6,2},{3,7},{7,3},{8,12},{12,8},{9,1... | collective-permute-start | bytes 2654216 | tf_op jit(solution)/shard_map/ppermute | solution.py:655
  13.5 1.9 %collective-permute-start.4 = (f32[12,16,1152]{2,1,0:T(8,128)S(1)}, f32[12,16,1152]{2,1,0:T(8,128)S(1)}, u32[]{:S(2)}, u32[]{:S(2)}) collective-permute-start(f32[12,16,1152]{2,1,0:T(8,128)S(1)} %get-tuple-element.16), channel_id=1, source_target_pairs={{0,8},{8,16},{16,24},{1,9},{9,17},{17,25},{2,10},{10,18},{18,26},{... | collective-permute-start | bytes 2654216 | tf_op jit(solution)/shard_map/ppermute | solution.py:656
  15.4 3.6 %collective-permute-start.5 = (f32[12,16,1152]{2,1,0:T(8,128)S(1)}, f32[12,16,1152]{2,1,0:T(8,128)S(1)}, u32[]{:S(2)}, u32[]{:S(2)}) collective-permute-start(f32[12,16,1152]{2,1,0:T(8,128)S(1)} %get-tuple-element.18), channel_id=1, source_target_pairs={{8,0},{16,8},{24,16},{9,1},{17,9},{25,17},{10,2},{18,10},{26,18},{... | collective-permute-start | bytes 2654216 | tf_op jit(solution)/shard_map/ppermute | solution.py:657
  19.9 8.2 %moments.2.a_2_ = f32[16,128]{1,0:T(8,128)S(1)} custom-call(s32[12]{0:T(128)S(1)} %copy-done.26, s32[1,2]{1,0:T(1,128)S(1)} %bitcast.3, f32[8,16,27648]{2,1,0:T(8,128)S(1)} %copy-done.3, f32[8,2304]{1,0:T(8,128)S(1)} %copy-done.5), custom_call_target="tpu_custom_call" | custom-call | tf_op jit(solution)/shard_map/moments/pallas_call | solution.py:585
  28.2 3.7 %collective-permute-start.2 = (f32[16,128]{1,0:T(8,128)S(1)}, f32[16,128]{1,0:T(8,128)S(1)}, u32[]{:S(2)}, u32[]{:S(2)}) collective-permute-start(f32[16,128]{1,0:T(8,128)S(1)} %moments.2.a_2_), channel_id=1, source_target_pairs={{0,3},{1,2},{2,1},{3,0},{4,7},{5,6},{6,5},{7,4},{8,11},{9,10},{10,... | collective-permute-start | bytes 24584 | tf_op jit(solution)/shard_map/ppermute | solution.py:651
  31.8 1.8 %collective-permute-done.2.a_5_ = f32[16,128]{1,0:T(8,128)S(1)} collective-permute-done((f32[16,128]{1,0:T(8,128)S(1)}, f32[16,128]{1,0:T(8,128)S(1)}, u32[]{:S(2)}, u32[]{:S(2)}) %collective-permute-start.2) | collective-permute-done | bytes 8224 | tf_op jit(solution)/shard_map/ppermute | solution.py:651
  33.7 8.6 %inner_increments.2.a_7_ = bf16[8,16,27648]{2,1,0:T(8,128)(2,1)S(1)} custom-call(s32[12]{0:T(128)S(1)} %copy-done.26, s32[1,2]{1,0:T(1,128)S(1)} %bitcast.4, f32[8,16,27648]{2,1,0:T(8,128)S(1)} %copy-done.3, f32[8,2304]{1,0:T(8,128)S(1)} %copy-done.5, f32[128,128]{1,0:T(8,128)S(1)} %copy-done.19, bf16[3,128,128]{2,1,0:T(8,128)(2,1)S(1)} %copy-done.18, ...), custom_call_target="tpu_custom_call" | custom-call | tf_op jit(solution)/shard_map/inner_increments/pallas_call | solution.py:585
  42.4 13.6 %update.1.a_2_.a_6_ = f32[8,16,27648]{2,1,0:T(8,128)S(1)} custom-call(s32[12]{0:T(128)S(1)} %copy-done.26, s32[1,2]{1,0:T(1,128)S(1)} %bitcast.5, f32[16,128]{1,0:T(8,128)S(1)} %moments.2.a_2_, f32[16,128]{1,0:T(8,128)S(1)} %collective-permute-done.a_3_, f32[16,128]{1,0:T(8,128)S(1)} %collective-permute-done.1.a_4_, ...), custom_call_target="tpu_custom_call" | custom-call | tf_op jit(solution)/shard_map/update/pallas_call | solution.py:585
  56.0 3.2 %traces.3 = (f32[12,16,1152]{2,1,0:T(8,128)S(1)}, f32[12,16,1152]{2,1,0:T(8,128)S(1)}, f32[12,16,1152]{2,1,0:T(8,128)S(1)}, f32[12,8,2304]{2,1,0:T(8,128)S(1)}) custom-call(s32[12]{0:T(128)S(1)} %copy-done.26, s32[1,2]{1,0:T(1,128)S(1)} %bitcast.6, f32[8,16,27648]{2,1,0:T(8,128)S(1)} %update.1.a_2_.a_6_, bf16[2,2,32,128]{3,2,1,0:T(8,128)(2,1)S(1)} %copy-done.21, ...), custom_call_target="tpu_custom_call" | custom-call | tf_op jit(solution)/shard_map/traces/pallas_call | solution.py:585
  60.1 1.9 %collective-permute-start.10 = (f32[12,16,1152]{2,1,0:T(8,128)S(1)}, f32[12,16,1152]{2,1,0:T(8,128)S(1)}, u32[]{:S(2)}, u32[]{:S(2)}) collective-permute-start(f32[12,16,1152]{2,1,0:T(8,128)S(1)} %get-tuple-element.20), channel_id=1, source_target_pairs={{0,8},{8,16},{16,24},{1,9},{9,17},{17,25},{2,10},{10,18},{18,26},{... | collective-permute-start | bytes 2654216 | tf_op jit(solution)/shard_map/ppermute | solution.py:656
  62.0 3.8 %collective-permute-start.11 = (f32[12,16,1152]{2,1,0:T(8,128)S(1)}, f32[12,16,1152]{2,1,0:T(8,128)S(1)}, u32[]{:S(2)}, u32[]{:S(2)}) collective-permute-start(f32[12,16,1152]{2,1,0:T(8,128)S(1)} %get-tuple-element.22), channel_id=1, source_target_pairs={{8,0},{16,8},{24,16},{9,1},{17,9},{25,17},{10,2},{18,10},{26,18},{... | collective-permute-start | bytes 2654216 | tf_op jit(solution)/shard_map/ppermute | solution.py:657
  65.8 8.2 %moments.3.a_2_ = f32[16,128]{1,0:T(8,128)S(1)} custom-call(s32[12]{0:T(128)S(1)} %copy-done.26, s32[1,2]{1,0:T(1,128)S(1)} %bitcast.7, f32[8,16,27648]{2,1,0:T(8,128)S(1)} %update.1.a_2_.a_6_, f32[8,2304]{1,0:T(8,128)S(1)} %copy-done.5), custom_call_target="tpu_custom_call" | custom-call | tf_op jit(solution)/shard_map/moments/pallas_call | solution.py:585
  74.1 3.7 %collective-permute-start.8 = (f32[16,128]{1,0:T(8,128)S(1)}, f32[16,128]{1,0:T(8,128)S(1)}, u32[]{:S(2)}, u32[]{:S(2)}) collective-permute-start(f32[16,128]{1,0:T(8,128)S(1)} %moments.3.a_2_), channel_id=1, source_target_pairs={{0,3},{1,2},{2,1},{3,0},{4,7},{5,6},{6,5},{7,4},{8,11},{9,10},{10,... | collective-permute-start | bytes 24584 | tf_op jit(solution)/shard_map/ppermute | solution.py:651
  78.3 1.2 collective-permute-done.8.a_5_
  79.6 0.9 collective-permute-start.6
  80.5 8.6 %inner_increments.3.a_7_ = bf16[8,16,27648]{2,1,0:T(8,128)(2,1)S(1)} custom-call(s32[12]{0:T(128)S(1)} %copy-done.26, s32[1,2]{1,0:T(1,128)S(1)} %bitcast.8, f32[8,16,27648]{2,1,0:T(8,128)S(1)} %update.1.a_2_.a_6_, f32[8,2304]{1,0:T(8,128)S(1)} %copy-done.5, f32[128,128]{1,0:T(8,128)S(1)} %copy-done.19, bf16[3,128,128]{2,1,0:T(8,128)(2,1)S(1)} %copy-done.18, ...), custom_call_target="tpu_custom_call" | custom-call | tf_op jit(solution)/shard_map/inner_increments/pallas_call | solution.py:585
  89.1 0.9 copy-done.9
  90.1 0.9 copy-done.11
  91.0 0.9 copy-done.13
  91.9 5.0 %copy-done.1 = f32[8,16,27648]{2,1,0:T(8,128)S(1)} copy-done((f32[8,16,27648]{2,1,0:T(8,128)S(1)}, f32[8,16,27648]{2,1,0:T(8,128)}, u32[]{:S(2)}) %copy-start.1) | copy-done | bytes 14155800
  96.9 1.2 copy-done.10
  98.1 1.2 copy-done.12
  99.2 1.2 copy-done.14
  100.4 20.6 %last_update.1 = (f32[8,16,27648]{2,1,0:T(8,128)}, f32[16,128]{1,0:T(8,128)S(1)}) custom-call(s32[12]{0:T(128)S(1)} %copy-done.26, s32[1,2]{1,0:T(1,128)S(1)} %bitcast.9, f32[16,128]{1,0:T(8,128)S(1)} %moments.3.a_2_, f32[16,128]{1,0:T(8,128)S(1)} %collective-permute-done.6.a_3_, f32[16,128]{1,0:T(8,128)S(1)} %collective-permute-done.7.a_4_, ...), custom_call_target="tpu_custom_call" | custom-call | tf_op jit(solution)/shard_map/last_update/pallas_call | solution.py:585
  121.0 2.9 %collective-permute-start.14 = (f32[16,128]{1,0:T(8,128)S(1)}, f32[16,128]{1,0:T(8,128)S(1)}, u32[]{:S(2)}, u32[]{:S(2)}) collective-permute-start(f32[16,128]{1,0:T(8,128)S(1)} %get-tuple-element.24.a_1_), channel_id=1, source_target_pairs={{0,3},{1,2},{2,1},{3,0},{4,7},{5,6},{6,5},{7,4},{8,11},{9,10},{10,... | collective-permute-start | bytes 24584 | tf_op jit(solution)/shard_map/ppermute | solution.py:651
  124.3 1.1 collective-permute-start.12
  125.4 1.1 collective-permute-done.14.a_4_
  126.4 2.0 %collective-permute-done.13.a_3_ = f32[16,128]{1,0:T(8,128)S(1)} collective-permute-done((f32[16,128]{1,0:T(8,128)S(1)}, f32[16,128]{1,0:T(8,128)S(1)}, u32[]{:S(2)}, u32[]{:S(2)}) %collective-permute-start.13) | collective-permute-done | bytes 8224 | tf_op jit(solution)/shard_map/ppermute | solution.py:651
  129.6 2.2 %macroscopic.1 = (f32[8,8,16]{2,1,0:T(8,128)}, f32[1,8]{1,0:T(1,128)}) custom-call(s32[1,2]{1,0:T(1,128)} %bitcast.1, f32[16,128]{1,0:T(8,128)} %copy-done.27, f32[16,128]{1,0:T(8,128)} %copy-done.30, f32[16,128]{1,0:T(8,128)} %copy-done.29, f32[16,128]{1,0:T(8,128)} %copy-done.28, f32[2,8,128]{2,1,0:T(8,128)} %constant.22.clone.a_13_.a_5_), custom_call_target="tpu_custom_call" | custom-call | tf_op jit(solution)/shard_map/macroscopic/pallas_call | solution.py:668
  (69 shorter events, 6.1 us)
Async XLA Ops:
  0.6 18.4 %copy-start.26 = (s32[12]{0:T(128)S(1)}, s32[12]{0:T(128)}, u32[]{:S(2)}) copy-start(s32[12]{0:T(128)} %a_0_.15) | copy-start | bytes 148
  0.6 18.4 %copy-start.24 = (s32[2,1]{0,1:T(1,128)S(1)}, s32[2,1]{0,1:T(1,128)}, u32[]{:S(2)}) copy-start(s32[2,1]{0,1:T(1,128)} %param.15) | copy-start | bytes 28
  0.7 5.0 %copy-start.2 = (f32[8,16,27648]{2,1,0:T(8,128)S(1)}, f32[8,16,27648]{2,1,0:T(8,128)}, u32[]{:S(2)}) copy-start(f32[8,16,27648]{2,1,0:T(8,128)} %a_6_.3) | copy-start | bytes 42467332
  8.7 10.3 %copy-start.3 = (f32[8,16,27648]{2,1,0:T(8,128)S(1)}, f32[8,16,27648]{2,1,0:T(8,128)}, u32[]{:S(2)}) copy-start(f32[8,16,27648]{2,1,0:T(8,128)} %a_6_.3) | copy-start | bytes 42467332
  8.7 25.0 %copy-start.4 = (bf16[9,512,256]{2,1,0:T(8,128)(2,1)S(1)}, bf16[9,512,256]{2,1,0:T(8,128)(2,1)}, u32[]{:S(2)}) copy-start(bf16[9,512,256]{2,1,0:T(8,128)(2,1)} %constant.29.clone.a_7_) | copy-start | bytes 7077892
  11.9 30.4 %collective-permute-start.3 = (f32[12,8,2304]{2,1,0:T(8,128)S(1)}, f32[12,8,2304]{2,1,0:T(8,128)S(1)}, u32[]{:S(2)}, u32[]{:S(2)}) collective-permute-start(f32[12,8,2304]{2,1,0:T(8,128)S(1)} %get-tuple-element.15), channel_id=1, source_target_pairs={{0,4},{4,0},{1,5},{5,1},{2,6},{6,2},{3,7},{7,3},{8,12},{12,8},{9,1... | collective-permute-start | bytes 2654216 | tf_op jit(solution)/shard_map/ppermute | solution.py:655
  13.5 28.9 %collective-permute-start.4 = (f32[12,16,1152]{2,1,0:T(8,128)S(1)}, f32[12,16,1152]{2,1,0:T(8,128)S(1)}, u32[]{:S(2)}, u32[]{:S(2)}) collective-permute-start(f32[12,16,1152]{2,1,0:T(8,128)S(1)} %get-tuple-element.16), channel_id=1, source_target_pairs={{0,8},{8,16},{16,24},{1,9},{9,17},{17,25},{2,10},{10,18},{18,26},{... | collective-permute-start | bytes 2654216 | tf_op jit(solution)/shard_map/ppermute | solution.py:656
  15.4 27.0 %collective-permute-start.5 = (f32[12,16,1152]{2,1,0:T(8,128)S(1)}, f32[12,16,1152]{2,1,0:T(8,128)S(1)}, u32[]{:S(2)}, u32[]{:S(2)}) collective-permute-start(f32[12,16,1152]{2,1,0:T(8,128)S(1)} %get-tuple-element.18), channel_id=1, source_target_pairs={{8,0},{16,8},{24,16},{9,1},{17,9},{25,17},{10,2},{18,10},{26,18},{... | collective-permute-start | bytes 2654216 | tf_op jit(solution)/shard_map/ppermute | solution.py:657
  19.9 13.8 %copy-start.15 = (f32[3,128,128]{2,1,0:T(8,128)S(1)}, f32[3,128,128]{2,1,0:T(8,128)}, u32[]{:S(2)}) copy-start(f32[3,128,128]{2,1,0:T(8,128)} %constant.24.clone.a_6_) | copy-start | bytes 589828
  19.9 13.8 %copy-start.18 = (bf16[3,128,128]{2,1,0:T(8,128)(2,1)S(1)}, bf16[3,128,128]{2,1,0:T(8,128)(2,1)}, u32[]{:S(2)}) copy-start(bf16[3,128,128]{2,1,0:T(8,128)(2,1)} %constant.23.clone.a_5_) | copy-start | bytes 294916
  19.9 13.8 %copy-start.19 = (f32[128,128]{1,0:T(8,128)S(1)}, f32[128,128]{1,0:T(8,128)}, u32[]{:S(2)}) copy-start(f32[128,128]{1,0:T(8,128)} %constant.21.clone.a_4_) | copy-start | bytes 196612
  28.1 14.2 %copy-start.16 = (f32[2,128,128]{2,1,0:T(8,128)S(1)}, f32[2,128,128]{2,1,0:T(8,128)}, u32[]{:S(2)}) copy-start(f32[2,128,128]{2,1,0:T(8,128)} %constant.26.clone.a_15_) | copy-start | bytes 393220
  28.2 14.2 %copy-start.17 = (f32[2,128,128]{2,1,0:T(8,128)S(1)}, f32[2,128,128]{2,1,0:T(8,128)}, u32[]{:S(2)}) copy-start(f32[2,128,128]{2,1,0:T(8,128)} %constant.25.clone.a_14_) | copy-start | bytes 393220
  28.2 14.2 %copy-start.22 = (f32[2,8,128]{2,1,0:T(8,128)S(1)}, f32[2,8,128]{2,1,0:T(8,128)}, u32[]{:S(2)}) copy-start(f32[2,8,128]{2,1,0:T(8,128)} %constant.22.clone.a_13_.a_5_) | copy-start | bytes 24580
  28.2 5.5 %collective-permute-start.2 = (f32[16,128]{1,0:T(8,128)S(1)}, f32[16,128]{1,0:T(8,128)S(1)}, u32[]{:S(2)}, u32[]{:S(2)}) collective-permute-start(f32[16,128]{1,0:T(8,128)S(1)} %moments.2.a_2_), channel_id=1, source_target_pairs={{0,3},{1,2},{2,1},{3,0},{4,7},{5,6},{6,5},{7,4},{8,11},{9,10},{10,... | collective-permute-start | bytes 24584 | tf_op jit(solution)/shard_map/ppermute | solution.py:651
  31.8 10.5 %collective-permute-start.1 = (f32[16,128]{1,0:T(8,128)S(1)}, f32[16,128]{1,0:T(8,128)S(1)}, u32[]{:S(2)}, u32[]{:S(2)}) collective-permute-start(f32[16,128]{1,0:T(8,128)S(1)} %moments.2.a_2_), channel_id=1, source_target_pairs={{0,2},{1,3},{2,0},{3,1},{4,6},{5,7},{6,4},{7,5},{8,10},{9,11},{10,... | collective-permute-start | bytes 24584 | tf_op jit(solution)/shard_map/ppermute | solution.py:651
  33.7 8.6 %collective-permute-start = (f32[16,128]{1,0:T(8,128)S(1)}, f32[16,128]{1,0:T(8,128)S(1)}, u32[]{:S(2)}, u32[]{:S(2)}) collective-permute-start(f32[16,128]{1,0:T(8,128)S(1)} %moments.2.a_2_), channel_id=1, source_target_pairs={{0,1},{1,0},{2,3},{3,2},{4,5},{5,4},{6,7},{7,6},{8,9},{9,8},{10,11... | collective-permute-start | bytes 24584 | tf_op jit(solution)/shard_map/ppermute | solution.py:651
  42.4 13.6 %copy-start.8 = (bf16[384,384]{1,0:T(8,128)(2,1)S(1)}, bf16[384,384]{1,0:T(8,128)(2,1)}, u32[]{:S(2)}) copy-start(bf16[384,384]{1,0:T(8,128)(2,1)} %constant.28.clone.a_4_) | copy-start | bytes 884740
  42.4 13.6 %copy-start.21 = (bf16[2,2,32,128]{3,2,1,0:T(8,128)(2,1)S(1)}, bf16[2,2,32,128]{3,2,1,0:T(8,128)(2,1)}, u32[]{:S(2)}) copy-start(bf16[2,2,32,128]{3,2,1,0:T(8,128)(2,1)} %constant.27.clone.a_3_) | copy-start | bytes 98308
  56.0 24.5 %copy-start = (f32[8,16,27648]{2,1,0:T(8,128)}, f32[8,16,27648]{2,1,0:T(8,128)S(1)}, u32[]{:S(2)}) copy-start(f32[8,16,27648]{2,1,0:T(8,128)S(1)} %update.1.a_2_.a_6_) | copy-start | bytes 42467332
  59.2 29.9 %collective-permute-start.9 = (f32[12,8,2304]{2,1,0:T(8,128)S(1)}, f32[12,8,2304]{2,1,0:T(8,128)S(1)}, u32[]{:S(2)}, u32[]{:S(2)}) collective-permute-start(f32[12,8,2304]{2,1,0:T(8,128)S(1)} %get-tuple-element.19), channel_id=1, source_target_pairs={{0,4},{4,0},{1,5},{5,1},{2,6},{6,2},{3,7},{7,3},{8,12},{12,8},{9,1... | collective-permute-start | bytes 2654216 | tf_op jit(solution)/shard_map/ppermute | solution.py:655
  60.1 30.0 %collective-permute-start.10 = (f32[12,16,1152]{2,1,0:T(8,128)S(1)}, f32[12,16,1152]{2,1,0:T(8,128)S(1)}, u32[]{:S(2)}, u32[]{:S(2)}) collective-permute-start(f32[12,16,1152]{2,1,0:T(8,128)S(1)} %get-tuple-element.20), channel_id=1, source_target_pairs={{0,8},{8,16},{16,24},{1,9},{9,17},{17,25},{2,10},{10,18},{18,26},{... | collective-permute-start | bytes 2654216 | tf_op jit(solution)/shard_map/ppermute | solution.py:656
  62.0 29.0 %collective-permute-start.11 = (f32[12,16,1152]{2,1,0:T(8,128)S(1)}, f32[12,16,1152]{2,1,0:T(8,128)S(1)}, u32[]{:S(2)}, u32[]{:S(2)}) collective-permute-start(f32[12,16,1152]{2,1,0:T(8,128)S(1)} %get-tuple-element.22), channel_id=1, source_target_pairs={{8,0},{16,8},{24,16},{9,1},{17,9},{25,17},{10,2},{18,10},{26,18},{... | collective-permute-start | bytes 2654216 | tf_op jit(solution)/shard_map/ppermute | solution.py:657
  74.0 17.8 %copy-start.6 = (f32[8,2304]{1,0:T(8,128)S(1)}, f32[8,2304]{1,0:T(8,128)}, u32[]{:S(2)}) copy-start(f32[8,2304]{1,0:T(8,128)} %constant.20.clone.a_3_.a_12_) | copy-start | bytes 221188
  74.1 5.5 %collective-permute-start.8 = (f32[16,128]{1,0:T(8,128)S(1)}, f32[16,128]{1,0:T(8,128)S(1)}, u32[]{:S(2)}, u32[]{:S(2)}) collective-permute-start(f32[16,128]{1,0:T(8,128)S(1)} %moments.3.a_2_), channel_id=1, source_target_pairs={{0,3},{1,2},{2,1},{3,0},{4,7},{5,6},{6,5},{7,4},{8,11},{9,10},{10,... | collective-permute-start | bytes 24584 | tf_op jit(solution)/shard_map/ppermute | solution.py:651
  77.7 11.4 %collective-permute-start.7 = (f32[16,128]{1,0:T(8,128)S(1)}, f32[16,128]{1,0:T(8,128)S(1)}, u32[]{:S(2)}, u32[]{:S(2)}) collective-permute-start(f32[16,128]{1,0:T(8,128)S(1)} %moments.3.a_2_), channel_id=1, source_target_pairs={{0,2},{1,3},{2,0},{3,1},{4,6},{5,7},{6,4},{7,5},{8,10},{9,11},{10,... | collective-permute-start | bytes 24584 | tf_op jit(solution)/shard_map/ppermute | solution.py:651
  79.6 9.5 %collective-permute-start.6 = (f32[16,128]{1,0:T(8,128)S(1)}, f32[16,128]{1,0:T(8,128)S(1)}, u32[]{:S(2)}, u32[]{:S(2)}) collective-permute-start(f32[16,128]{1,0:T(8,128)S(1)} %moments.3.a_2_), channel_id=1, source_target_pairs={{0,1},{1,0},{2,3},{3,2},{4,5},{5,4},{6,7},{7,6},{8,9},{9,8},{10,11... | collective-permute-start | bytes 24584 | tf_op jit(solution)/shard_map/ppermute | solution.py:651
  91.9 5.0 %copy-start.1 = (f32[8,16,27648]{2,1,0:T(8,128)S(1)}, f32[8,16,27648]{2,1,0:T(8,128)}, u32[]{:S(2)}) copy-start(f32[8,16,27648]{2,1,0:T(8,128)} %copy-done) | copy-start | bytes 42467332
  121.0 7.4 %copy-start.27 = (f32[16,128]{1,0:T(8,128)}, f32[16,128]{1,0:T(8,128)S(1)}, u32[]{:S(2)}) copy-start(f32[16,128]{1,0:T(8,128)S(1)} %get-tuple-element.24.a_1_) | copy-start | bytes 24580
  121.0 5.4 %collective-permute-start.14 = (f32[16,128]{1,0:T(8,128)S(1)}, f32[16,128]{1,0:T(8,128)S(1)}, u32[]{:S(2)}, u32[]{:S(2)}) collective-permute-start(f32[16,128]{1,0:T(8,128)S(1)} %get-tuple-element.24.a_1_), channel_id=1, source_target_pairs={{0,3},{1,2},{2,1},{3,0},{4,7},{5,6},{6,5},{7,4},{8,11},{9,10},{10,... | collective-permute-start | bytes 24584 | tf_op jit(solution)/shard_map/ppermute | solution.py:651
  123.9 4.5 %collective-permute-start.13 = (f32[16,128]{1,0:T(8,128)S(1)}, f32[16,128]{1,0:T(8,128)S(1)}, u32[]{:S(2)}, u32[]{:S(2)}) collective-permute-start(f32[16,128]{1,0:T(8,128)S(1)} %get-tuple-element.24.a_1_), channel_id=1, source_target_pairs={{0,2},{1,3},{2,0},{3,1},{4,6},{5,7},{6,4},{7,5},{8,10},{9,11},{10,... | collective-permute-start | bytes 24584 | tf_op jit(solution)/shard_map/ppermute | solution.py:651
  124.3 4.2 %collective-permute-start.12 = (f32[16,128]{1,0:T(8,128)S(1)}, f32[16,128]{1,0:T(8,128)S(1)}, u32[]{:S(2)}, u32[]{:S(2)}) collective-permute-start(f32[16,128]{1,0:T(8,128)S(1)} %get-tuple-element.24.a_1_), channel_id=1, source_target_pairs={{0,1},{1,0},{2,3},{3,2},{4,5},{5,4},{6,7},{7,6},{8,9},{9,8},{10,11... | collective-permute-start | bytes 24584 | tf_op jit(solution)/shard_map/ppermute | solution.py:651
  (14 other events, 13.4 us)

commit v9 on v8

--- a/solution.py
+++ b/solution.py
@@ -115,16 +115,13 @@
     zout = np.block([[down, np.outer(LIFT_R, END_L)], [zero, DERIV]])
     axial = np.stack([np.kron(ident, zdown), np.kron(ident, zup), np.kron(ident, zout)])
     ghost_r = np.zeros((2, NODE_COUNT, 128))
-    ghost_z = np.zeros((2, NODE_COUNT, 128))
+    ghost_z = np.zeros((2, LOCAL_Z, 128))
     for r in range(NODES):
-        for z in range(LOCAL_Z):
-            n = r * LOCAL_Z + z
-            ghost_r[0, n, z] = -LIFT_R[r]
-            ghost_r[1, n, z] = LIFT_L[r]
-            if z >= NODES:
-                ghost_z[0, n, LOCAL_Z + r] = LIFT_R[z - NODES]
-            else:
-                ghost_z[1, n, LOCAL_Z + r] = LIFT_L[z]
+        ghost_r[0, r * LOCAL_Z : (r + 1) * LOCAL_Z] = -LIFT_R[r]
+        ghost_r[1, r * LOCAL_Z : (r + 1) * LOCAL_Z] = LIFT_L[r]
+    for k in range(NODES):
+        ghost_z[0, NODES + k] = LIFT_R[k]
+        ghost_z[1, k] = LIFT_L[k]
     trace = np.zeros((2, 2, GHOST_ROWS, NODE_COUNT))
     for side in range(2):
         radial_row = END_R if side == 1 else END_L
@@ -320,37 +317,16 @@
     turn_traces(count, row, mirror_ref, left_ref, turned_ref)
 
 
-def moment_kernel(count, order, codes, f_ref, rows_ref, mom_ref, sums_ref, table_ref):
+def inner_kernel(
+    count, order, codes, f_ref, rows_ref, pos_ref, radial_ref, axial_m_ref, rot_ref,
+    out_ref, mom_ref, sums_ref, table_ref, inverse_ref, pad_ref, lhs_ref,
+):
     step = pl.program_id(0)
+    row, place = places_of()
 
     @pl.when(step == 0)
     def _():
         clear_sums(sums_ref)
-
-    speeds = [slot_speed(order, step * count + s) for s in range(count)]
-    for j in range(0, PLANE, 128):
-        at = pl.ds(j, 128)
-        for r in range(NODES):
-            sums = [sums_ref[k, r, :, at] for k in range(5)]
-            for s in range(count):
-                sums = add_speed_sums(f_ref[r, :, pl.ds(s * PLANE + j, 128)], speeds[s], sums)
-            for k in range(5):
-                sums_ref[k, r, :, at] = sums[k]
-
-    @pl.when(step == pl.num_programs(0) - 1)
-    def _():
-        finish_moments(sums_ref, rows_ref, table_ref, mom_ref)
-
-
-def inner_kernel(
-    count, order, codes, f_ref, rows_ref, pos_ref, radial_ref, axial_m_ref, rot_ref,
-    out_ref, inverse_ref, pad_ref, lhs_ref,
-):
-    step = pl.program_id(0)
-    row, place = places_of()
-
-    @pl.when(step == 0)
-    def _():
         pad_ref[:, :, 0:128] = jnp.zeros((count, NODE_COUNT, 128), BF16)
         pad_ref[:, :, 128 + PLANE :] = jnp.zeros((count, NODE_COUNT, 128), BF16)
         inverse_ref[...] = 1.0 / (ELEMENT_WIDTH * (row.astype(F32) + pos_ref[...]))
@@ -361,8 +337,9 @@
 
     kind_out = jnp.where(jnp.logical_and(place == 1, codes[0, TOP] == 2), 2, 0)
     inverse = inverse_ref[...]
+    speeds = [slot_speed(order, step * count + s) for s in range(count)]
     for s in range(count):
-        vz = slot_speed(order, step * count + s)
+        vz = speeds[s]
         axial = (vz * axial_m_ref[jnp.where(vz > 0, 1, kind_out)]).astype(BF16)
         lhs_ref[s, 0, :, NODE_COUNT:] = axial
         lhs_ref[s, 1, :, NODE_COUNT:] = axial
@@ -385,6 +362,18 @@
                 change = turned[s * NODE_COUNT : (s + 1) * NODE_COUNT, inside : inside + lanes]
                 change = change + dot(lhs_ref[s, side], both)
                 out_ref[:, :, here : here + lanes] = change.astype(BF16).reshape(NODES, LOCAL_Z, lanes)
+            for j in range(first, first + lanes, 128):
+                at = pl.ds(j, 128)
+                for r in range(NODES):
+                    sums = [sums_ref[k, r, :, at] for k in range(5)]
+                    for s in range(count):
+                        sums = add_speed_sums(f_ref[r, :, pl.ds(s * PLANE + j, 128)], speeds[s], sums)
+                    for k in range(5):
+                        sums_ref[k, r, :, at] = sums[k]
+
+    @pl.when(step == pl.num_programs(0) - 1)
+    def _():
+        finish_moments(sums_ref, rows_ref, table_ref, mom_ref)
 
 
 def total_of(parts):
@@ -444,13 +433,9 @@
     return node_ref[4] * jnp.exp(square * node_ref[1]), cz * node_ref[2], square * node_ref[3] - 5.0
 
 
-def ghost_lifts(vz, ghost_r_ref, ghost_z_ref, lhs_ref):
-    lean = jnp.abs(vz) * ghost_z_ref[jnp.where(vz > 0, 1, 0)]
-    lhs_ref[0] = (ghost_r_ref[0] + lean).astype(BF16)
-    lhs_ref[1] = (ghost_r_ref[1] + lean).astype(BF16)
-
-
-def ghost_rows(s, vz, place, in_left_ref, in_turned_ref, in_right_ref, in_axial_ref, rows_ref, wall_ref, ghost_ref):
+def ghost_rows(
+    s, vz, place, in_axial_ref, in_left_ref, in_turned_ref, in_right_ref, rows_ref, wall_ref, radial_ref, axial_ref
+):
     own = (place == 0) == (vz > 0)
     strength = jnp.exp(-0.5 * vz * vz + jnp.zeros((NODES, 128), F32)) * wall_ref[...]
     for j in range(PLANE // 128):
@@ -460,9 +445,10 @@
         else:
             back = pl.ds(j * 128 - HALF, 128)
             radial = in_left_ref[s, :, back] + in_turned_ref[s, :, back]
+        radial_ref[s, :, at] = rows_ref[0:1, at] * radial
         axial = jnp.where(own, strength * rows_ref[2:3, at], in_axial_ref[s, :, at])
-        rows = jnp.concatenate([rows_ref[0:1, at] * radial, axial, jnp.zeros((8, 128), F32)], axis=0)
-        ghost_ref[:, at] = rows.astype(BF16)
+        for r in range(NODES):
+            axial_ref[s, r, :, at] = jnp.broadcast_to(axial[r : r + 1], (NODES, 128))
 
 
 def outer_kernel(count, part_count, last, order, codes, *refs):
@@ -472,7 +458,7 @@
     refs = refs[11:]
     if last:
         (mom_ref, sums_ref), refs = refs[:2], refs[2:]
-    plane_ref, node_ref, wall_ref, slot_ref, work_ref, lhs_ref, ghost_ref, table_ref = refs
+    plane_ref, node_ref, wall_ref, slot_ref, lean_ref, radial_ref, axial_ref, table_ref = refs
     step = pl.program_id(0)
     row, place = places_of()
 
@@ -488,19 +474,18 @@
         vz = speeds[s]
         for k, value in enumerate(slot_factors(vz, node_ref)):
             slot_ref[s, k] = value
-        ghost_lifts(vz, ghost_r_ref, ghost_z_ref, lhs_ref)
+        lean_ref[s] = jnp.abs(vz) * ghost_z_ref[jnp.where(vz > 0, 1, 0)]
         ghost_rows(
-            s, vz, place, in_left_ref, in_turned_ref, in_right_ref, in_axial_ref, rows_ref, wall_ref, ghost_ref
+            s, vz, place, in_axial_ref, in_left_ref, in_turned_ref, in_right_ref, rows_ref, wall_ref,
+            radial_ref, axial_ref,
         )
-        for first, lanes, side in PIECES:
-            work_ref[s, :, first : first + lanes] = dot(
-                lhs_ref[side, :, 0:GHOST_ROWS], ghost_ref[:, first : first + lanes]
-            )
 
     def update(r, carry):
         rows = pl.ds(pl.multiple_of(r * LOCAL_Z, LOCAL_Z), LOCAL_Z)
         keep = node_ref[5, rows, :]
+        lifts = [ghost_r_ref[side, rows, :] for side in range(2)]
         factor = [[slot_ref[s, k, rows, :] for k in range(3)] for s in range(count)]
+        lean = [lean_ref[s] for s in range(count)]
         for j in range(PLANE // 128):
             at = pl.ds(j * 128, 128)
             gauss, along, reach = (plane_ref[k, rows, at] for k in range(3))
@@ -508,7 +493,10 @@
                 sums = [sums_ref[k, r, :, at] for k in range(5)]
             for s in range(count):
                 here = pl.ds(s * PLANE + j * 128, 128)
-                new = f_ref[r, :, here] * keep + work_ref[s, rows, at] + inner_ref[r, :, here].astype(F32)
+                new = f_ref[r, :, here] * keep + inner_ref[r, :, here].astype(F32)
+                new = new + radial_ref[s, :, at] * lifts[1 if j * 128 >= HALF else 0]
+                across = axial_ref[s, r, :, at]
+                new = new + jnp.concatenate([across, across], axis=0) * lean[s]
                 bend = (along + factor[s][1]) * (reach + factor[s][2]) + 1.0
                 new = new + (gauss * factor[s][0]) * bend
                 out_ref[r, :, here] = new
@@ -605,35 +593,32 @@
             trace_specs(group), trace_shapes, [], [f, trace_m, mirror_m],
         )
 
-    def moments_of(f, limit):
-        return call(
-            lambda *a: moment_kernel(group, *a), "moments", group, limit, [slab(group)] + all_whole([rows]),
-            mom_spec, mom_shape, [pltpu.VMEM((5, NODES, LOCAL_Z, PLANE), F32), square], [f, rows],
-        )
-
     def inner(f, limit):
+        group = math.gcd(slots, 2)
         tables = [rows, pos, radial_m, axial_m, rot_m]
         scratch = [
+            pltpu.VMEM((5, NODES, LOCAL_Z, PLANE), F32),
+            square,
             square,
             pltpu.VMEM((group, NODE_COUNT, PLANE + 256), BF16),
             pltpu.VMEM((group, 2, NODE_COUNT, 2 * NODE_COUNT), BF16),
         ]
         return call(
             lambda *a: inner_kernel(group, *a), "inner_increments", group, limit, [slab(group)] + all_whole(tables),
-            slab(group), jax.ShapeDtypeStruct(f.shape, BF16), scratch, [f] + tables,
+            [slab(group), mom_spec], [jax.ShapeDtypeStruct(f.shape, BF16), mom_shape], scratch, [f] + tables,
         )
 
     def outer(f, change, ghosts, parts, last, limit):
-        count = math.gcd(slots, 2)
+        count = 1 if last else math.gcd(slots, 2)
         tables = [rows, edge, ghost_r, ghost_z]
         scratch = [
             pltpu.VMEM((3, NODE_COUNT, PLANE), F32),
             pltpu.VMEM((10, NODE_COUNT, 128), F32),
             pltpu.VMEM((NODES, 128), F32),
             pltpu.VMEM((count, 3, NODE_COUNT, 128), F32),
-            pltpu.VMEM((count, NODE_COUNT, PLANE), F32),
-            pltpu.VMEM((2, NODE_COUNT, 128), BF16),
-            pltpu.VMEM((GHOST_ROWS, PLANE), BF16),
+            pltpu.VMEM((count, LOCAL_Z, 128), F32),
+            pltpu.VMEM((count, LOCAL_Z, PLANE), F32),
+            pltpu.VMEM((count, NODES, NODES, PLANE), F32),
             square,
         ]
         return call(
@@ -660,11 +645,11 @@
     current = distribution
     for number in range(STEPS):
         last = number == STEPS - 1
-        ghosts = halo(*traces_of(current, 12))
-        parts = spread(moments_of(current, 18))
-        change = inner(current, 20)
-        current, *moments = outer(current, change, ghosts, parts, last, 28 if last else 20)
-    parts = spread(moments[0])
+        ghosts = halo(*traces_of(current, 20))
+        change, moments = inner(current, 21)
+        parts = spread(moments)
+        current, *final = outer(current, change, ghosts, parts, last, 20)
+    parts = spread(final[0])
     macro, flux = pl.pallas_call(
         lambda *a: last_kernel(len(parts), *a),
         grid_spec=pltpu.PrefetchScalarGridSpec(

time: 132 us -> 132 us (level)
  local copies, waits for them, and re-layouts: 21.4 us -> 12.7 us
  waiting for transfers between devices: 6.15 us -> 14.8 us
  starting transfers between devices: 27 us -> 25.1 us
    unnamed x62 -> x46, local copies, waits for them, and re-layouts: 21.4 us -> 12.7 us
    ppermute x9, waiting for transfers between devices: 6.13 us -> 14.7 us  [spread(): lax.ppermute(moments, 'vert', [(i, i ^ shift) for i in range(verts)])]
    ppermute x9, starting transfers between devices: 13.3 us -> 11.8 us  [spread(): lax.ppermute(moments, 'vert', [(i, i ^ shift) for i in range(verts)])]
    pallas_call x8 -> x6, Pallas kernels: 74.1 us -> 75.5 us  [call(): pl.pallas_call(body, grid_spec=pltpu.PrefetchScalarGridSpec(num_scalar_pr...]
  transfers between devices with their start and end apart: 15 -> 15, of which waited for: 4 -> 8; matrix products, arithmetic and copies ran while one was open for 0% -> 0% of each run, Pallas kernels for 25% -> 26%
where the time goes in v9:
time: 132 us; the launch traced here: 131 us
  Pallas kernels  77.6 us (59%)
  starting transfers between devices  25.1 us (19%)
  waiting for transfers between devices  14.8 us (11%)
  local copies, waits for them, and re-layouts  12.7 us (10%)
    pallas_call x6, Pallas kernels, call(): pl.pallas_call(body, grid_spec=pltpu.PrefetchScalarGridSpec(num_scalar_pr...  75.5 us
    ppermute x9, waiting for transfers between devices, spread(): lax.ppermute(moments, 'vert', [(i, i ^ shift) for i in range(verts)])  14.7 us
    unnamed x46, local copies, waits for them, and re-layouts  12.7 us
    ppermute x9, starting transfers between devices, spread(): lax.ppermute(moments, 'vert', [(i, i ^ shift) for i in range(verts)])  11.8 us
    ppermute x2, starting transfers between devices, halo(): lax.ppermute(left, 'row', [(i + 1, i) for i in range(rows_total - 1)])  7.28 us
    ppermute x2, starting transfers between devices, halo(): lax.ppermute(right, 'row', [(i, i + 1) for i in range(rows_total - 1)])  3.82 us
  transfers between devices with their start and end apart: 15, of which 8 were waited for; matrix products, arithmetic and copies ran while one was open for 0% of the time, Pallas kernels for 26%

profile of v9, /device:TPU:4, one launch (start us, length us, event | category | flops | bytes accessed | tf_op | source)
XLA Modules:
  0.0 131.1 jit_solution(1632983640243219623)
XLA Ops:
  0.7 5.0 %copy-done = f32[8,16,27648]{2,1,0:T(8,128)S(1)} copy-done((f32[8,16,27648]{2,1,0:T(8,128)S(1)}, f32[8,16,27648]{2,1,0:T(8,128)}, u32[]{:S(2)}) %copy-start) | copy-done | bytes 14155800
  5.7 1.0 copy-done.4
  6.7 0.8 copy-done.12
  8.1 0.7 copy-done.17
  8.7 3.2 %traces.2 = (f32[12,16,1152]{2,1,0:T(8,128)S(1)}, f32[12,16,1152]{2,1,0:T(8,128)S(1)}, f32[12,16,1152]{2,1,0:T(8,128)S(1)}, f32[12,8,2304]{2,1,0:T(8,128)S(1)}) custom-call(s32[12]{0:T(128)S(1)} %copy-done.17, s32[1,2]{1,0:T(1,128)S(1)} %bitcast.2, f32[8,16,27648]{2,1,0:T(8,128)S(1)} %copy-done, bf16[2,2,32,128]{3,2,1,0:T(8,128)(2,1)S(1)} %copy-done.12, ...), custom_call_target="tpu_custom_call" | custom-call | tf_op jit(solution)/shard_map/traces/pallas_call | solution.py:573
  11.9 1.6 %collective-permute-start.3 = (f32[12,8,2304]{2,1,0:T(8,128)S(1)}, f32[12,8,2304]{2,1,0:T(8,128)S(1)}, u32[]{:S(2)}, u32[]{:S(2)}) collective-permute-start(f32[12,8,2304]{2,1,0:T(8,128)S(1)} %get-tuple-element.21), channel_id=1, source_target_pairs={{0,4},{4,0},{1,5},{5,1},{2,6},{6,2},{3,7},{7,3},{8,12},{12,8},{9,1... | collective-permute-start | bytes 2654216 | tf_op jit(solution)/shard_map/ppermute | solution.py:640
  13.5 1.9 %collective-permute-start.4 = (f32[12,16,1152]{2,1,0:T(8,128)S(1)}, f32[12,16,1152]{2,1,0:T(8,128)S(1)}, u32[]{:S(2)}, u32[]{:S(2)}) collective-permute-start(f32[12,16,1152]{2,1,0:T(8,128)S(1)} %get-tuple-element.22), channel_id=1, source_target_pairs={{0,8},{8,16},{16,24},{1,9},{9,17},{17,25},{2,10},{10,18},{18,26},{... | collective-permute-start | bytes 2654216 | tf_op jit(solution)/shard_map/ppermute | solution.py:641
  15.4 3.6 %collective-permute-start.5 = (f32[12,16,1152]{2,1,0:T(8,128)S(1)}, f32[12,16,1152]{2,1,0:T(8,128)S(1)}, u32[]{:S(2)}, u32[]{:S(2)}) collective-permute-start(f32[12,16,1152]{2,1,0:T(8,128)S(1)} %get-tuple-element.24), channel_id=1, source_target_pairs={{8,0},{16,8},{24,16},{9,1},{17,9},{25,17},{10,2},{18,10},{26,18},{... | collective-permute-start | bytes 2654216 | tf_op jit(solution)/shard_map/ppermute | solution.py:642
  19.1 1.7 %copy-done.2 = bf16[9,512,256]{2,1,0:T(8,128)(2,1)S(1)} copy-done((bf16[9,512,256]{2,1,0:T(8,128)(2,1)S(1)}, bf16[9,512,256]{2,1,0:T(8,128)(2,1)}, u32[]{:S(2)}) %copy-start.2) | copy-done | bytes 2359320
  20.8 0.9 copy-done.8
  21.7 0.8 copy-done.10
  22.5 17.2 %inner_increments.2 = (bf16[8,16,27648]{2,1,0:T(8,128)(2,1)S(1)}, f32[16,128]{1,0:T(8,128)S(1)}) custom-call(s32[12]{0:T(128)S(1)} %copy-done.18, s32[1,2]{1,0:T(1,128)S(1)} %bitcast.3, f32[8,16,27648]{2,1,0:T(8,128)S(1)} %copy-done.1, f32[8,2304]{1,0:T(8,128)S(1)} %copy-done.5, f32[128,128]{1,0:T(8,128)S(1)} %copy-done.10, ...), custom_call_target="tpu_custom_call" | custom-call | tf_op jit(solution)/shard_map/inner_increments/pallas_call | solution.py:573
  39.7 3.7 %collective-permute-start.2 = (f32[16,128]{1,0:T(8,128)S(1)}, f32[16,128]{1,0:T(8,128)S(1)}, u32[]{:S(2)}, u32[]{:S(2)}) collective-permute-start(f32[16,128]{1,0:T(8,128)S(1)} %get-tuple-element.19.a_2_), channel_id=1, source_target_pairs={{0,3},{1,2},{2,1},{3,0},{4,7},{5,6},{6,5},{7,4},{8,11},{9,10},{10,... | collective-permute-start | bytes 24584 | tf_op jit(solution)/shard_map/ppermute | solution.py:636
  43.4 1.8 %collective-permute-done.2.a_5_ = f32[16,128]{1,0:T(8,128)S(1)} collective-permute-done((f32[16,128]{1,0:T(8,128)S(1)}, f32[16,128]{1,0:T(8,128)S(1)}, u32[]{:S(2)}, u32[]{:S(2)}) %collective-permute-start.2) | collective-permute-done | bytes 8224 | tf_op jit(solution)/shard_map/ppermute | solution.py:636
  45.2 2.7 %collective-permute-done.1.a_4_ = f32[16,128]{1,0:T(8,128)S(1)} collective-permute-done((f32[16,128]{1,0:T(8,128)S(1)}, f32[16,128]{1,0:T(8,128)S(1)}, u32[]{:S(2)}, u32[]{:S(2)}) %collective-permute-start.1) | collective-permute-done | bytes 8224 | tf_op jit(solution)/shard_map/ppermute | solution.py:636
  47.9 0.9 collective-permute-done.a_3_
  48.9 13.5 %update.1.a_2_.a_6_ = f32[8,16,27648]{2,1,0:T(8,128)S(1)} custom-call(s32[12]{0:T(128)S(1)} %copy-done.18, s32[1,2]{1,0:T(1,128)S(1)} %bitcast.4, f32[16,128]{1,0:T(8,128)S(1)} %get-tuple-element.19.a_2_, f32[16,128]{1,0:T(8,128)S(1)} %collective-permute-done.a_3_, f32[16,128]{1,0:T(8,128)S(1)} %collective-permute-done.1.a_4_, ...), custom_call_target="tpu_custom_call" | custom-call | tf_op jit(solution)/shard_map/update/pallas_call | solution.py:573
  62.5 3.2 %traces.3 = (f32[12,16,1152]{2,1,0:T(8,128)S(1)}, f32[12,16,1152]{2,1,0:T(8,128)S(1)}, f32[12,16,1152]{2,1,0:T(8,128)S(1)}, f32[12,8,2304]{2,1,0:T(8,128)S(1)}) custom-call(s32[12]{0:T(128)S(1)} %copy-done.18, s32[1,2]{1,0:T(1,128)S(1)} %bitcast.5, f32[8,16,27648]{2,1,0:T(8,128)S(1)} %update.1.a_2_.a_6_, bf16[2,2,32,128]{3,2,1,0:T(8,128)(2,1)S(1)} %copy-done.12, ...), custom_call_target="tpu_custom_call" | custom-call | tf_op jit(solution)/shard_map/traces/pallas_call | solution.py:573
  65.7 0.7 collective-permute-start.9
  66.4 1.9 %collective-permute-start.10 = (f32[12,16,1152]{2,1,0:T(8,128)S(1)}, f32[12,16,1152]{2,1,0:T(8,128)S(1)}, u32[]{:S(2)}, u32[]{:S(2)}) collective-permute-start(f32[12,16,1152]{2,1,0:T(8,128)S(1)} %get-tuple-element.28), channel_id=1, source_target_pairs={{0,8},{8,16},{16,24},{1,9},{9,17},{17,25},{2,10},{10,18},{18,26},{... | collective-permute-start | bytes 2654216 | tf_op jit(solution)/shard_map/ppermute | solution.py:641
  68.3 3.6 %collective-permute-start.11 = (f32[12,16,1152]{2,1,0:T(8,128)S(1)}, f32[12,16,1152]{2,1,0:T(8,128)S(1)}, u32[]{:S(2)}, u32[]{:S(2)}) collective-permute-start(f32[12,16,1152]{2,1,0:T(8,128)S(1)} %get-tuple-element.30), channel_id=1, source_target_pairs={{8,0},{16,8},{24,16},{9,1},{17,9},{25,17},{10,2},{18,10},{26,18},{... | collective-permute-start | bytes 2654216 | tf_op jit(solution)/shard_map/ppermute | solution.py:642
  72.0 17.2 %inner_increments.3 = (bf16[8,16,27648]{2,1,0:T(8,128)(2,1)S(1)}, f32[16,128]{1,0:T(8,128)S(1)}) custom-call(s32[12]{0:T(128)S(1)} %copy-done.18, s32[1,2]{1,0:T(1,128)S(1)} %bitcast.6, f32[8,16,27648]{2,1,0:T(8,128)S(1)} %update.1.a_2_.a_6_, f32[8,2304]{1,0:T(8,128)S(1)} %copy-done.5, f32[128,128]{1,0:T(8,128)S(1)} %copy-done.11, ...), custom_call_target="tpu_custom_call" | custom-call | tf_op jit(solution)/shard_map/inner_increments/pallas_call | solution.py:573
  89.2 3.7 %collective-permute-start.8 = (f32[16,128]{1,0:T(8,128)S(1)}, f32[16,128]{1,0:T(8,128)S(1)}, u32[]{:S(2)}, u32[]{:S(2)}) collective-permute-start(f32[16,128]{1,0:T(8,128)S(1)} %get-tuple-element.25.a_2_), channel_id=1, source_target_pairs={{0,3},{1,2},{2,1},{3,0},{4,7},{5,6},{6,5},{7,4},{8,11},{9,10},{10,... | collective-permute-start | bytes 24584 | tf_op jit(solution)/shard_map/ppermute | solution.py:636
  92.9 1.8 %collective-permute-done.8.a_5_ = f32[16,128]{1,0:T(8,128)S(1)} collective-permute-done((f32[16,128]{1,0:T(8,128)S(1)}, f32[16,128]{1,0:T(8,128)S(1)}, u32[]{:S(2)}, u32[]{:S(2)}) %collective-permute-start.8) | collective-permute-done | bytes 8224 | tf_op jit(solution)/shard_map/ppermute | solution.py:636
  94.7 2.7 %collective-permute-done.7.a_4_ = f32[16,128]{1,0:T(8,128)S(1)} collective-permute-done((f32[16,128]{1,0:T(8,128)S(1)}, f32[16,128]{1,0:T(8,128)S(1)}, u32[]{:S(2)}, u32[]{:S(2)}) %collective-permute-start.7) | collective-permute-done | bytes 8224 | tf_op jit(solution)/shard_map/ppermute | solution.py:636
  97.4 0.9 collective-permute-done.6.a_3_
  98.4 21.2 %last_update.1 = (f32[8,16,27648]{2,1,0:T(8,128)}, f32[16,128]{1,0:T(8,128)S(1)}) custom-call(s32[12]{0:T(128)S(1)} %copy-done.18, s32[1,2]{1,0:T(1,128)S(1)} %bitcast.7, f32[16,128]{1,0:T(8,128)S(1)} %get-tuple-element.25.a_2_, f32[16,128]{1,0:T(8,128)S(1)} %collective-permute-done.6.a_3_, f32[16,128]{1,0:T(8,128)S(1)} %collective-permute-done.7.a_4_, ...), custom_call_target="tpu_custom_call" | custom-call | tf_op jit(solution)/shard_map/last_update/pallas_call | solution.py:573
  119.6 3.6 %collective-permute-start.14 = (f32[16,128]{1,0:T(8,128)S(1)}, f32[16,128]{1,0:T(8,128)S(1)}, u32[]{:S(2)}, u32[]{:S(2)}) collective-permute-start(f32[16,128]{1,0:T(8,128)S(1)} %get-tuple-element.32.a_1_), channel_id=1, source_target_pairs={{0,3},{1,2},{2,1},{3,0},{4,7},{5,6},{6,5},{7,4},{8,11},{9,10},{10,... | collective-permute-start | bytes 24584 | tf_op jit(solution)/shard_map/ppermute | solution.py:636
  123.2 0.8 collective-permute-start.12
  123.9 1.1 collective-permute-done.14.a_4_
  125.0 2.7 %collective-permute-done.13.a_3_ = f32[16,128]{1,0:T(8,128)S(1)} collective-permute-done((f32[16,128]{1,0:T(8,128)S(1)}, f32[16,128]{1,0:T(8,128)S(1)}, u32[]{:S(2)}, u32[]{:S(2)}) %collective-permute-start.13) | collective-permute-done | bytes 8224 | tf_op jit(solution)/shard_map/ppermute | solution.py:636
  128.9 2.2 %macroscopic.1 = (f32[8,8,16]{2,1,0:T(8,128)}, f32[1,8]{1,0:T(1,128)}) custom-call(s32[1,2]{1,0:T(1,128)} %bitcast.1, f32[16,128]{1,0:T(8,128)} %copy-done.19, f32[16,128]{1,0:T(8,128)} %copy-done.22, f32[16,128]{1,0:T(8,128)} %copy-done.21, f32[16,128]{1,0:T(8,128)} %copy-done.20, f32[2,8,128]{2,1,0:T(8,128)} %constant.22.clone.a_13_.a_5_), custom_call_target="tpu_custom_call" | custom-call | tf_op jit(solution)/shard_map/macroscopic/pallas_call | solution.py:653
  (51 shorter events, 1.9 us)
Async XLA Ops:
  0.6 18.4 %copy-start.18 = (s32[12]{0:T(128)S(1)}, s32[12]{0:T(128)}, u32[]{:S(2)}) copy-start(s32[12]{0:T(128)} %a_0_.11) | copy-start | bytes 148
  0.6 18.4 %copy-start.16 = (s32[2,1]{0,1:T(1,128)S(1)}, s32[2,1]{0,1:T(1,128)}, u32[]{:S(2)}) copy-start(s32[2,1]{0,1:T(1,128)} %param.15) | copy-start | bytes 28
  0.7 5.0 %copy-start = (f32[8,16,27648]{2,1,0:T(8,128)S(1)}, f32[8,16,27648]{2,1,0:T(8,128)}, u32[]{:S(2)}) copy-start(f32[8,16,27648]{2,1,0:T(8,128)} %a_6_.3) | copy-start | bytes 42467332
  5.7 1.0 copy-start.4
  8.7 10.3 %copy-start.1 = (f32[8,16,27648]{2,1,0:T(8,128)S(1)}, f32[8,16,27648]{2,1,0:T(8,128)}, u32[]{:S(2)}) copy-start(f32[8,16,27648]{2,1,0:T(8,128)} %a_6_.3) | copy-start | bytes 42467332
  8.7 10.4 %copy-start.5 = (f32[8,2304]{1,0:T(8,128)S(1)}, f32[8,2304]{1,0:T(8,128)}, u32[]{:S(2)}) copy-start(f32[8,2304]{1,0:T(8,128)} %constant.20.clone.a_3_.a_12_) | copy-start | bytes 221188
  8.7 10.4 %copy-start.6 = (f32[3,128,128]{2,1,0:T(8,128)S(1)}, f32[3,128,128]{2,1,0:T(8,128)}, u32[]{:S(2)}) copy-start(f32[3,128,128]{2,1,0:T(8,128)} %constant.24.clone.a_6_) | copy-start | bytes 589828
  8.7 40.2 %copy-start.13 = (f32[2,8,128]{2,1,0:T(8,128)S(1)}, f32[2,8,128]{2,1,0:T(8,128)}, u32[]{:S(2)}) copy-start(f32[2,8,128]{2,1,0:T(8,128)} %constant.22.clone.a_13_.a_5_) | copy-start | bytes 24580
  8.7 40.2 %copy-start.14 = (f32[2,16,128]{2,1,0:T(8,128)S(1)}, f32[2,16,128]{2,1,0:T(8,128)}, u32[]{:S(2)}) copy-start(f32[2,16,128]{2,1,0:T(8,128)} %constant.26.clone.a_15_) | copy-start | bytes 49156
  11.9 37.0 %collective-permute-start.3 = (f32[12,8,2304]{2,1,0:T(8,128)S(1)}, f32[12,8,2304]{2,1,0:T(8,128)S(1)}, u32[]{:S(2)}, u32[]{:S(2)}) collective-permute-start(f32[12,8,2304]{2,1,0:T(8,128)S(1)} %get-tuple-element.21), channel_id=1, source_target_pairs={{0,4},{4,0},{1,5},{5,1},{2,6},{6,2},{3,7},{7,3},{8,12},{12,8},{9,1... | collective-permute-start | bytes 2654216 | tf_op jit(solution)/shard_map/ppermute | solution.py:640
  13.5 35.4 %collective-permute-start.4 = (f32[12,16,1152]{2,1,0:T(8,128)S(1)}, f32[12,16,1152]{2,1,0:T(8,128)S(1)}, u32[]{:S(2)}, u32[]{:S(2)}) collective-permute-start(f32[12,16,1152]{2,1,0:T(8,128)S(1)} %get-tuple-element.22), channel_id=1, source_target_pairs={{0,8},{8,16},{16,24},{1,9},{9,17},{17,25},{2,10},{10,18},{18,26},{... | collective-permute-start | bytes 2654216 | tf_op jit(solution)/shard_map/ppermute | solution.py:641
  15.4 33.5 %collective-permute-start.5 = (f32[12,16,1152]{2,1,0:T(8,128)S(1)}, f32[12,16,1152]{2,1,0:T(8,128)S(1)}, u32[]{:S(2)}, u32[]{:S(2)}) collective-permute-start(f32[12,16,1152]{2,1,0:T(8,128)S(1)} %get-tuple-element.24), channel_id=1, source_target_pairs={{8,0},{16,8},{24,16},{9,1},{17,9},{25,17},{10,2},{18,10},{26,18},{... | collective-permute-start | bytes 2654216 | tf_op jit(solution)/shard_map/ppermute | solution.py:642
  19.1 1.7 %copy-start.2 = (bf16[9,512,256]{2,1,0:T(8,128)(2,1)S(1)}, bf16[9,512,256]{2,1,0:T(8,128)(2,1)}, u32[]{:S(2)}) copy-start(bf16[9,512,256]{2,1,0:T(8,128)(2,1)} %constant.29.clone.a_7_) | copy-start | bytes 7077892
  20.8 0.9 copy-start.8
  22.5 26.4 %copy-start.7 = (f32[2,128,128]{2,1,0:T(8,128)S(1)}, f32[2,128,128]{2,1,0:T(8,128)}, u32[]{:S(2)}) copy-start(f32[2,128,128]{2,1,0:T(8,128)} %constant.25.clone.a_14_) | copy-start | bytes 393220
  39.7 5.5 %collective-permute-start.2 = (f32[16,128]{1,0:T(8,128)S(1)}, f32[16,128]{1,0:T(8,128)S(1)}, u32[]{:S(2)}, u32[]{:S(2)}) collective-permute-start(f32[16,128]{1,0:T(8,128)S(1)} %get-tuple-element.19.a_2_), channel_id=1, source_target_pairs={{0,3},{1,2},{2,1},{3,0},{4,7},{5,6},{6,5},{7,4},{8,11},{9,10},{10,... | collective-permute-start | bytes 24584 | tf_op jit(solution)/shard_map/ppermute | solution.py:636
  43.4 4.5 %collective-permute-start.1 = (f32[16,128]{1,0:T(8,128)S(1)}, f32[16,128]{1,0:T(8,128)S(1)}, u32[]{:S(2)}, u32[]{:S(2)}) collective-permute-start(f32[16,128]{1,0:T(8,128)S(1)} %get-tuple-element.19.a_2_), channel_id=1, source_target_pairs={{0,2},{1,3},{2,0},{3,1},{4,6},{5,7},{6,4},{7,5},{8,10},{9,11},{10,... | collective-permute-start | bytes 24584 | tf_op jit(solution)/shard_map/ppermute | solution.py:636
  45.2 3.7 %collective-permute-start = (f32[16,128]{1,0:T(8,128)S(1)}, f32[16,128]{1,0:T(8,128)S(1)}, u32[]{:S(2)}, u32[]{:S(2)}) collective-permute-start(f32[16,128]{1,0:T(8,128)S(1)} %get-tuple-element.19.a_2_), channel_id=1, source_target_pairs={{0,1},{1,0},{2,3},{3,2},{4,5},{5,4},{6,7},{7,6},{8,9},{9,8},{10,11... | collective-permute-start | bytes 24584 | tf_op jit(solution)/shard_map/ppermute | solution.py:636
  62.4 9.5 %copy-start.3 = (bf16[9,512,256]{2,1,0:T(8,128)(2,1)S(1)}, bf16[9,512,256]{2,1,0:T(8,128)(2,1)}, u32[]{:S(2)}) copy-start(bf16[9,512,256]{2,1,0:T(8,128)(2,1)} %constant.29.clone.a_7_) | copy-start | bytes 7077892
  62.4 9.5 %copy-start.9 = (bf16[3,128,128]{2,1,0:T(8,128)(2,1)S(1)}, bf16[3,128,128]{2,1,0:T(8,128)(2,1)}, u32[]{:S(2)}) copy-start(bf16[3,128,128]{2,1,0:T(8,128)(2,1)} %constant.23.clone.a_5_) | copy-start | bytes 294916
  62.5 9.5 %copy-start.11 = (f32[128,128]{1,0:T(8,128)S(1)}, f32[128,128]{1,0:T(8,128)}, u32[]{:S(2)}) copy-start(f32[128,128]{1,0:T(8,128)} %constant.21.clone.a_4_) | copy-start | bytes 196612
  65.7 32.7 %collective-permute-start.9 = (f32[12,8,2304]{2,1,0:T(8,128)S(1)}, f32[12,8,2304]{2,1,0:T(8,128)S(1)}, u32[]{:S(2)}, u32[]{:S(2)}) collective-permute-start(f32[12,8,2304]{2,1,0:T(8,128)S(1)} %get-tuple-element.27), channel_id=1, source_target_pairs={{0,4},{4,0},{1,5},{5,1},{2,6},{6,2},{3,7},{7,3},{8,12},{12,8},{9,1... | collective-permute-start | bytes 2654216 | tf_op jit(solution)/shard_map/ppermute | solution.py:640
  66.4 32.0 %collective-permute-start.10 = (f32[12,16,1152]{2,1,0:T(8,128)S(1)}, f32[12,16,1152]{2,1,0:T(8,128)S(1)}, u32[]{:S(2)}, u32[]{:S(2)}) collective-permute-start(f32[12,16,1152]{2,1,0:T(8,128)S(1)} %get-tuple-element.28), channel_id=1, source_target_pairs={{0,8},{8,16},{16,24},{1,9},{9,17},{17,25},{2,10},{10,18},{18,26},{... | collective-permute-start | bytes 2654216 | tf_op jit(solution)/shard_map/ppermute | solution.py:641
  68.3 30.1 %collective-permute-start.11 = (f32[12,16,1152]{2,1,0:T(8,128)S(1)}, f32[12,16,1152]{2,1,0:T(8,128)S(1)}, u32[]{:S(2)}, u32[]{:S(2)}) collective-permute-start(f32[12,16,1152]{2,1,0:T(8,128)S(1)} %get-tuple-element.30), channel_id=1, source_target_pairs={{8,0},{16,8},{24,16},{9,1},{17,9},{25,17},{10,2},{18,10},{26,18},{... | collective-permute-start | bytes 2654216 | tf_op jit(solution)/shard_map/ppermute | solution.py:642
  89.2 5.5 %collective-permute-start.8 = (f32[16,128]{1,0:T(8,128)S(1)}, f32[16,128]{1,0:T(8,128)S(1)}, u32[]{:S(2)}, u32[]{:S(2)}) collective-permute-start(f32[16,128]{1,0:T(8,128)S(1)} %get-tuple-element.25.a_2_), channel_id=1, source_target_pairs={{0,3},{1,2},{2,1},{3,0},{4,7},{5,6},{6,5},{7,4},{8,11},{9,10},{10,... | collective-permute-start | bytes 24584 | tf_op jit(solution)/shard_map/ppermute | solution.py:636
  92.9 4.5 %collective-permute-start.7 = (f32[16,128]{1,0:T(8,128)S(1)}, f32[16,128]{1,0:T(8,128)S(1)}, u32[]{:S(2)}, u32[]{:S(2)}) collective-permute-start(f32[16,128]{1,0:T(8,128)S(1)} %get-tuple-element.25.a_2_), channel_id=1, source_target_pairs={{0,2},{1,3},{2,0},{3,1},{4,6},{5,7},{6,4},{7,5},{8,10},{9,11},{10,... | collective-permute-start | bytes 24584 | tf_op jit(solution)/shard_map/ppermute | solution.py:636
  94.7 3.7 %collective-permute-start.6 = (f32[16,128]{1,0:T(8,128)S(1)}, f32[16,128]{1,0:T(8,128)S(1)}, u32[]{:S(2)}, u32[]{:S(2)}) collective-permute-start(f32[16,128]{1,0:T(8,128)S(1)} %get-tuple-element.25.a_2_), channel_id=1, source_target_pairs={{0,1},{1,0},{2,3},{3,2},{4,5},{5,4},{6,7},{7,6},{8,9},{9,8},{10,11... | collective-permute-start | bytes 24584 | tf_op jit(solution)/shard_map/ppermute | solution.py:636
  119.6 8.2 %copy-start.19 = (f32[16,128]{1,0:T(8,128)}, f32[16,128]{1,0:T(8,128)S(1)}, u32[]{:S(2)}) copy-start(f32[16,128]{1,0:T(8,128)S(1)} %get-tuple-element.32.a_1_) | copy-start | bytes 24580
  119.6 5.4 %collective-permute-start.14 = (f32[16,128]{1,0:T(8,128)S(1)}, f32[16,128]{1,0:T(8,128)S(1)}, u32[]{:S(2)}, u32[]{:S(2)}) collective-permute-start(f32[16,128]{1,0:T(8,128)S(1)} %get-tuple-element.32.a_1_), channel_id=1, source_target_pairs={{0,3},{1,2},{2,1},{3,0},{4,7},{5,6},{6,5},{7,4},{8,11},{9,10},{10,... | collective-permute-start | bytes 24584 | tf_op jit(solution)/shard_map/ppermute | solution.py:636
  123.2 4.5 %collective-permute-start.13 = (f32[16,128]{1,0:T(8,128)S(1)}, f32[16,128]{1,0:T(8,128)S(1)}, u32[]{:S(2)}, u32[]{:S(2)}) collective-permute-start(f32[16,128]{1,0:T(8,128)S(1)} %get-tuple-element.32.a_1_), channel_id=1, source_target_pairs={{0,2},{1,3},{2,0},{3,1},{4,6},{5,7},{6,4},{7,5},{8,10},{9,11},{10,... | collective-permute-start | bytes 24584 | tf_op jit(solution)/shard_map/ppermute | solution.py:636
  123.2 4.6 %collective-permute-start.12 = (f32[16,128]{1,0:T(8,128)S(1)}, f32[16,128]{1,0:T(8,128)S(1)}, u32[]{:S(2)}, u32[]{:S(2)}) collective-permute-start(f32[16,128]{1,0:T(8,128)S(1)} %get-tuple-element.32.a_1_), channel_id=1, source_target_pairs={{0,1},{1,0},{2,3},{3,2},{4,5},{5,4},{6,7},{7,6},{8,9},{9,8},{10,11... | collective-permute-start | bytes 24584 | tf_op jit(solution)/shard_map/ppermute | solution.py:636
  125.0 2.7 %copy-start.20 = (f32[16,128]{1,0:T(8,128)}, f32[16,128]{1,0:T(8,128)S(1)}, u32[]{:S(2)}) copy-start(f32[16,128]{1,0:T(8,128)S(1)} %collective-permute-done.14.a_4_) | copy-start | bytes 24580
  (6 other events, 4.1 us)

commit v10 on v9

--- a/solution.py
+++ b/solution.py
@@ -306,20 +306,16 @@
     return ref[:, :, first : first + lanes].reshape(NODE_COUNT, lanes)
 
 
-def trace_kernel(
-    count, order, codes, f_ref, trace_ref, mirror_ref, right_ref, left_ref, turned_ref, axial_ref
-):
+def trace_kernel(count, order, codes, f_ref, trace_ref, right_ref, left_ref, axial_ref):
     row, place = places_of()
     for s in range(count):
         for first, lanes, side in PIECES:
             narrow = nodes_of(f_ref, s * PLANE + first, lanes).astype(BF16)
             send_piece(s, first, lanes, side, place, narrow, trace_ref, right_ref, left_ref, axial_ref)
-    turn_traces(count, row, mirror_ref, left_ref, turned_ref)
-
-
-def inner_kernel(
-    count, order, codes, f_ref, rows_ref, pos_ref, radial_ref, axial_m_ref, rot_ref,
-    out_ref, mom_ref, sums_ref, table_ref, inverse_ref, pad_ref, lhs_ref,
+
+
+def moment_kernel(
+    count, order, codes, f_ref, left_ref, rows_ref, mirror_ref, mom_ref, turned_ref, sums_ref, table_ref
 ):
     step = pl.program_id(0)
     row, place = places_of()
@@ -327,6 +323,32 @@
     @pl.when(step == 0)
     def _():
         clear_sums(sums_ref)
+
+    turn_traces(count, row, mirror_ref, left_ref, turned_ref)
+    speeds = [slot_speed(order, step * count + s) for s in range(count)]
+    for j in range(0, PLANE, 128):
+        at = pl.ds(j, 128)
+        for r in range(NODES):
+            sums = [sums_ref[k, r, :, at] for k in range(5)]
+            for s in range(count):
+                sums = add_speed_sums(f_ref[r, :, pl.ds(s * PLANE + j, 128)], speeds[s], sums)
+            for k in range(5):
+                sums_ref[k, r, :, at] = sums[k]
+
+    @pl.when(step == pl.num_programs(0) - 1)
+    def _():
+        finish_moments(sums_ref, rows_ref, table_ref, mom_ref)
+
+
+def inner_kernel(
+    count, order, codes, f_ref, rows_ref, pos_ref, radial_ref, axial_m_ref, rot_ref,
+    out_ref, inverse_ref, pad_ref, lhs_ref,
+):
+    step = pl.program_id(0)
+    row, place = places_of()
+
+    @pl.when(step == 0)
+    def _():
         pad_ref[:, :, 0:128] = jnp.zeros((count, NODE_COUNT, 128), BF16)
         pad_ref[:, :, 128 + PLANE :] = jnp.zeros((count, NODE_COUNT, 128), BF16)
         inverse_ref[...] = 1.0 / (ELEMENT_WIDTH * (row.astype(F32) + pos_ref[...]))
@@ -362,18 +384,6 @@
                 change = turned[s * NODE_COUNT : (s + 1) * NODE_COUNT, inside : inside + lanes]
                 change = change + dot(lhs_ref[s, side], both)
                 out_ref[:, :, here : here + lanes] = change.astype(BF16).reshape(NODES, LOCAL_Z, lanes)
-            for j in range(first, first + lanes, 128):
-                at = pl.ds(j, 128)
-                for r in range(NODES):
-                    sums = [sums_ref[k, r, :, at] for k in range(5)]
-                    for s in range(count):
-                        sums = add_speed_sums(f_ref[r, :, pl.ds(s * PLANE + j, 128)], speeds[s], sums)
-                    for k in range(5):
-                        sums_ref[k, r, :, at] = sums[k]
-
-    @pl.when(step == pl.num_programs(0) - 1)
-    def _():
-        finish_moments(sums_ref, rows_ref, table_ref, mom_ref)
 
 
 def total_of(parts):
@@ -544,10 +554,12 @@
     verts = lax.axis_size("vert")
     assert lax.axis_size("gz") == 2
     codes = edge_codes.T
-    rows, pos, edge = jnp.asarray(ROWS), jnp.asarray(NODE_POS), jnp.asarray(EDGE)
-    radial_m, axial_m = jnp.asarray(RADIAL_M), jnp.asarray(AXIAL_M)
-    ghost_r, ghost_z = jnp.asarray(GHOST_R), jnp.asarray(GHOST_Z)
-    trace_m, mirror_m, rot_m = jnp.asarray(TRACE_M), jnp.asarray(MIRROR_M), jnp.asarray(ROTATION_M)
+    fixed = lambda x: pltpu.with_memory_space_constraint(jnp.asarray(x), pltpu.HBM)
+    codes, z_order = fixed(codes), fixed(z_order)
+    rows, pos, edge = fixed(ROWS), fixed(NODE_POS), fixed(EDGE)
+    radial_m, axial_m = fixed(RADIAL_M), fixed(AXIAL_M)
+    ghost_r, ghost_z = fixed(GHOST_R), fixed(GHOST_Z)
+    trace_m, mirror_m, rot_m = fixed(TRACE_M), fixed(MIRROR_M), fixed(ROTATION_M)
 
     def slab(count):
         return pl.BlockSpec((NODES, LOCAL_Z, count * PLANE), lambda i, *n: (0, 0, i))
@@ -587,28 +599,34 @@
     def all_whole(tables):
         return [whole(x.shape) for x in tables]
 
-    def traces_of(f, limit):
+    def traces_of(f):
         return call(
-            lambda *a: trace_kernel(group, *a), "traces", group, limit, [slab(group)] + all_whole([trace_m, mirror_m]),
-            trace_specs(group), trace_shapes, [], [f, trace_m, mirror_m],
+            lambda *a: trace_kernel(group, *a), "traces", group, 20, [slab(group)] + all_whole([trace_m]),
+            [radial_spec(group), radial_spec(group), axial_spec(group)], [radial_shape, radial_shape, axial_shape],
+            [], [f, trace_m],
         )
 
-    def inner(f, limit):
-        group = math.gcd(slots, 2)
+    def moments_of(f, left):
+        return call(
+            lambda *a: moment_kernel(group, *a), "moments", group, 20,
+            [slab(group), radial_spec(group)] + all_whole([rows, mirror_m]),
+            [mom_spec, radial_spec(group)], [mom_shape, radial_shape],
+            [pltpu.VMEM((5, NODES, LOCAL_Z, PLANE), F32), square], [f, left, rows, mirror_m],
+        )
+
+    def inner(f):
         tables = [rows, pos, radial_m, axial_m, rot_m]
         scratch = [
-            pltpu.VMEM((5, NODES, LOCAL_Z, PLANE), F32),
-            square,
             square,
             pltpu.VMEM((group, NODE_COUNT, PLANE + 256), BF16),
             pltpu.VMEM((group, 2, NODE_COUNT, 2 * NODE_COUNT), BF16),
         ]
         return call(
-            lambda *a: inner_kernel(group, *a), "inner_increments", group, limit, [slab(group)] + all_whole(tables),
-            [slab(group), mom_spec], [jax.ShapeDtypeStruct(f.shape, BF16), mom_shape], scratch, [f] + tables,
+            lambda *a: inner_kernel(group, *a), "inner_increments", group, 20, [slab(group)] + all_whole(tables),
+            slab(group), jax.ShapeDtypeStruct(f.shape, BF16), scratch, [f] + tables,
         )
 
-    def outer(f, change, ghosts, parts, last, limit):
+    def outer(f, change, ghosts, parts, last):
         count = 1 if last else math.gcd(slots, 2)
         tables = [rows, edge, ghost_r, ghost_z]
         scratch = [
@@ -622,7 +640,7 @@
             square,
         ]
         return call(
-            lambda *a: outer_kernel(count, len(parts), last, *a), "last_update" if last else "update", count, limit,
+            lambda *a: outer_kernel(count, len(parts), last, *a), "last_update" if last else "update", count, 20,
             [mom_spec] * len(parts) + [slab(count), slab(count), axial_spec(count)] + [radial_spec(count)] * 3
             + all_whole(tables),
             [slab(count)] + ([mom_spec] if last else []), [big_shape] + ([mom_shape] if last else []),
@@ -636,19 +654,22 @@
             parts.append(lax.ppermute(moments, "vert", [(i, i ^ shift) for i in range(verts)]))
         return parts
 
-    def halo(right, left, turned, axial):
+    def halo(right, left, axial):
         from_axial = lax.ppermute(axial, "gz", [(0, 1), (1, 0)])
         from_left = lax.ppermute(right, "row", [(i, i + 1) for i in range(rows_total - 1)])
         from_right = lax.ppermute(left, "row", [(i + 1, i) for i in range(rows_total - 1)])
-        return from_axial, from_left, turned, from_right
+        return from_axial, from_left, from_right
 
     current = distribution
     for number in range(STEPS):
         last = number == STEPS - 1
-        ghosts = halo(*traces_of(current, 20))
-        change, moments = inner(current, 21)
+        traces = traces_of(current)
+        from_axial, from_left, from_right = halo(*traces)
+        moments, turned = moments_of(current, traces[1])
         parts = spread(moments)
-        current, *final = outer(current, change, ghosts, parts, last, 20)
+        change = inner(current)
+        ghosts = [from_axial, from_left, turned, from_right]
+        current, *final = outer(current, change, ghosts, parts, last)
     parts = spread(final[0])
     macro, flux = pl.pallas_call(
         lambda *a: last_kernel(len(parts), *a),

time: 132 us -> 125 us (0.947)
  waiting for transfers between devices: 14.8 us -> 6.14 us
  Pallas kernels: 77.6 us -> 84.8 us
  local copies, waits for them, and re-layouts: 12.7 us -> 6.19 us
  starting transfers between devices: 25.1 us -> 26.7 us
    ppermute x9, waiting for transfers between devices: 14.7 us -> 6.12 us  [spread(): lax.ppermute(moments, 'vert', [(i, i ^ shift) for i in range(verts)])]
    pallas_call x6 -> x8, Pallas kernels: 75.5 us -> 82.6 us  [call(): pl.pallas_call(body, grid_spec=pltpu.PrefetchScalarGridSpec(num_scalar_pr...]
    unnamed x46 -> x10, local copies, waits for them, and re-layouts: 12.7 us -> 6.19 us
    ppermute x9, starting transfers between devices: 11.8 us -> 13.3 us  [spread(): lax.ppermute(moments, 'vert', [(i, i ^ shift) for i in range(verts)])]
  transfers between devices with their start and end apart: 15 -> 15, of which waited for: 8 -> 4; matrix products, arithmetic and copies ran while one was open for 0% -> 0% of each run, Pallas kernels for 26% -> 31%
where the time goes in v10:
time: 125 us
  Pallas kernels  84.8 us (68%)
  starting transfers between devices  26.7 us (21%)
  local copies, waits for them, and re-layouts  6.19 us (5%)
  waiting for transfers between devices  6.14 us (5%)
    pallas_call x8, Pallas kernels, call(): pl.pallas_call(body, grid_spec=pltpu.PrefetchScalarGridSpec(num_scalar_pr...  82.6 us
    ppermute x9, starting transfers between devices, spread(): lax.ppermute(moments, 'vert', [(i, i ^ shift) for i in range(verts)])  13.3 us
    ppermute x2, starting transfers between devices, halo(): lax.ppermute(left, 'row', [(i + 1, i) for i in range(rows_total - 1)])  7.46 us
    unnamed x10, local copies, waits for them, and re-layouts  6.19 us
    ppermute x9, waiting for transfers between devices, spread(): lax.ppermute(moments, 'vert', [(i, i ^ shift) for i in range(verts)])  6.12 us
    ppermute x2, starting transfers between devices, halo(): lax.ppermute(right, 'row', [(i, i + 1) for i in range(rows_total - 1)])  3.82 us
  transfers between devices with their start and end apart: 15, of which 4 were waited for; matrix products, arithmetic and copies ran while one was open for 0% of the time, Pallas kernels for 31%

profile of v10, /device:TPU:4, one launch (start us, length us, event | category | flops | bytes accessed | tf_op | source)
XLA Modules:
  0.0 124.7 jit_solution(15044823904138327975)
XLA Ops:
  0.6 0.0 copy-start
  0.6 5.0 %copy-done = f32[8,16,27648]{2,1,0:T(8,128)S(1)} copy-done((f32[8,16,27648]{2,1,0:T(8,128)S(1)}, f32[8,16,27648]{2,1,0:T(8,128)}, u32[]{:S(2)}) %copy-start) | copy-done | bytes 14155800
  5.7 3.7 %traces.2 = (f32[12,16,1152]{2,1,0:T(8,128)S(1)}, f32[12,16,1152]{2,1,0:T(8,128)S(1)}, f32[12,8,2304]{2,1,0:T(8,128)S(1)}) custom-call(s32[12]{0:T(128)} %a_0_.15, s32[1,2]{1,0:T(1,128)} %bitcast.1, f32[8,16,27648]{2,1,0:T(8,128)S(1)} %copy-done, bf16[2,2,32,128]{3,2,1,0:T(8,128)(2,1)} %constant.27.clone.a_3_), custom_call_target="tpu_custom_call" | custom-call | tf_op jit(solution)/shard_map/traces/pallas_call | solution.py:585
  9.4 1.6 %collective-permute-start.3 = (f32[12,8,2304]{2,1,0:T(8,128)S(1)}, f32[12,8,2304]{2,1,0:T(8,128)S(1)}, u32[]{:S(2)}, u32[]{:S(2)}) collective-permute-start(f32[12,8,2304]{2,1,0:T(8,128)S(1)} %get-tuple-element.19), channel_id=1, source_target_pairs={{0,4},{4,0},{1,5},{5,1},{2,6},{6,2},{3,7},{7,3},{8,12},{12,8},{9,1... | collective-permute-start | bytes 2654216 | tf_op jit(solution)/shard_map/ppermute | solution.py:658
  10.9 1.9 %collective-permute-start.4 = (f32[12,16,1152]{2,1,0:T(8,128)S(1)}, f32[12,16,1152]{2,1,0:T(8,128)S(1)}, u32[]{:S(2)}, u32[]{:S(2)}) collective-permute-start(f32[12,16,1152]{2,1,0:T(8,128)S(1)} %get-tuple-element.20), channel_id=1, source_target_pairs={{0,8},{8,16},{16,24},{1,9},{9,17},{17,25},{2,10},{10,18},{18,26},{... | collective-permute-start | bytes 2654216 | tf_op jit(solution)/shard_map/ppermute | solution.py:659
  12.9 3.6 %collective-permute-start.5 = (f32[12,16,1152]{2,1,0:T(8,128)S(1)}, f32[12,16,1152]{2,1,0:T(8,128)S(1)}, u32[]{:S(2)}, u32[]{:S(2)}) collective-permute-start(f32[12,16,1152]{2,1,0:T(8,128)S(1)} %get-tuple-element.17.a_3_), channel_id=1, source_target_pairs={{8,0},{16,8},{24,16},{9,1},{17,9},{25,17},{10,2},{18,10},{26,18},{... | collective-permute-start | bytes 2654216 | tf_op jit(solution)/shard_map/ppermute | solution.py:660
  16.5 9.1 %moments.2 = (f32[16,128]{1,0:T(8,128)S(1)}, f32[12,16,1152]{2,1,0:T(8,128)S(1)}) custom-call(s32[12]{0:T(128)} %a_0_.15, s32[1,2]{1,0:T(1,128)} %bitcast.2, f32[8,16,27648]{2,1,0:T(8,128)S(1)} %copy-done, f32[12,16,1152]{2,1,0:T(8,128)S(1)} %get-tuple-element.17.a_3_, f32[8,2304]{1,0:T(8,128)} %constant.20.clone.a_4_.a_3_.a_12_, ...), custom_call_target="tpu_custom_call" | custom-call | tf_op jit(solution)/shard_map/moments/pallas_call | solution.py:585
  25.7 3.7 %collective-permute-start.2 = (f32[16,128]{1,0:T(8,128)S(1)}, f32[16,128]{1,0:T(8,128)S(1)}, u32[]{:S(2)}, u32[]{:S(2)}) collective-permute-start(f32[16,128]{1,0:T(8,128)S(1)} %get-tuple-element.18.a_2_), channel_id=1, source_target_pairs={{0,3},{1,2},{2,1},{3,0},{4,7},{5,6},{6,5},{7,4},{8,11},{9,10},{10,... | collective-permute-start | bytes 24584 | tf_op jit(solution)/shard_map/ppermute | solution.py:654
  29.3 1.8 %collective-permute-done.2.a_5_ = f32[16,128]{1,0:T(8,128)S(1)} collective-permute-done((f32[16,128]{1,0:T(8,128)S(1)}, f32[16,128]{1,0:T(8,128)S(1)}, u32[]{:S(2)}, u32[]{:S(2)}) %collective-permute-start.2) | collective-permute-done | bytes 8224 | tf_op jit(solution)/shard_map/ppermute | solution.py:654
  31.2 10.4 %inner_increments.2.a_7_ = bf16[8,16,27648]{2,1,0:T(8,128)(2,1)S(1)} custom-call(s32[12]{0:T(128)} %a_0_.15, s32[1,2]{1,0:T(1,128)} %bitcast.3, f32[8,16,27648]{2,1,0:T(8,128)S(1)} %copy-done, f32[8,2304]{1,0:T(8,128)} %constant.20.clone.a_4_.a_3_.a_12_, f32[128,128]{1,0:T(8,128)} %constant.21.clone.a_4_, bf16[3,128,128]{2,1,0:T(8,128)(2,1)} %constant.23.clone.a_5_, ...), custom_call_target="tpu_custom_call" | custom-call | tf_op jit(solution)/shard_map/inner_increments/pallas_call | solution.py:585
  41.6 0.0 collective-permute-done.1.a_4_
  41.6 0.0 collective-permute-done.3.a_8_
  41.7 13.7 %update.1.a_2_.a_6_ = f32[8,16,27648]{2,1,0:T(8,128)S(1)} custom-call(s32[12]{0:T(128)} %a_0_.15, s32[1,2]{1,0:T(1,128)} %bitcast.4, f32[16,128]{1,0:T(8,128)S(1)} %get-tuple-element.18.a_2_, f32[16,128]{1,0:T(8,128)S(1)} %collective-permute-done.a_3_, f32[16,128]{1,0:T(8,128)S(1)} %collective-permute-done.1.a_4_, ...), custom_call_target="tpu_custom_call" | custom-call | tf_op jit(solution)/shard_map/update/pallas_call | solution.py:585
  55.3 3.7 %traces.3 = (f32[12,16,1152]{2,1,0:T(8,128)S(1)}, f32[12,16,1152]{2,1,0:T(8,128)S(1)}, f32[12,8,2304]{2,1,0:T(8,128)S(1)}) custom-call(s32[12]{0:T(128)} %a_0_.15, s32[1,2]{1,0:T(1,128)} %bitcast.5, f32[8,16,27648]{2,1,0:T(8,128)S(1)} %update.1.a_2_.a_6_, bf16[2,2,32,128]{3,2,1,0:T(8,128)(2,1)} %constant.27.clone.a_3_), custom_call_target="tpu_custom_call" | custom-call | tf_op jit(solution)/shard_map/traces/pallas_call | solution.py:585
  59.1 0.6 collective-permute-start.9
  59.7 1.9 %collective-permute-start.10 = (f32[12,16,1152]{2,1,0:T(8,128)S(1)}, f32[12,16,1152]{2,1,0:T(8,128)S(1)}, u32[]{:S(2)}, u32[]{:S(2)}) collective-permute-start(f32[12,16,1152]{2,1,0:T(8,128)S(1)} %get-tuple-element.25), channel_id=1, source_target_pairs={{0,8},{8,16},{16,24},{1,9},{9,17},{17,25},{2,10},{10,18},{18,26},{... | collective-permute-start | bytes 2654216 | tf_op jit(solution)/shard_map/ppermute | solution.py:659
  61.6 3.8 %collective-permute-start.11 = (f32[12,16,1152]{2,1,0:T(8,128)S(1)}, f32[12,16,1152]{2,1,0:T(8,128)S(1)}, u32[]{:S(2)}, u32[]{:S(2)}) collective-permute-start(f32[12,16,1152]{2,1,0:T(8,128)S(1)} %get-tuple-element.22.a_3_), channel_id=1, source_target_pairs={{8,0},{16,8},{24,16},{9,1},{17,9},{25,17},{10,2},{18,10},{26,18},{... | collective-permute-start | bytes 2654216 | tf_op jit(solution)/shard_map/ppermute | solution.py:660
  65.4 9.1 %moments.3 = (f32[16,128]{1,0:T(8,128)S(1)}, f32[12,16,1152]{2,1,0:T(8,128)S(1)}) custom-call(s32[12]{0:T(128)} %a_0_.15, s32[1,2]{1,0:T(1,128)} %bitcast.6, f32[8,16,27648]{2,1,0:T(8,128)S(1)} %update.1.a_2_.a_6_, f32[12,16,1152]{2,1,0:T(8,128)S(1)} %get-tuple-element.22.a_3_, f32[8,2304]{1,0:T(8,128)} %constant.20.clone.a_4_.a_3_.a_12_, ...), custom_call_target="tpu_custom_call" | custom-call | tf_op jit(solution)/shard_map/moments/pallas_call | solution.py:585
  74.6 3.7 %collective-permute-start.8 = (f32[16,128]{1,0:T(8,128)S(1)}, f32[16,128]{1,0:T(8,128)S(1)}, u32[]{:S(2)}, u32[]{:S(2)}) collective-permute-start(f32[16,128]{1,0:T(8,128)S(1)} %get-tuple-element.23.a_2_), channel_id=1, source_target_pairs={{0,3},{1,2},{2,1},{3,0},{4,7},{5,6},{6,5},{7,4},{8,11},{9,10},{10,... | collective-permute-start | bytes 24584 | tf_op jit(solution)/shard_map/ppermute | solution.py:654
  78.2 0.6 collective-permute-start.7
  78.9 1.2 collective-permute-done.8.a_5_
  80.1 0.9 collective-permute-start.6
  81.0 10.4 %inner_increments.3.a_7_ = bf16[8,16,27648]{2,1,0:T(8,128)(2,1)S(1)} custom-call(s32[12]{0:T(128)} %a_0_.15, s32[1,2]{1,0:T(1,128)} %bitcast.7, f32[8,16,27648]{2,1,0:T(8,128)S(1)} %update.1.a_2_.a_6_, f32[8,2304]{1,0:T(8,128)} %constant.20.clone.a_4_.a_3_.a_12_, f32[128,128]{1,0:T(8,128)} %constant.21.clone.a_4_, bf16[3,128,128]{2,1,0:T(8,128)(2,1)} %constant.23.clone.a_5_, ...), custom_call_target="tpu_custom_call" | custom-call | tf_op jit(solution)/shard_map/inner_increments/pallas_call | solution.py:585
  91.5 22.3 %last_update.1 = (f32[8,16,27648]{2,1,0:T(8,128)}, f32[16,128]{1,0:T(8,128)S(1)}) custom-call(s32[12]{0:T(128)} %a_0_.15, s32[1,2]{1,0:T(1,128)} %bitcast.8, f32[16,128]{1,0:T(8,128)S(1)} %get-tuple-element.23.a_2_, f32[16,128]{1,0:T(8,128)S(1)} %collective-permute-done.6.a_3_, f32[16,128]{1,0:T(8,128)S(1)} %collective-permute-done.7.a_4_, ...), custom_call_target="tpu_custom_call" | custom-call | tf_op jit(solution)/shard_map/last_update/pallas_call | solution.py:585
  113.8 2.9 %collective-permute-start.14 = (f32[16,128]{1,0:T(8,128)S(1)}, f32[16,128]{1,0:T(8,128)S(1)}, u32[]{:S(2)}, u32[]{:S(2)}) collective-permute-start(f32[16,128]{1,0:T(8,128)S(1)} %get-tuple-element.28.a_1_), channel_id=1, source_target_pairs={{0,3},{1,2},{2,1},{3,0},{4,7},{5,6},{6,5},{7,4},{8,11},{9,10},{10,... | collective-permute-start | bytes 24584 | tf_op jit(solution)/shard_map/ppermute | solution.py:654
  116.7 0.4 collective-permute-start.13
  117.1 1.1 collective-permute-start.12
  118.2 1.1 collective-permute-done.14.a_4_
  119.3 2.0 %collective-permute-done.13.a_3_ = f32[16,128]{1,0:T(8,128)S(1)} collective-permute-done((f32[16,128]{1,0:T(8,128)S(1)}, f32[16,128]{1,0:T(8,128)S(1)}, u32[]{:S(2)}, u32[]{:S(2)}) %collective-permute-start.13) | collective-permute-done | bytes 8224 | tf_op jit(solution)/shard_map/ppermute | solution.py:654
  121.3 0.6 copy-done.3
  121.9 0.6 copy-done.4
  122.5 2.2 %macroscopic.1 = (f32[8,8,16]{2,1,0:T(8,128)}, f32[1,8]{1,0:T(1,128)}) custom-call(s32[1,2]{1,0:T(1,128)} %bitcast.9, f32[16,128]{1,0:T(8,128)} %copy-done.1, f32[16,128]{1,0:T(8,128)} %copy-done.4, f32[16,128]{1,0:T(8,128)} %copy-done.3, f32[16,128]{1,0:T(8,128)} %copy-done.2, f32[2,8,128]{2,1,0:T(8,128)} %constant.22.clone.a_13_.a_5_), custom_call_target="tpu_custom_call" | custom-call | tf_op jit(solution)/shard_map/macroscopic/pallas_call | solution.py:674
  (17 shorter events, 0.0 us)
Async XLA Ops:
  0.6 5.0 %copy-start = (f32[8,16,27648]{2,1,0:T(8,128)S(1)}, f32[8,16,27648]{2,1,0:T(8,128)}, u32[]{:S(2)}) copy-start(f32[8,16,27648]{2,1,0:T(8,128)} %a_6_.3) | copy-start | bytes 42467332
  9.4 32.2 %collective-permute-start.3 = (f32[12,8,2304]{2,1,0:T(8,128)S(1)}, f32[12,8,2304]{2,1,0:T(8,128)S(1)}, u32[]{:S(2)}, u32[]{:S(2)}) collective-permute-start(f32[12,8,2304]{2,1,0:T(8,128)S(1)} %get-tuple-element.19), channel_id=1, source_target_pairs={{0,4},{4,0},{1,5},{5,1},{2,6},{6,2},{3,7},{7,3},{8,12},{12,8},{9,1... | collective-permute-start | bytes 2654216 | tf_op jit(solution)/shard_map/ppermute | solution.py:658
  10.9 30.7 %collective-permute-start.4 = (f32[12,16,1152]{2,1,0:T(8,128)S(1)}, f32[12,16,1152]{2,1,0:T(8,128)S(1)}, u32[]{:S(2)}, u32[]{:S(2)}) collective-permute-start(f32[12,16,1152]{2,1,0:T(8,128)S(1)} %get-tuple-element.20), channel_id=1, source_target_pairs={{0,8},{8,16},{16,24},{1,9},{9,17},{17,25},{2,10},{10,18},{18,26},{... | collective-permute-start | bytes 2654216 | tf_op jit(solution)/shard_map/ppermute | solution.py:659
  12.9 28.8 %collective-permute-start.5 = (f32[12,16,1152]{2,1,0:T(8,128)S(1)}, f32[12,16,1152]{2,1,0:T(8,128)S(1)}, u32[]{:S(2)}, u32[]{:S(2)}) collective-permute-start(f32[12,16,1152]{2,1,0:T(8,128)S(1)} %get-tuple-element.17.a_3_), channel_id=1, source_target_pairs={{8,0},{16,8},{24,16},{9,1},{17,9},{25,17},{10,2},{18,10},{26,18},{... | collective-permute-start | bytes 2654216 | tf_op jit(solution)/shard_map/ppermute | solution.py:660
  25.7 5.5 %collective-permute-start.2 = (f32[16,128]{1,0:T(8,128)S(1)}, f32[16,128]{1,0:T(8,128)S(1)}, u32[]{:S(2)}, u32[]{:S(2)}) collective-permute-start(f32[16,128]{1,0:T(8,128)S(1)} %get-tuple-element.18.a_2_), channel_id=1, source_target_pairs={{0,3},{1,2},{2,1},{3,0},{4,7},{5,6},{6,5},{7,4},{8,11},{9,10},{10,... | collective-permute-start | bytes 24584 | tf_op jit(solution)/shard_map/ppermute | solution.py:654
  29.3 12.3 %collective-permute-start.1 = (f32[16,128]{1,0:T(8,128)S(1)}, f32[16,128]{1,0:T(8,128)S(1)}, u32[]{:S(2)}, u32[]{:S(2)}) collective-permute-start(f32[16,128]{1,0:T(8,128)S(1)} %get-tuple-element.18.a_2_), channel_id=1, source_target_pairs={{0,2},{1,3},{2,0},{3,1},{4,6},{5,7},{6,4},{7,5},{8,10},{9,11},{10,... | collective-permute-start | bytes 24584 | tf_op jit(solution)/shard_map/ppermute | solution.py:654
  31.2 10.5 %collective-permute-start = (f32[16,128]{1,0:T(8,128)S(1)}, f32[16,128]{1,0:T(8,128)S(1)}, u32[]{:S(2)}, u32[]{:S(2)}) collective-permute-start(f32[16,128]{1,0:T(8,128)S(1)} %get-tuple-element.18.a_2_), channel_id=1, source_target_pairs={{0,1},{1,0},{2,3},{3,2},{4,5},{5,4},{6,7},{7,6},{8,9},{9,8},{10,11... | collective-permute-start | bytes 24584 | tf_op jit(solution)/shard_map/ppermute | solution.py:654
  59.1 32.4 %collective-permute-start.9 = (f32[12,8,2304]{2,1,0:T(8,128)S(1)}, f32[12,8,2304]{2,1,0:T(8,128)S(1)}, u32[]{:S(2)}, u32[]{:S(2)}) collective-permute-start(f32[12,8,2304]{2,1,0:T(8,128)S(1)} %get-tuple-element.24), channel_id=1, source_target_pairs={{0,4},{4,0},{1,5},{5,1},{2,6},{6,2},{3,7},{7,3},{8,12},{12,8},{9,1... | collective-permute-start | bytes 2654216 | tf_op jit(solution)/shard_map/ppermute | solution.py:658
  59.7 31.8 %collective-permute-start.10 = (f32[12,16,1152]{2,1,0:T(8,128)S(1)}, f32[12,16,1152]{2,1,0:T(8,128)S(1)}, u32[]{:S(2)}, u32[]{:S(2)}) collective-permute-start(f32[12,16,1152]{2,1,0:T(8,128)S(1)} %get-tuple-element.25), channel_id=1, source_target_pairs={{0,8},{8,16},{16,24},{1,9},{9,17},{17,25},{2,10},{10,18},{18,26},{... | collective-permute-start | bytes 2654216 | tf_op jit(solution)/shard_map/ppermute | solution.py:659
  61.6 29.9 %collective-permute-start.11 = (f32[12,16,1152]{2,1,0:T(8,128)S(1)}, f32[12,16,1152]{2,1,0:T(8,128)S(1)}, u32[]{:S(2)}, u32[]{:S(2)}) collective-permute-start(f32[12,16,1152]{2,1,0:T(8,128)S(1)} %get-tuple-element.22.a_3_), channel_id=1, source_target_pairs={{8,0},{16,8},{24,16},{9,1},{17,9},{25,17},{10,2},{18,10},{26,18},{... | collective-permute-start | bytes 2654216 | tf_op jit(solution)/shard_map/ppermute | solution.py:660
  74.6 5.5 %collective-permute-start.8 = (f32[16,128]{1,0:T(8,128)S(1)}, f32[16,128]{1,0:T(8,128)S(1)}, u32[]{:S(2)}, u32[]{:S(2)}) collective-permute-start(f32[16,128]{1,0:T(8,128)S(1)} %get-tuple-element.23.a_2_), channel_id=1, source_target_pairs={{0,3},{1,2},{2,1},{3,0},{4,7},{5,6},{6,5},{7,4},{8,11},{9,10},{10,... | collective-permute-start | bytes 24584 | tf_op jit(solution)/shard_map/ppermute | solution.py:654
  78.2 13.2 %collective-permute-start.7 = (f32[16,128]{1,0:T(8,128)S(1)}, f32[16,128]{1,0:T(8,128)S(1)}, u32[]{:S(2)}, u32[]{:S(2)}) collective-permute-start(f32[16,128]{1,0:T(8,128)S(1)} %get-tuple-element.23.a_2_), channel_id=1, source_target_pairs={{0,2},{1,3},{2,0},{3,1},{4,6},{5,7},{6,4},{7,5},{8,10},{9,11},{10,... | collective-permute-start | bytes 24584 | tf_op jit(solution)/shard_map/ppermute | solution.py:654
  80.1 11.4 %collective-permute-start.6 = (f32[16,128]{1,0:T(8,128)S(1)}, f32[16,128]{1,0:T(8,128)S(1)}, u32[]{:S(2)}, u32[]{:S(2)}) collective-permute-start(f32[16,128]{1,0:T(8,128)S(1)} %get-tuple-element.23.a_2_), channel_id=1, source_target_pairs={{0,1},{1,0},{2,3},{3,2},{4,5},{5,4},{6,7},{7,6},{8,9},{9,8},{10,11... | collective-permute-start | bytes 24584 | tf_op jit(solution)/shard_map/ppermute | solution.py:654
  113.8 7.5 %copy-start.1 = (f32[16,128]{1,0:T(8,128)}, f32[16,128]{1,0:T(8,128)S(1)}, u32[]{:S(2)}) copy-start(f32[16,128]{1,0:T(8,128)S(1)} %get-tuple-element.28.a_1_) | copy-start | bytes 24580
  113.8 5.4 %collective-permute-start.14 = (f32[16,128]{1,0:T(8,128)S(1)}, f32[16,128]{1,0:T(8,128)S(1)}, u32[]{:S(2)}, u32[]{:S(2)}) collective-permute-start(f32[16,128]{1,0:T(8,128)S(1)} %get-tuple-element.28.a_1_), channel_id=1, source_target_pairs={{0,3},{1,2},{2,1},{3,0},{4,7},{5,6},{6,5},{7,4},{8,11},{9,10},{10,... | collective-permute-start | bytes 24584 | tf_op jit(solution)/shard_map/ppermute | solution.py:654
  116.7 4.5 %collective-permute-start.13 = (f32[16,128]{1,0:T(8,128)S(1)}, f32[16,128]{1,0:T(8,128)S(1)}, u32[]{:S(2)}, u32[]{:S(2)}) collective-permute-start(f32[16,128]{1,0:T(8,128)S(1)} %get-tuple-element.28.a_1_), channel_id=1, source_target_pairs={{0,2},{1,3},{2,0},{3,1},{4,6},{5,7},{6,4},{7,5},{8,10},{9,11},{10,... | collective-permute-start | bytes 24584 | tf_op jit(solution)/shard_map/ppermute | solution.py:654
  117.1 4.2 %collective-permute-start.12 = (f32[16,128]{1,0:T(8,128)S(1)}, f32[16,128]{1,0:T(8,128)S(1)}, u32[]{:S(2)}, u32[]{:S(2)}) collective-permute-start(f32[16,128]{1,0:T(8,128)S(1)} %get-tuple-element.28.a_1_), channel_id=1, source_target_pairs={{0,1},{1,0},{2,3},{3,2},{4,5},{5,4},{6,7},{7,6},{8,9},{9,8},{10,11... | collective-permute-start | bytes 24584 | tf_op jit(solution)/shard_map/ppermute | solution.py:654
  119.3 2.0 %copy-start.2 = (f32[16,128]{1,0:T(8,128)}, f32[16,128]{1,0:T(8,128)S(1)}, u32[]{:S(2)}) copy-start(f32[16,128]{1,0:T(8,128)S(1)} %collective-permute-done.14.a_4_) | copy-start | bytes 24580
  121.3 0.6 copy-start.3
  121.9 0.6 copy-start.4

commit v11 on v10

--- a/solution.py
+++ b/solution.py
@@ -37,6 +37,7 @@
 PIECES = [(t, TILE, 0) for t in range(0, 1024, TILE)] + [(1024, 128, 0), (1152, 128, 1)] + [
     (t, TILE, 1) for t in range(1280, PLANE, TILE)
 ]
+HALF_PIECES = [(t, TILE) for t in range(0, 1024, TILE)] + [(1024, 128)]
 
 
 def legendre_pair(position, point_count):
@@ -138,7 +139,7 @@
     return (
         (-SCALE * radial).astype(ml_dtypes.bfloat16),
         (-SCALE * axial).astype(np.float32),
-        (SCALE * ghost_r).astype(np.float32),
+        (SCALE * ghost_r).astype(ml_dtypes.bfloat16),
         (SCALE * ghost_z).astype(np.float32),
         trace.astype(ml_dtypes.bfloat16),
     )
@@ -233,13 +234,7 @@
 def add_speed_sums(field, vz, sums):
     one = field * vz
     two = one * vz
-    return [
-        sums[0] + field,
-        sums[1] + one,
-        sums[2] + two,
-        sums[3] + two * vz,
-        sums[4] + field * jnp.abs(vz),
-    ]
+    return [sums[0] + field, sums[1] + one, sums[2] + two, sums[3] + two * vz]
 
 
 def finish_moments(sums_ref, rows_ref, table_ref, out_ref):
@@ -279,15 +274,6 @@
     return lax.axis_index("row"), lax.axis_index("gz")
 
 
-def send_piece(s, first, lanes, side, place, narrow, trace_ref, right_ref, left_ref, axial_ref):
-    got = dot(trace_ref[side, place], narrow)
-    if side == 1:
-        right_ref[s, :, first - HALF : first - HALF + lanes] = got[0:LOCAL_Z]
-    else:
-        left_ref[s, :, first : first + lanes] = got[0:LOCAL_Z]
-    axial_ref[s, :, first : first + lanes] = got[LOCAL_Z : LOCAL_Z + NODES]
-
-
 def turn_traces(count, row, mirror_ref, left_ref, turned_ref):
     @pl.when(row == 0)
     def _():
@@ -306,12 +292,20 @@
     return ref[:, :, first : first + lanes].reshape(NODE_COUNT, lanes)
 
 
-def trace_kernel(count, order, codes, f_ref, trace_ref, right_ref, left_ref, axial_ref):
+def trace_kernel(count, order, codes, f_ref, trace_ref, near_ref, far_ref, axial_ref):
     row, place = places_of()
+    even = lax.rem(row, 2) == 0
     for s in range(count):
-        for first, lanes, side in PIECES:
-            narrow = nodes_of(f_ref, s * PLANE + first, lanes).astype(BF16)
-            send_piece(s, first, lanes, side, place, narrow, trace_ref, right_ref, left_ref, axial_ref)
+        for first, lanes in HALF_PIECES:
+            got = []
+            for side in range(2):
+                here = side * HALF + first
+                narrow = nodes_of(f_ref, s * PLANE + here, lanes).astype(BF16)
+                got.append(dot(trace_ref[side, place], narrow))
+                axial_ref[s, :, here : here + lanes] = got[side][LOCAL_Z : LOCAL_Z + NODES]
+            left, right = got[0][0:LOCAL_Z], got[1][0:LOCAL_Z]
+            near_ref[s, :, first : first + lanes] = jnp.where(even, right, left)
+            far_ref[s, :, first : first + lanes] = jnp.where(even, left, right)
 
 
 def moment_kernel(
@@ -325,15 +319,20 @@
         clear_sums(sums_ref)
 
     turn_traces(count, row, mirror_ref, left_ref, turned_ref)
+    edge = pl.ds(pl.multiple_of(place * NODES, NODES), NODES)
     speeds = [slot_speed(order, step * count + s) for s in range(count)]
     for j in range(0, PLANE, 128):
         at = pl.ds(j, 128)
         for r in range(NODES):
-            sums = [sums_ref[k, r, :, at] for k in range(5)]
+            sums = [sums_ref[k, r, :, at] for k in range(4)]
+            gross = sums_ref[4, r, edge, at]
             for s in range(count):
-                sums = add_speed_sums(f_ref[r, :, pl.ds(s * PLANE + j, 128)], speeds[s], sums)
-            for k in range(5):
+                here = pl.ds(s * PLANE + j, 128)
+                sums = add_speed_sums(f_ref[r, :, here], speeds[s], sums)
+                gross = gross + f_ref[r, edge, here] * jnp.abs(speeds[s])
+            for k in range(4):
                 sums_ref[k, r, :, at] = sums[k]
+            sums_ref[4, r, edge, at] = gross
 
     @pl.when(step == pl.num_programs(0) - 1)
     def _():
@@ -444,26 +443,27 @@
 
 
 def ghost_rows(
-    s, vz, place, in_axial_ref, in_left_ref, in_turned_ref, in_right_ref, rows_ref, wall_ref, radial_ref, axial_ref
+    s, vz, row, place, in_axial_ref, in_near_ref, in_turned_ref, in_far_ref, rows_ref, wall_ref, radial_ref, axial_ref
 ):
     own = (place == 0) == (vz > 0)
+    even = lax.rem(row, 2) == 0
     strength = jnp.exp(-0.5 * vz * vz + jnp.zeros((NODES, 128), F32)) * wall_ref[...]
     for j in range(PLANE // 128):
         at = pl.ds(j * 128, 128)
         if j * 128 < HALF:
-            radial = in_right_ref[s, :, at]
+            radial = jnp.where(even, in_near_ref[s, :, at], in_far_ref[s, :, at])
         else:
             back = pl.ds(j * 128 - HALF, 128)
-            radial = in_left_ref[s, :, back] + in_turned_ref[s, :, back]
-        radial_ref[s, :, at] = rows_ref[0:1, at] * radial
+            radial = jnp.where(even, in_far_ref[s, :, back], in_near_ref[s, :, back]) + in_turned_ref[s, :, back]
+        radial_ref[s, :, at] = (rows_ref[0:1, at] * radial).astype(BF16)
         axial = jnp.where(own, strength * rows_ref[2:3, at], in_axial_ref[s, :, at])
         for r in range(NODES):
-            axial_ref[s, r, :, at] = jnp.broadcast_to(axial[r : r + 1], (NODES, 128))
+            axial_ref[s, r, :, at] = jnp.broadcast_to(axial[r : r + 1], (LOCAL_Z, 128)).astype(BF16)
 
 
 def outer_kernel(count, part_count, last, order, codes, *refs):
     part_refs, refs = refs[:part_count], refs[part_count:]
-    f_ref, inner_ref, in_axial_ref, in_left_ref, in_turned_ref, in_right_ref = refs[:6]
+    f_ref, inner_ref, in_axial_ref, in_near_ref, in_turned_ref, in_far_ref = refs[:6]
     rows_ref, edge_ref, ghost_r_ref, ghost_z_ref, out_ref = refs[6:11]
     refs = refs[11:]
     if last:
@@ -479,14 +479,15 @@
         total = total_of([p[...] for p in part_refs])
         prepare_nodes(total, codes, place, rows_ref, edge_ref, table_ref, node_ref, wall_ref, plane_ref)
 
+    edge = pl.ds(pl.multiple_of(place * NODES, NODES), NODES)
     speeds = [slot_speed(order, step * count + s) for s in range(count)]
     for s in range(count):
         vz = speeds[s]
         for k, value in enumerate(slot_factors(vz, node_ref)):
             slot_ref[s, k] = value
-        lean_ref[s] = jnp.abs(vz) * ghost_z_ref[jnp.where(vz > 0, 1, 0)]
+        lean_ref[s] = (jnp.abs(vz) * ghost_z_ref[jnp.where(vz > 0, 1, 0)]).astype(BF16)
         ghost_rows(
-            s, vz, place, in_axial_ref, in_left_ref, in_turned_ref, in_right_ref, rows_ref, wall_ref,
+            s, vz, row, place, in_axial_ref, in_near_ref, in_turned_ref, in_far_ref, rows_ref, wall_ref,
             radial_ref, axial_ref,
         )
 
@@ -500,21 +501,23 @@
             at = pl.ds(j * 128, 128)
             gauss, along, reach = (plane_ref[k, rows, at] for k in range(3))
             if last:
-                sums = [sums_ref[k, r, :, at] for k in range(5)]
+                sums = [sums_ref[k, r, :, at] for k in range(4)]
+                gross = sums_ref[4, r, edge, at]
             for s in range(count):
                 here = pl.ds(s * PLANE + j * 128, 128)
-                new = f_ref[r, :, here] * keep + inner_ref[r, :, here].astype(F32)
-                new = new + radial_ref[s, :, at] * lifts[1 if j * 128 >= HALF else 0]
-                across = axial_ref[s, r, :, at]
-                new = new + jnp.concatenate([across, across], axis=0) * lean[s]
+                change = inner_ref[r, :, here] + radial_ref[s, :, at] * lifts[1 if j * 128 >= HALF else 0]
+                change = change + axial_ref[s, r, :, at] * lean[s]
+                new = f_ref[r, :, here] * keep + change.astype(F32)
                 bend = (along + factor[s][1]) * (reach + factor[s][2]) + 1.0
                 new = new + (gauss * factor[s][0]) * bend
                 out_ref[r, :, here] = new
                 if last:
                     sums = add_speed_sums(new, speeds[s], sums)
+                    gross = gross + jnp.where(place == 0, new[0:NODES], new[NODES:]) * jnp.abs(speeds[s])
             if last:
-                for k in range(5):
+                for k in range(4):
                     sums_ref[k, r, :, at] = sums[k]
+                sums_ref[4, r, edge, at] = gross
         return carry
 
     lax.fori_loop(0, NODES, update, 0)
@@ -552,14 +555,14 @@
     group = math.gcd(slots, 3)
     rows_total = lax.axis_size("row")
     verts = lax.axis_size("vert")
-    assert lax.axis_size("gz") == 2
+    assert lax.axis_size("gz") == 2 and rows_total % 2 == 0
     codes = edge_codes.T
     fixed = lambda x: pltpu.with_memory_space_constraint(jnp.asarray(x), pltpu.HBM)
     codes, z_order = fixed(codes), fixed(z_order)
     rows, pos, edge = fixed(ROWS), fixed(NODE_POS), fixed(EDGE)
     radial_m, axial_m = fixed(RADIAL_M), fixed(AXIAL_M)
     ghost_r, ghost_z = fixed(GHOST_R), fixed(GHOST_Z)
-    trace_m, mirror_m, rot_m = fixed(TRACE_M), fixed(MIRROR_M), fixed(ROTATION_M)
+    trace_m, mirror_m, rot_m = fixed(TRACE_M), fixed(MIRROR_M), jnp.asarray(ROTATION_M)
 
     def slab(count):
         return pl.BlockSpec((NODES, LOCAL_Z, count * PLANE), lambda i, *n: (0, 0, i))
@@ -634,9 +637,9 @@
             pltpu.VMEM((10, NODE_COUNT, 128), F32),
             pltpu.VMEM((NODES, 128), F32),
             pltpu.VMEM((count, 3, NODE_COUNT, 128), F32),
-            pltpu.VMEM((count, LOCAL_Z, 128), F32),
-            pltpu.VMEM((count, LOCAL_Z, PLANE), F32),
-            pltpu.VMEM((count, NODES, NODES, PLANE), F32),
+            pltpu.VMEM((count, LOCAL_Z, 128), BF16),
+            pltpu.VMEM((count, LOCAL_Z, PLANE), BF16),
+            pltpu.VMEM((count, NODES, LOCAL_Z, PLANE), BF16),
             square,
         ]
         return call(
@@ -654,21 +657,23 @@
             parts.append(lax.ppermute(moments, "vert", [(i, i ^ shift) for i in range(verts)]))
         return parts
 
-    def halo(right, left, axial):
+    def halo(near, far, axial):
         from_axial = lax.ppermute(axial, "gz", [(0, 1), (1, 0)])
-        from_left = lax.ppermute(right, "row", [(i, i + 1) for i in range(rows_total - 1)])
-        from_right = lax.ppermute(left, "row", [(i + 1, i) for i in range(rows_total - 1)])
-        return from_axial, from_left, from_right
+        pairs = [(i, i ^ 1) for i in range(rows_total)]
+        from_near = lax.ppermute(near, "row", pairs)
+        between = [(i, i + 1) for i in range(1, rows_total - 1, 2)]
+        from_far = lax.ppermute(far, "row", between + [(b, a) for a, b in between])
+        return from_axial, from_near, from_far
 
     current = distribution
     for number in range(STEPS):
         last = number == STEPS - 1
         traces = traces_of(current)
-        from_axial, from_left, from_right = halo(*traces)
+        from_axial, from_near, from_far = halo(*traces)
         moments, turned = moments_of(current, traces[1])
         parts = spread(moments)
         change = inner(current)
-        ghosts = [from_axial, from_left, turned, from_right]
+        ghosts = [from_axial, from_near, turned, from_far]
         current, *final = outer(current, change, ghosts, parts, last)
     parts = spread(final[0])
     macro, flux = pl.pallas_call(
@@ -683,6 +688,7 @@
             jax.ShapeDtypeStruct((8, NODES, LOCAL_Z), F32),
             jax.ShapeDtypeStruct((1, NODES), F32),
         ],
+        compiler_params=pltpu.CompilerParams(vmem_limit_bytes=4 * 1024 * 1024),
         name="macroscopic",
     )(codes, *parts, edge)
     return (current, macro, flux)

time: 125 us -> 120 us (0.960)
  starting transfers between devices: 26.7 us -> 20.9 us
    ppermute x4, starting transfers between devices: 11.3 us -> 4.61 us  [the longest x2 4.61 us: halo(): from_far = lax.ppermute(far, 'row', between + [(b, a) for a, b in between])]
    unnamed x10 -> x4, local copies, waits for them, and re-layouts: 6.19 us -> 5.02 us
  transfers between devices with their start and end apart: 15 -> 15, of which waited for: 4 -> 4; matrix products, arithmetic and copies ran while one was open for 0% -> 0% of each run, Pallas kernels for 31% -> 33%
where the time goes in v11:
time: 120 us; the launch traced here: 119 us
  Pallas kernels  85.9 us (72%)
  starting transfers between devices  20.9 us (17%)
  waiting for transfers between devices  5.93 us (5%)
  local copies, waits for them, and re-layouts  5.02 us (4%)
    pallas_call x8, Pallas kernels, call(): pl.pallas_call(body, grid_spec=pltpu.PrefetchScalarGridSpec(num_scalar_pr...  83.8 us
    ppermute x9, starting transfers between devices, spread(): lax.ppermute(moments, 'vert', [(i, i ^ shift) for i in range(verts)])  13.7 us
    ppermute x9, waiting for transfers between devices, spread(): lax.ppermute(moments, 'vert', [(i, i ^ shift) for i in range(verts)])  5.91 us
    unnamed x4, local copies, waits for them, and re-layouts  5.02 us
    ppermute x2, starting transfers between devices, halo(): from_far = lax.ppermute(far, 'row', between + [(b, a) for a, b in between])  4.61 us
    ppermute x2, starting transfers between devices, halo(): from_axial = lax.ppermute(axial, 'gz', [(0, 1), (1, 0)])  2.54 us
  transfers between devices with their start and end apart: 15, of which 4 were waited for; matrix products, arithmetic and copies ran while one was open for 0% of the time, Pallas kernels for 33%

profile of v11, /device:TPU:4, one launch (start us, length us, event | category | flops | bytes accessed | tf_op | source)
XLA Modules:
  0.0 118.5 jit_solution(9947881572297250859)
XLA Ops:
  0.6 0.0 copy-start
  0.6 5.0 %copy-done = f32[8,16,27648]{2,1,0:T(8,128)S(1)} copy-done((f32[8,16,27648]{2,1,0:T(8,128)S(1)}, f32[8,16,27648]{2,1,0:T(8,128)}, u32[]{:S(2)}) %copy-start) | copy-done | bytes 14155800
  5.7 3.8 %traces.2 = (f32[12,16,1152]{2,1,0:T(8,128)S(1)}, f32[12,16,1152]{2,1,0:T(8,128)S(1)}, f32[12,8,2304]{2,1,0:T(8,128)S(1)}) custom-call(s32[12]{0:T(128)} %a_0_.15, s32[1,2]{1,0:T(1,128)} %bitcast.1, f32[8,16,27648]{2,1,0:T(8,128)S(1)} %copy-done, bf16[2,2,32,128]{3,2,1,0:T(8,128)(2,1)} %constant.27.clone.a_3_), custom_call_target="tpu_custom_call" | custom-call | tf_op jit(solution)/shard_map/traces/pallas_call | solution.py:588
  9.5 1.6 %collective-permute-start.3 = (f32[12,8,2304]{2,1,0:T(8,128)S(1)}, f32[12,8,2304]{2,1,0:T(8,128)S(1)}, u32[]{:S(2)}, u32[]{:S(2)}) collective-permute-start(f32[12,8,2304]{2,1,0:T(8,128)S(1)} %get-tuple-element.19), channel_id=1, source_target_pairs={{0,4},{4,0},{1,5},{5,1},{2,6},{6,2},{3,7},{7,3},{8,12},{12,8},{9,1... | collective-permute-start | bytes 2654216 | tf_op jit(solution)/shard_map/ppermute | solution.py:661
  11.1 2.5 %collective-permute-start.5 = (f32[12,16,1152]{2,1,0:T(8,128)S(1)}, f32[12,16,1152]{2,1,0:T(8,128)S(1)}, u32[]{:S(2)}, u32[]{:S(2)}) collective-permute-start(f32[12,16,1152]{2,1,0:T(8,128)S(1)} %get-tuple-element.17.a_3_), channel_id=1, source_target_pairs={{8,16},{16,8},{9,17},{17,9},{10,18},{18,10},{11,19},{19,11},{12,20... | collective-permute-start | bytes 2654216 | tf_op jit(solution)/shard_map/ppermute | solution.py:665
  13.6 9.5 %moments.2 = (f32[16,128]{1,0:T(8,128)S(1)}, f32[12,16,1152]{2,1,0:T(8,128)S(1)}) custom-call(s32[12]{0:T(128)} %a_0_.15, s32[1,2]{1,0:T(1,128)} %bitcast.2, f32[8,16,27648]{2,1,0:T(8,128)S(1)} %copy-done, f32[12,16,1152]{2,1,0:T(8,128)S(1)} %get-tuple-element.17.a_3_, f32[8,2304]{1,0:T(8,128)} %constant.20.clone.a_4_.a_3_.a_12_, ...), custom_call_target="tpu_custom_call" | custom-call | tf_op jit(solution)/shard_map/moments/pallas_call | solution.py:588
  23.1 3.7 %collective-permute-start.2 = (f32[16,128]{1,0:T(8,128)S(1)}, f32[16,128]{1,0:T(8,128)S(1)}, u32[]{:S(2)}, u32[]{:S(2)}) collective-permute-start(f32[16,128]{1,0:T(8,128)S(1)} %get-tuple-element.18.a_2_), channel_id=1, source_target_pairs={{0,3},{1,2},{2,1},{3,0},{4,7},{5,6},{6,5},{7,4},{8,11},{9,10},{10,... | collective-permute-start | bytes 24584 | tf_op jit(solution)/shard_map/ppermute | solution.py:657
  26.8 0.0 collective-permute-start.1
  26.8 1.8 %collective-permute-done.2.a_5_ = f32[16,128]{1,0:T(8,128)S(1)} collective-permute-done((f32[16,128]{1,0:T(8,128)S(1)}, f32[16,128]{1,0:T(8,128)S(1)}, u32[]{:S(2)}, u32[]{:S(2)}) %collective-permute-start.2) | collective-permute-done | bytes 8224 | tf_op jit(solution)/shard_map/ppermute | solution.py:657
  28.6 0.0 collective-permute-start
  28.6 9.9 %inner_increments.2.a_7_ = bf16[8,16,27648]{2,1,0:T(8,128)(2,1)S(1)} custom-call(s32[12]{0:T(128)} %a_0_.15, s32[1,2]{1,0:T(1,128)} %bitcast.3, f32[8,16,27648]{2,1,0:T(8,128)S(1)} %copy-done, f32[8,2304]{1,0:T(8,128)} %constant.20.clone.a_4_.a_3_.a_12_, f32[128,128]{1,0:T(8,128)} %constant.21.clone.a_4_, bf16[3,128,128]{2,1,0:T(8,128)(2,1)} %constant.23.clone.a_5_, ...), custom_call_target="tpu_custom_call" | custom-call | tf_op jit(solution)/shard_map/inner_increments/pallas_call | solution.py:588
  38.5 0.0 collective-permute-done.a_3_
  38.5 0.0 collective-permute-done.3.a_8_
  38.5 0.0 collective-permute-done.5.a_11_
  38.5 14.2 %update.1.a_2_.a_6_ = f32[8,16,27648]{2,1,0:T(8,128)S(1)} custom-call(s32[12]{0:T(128)} %a_0_.15, s32[1,2]{1,0:T(1,128)} %bitcast.4, f32[16,128]{1,0:T(8,128)S(1)} %get-tuple-element.18.a_2_, f32[16,128]{1,0:T(8,128)S(1)} %collective-permute-done.a_3_, f32[16,128]{1,0:T(8,128)S(1)} %collective-permute-done.1.a_4_, ...), custom_call_target="tpu_custom_call" | custom-call | tf_op jit(solution)/shard_map/update/pallas_call | solution.py:588
  52.7 3.7 %traces.3 = (f32[12,16,1152]{2,1,0:T(8,128)S(1)}, f32[12,16,1152]{2,1,0:T(8,128)S(1)}, f32[12,8,2304]{2,1,0:T(8,128)S(1)}) custom-call(s32[12]{0:T(128)} %a_0_.15, s32[1,2]{1,0:T(1,128)} %bitcast.5, f32[8,16,27648]{2,1,0:T(8,128)S(1)} %update.1.a_2_.a_6_, bf16[2,2,32,128]{3,2,1,0:T(8,128)(2,1)} %constant.27.clone.a_3_), custom_call_target="tpu_custom_call" | custom-call | tf_op jit(solution)/shard_map/traces/pallas_call | solution.py:588
  56.4 1.0 collective-permute-start.9
  57.4 0.0 collective-permute-start.10
  57.4 2.1 %collective-permute-start.11 = (f32[12,16,1152]{2,1,0:T(8,128)S(1)}, f32[12,16,1152]{2,1,0:T(8,128)S(1)}, u32[]{:S(2)}, u32[]{:S(2)}) collective-permute-start(f32[12,16,1152]{2,1,0:T(8,128)S(1)} %get-tuple-element.22.a_3_), channel_id=1, source_target_pairs={{8,16},{16,8},{9,17},{17,9},{10,18},{18,10},{11,19},{19,11},{12,20... | collective-permute-start | bytes 2654216 | tf_op jit(solution)/shard_map/ppermute | solution.py:665
  59.5 9.5 %moments.3 = (f32[16,128]{1,0:T(8,128)S(1)}, f32[12,16,1152]{2,1,0:T(8,128)S(1)}) custom-call(s32[12]{0:T(128)} %a_0_.15, s32[1,2]{1,0:T(1,128)} %bitcast.6, f32[8,16,27648]{2,1,0:T(8,128)S(1)} %update.1.a_2_.a_6_, f32[12,16,1152]{2,1,0:T(8,128)S(1)} %get-tuple-element.22.a_3_, f32[8,2304]{1,0:T(8,128)} %constant.20.clone.a_4_.a_3_.a_12_, ...), custom_call_target="tpu_custom_call" | custom-call | tf_op jit(solution)/shard_map/moments/pallas_call | solution.py:588
  69.0 3.9 %collective-permute-start.8 = (f32[16,128]{1,0:T(8,128)S(1)}, f32[16,128]{1,0:T(8,128)S(1)}, u32[]{:S(2)}, u32[]{:S(2)}) collective-permute-start(f32[16,128]{1,0:T(8,128)S(1)} %get-tuple-element.23.a_2_), channel_id=1, source_target_pairs={{0,3},{1,2},{2,1},{3,0},{4,7},{5,6},{6,5},{7,4},{8,11},{9,10},{10,... | collective-permute-start | bytes 24584 | tf_op jit(solution)/shard_map/ppermute | solution.py:657
  72.9 0.6 collective-permute-start.7
  73.5 1.0 collective-permute-done.8.a_5_
  74.5 1.1 collective-permute-start.6
  75.6 9.8 %inner_increments.3.a_7_ = bf16[8,16,27648]{2,1,0:T(8,128)(2,1)S(1)} custom-call(s32[12]{0:T(128)} %a_0_.15, s32[1,2]{1,0:T(1,128)} %bitcast.7, f32[8,16,27648]{2,1,0:T(8,128)S(1)} %update.1.a_2_.a_6_, f32[8,2304]{1,0:T(8,128)} %constant.20.clone.a_4_.a_3_.a_12_, f32[128,128]{1,0:T(8,128)} %constant.21.clone.a_4_, bf16[3,128,128]{2,1,0:T(8,128)(2,1)} %constant.23.clone.a_5_, ...), custom_call_target="tpu_custom_call" | custom-call | tf_op jit(solution)/shard_map/inner_increments/pallas_call | solution.py:588
  85.5 23.4 %last_update.1 = (f32[8,16,27648]{2,1,0:T(8,128)}, f32[16,128]{1,0:T(8,128)S(1)}) custom-call(s32[12]{0:T(128)} %a_0_.15, s32[1,2]{1,0:T(1,128)} %bitcast.8, f32[16,128]{1,0:T(8,128)S(1)} %get-tuple-element.23.a_2_, f32[16,128]{1,0:T(8,128)S(1)} %collective-permute-done.6.a_3_, f32[16,128]{1,0:T(8,128)S(1)} %collective-permute-done.7.a_4_, ...), custom_call_target="tpu_custom_call" | custom-call | tf_op jit(solution)/shard_map/last_update/pallas_call | solution.py:588
  108.9 2.9 %collective-permute-start.14 = (f32[16,128]{1,0:T(8,128)S(1)}, f32[16,128]{1,0:T(8,128)S(1)}, u32[]{:S(2)}, u32[]{:S(2)}) collective-permute-start(f32[16,128]{1,0:T(8,128)S(1)} %get-tuple-element.28.a_1_), channel_id=1, source_target_pairs={{0,3},{1,2},{2,1},{3,0},{4,7},{5,6},{6,5},{7,4},{8,11},{9,10},{10,... | collective-permute-start | bytes 24584 | tf_op jit(solution)/shard_map/ppermute | solution.py:657
  111.9 0.3 collective-permute-start.13
  112.2 1.1 collective-permute-start.12
  113.3 1.1 collective-permute-done.14.a_4_
  114.4 2.0 %collective-permute-done.13.a_3_ = f32[16,128]{1,0:T(8,128)S(1)} collective-permute-done((f32[16,128]{1,0:T(8,128)S(1)}, f32[16,128]{1,0:T(8,128)S(1)}, u32[]{:S(2)}, u32[]{:S(2)}) %collective-permute-start.13) | collective-permute-done | bytes 8224 | tf_op jit(solution)/shard_map/ppermute | solution.py:657
  116.4 2.1 %macroscopic.1 = (f32[8,8,16]{2,1,0:T(8,128)}, f32[1,8]{1,0:T(1,128)}) custom-call(s32[1,2]{1,0:T(1,128)} %bitcast.9, f32[16,128]{1,0:T(8,128)S(1)} %get-tuple-element.28.a_1_, f32[16,128]{1,0:T(8,128)S(1)} %collective-permute-done.12.a_2_, f32[16,128]{1,0:T(8,128)S(1)} %collective-permute-done.13.a_3_, f32[16,128]{1,0:T(8,128)S(1)} %collective-permute-done.14.a_4_, ...), custom_call_target="tpu_custom_call" | custom-call | tf_op jit(solution)/shard_map/macroscopic/pallas_call | solution.py:679
  (11 shorter events, 0.0 us)
Async XLA Ops:
  0.6 5.0 %copy-start = (f32[8,16,27648]{2,1,0:T(8,128)S(1)}, f32[8,16,27648]{2,1,0:T(8,128)}, u32[]{:S(2)}) copy-start(f32[8,16,27648]{2,1,0:T(8,128)} %a_6_.3) | copy-start | bytes 42467332
  5.7 23.0 %copy-start.1 = (bf16[9,512,256]{2,1,0:T(8,128)(2,1)S(1)}, bf16[9,512,256]{2,1,0:T(8,128)(2,1)}, u32[]{:S(2)}) copy-start(bf16[9,512,256]{2,1,0:T(8,128)(2,1)} %constant.29.clone.a_7_) | copy-start | bytes 7077892
  9.5 29.0 %collective-permute-start.3 = (f32[12,8,2304]{2,1,0:T(8,128)S(1)}, f32[12,8,2304]{2,1,0:T(8,128)S(1)}, u32[]{:S(2)}, u32[]{:S(2)}) collective-permute-start(f32[12,8,2304]{2,1,0:T(8,128)S(1)} %get-tuple-element.19), channel_id=1, source_target_pairs={{0,4},{4,0},{1,5},{5,1},{2,6},{6,2},{3,7},{7,3},{8,12},{12,8},{9,1... | collective-permute-start | bytes 2654216 | tf_op jit(solution)/shard_map/ppermute | solution.py:661
  11.1 27.4 %collective-permute-start.4 = (f32[12,16,1152]{2,1,0:T(8,128)S(1)}, f32[12,16,1152]{2,1,0:T(8,128)S(1)}, u32[]{:S(2)}, u32[]{:S(2)}) collective-permute-start(f32[12,16,1152]{2,1,0:T(8,128)S(1)} %get-tuple-element.20), channel_id=1, source_target_pairs={{0,8},{8,0},{16,24},{24,16},{1,9},{9,1},{17,25},{25,17},{2,10},{10... | collective-permute-start | bytes 2654216 | tf_op jit(solution)/shard_map/ppermute | solution.py:663
  11.1 27.4 %collective-permute-start.5 = (f32[12,16,1152]{2,1,0:T(8,128)S(1)}, f32[12,16,1152]{2,1,0:T(8,128)S(1)}, u32[]{:S(2)}, u32[]{:S(2)}) collective-permute-start(f32[12,16,1152]{2,1,0:T(8,128)S(1)} %get-tuple-element.17.a_3_), channel_id=1, source_target_pairs={{8,16},{16,8},{9,17},{17,9},{10,18},{18,10},{11,19},{19,11},{12,20... | collective-permute-start | bytes 2654216 | tf_op jit(solution)/shard_map/ppermute | solution.py:665
  23.1 5.5 %collective-permute-start.2 = (f32[16,128]{1,0:T(8,128)S(1)}, f32[16,128]{1,0:T(8,128)S(1)}, u32[]{:S(2)}, u32[]{:S(2)}) collective-permute-start(f32[16,128]{1,0:T(8,128)S(1)} %get-tuple-element.18.a_2_), channel_id=1, source_target_pairs={{0,3},{1,2},{2,1},{3,0},{4,7},{5,6},{6,5},{7,4},{8,11},{9,10},{10,... | collective-permute-start | bytes 24584 | tf_op jit(solution)/shard_map/ppermute | solution.py:657
  26.8 11.7 %collective-permute-start.1 = (f32[16,128]{1,0:T(8,128)S(1)}, f32[16,128]{1,0:T(8,128)S(1)}, u32[]{:S(2)}, u32[]{:S(2)}) collective-permute-start(f32[16,128]{1,0:T(8,128)S(1)} %get-tuple-element.18.a_2_), channel_id=1, source_target_pairs={{0,2},{1,3},{2,0},{3,1},{4,6},{5,7},{6,4},{7,5},{8,10},{9,11},{10,... | collective-permute-start | bytes 24584 | tf_op jit(solution)/shard_map/ppermute | solution.py:657
  28.6 9.9 %collective-permute-start = (f32[16,128]{1,0:T(8,128)S(1)}, f32[16,128]{1,0:T(8,128)S(1)}, u32[]{:S(2)}, u32[]{:S(2)}) collective-permute-start(f32[16,128]{1,0:T(8,128)S(1)} %get-tuple-element.18.a_2_), channel_id=1, source_target_pairs={{0,1},{1,0},{2,3},{3,2},{4,5},{5,4},{6,7},{7,6},{8,9},{9,8},{10,11... | collective-permute-start | bytes 24584 | tf_op jit(solution)/shard_map/ppermute | solution.py:657
  56.4 29.1 %collective-permute-start.9 = (f32[12,8,2304]{2,1,0:T(8,128)S(1)}, f32[12,8,2304]{2,1,0:T(8,128)S(1)}, u32[]{:S(2)}, u32[]{:S(2)}) collective-permute-start(f32[12,8,2304]{2,1,0:T(8,128)S(1)} %get-tuple-element.24), channel_id=1, source_target_pairs={{0,4},{4,0},{1,5},{5,1},{2,6},{6,2},{3,7},{7,3},{8,12},{12,8},{9,1... | collective-permute-start | bytes 2654216 | tf_op jit(solution)/shard_map/ppermute | solution.py:661
  57.4 28.1 %collective-permute-start.10 = (f32[12,16,1152]{2,1,0:T(8,128)S(1)}, f32[12,16,1152]{2,1,0:T(8,128)S(1)}, u32[]{:S(2)}, u32[]{:S(2)}) collective-permute-start(f32[12,16,1152]{2,1,0:T(8,128)S(1)} %get-tuple-element.25), channel_id=1, source_target_pairs={{0,8},{8,0},{16,24},{24,16},{1,9},{9,1},{17,25},{25,17},{2,10},{10... | collective-permute-start | bytes 2654216 | tf_op jit(solution)/shard_map/ppermute | solution.py:663
  57.4 28.1 %collective-permute-start.11 = (f32[12,16,1152]{2,1,0:T(8,128)S(1)}, f32[12,16,1152]{2,1,0:T(8,128)S(1)}, u32[]{:S(2)}, u32[]{:S(2)}) collective-permute-start(f32[12,16,1152]{2,1,0:T(8,128)S(1)} %get-tuple-element.22.a_3_), channel_id=1, source_target_pairs={{8,16},{16,8},{9,17},{17,9},{10,18},{18,10},{11,19},{19,11},{12,20... | collective-permute-start | bytes 2654216 | tf_op jit(solution)/shard_map/ppermute | solution.py:665
  69.0 5.5 %collective-permute-start.8 = (f32[16,128]{1,0:T(8,128)S(1)}, f32[16,128]{1,0:T(8,128)S(1)}, u32[]{:S(2)}, u32[]{:S(2)}) collective-permute-start(f32[16,128]{1,0:T(8,128)S(1)} %get-tuple-element.23.a_2_), channel_id=1, source_target_pairs={{0,3},{1,2},{2,1},{3,0},{4,7},{5,6},{6,5},{7,4},{8,11},{9,10},{10,... | collective-permute-start | bytes 24584 | tf_op jit(solution)/shard_map/ppermute | solution.py:657
  72.9 12.6 %collective-permute-start.7 = (f32[16,128]{1,0:T(8,128)S(1)}, f32[16,128]{1,0:T(8,128)S(1)}, u32[]{:S(2)}, u32[]{:S(2)}) collective-permute-start(f32[16,128]{1,0:T(8,128)S(1)} %get-tuple-element.23.a_2_), channel_id=1, source_target_pairs={{0,2},{1,3},{2,0},{3,1},{4,6},{5,7},{6,4},{7,5},{8,10},{9,11},{10,... | collective-permute-start | bytes 24584 | tf_op jit(solution)/shard_map/ppermute | solution.py:657
  74.5 11.0 %collective-permute-start.6 = (f32[16,128]{1,0:T(8,128)S(1)}, f32[16,128]{1,0:T(8,128)S(1)}, u32[]{:S(2)}, u32[]{:S(2)}) collective-permute-start(f32[16,128]{1,0:T(8,128)S(1)} %get-tuple-element.23.a_2_), channel_id=1, source_target_pairs={{0,1},{1,0},{2,3},{3,2},{4,5},{5,4},{6,7},{7,6},{8,9},{9,8},{10,11... | collective-permute-start | bytes 24584 | tf_op jit(solution)/shard_map/ppermute | solution.py:657
  108.9 5.4 %collective-permute-start.14 = (f32[16,128]{1,0:T(8,128)S(1)}, f32[16,128]{1,0:T(8,128)S(1)}, u32[]{:S(2)}, u32[]{:S(2)}) collective-permute-start(f32[16,128]{1,0:T(8,128)S(1)} %get-tuple-element.28.a_1_), channel_id=1, source_target_pairs={{0,3},{1,2},{2,1},{3,0},{4,7},{5,6},{6,5},{7,4},{8,11},{9,10},{10,... | collective-permute-start | bytes 24584 | tf_op jit(solution)/shard_map/ppermute | solution.py:657
  111.9 4.5 %collective-permute-start.13 = (f32[16,128]{1,0:T(8,128)S(1)}, f32[16,128]{1,0:T(8,128)S(1)}, u32[]{:S(2)}, u32[]{:S(2)}) collective-permute-start(f32[16,128]{1,0:T(8,128)S(1)} %get-tuple-element.28.a_1_), channel_id=1, source_target_pairs={{0,2},{1,3},{2,0},{3,1},{4,6},{5,7},{6,4},{7,5},{8,10},{9,11},{10,... | collective-permute-start | bytes 24584 | tf_op jit(solution)/shard_map/ppermute | solution.py:657
  112.2 4.2 %collective-permute-start.12 = (f32[16,128]{1,0:T(8,128)S(1)}, f32[16,128]{1,0:T(8,128)S(1)}, u32[]{:S(2)}, u32[]{:S(2)}) collective-permute-start(f32[16,128]{1,0:T(8,128)S(1)} %get-tuple-element.28.a_1_), channel_id=1, source_target_pairs={{0,1},{1,0},{2,3},{3,2},{4,5},{5,4},{6,7},{7,6},{8,9},{9,8},{10,11... | collective-permute-start | bytes 24584 | tf_op jit(solution)/shard_map/ppermute | solution.py:657

commit v12 on v11

--- a/solution.py
+++ b/solution.py
@@ -139,7 +139,7 @@
     return (
         (-SCALE * radial).astype(ml_dtypes.bfloat16),
         (-SCALE * axial).astype(np.float32),
-        (SCALE * ghost_r).astype(ml_dtypes.bfloat16),
+        (SCALE * ghost_r).astype(np.float32),
         (SCALE * ghost_z).astype(np.float32),
         trace.astype(ml_dtypes.bfloat16),
     )
@@ -234,7 +234,13 @@
 def add_speed_sums(field, vz, sums):
     one = field * vz
     two = one * vz
-    return [sums[0] + field, sums[1] + one, sums[2] + two, sums[3] + two * vz]
+    return [
+        sums[0] + field,
+        sums[1] + one,
+        sums[2] + two,
+        sums[3] + two * vz,
+        sums[4] + field * jnp.abs(vz),
+    ]
 
 
 def finish_moments(sums_ref, rows_ref, table_ref, out_ref):
@@ -319,70 +325,19 @@
         clear_sums(sums_ref)
 
     turn_traces(count, row, mirror_ref, left_ref, turned_ref)
-    edge = pl.ds(pl.multiple_of(place * NODES, NODES), NODES)
     speeds = [slot_speed(order, step * count + s) for s in range(count)]
     for j in range(0, PLANE, 128):
         at = pl.ds(j, 128)
         for r in range(NODES):
-            sums = [sums_ref[k, r, :, at] for k in range(4)]
-            gross = sums_ref[4, r, edge, at]
+            sums = [sums_ref[k, r, :, at] for k in range(5)]
             for s in range(count):
-                here = pl.ds(s * PLANE + j, 128)
-                sums = add_speed_sums(f_ref[r, :, here], speeds[s], sums)
-                gross = gross + f_ref[r, edge, here] * jnp.abs(speeds[s])
-            for k in range(4):
+                sums = add_speed_sums(f_ref[r, :, pl.ds(s * PLANE + j, 128)], speeds[s], sums)
+            for k in range(5):
                 sums_ref[k, r, :, at] = sums[k]
-            sums_ref[4, r, edge, at] = gross
 
     @pl.when(step == pl.num_programs(0) - 1)
     def _():
         finish_moments(sums_ref, rows_ref, table_ref, mom_ref)
-
-
-def inner_kernel(
-    count, order, codes, f_ref, rows_ref, pos_ref, radial_ref, axial_m_ref, rot_ref,
-    out_ref, inverse_ref, pad_ref, lhs_ref,
-):
-    step = pl.program_id(0)
-    row, place = places_of()
-
-    @pl.when(step == 0)
-    def _():
-        pad_ref[:, :, 0:128] = jnp.zeros((count, NODE_COUNT, 128), BF16)
-        pad_ref[:, :, 128 + PLANE :] = jnp.zeros((count, NODE_COUNT, 128), BF16)
-        inverse_ref[...] = 1.0 / (ELEMENT_WIDTH * (row.astype(F32) + pos_ref[...]))
-        minus = radial_ref[jnp.where(row == lax.axis_size("row") - 1, 2, 0)]
-        for s in range(count):
-            lhs_ref[s, 0, :, 0:NODE_COUNT] = minus
-            lhs_ref[s, 1, :, 0:NODE_COUNT] = radial_ref[1]
-
-    kind_out = jnp.where(jnp.logical_and(place == 1, codes[0, TOP] == 2), 2, 0)
-    inverse = inverse_ref[...]
-    speeds = [slot_speed(order, step * count + s) for s in range(count)]
-    for s in range(count):
-        vz = speeds[s]
-        axial = (vz * axial_m_ref[jnp.where(vz > 0, 1, kind_out)]).astype(BF16)
-        lhs_ref[s, 0, :, NODE_COUNT:] = axial
-        lhs_ref[s, 1, :, NODE_COUNT:] = axial
-        for j in range(PLANE // 128):
-            field = nodes_of(f_ref, s * PLANE + j * 128, 128)
-            pad_ref[s, :, 128 + j * 128 : 256 + j * 128] = (field * inverse).astype(BF16)
-
-    for tile in range(PLANE // TILE):
-        start = tile * TILE
-        turned = dot(pad_ref[:, :, start : start + WINDOW].reshape(count * NODE_COUNT, WINDOW), rot_ref[tile])
-        for first, lanes, side in PIECES:
-            if first // TILE != tile:
-                continue
-            vr = rows_ref[0:1, first : first + lanes]
-            inside = first - start
-            for s in range(count):
-                here = s * PLANE + first
-                field = nodes_of(f_ref, here, lanes)
-                both = jnp.concatenate([(field * vr).astype(BF16), field.astype(BF16)], axis=0)
-                change = turned[s * NODE_COUNT : (s + 1) * NODE_COUNT, inside : inside + lanes]
-                change = change + dot(lhs_ref[s, side], both)
-                out_ref[:, :, here : here + lanes] = change.astype(BF16).reshape(NODES, LOCAL_Z, lanes)
 
 
 def total_of(parts):
@@ -455,20 +410,21 @@
         else:
             back = pl.ds(j * 128 - HALF, 128)
             radial = jnp.where(even, in_far_ref[s, :, back], in_near_ref[s, :, back]) + in_turned_ref[s, :, back]
-        radial_ref[s, :, at] = (rows_ref[0:1, at] * radial).astype(BF16)
+        radial_ref[s, :, at] = rows_ref[0:1, at] * radial
         axial = jnp.where(own, strength * rows_ref[2:3, at], in_axial_ref[s, :, at])
         for r in range(NODES):
-            axial_ref[s, r, :, at] = jnp.broadcast_to(axial[r : r + 1], (LOCAL_Z, 128)).astype(BF16)
+            axial_ref[s, r, :, at] = jnp.broadcast_to(axial[r : r + 1], (NODES, 128))
 
 
 def outer_kernel(count, part_count, last, order, codes, *refs):
     part_refs, refs = refs[:part_count], refs[part_count:]
-    f_ref, inner_ref, in_axial_ref, in_near_ref, in_turned_ref, in_far_ref = refs[:6]
-    rows_ref, edge_ref, ghost_r_ref, ghost_z_ref, out_ref = refs[6:11]
-    refs = refs[11:]
+    f_ref, in_axial_ref, in_near_ref, in_turned_ref, in_far_ref = refs[:5]
+    rows_ref, edge_ref, ghost_r_ref, ghost_z_ref, pos_ref, radial_m_ref, axial_m_ref, rot_ref, out_ref = refs[5:14]
+    refs = refs[14:]
     if last:
         (mom_ref, sums_ref), refs = refs[:2], refs[2:]
-    plane_ref, node_ref, wall_ref, slot_ref, lean_ref, radial_ref, axial_ref, table_ref = refs
+    plane_ref, node_ref, wall_ref, slot_ref, lean_ref, radial_ref, axial_ref, table_ref = refs[:8]
+    inverse_ref, pad_ref, lhs_ref, work_ref = refs[8:]
     step = pl.program_id(0)
     row, place = places_of()
 
@@ -478,18 +434,48 @@
             clear_sums(sums_ref)
         total = total_of([p[...] for p in part_refs])
         prepare_nodes(total, codes, place, rows_ref, edge_ref, table_ref, node_ref, wall_ref, plane_ref)
-
-    edge = pl.ds(pl.multiple_of(place * NODES, NODES), NODES)
+        pad_ref[:, :, 0:128] = jnp.zeros((count, NODE_COUNT, 128), BF16)
+        pad_ref[:, :, 128 + PLANE :] = jnp.zeros((count, NODE_COUNT, 128), BF16)
+        inverse_ref[...] = 1.0 / (ELEMENT_WIDTH * (row.astype(F32) + pos_ref[...]))
+        minus = radial_m_ref[jnp.where(row == lax.axis_size("row") - 1, 2, 0)]
+        for s in range(count):
+            lhs_ref[s, 0, :, 0:NODE_COUNT] = minus
+            lhs_ref[s, 1, :, 0:NODE_COUNT] = radial_m_ref[1]
+
     speeds = [slot_speed(order, step * count + s) for s in range(count)]
     for s in range(count):
         vz = speeds[s]
         for k, value in enumerate(slot_factors(vz, node_ref)):
             slot_ref[s, k] = value
-        lean_ref[s] = (jnp.abs(vz) * ghost_z_ref[jnp.where(vz > 0, 1, 0)]).astype(BF16)
+        lean_ref[s] = jnp.abs(vz) * ghost_z_ref[jnp.where(vz > 0, 1, 0)]
         ghost_rows(
             s, vz, row, place, in_axial_ref, in_near_ref, in_turned_ref, in_far_ref, rows_ref, wall_ref,
             radial_ref, axial_ref,
         )
+
+    kind_out = jnp.where(jnp.logical_and(place == 1, codes[0, TOP] == 2), 2, 0)
+    inverse = inverse_ref[...]
+    for s in range(count):
+        axial = (speeds[s] * axial_m_ref[jnp.where(speeds[s] > 0, 1, kind_out)]).astype(BF16)
+        lhs_ref[s, 0, :, NODE_COUNT:] = axial
+        lhs_ref[s, 1, :, NODE_COUNT:] = axial
+        for j in range(PLANE // 128):
+            field = nodes_of(f_ref, s * PLANE + j * 128, 128)
+            pad_ref[s, :, 128 + j * 128 : 256 + j * 128] = (field * inverse).astype(BF16)
+
+    for tile in range(PLANE // TILE):
+        start = tile * TILE
+        turned = dot(pad_ref[:, :, start : start + WINDOW].reshape(count * NODE_COUNT, WINDOW), rot_ref[tile])
+        for first, lanes, side in PIECES:
+            if first // TILE != tile:
+                continue
+            vr = rows_ref[0:1, first : first + lanes]
+            inside = first - start
+            for s in range(count):
+                field = nodes_of(f_ref, s * PLANE + first, lanes)
+                both = jnp.concatenate([(field * vr).astype(BF16), field.astype(BF16)], axis=0)
+                change = turned[s * NODE_COUNT : (s + 1) * NODE_COUNT, inside : inside + lanes]
+                work_ref[s, :, first : first + lanes] = change + dot(lhs_ref[s, side], both)
 
     def update(r, carry):
         rows = pl.ds(pl.multiple_of(r * LOCAL_Z, LOCAL_Z), LOCAL_Z)
@@ -501,23 +487,21 @@
             at = pl.ds(j * 128, 128)
             gauss, along, reach = (plane_ref[k, rows, at] for k in range(3))
             if last:
-                sums = [sums_ref[k, r, :, at] for k in range(4)]
-                gross = sums_ref[4, r, edge, at]
+                sums = [sums_ref[k, r, :, at] for k in range(5)]
             for s in range(count):
                 here = pl.ds(s * PLANE + j * 128, 128)
-                change = inner_ref[r, :, here] + radial_ref[s, :, at] * lifts[1 if j * 128 >= HALF else 0]
-                change = change + axial_ref[s, r, :, at] * lean[s]
-                new = f_ref[r, :, here] * keep + change.astype(F32)
+                across = axial_ref[s, r, :, at]
+                new = f_ref[r, :, here] * keep + work_ref[s, rows, at]
+                new = new + radial_ref[s, :, at] * lifts[1 if j * 128 >= HALF else 0]
+                new = new + jnp.concatenate([across, across], axis=0) * lean[s]
                 bend = (along + factor[s][1]) * (reach + factor[s][2]) + 1.0
                 new = new + (gauss * factor[s][0]) * bend
                 out_ref[r, :, here] = new
                 if last:
                     sums = add_speed_sums(new, speeds[s], sums)
-                    gross = gross + jnp.where(place == 0, new[0:NODES], new[NODES:]) * jnp.abs(speeds[s])
             if last:
-                for k in range(4):
+                for k in range(5):
                     sums_ref[k, r, :, at] = sums[k]
-                sums_ref[4, r, edge, at] = gross
         return carry
 
     lax.fori_loop(0, NODES, update, 0)
@@ -617,38 +601,32 @@
             [pltpu.VMEM((5, NODES, LOCAL_Z, PLANE), F32), square], [f, left, rows, mirror_m],
         )
 
-    def inner(f):
-        tables = [rows, pos, radial_m, axial_m, rot_m]
-        scratch = [
-            square,
-            pltpu.VMEM((group, NODE_COUNT, PLANE + 256), BF16),
-            pltpu.VMEM((group, 2, NODE_COUNT, 2 * NODE_COUNT), BF16),
-        ]
-        return call(
-            lambda *a: inner_kernel(group, *a), "inner_increments", group, 20, [slab(group)] + all_whole(tables),
-            slab(group), jax.ShapeDtypeStruct(f.shape, BF16), scratch, [f] + tables,
-        )
-
-    def outer(f, change, ghosts, parts, last):
-        count = 1 if last else math.gcd(slots, 2)
-        tables = [rows, edge, ghost_r, ghost_z]
+    def outer(f, ghosts, parts, last):
+        count = math.gcd(slots, 2)
+        if last:
+            f = pltpu.with_memory_space_constraint(f, pltpu.HBM)
+        tables = [rows, edge, ghost_r, ghost_z, pos, radial_m, axial_m, rot_m]
         scratch = [
             pltpu.VMEM((3, NODE_COUNT, PLANE), F32),
             pltpu.VMEM((10, NODE_COUNT, 128), F32),
             pltpu.VMEM((NODES, 128), F32),
             pltpu.VMEM((count, 3, NODE_COUNT, 128), F32),
-            pltpu.VMEM((count, LOCAL_Z, 128), BF16),
-            pltpu.VMEM((count, LOCAL_Z, PLANE), BF16),
-            pltpu.VMEM((count, NODES, LOCAL_Z, PLANE), BF16),
+            pltpu.VMEM((count, LOCAL_Z, 128), F32),
+            pltpu.VMEM((count, LOCAL_Z, PLANE), F32),
+            pltpu.VMEM((count, NODES, NODES, PLANE), F32),
             square,
+            square,
+            pltpu.VMEM((count, NODE_COUNT, PLANE + 256), BF16),
+            pltpu.VMEM((count, 2, NODE_COUNT, 2 * NODE_COUNT), BF16),
+            pltpu.VMEM((count, NODE_COUNT, PLANE), F32),
         ]
         return call(
-            lambda *a: outer_kernel(count, len(parts), last, *a), "last_update" if last else "update", count, 20,
-            [mom_spec] * len(parts) + [slab(count), slab(count), axial_spec(count)] + [radial_spec(count)] * 3
+            lambda *a: outer_kernel(count, len(parts), last, *a), "last_update" if last else "update", count, 32 if last else 26,
+            [mom_spec] * len(parts) + [slab(count), axial_spec(count)] + [radial_spec(count)] * 3
             + all_whole(tables),
             [slab(count)] + ([mom_spec] if last else []), [big_shape] + ([mom_shape] if last else []),
             ([pltpu.VMEM((5, NODES, LOCAL_Z, PLANE), F32)] if last else []) + scratch,
-            [*parts, f, change, *ghosts, *tables],
+            [*parts, f, *ghosts, *tables],
         )
 
     def spread(moments):
@@ -672,9 +650,8 @@
         from_axial, from_near, from_far = halo(*traces)
         moments, turned = moments_of(current, traces[1])
         parts = spread(moments)
-        change = inner(current)
         ghosts = [from_axial, from_near, turned, from_far]
-        current, *final = outer(current, change, ghosts, parts, last)
+        current, *final = outer(current, ghosts, parts, last)
     parts = spread(final[0])
     macro, flux = pl.pallas_call(
         lambda *a: last_kernel(len(parts), *a),

time: 120 us -> 117 us (0.975)
  Pallas kernels: 85.9 us -> 76.9 us
  waiting for transfers between devices: 5.93 us -> 14.8 us
  starting transfers between devices: 20.9 us -> 19 us
    pallas_call x8 -> x6, Pallas kernels: 83.8 us -> 74.7 us  [call(): pl.pallas_call(body, grid_spec=pltpu.PrefetchScalarGridSpec(num_scalar_pr...]
    ppermute x9, waiting for transfers between devices: 5.91 us -> 14.7 us  [spread(): lax.ppermute(moments, 'vert', [(i, i ^ shift) for i in range(verts)])]
    ppermute x9, starting transfers between devices: 13.7 us -> 11.7 us  [spread(): lax.ppermute(moments, 'vert', [(i, i ^ shift) for i in range(verts)])]
    unnamed x4 -> x6, local copies, waits for them, and re-layouts: 5.02 us -> 5.03 us
  transfers between devices with their start and end apart: 15 -> 15, of which waited for: 4 -> 8; matrix products, arithmetic and copies ran while one was open for 0% -> 0% of each run, Pallas kernels for 33% -> 16%
where the time goes in v12:
time: 117 us; the launch traced here: 116 us
  Pallas kernels  76.9 us (66%)
  starting transfers between devices  19 us (16%)
  waiting for transfers between devices  14.8 us (13%)
  local copies, waits for them, and re-layouts  5.03 us (4%)
    pallas_call x6, Pallas kernels, call(): pl.pallas_call(body, grid_spec=pltpu.PrefetchScalarGridSpec(num_scalar_pr...  74.7 us
    ppermute x9, waiting for transfers between devices, spread(): lax.ppermute(moments, 'vert', [(i, i ^ shift) for i in range(verts)])  14.7 us
    ppermute x9, starting transfers between devices, spread(): lax.ppermute(moments, 'vert', [(i, i ^ shift) for i in range(verts)])  11.7 us
    ppermute x2, starting transfers between devices, halo(): from_far = lax.ppermute(far, 'row', between + [(b, a) for a, b in between])  5.03 us
    unnamed x6, local copies, waits for them, and re-layouts  5.03 us
  transfers between devices with their start and end apart: 15, of which 8 were waited for; matrix products, arithmetic and copies ran while one was open for 0% of the time, Pallas kernels for 16%

profile of v12, /device:TPU:4, one launch (start us, length us, event | category | flops | bytes accessed | tf_op | source)
XLA Modules:
  0.0 116.3 jit_solution(14542157796480687321)
XLA Ops:
  0.6 0.0 copy-start.1
  0.6 5.0 %copy-done.1 = f32[8,16,27648]{2,1,0:T(8,128)S(1)} copy-done((f32[8,16,27648]{2,1,0:T(8,128)S(1)}, f32[8,16,27648]{2,1,0:T(8,128)}, u32[]{:S(2)}) %copy-start.1) | copy-done | bytes 14155800
  5.7 3.8 %traces.2 = (f32[12,16,1152]{2,1,0:T(8,128)S(1)}, f32[12,16,1152]{2,1,0:T(8,128)S(1)}, f32[12,8,2304]{2,1,0:T(8,128)S(1)}) custom-call(s32[12]{0:T(128)} %a_0_.11, s32[1,2]{1,0:T(1,128)} %bitcast.1, f32[8,16,27648]{2,1,0:T(8,128)S(1)} %copy-done.1, bf16[2,2,32,128]{3,2,1,0:T(8,128)(2,1)} %constant.27.clone.a_3_), custom_call_target="tpu_custom_call" | custom-call | tf_op jit(solution)/shard_map/traces/pallas_call | solution.py:572
  9.5 1.6 %collective-permute-start.3 = (f32[12,8,2304]{2,1,0:T(8,128)S(1)}, f32[12,8,2304]{2,1,0:T(8,128)S(1)}, u32[]{:S(2)}, u32[]{:S(2)}) collective-permute-start(f32[12,8,2304]{2,1,0:T(8,128)S(1)} %get-tuple-element.19), channel_id=1, source_target_pairs={{0,4},{4,0},{1,5},{5,1},{2,6},{6,2},{3,7},{7,3},{8,12},{12,8},{9,1... | collective-permute-start | bytes 2654216 | tf_op jit(solution)/shard_map/ppermute | solution.py:639
  11.1 0.0 collective-permute-start.4
  11.1 2.5 %collective-permute-start.5 = (f32[12,16,1152]{2,1,0:T(8,128)S(1)}, f32[12,16,1152]{2,1,0:T(8,128)S(1)}, u32[]{:S(2)}, u32[]{:S(2)}) collective-permute-start(f32[12,16,1152]{2,1,0:T(8,128)S(1)} %get-tuple-element.17.a_3_), channel_id=1, source_target_pairs={{8,16},{16,8},{9,17},{17,9},{10,18},{18,10},{11,19},{19,11},{12,20... | collective-permute-start | bytes 2654216 | tf_op jit(solution)/shard_map/ppermute | solution.py:643
  13.6 9.1 %moments.2 = (f32[16,128]{1,0:T(8,128)S(1)}, f32[12,16,1152]{2,1,0:T(8,128)S(1)}) custom-call(s32[12]{0:T(128)} %a_0_.11, s32[1,2]{1,0:T(1,128)} %bitcast.2, f32[8,16,27648]{2,1,0:T(8,128)S(1)} %copy-done.1, f32[12,16,1152]{2,1,0:T(8,128)S(1)} %get-tuple-element.17.a_3_, f32[8,2304]{1,0:T(8,128)} %constant.20.clone.a_4_.a_11_, ...), custom_call_target="tpu_custom_call" | custom-call | tf_op jit(solution)/shard_map/moments/pallas_call | solution.py:572
  22.7 3.7 %collective-permute-start.2 = (f32[16,128]{1,0:T(8,128)S(1)}, f32[16,128]{1,0:T(8,128)S(1)}, u32[]{:S(2)}, u32[]{:S(2)}) collective-permute-start(f32[16,128]{1,0:T(8,128)S(1)} %get-tuple-element.18.a_2_), channel_id=1, source_target_pairs={{0,3},{1,2},{2,1},{3,0},{4,7},{5,6},{6,5},{7,4},{8,11},{9,10},{10,... | collective-permute-start | bytes 24584 | tf_op jit(solution)/shard_map/ppermute | solution.py:635
  26.4 0.0 collective-permute-start.1
  26.4 1.8 %collective-permute-done.2.a_5_ = f32[16,128]{1,0:T(8,128)S(1)} collective-permute-done((f32[16,128]{1,0:T(8,128)S(1)}, f32[16,128]{1,0:T(8,128)S(1)}, u32[]{:S(2)}, u32[]{:S(2)}) %collective-permute-start.2) | collective-permute-done | bytes 8224 | tf_op jit(solution)/shard_map/ppermute | solution.py:635
  28.2 0.0 collective-permute-start
  28.2 2.7 %collective-permute-done.1.a_4_ = f32[16,128]{1,0:T(8,128)S(1)} collective-permute-done((f32[16,128]{1,0:T(8,128)S(1)}, f32[16,128]{1,0:T(8,128)S(1)}, u32[]{:S(2)}, u32[]{:S(2)}) %collective-permute-start.1) | collective-permute-done | bytes 8224 | tf_op jit(solution)/shard_map/ppermute | solution.py:635
  30.9 0.9 collective-permute-done.a_3_
  31.9 20.5 %update.1.a_2_.a_6_ = f32[8,16,27648]{2,1,0:T(8,128)S(1)} custom-call(s32[12]{0:T(128)} %a_0_.11, s32[1,2]{1,0:T(1,128)} %bitcast.3, f32[16,128]{1,0:T(8,128)S(1)} %get-tuple-element.18.a_2_, f32[16,128]{1,0:T(8,128)S(1)} %collective-permute-done.a_3_, f32[16,128]{1,0:T(8,128)S(1)} %collective-permute-done.1.a_4_, ...), custom_call_target="tpu_custom_call" | custom-call | tf_op jit(solution)/shard_map/update/pallas_call | solution.py:572
  52.4 3.7 %traces.3 = (f32[12,16,1152]{2,1,0:T(8,128)S(1)}, f32[12,16,1152]{2,1,0:T(8,128)S(1)}, f32[12,8,2304]{2,1,0:T(8,128)S(1)}) custom-call(s32[12]{0:T(128)} %a_0_.11, s32[1,2]{1,0:T(1,128)} %bitcast.4, f32[8,16,27648]{2,1,0:T(8,128)S(1)} %update.1.a_2_.a_6_, bf16[2,2,32,128]{3,2,1,0:T(8,128)(2,1)} %constant.27.clone.a_3_), custom_call_target="tpu_custom_call" | custom-call | tf_op jit(solution)/shard_map/traces/pallas_call | solution.py:572
  56.2 0.6 collective-permute-start.9
  56.8 0.0 collective-permute-start.10
  56.8 2.5 %collective-permute-start.11 = (f32[12,16,1152]{2,1,0:T(8,128)S(1)}, f32[12,16,1152]{2,1,0:T(8,128)S(1)}, u32[]{:S(2)}, u32[]{:S(2)}) collective-permute-start(f32[12,16,1152]{2,1,0:T(8,128)S(1)} %get-tuple-element.22.a_3_), channel_id=1, source_target_pairs={{8,16},{16,8},{9,17},{17,9},{10,18},{18,10},{11,19},{19,11},{12,20... | collective-permute-start | bytes 2654216 | tf_op jit(solution)/shard_map/ppermute | solution.py:643
  59.3 9.1 %moments.3 = (f32[16,128]{1,0:T(8,128)S(1)}, f32[12,16,1152]{2,1,0:T(8,128)S(1)}) custom-call(s32[12]{0:T(128)} %a_0_.11, s32[1,2]{1,0:T(1,128)} %bitcast.5, f32[8,16,27648]{2,1,0:T(8,128)S(1)} %update.1.a_2_.a_6_, f32[12,16,1152]{2,1,0:T(8,128)S(1)} %get-tuple-element.22.a_3_, f32[8,2304]{1,0:T(8,128)} %constant.20.clone.a_4_.a_11_, ...), custom_call_target="tpu_custom_call" | custom-call | tf_op jit(solution)/shard_map/moments/pallas_call | solution.py:572
  68.5 3.7 %collective-permute-start.8 = (f32[16,128]{1,0:T(8,128)S(1)}, f32[16,128]{1,0:T(8,128)S(1)}, u32[]{:S(2)}, u32[]{:S(2)}) collective-permute-start(f32[16,128]{1,0:T(8,128)S(1)} %get-tuple-element.23.a_2_), channel_id=1, source_target_pairs={{0,3},{1,2},{2,1},{3,0},{4,7},{5,6},{6,5},{7,4},{8,11},{9,10},{10,... | collective-permute-start | bytes 24584 | tf_op jit(solution)/shard_map/ppermute | solution.py:635
  72.1 0.0 collective-permute-start.7
  72.1 1.8 %collective-permute-done.8.a_5_ = f32[16,128]{1,0:T(8,128)S(1)} collective-permute-done((f32[16,128]{1,0:T(8,128)S(1)}, f32[16,128]{1,0:T(8,128)S(1)}, u32[]{:S(2)}, u32[]{:S(2)}) %collective-permute-start.8) | collective-permute-done | bytes 8224 | tf_op jit(solution)/shard_map/ppermute | solution.py:635
  74.0 2.7 %collective-permute-done.7.a_4_ = f32[16,128]{1,0:T(8,128)S(1)} collective-permute-done((f32[16,128]{1,0:T(8,128)S(1)}, f32[16,128]{1,0:T(8,128)S(1)}, u32[]{:S(2)}, u32[]{:S(2)}) %collective-permute-start.7) | collective-permute-done | bytes 8224 | tf_op jit(solution)/shard_map/ppermute | solution.py:635
  76.7 0.9 collective-permute-done.6.a_3_
  77.6 0.0 collective-permute-done.11.a_10_
  77.6 28.4 %last_update.1 = (f32[8,16,27648]{2,1,0:T(8,128)}, f32[16,128]{1,0:T(8,128)S(1)}) custom-call(s32[12]{0:T(128)} %a_0_.11, s32[1,2]{1,0:T(1,128)} %bitcast.6, f32[16,128]{1,0:T(8,128)S(1)} %get-tuple-element.23.a_2_, f32[16,128]{1,0:T(8,128)S(1)} %collective-permute-done.6.a_3_, f32[16,128]{1,0:T(8,128)S(1)} %collective-permute-done.7.a_4_, ...), custom_call_target="tpu_custom_call" | custom-call | tf_op jit(solution)/shard_map/last_update/pallas_call | solution.py:572
  106.0 3.6 %collective-permute-start.14 = (f32[16,128]{1,0:T(8,128)S(1)}, f32[16,128]{1,0:T(8,128)S(1)}, u32[]{:S(2)}, u32[]{:S(2)}) collective-permute-start(f32[16,128]{1,0:T(8,128)S(1)} %get-tuple-element.28.a_1_), channel_id=1, source_target_pairs={{0,3},{1,2},{2,1},{3,0},{4,7},{5,6},{6,5},{7,4},{8,11},{9,10},{10,... | collective-permute-start | bytes 24584 | tf_op jit(solution)/shard_map/ppermute | solution.py:635
  109.7 0.0 collective-permute-start.13
  109.7 0.8 collective-permute-start.12
  110.4 1.1 collective-permute-done.14.a_4_
  111.5 2.7 %collective-permute-done.13.a_3_ = f32[16,128]{1,0:T(8,128)S(1)} collective-permute-done((f32[16,128]{1,0:T(8,128)S(1)}, f32[16,128]{1,0:T(8,128)S(1)}, u32[]{:S(2)}, u32[]{:S(2)}) %collective-permute-start.13) | collective-permute-done | bytes 8224 | tf_op jit(solution)/shard_map/ppermute | solution.py:635
  114.2 2.1 %macroscopic.1 = (f32[8,8,16]{2,1,0:T(8,128)}, f32[1,8]{1,0:T(1,128)}) custom-call(s32[1,2]{1,0:T(1,128)} %bitcast.7, f32[16,128]{1,0:T(8,128)S(1)} %get-tuple-element.28.a_1_, f32[16,128]{1,0:T(8,128)S(1)} %collective-permute-done.12.a_2_, f32[16,128]{1,0:T(8,128)S(1)} %collective-permute-done.13.a_3_, f32[16,128]{1,0:T(8,128)S(1)} %collective-permute-done.14.a_4_, ...), custom_call_target="tpu_custom_call" | custom-call | tf_op jit(solution)/shard_map/macroscopic/pallas_call | solution.py:656
  (11 shorter events, 0.0 us)
Async XLA Ops:
  0.6 5.0 %copy-start.1 = (f32[8,16,27648]{2,1,0:T(8,128)S(1)}, f32[8,16,27648]{2,1,0:T(8,128)}, u32[]{:S(2)}) copy-start(f32[8,16,27648]{2,1,0:T(8,128)} %a_6_.1) | copy-start | bytes 42467332
  5.7 26.3 %copy-start.2 = (bf16[9,512,256]{2,1,0:T(8,128)(2,1)S(1)}, bf16[9,512,256]{2,1,0:T(8,128)(2,1)}, u32[]{:S(2)}) copy-start(bf16[9,512,256]{2,1,0:T(8,128)(2,1)} %constant.29.clone.a_18_) | copy-start | bytes 7077892
  9.5 22.4 %collective-permute-start.3 = (f32[12,8,2304]{2,1,0:T(8,128)S(1)}, f32[12,8,2304]{2,1,0:T(8,128)S(1)}, u32[]{:S(2)}, u32[]{:S(2)}) collective-permute-start(f32[12,8,2304]{2,1,0:T(8,128)S(1)} %get-tuple-element.19), channel_id=1, source_target_pairs={{0,4},{4,0},{1,5},{5,1},{2,6},{6,2},{3,7},{7,3},{8,12},{12,8},{9,1... | collective-permute-start | bytes 2654216 | tf_op jit(solution)/shard_map/ppermute | solution.py:639
  11.1 20.8 %collective-permute-start.4 = (f32[12,16,1152]{2,1,0:T(8,128)S(1)}, f32[12,16,1152]{2,1,0:T(8,128)S(1)}, u32[]{:S(2)}, u32[]{:S(2)}) collective-permute-start(f32[12,16,1152]{2,1,0:T(8,128)S(1)} %get-tuple-element.20), channel_id=1, source_target_pairs={{0,8},{8,0},{16,24},{24,16},{1,9},{9,1},{17,25},{25,17},{2,10},{10... | collective-permute-start | bytes 2654216 | tf_op jit(solution)/shard_map/ppermute | solution.py:641
  11.1 20.8 %collective-permute-start.5 = (f32[12,16,1152]{2,1,0:T(8,128)S(1)}, f32[12,16,1152]{2,1,0:T(8,128)S(1)}, u32[]{:S(2)}, u32[]{:S(2)}) collective-permute-start(f32[12,16,1152]{2,1,0:T(8,128)S(1)} %get-tuple-element.17.a_3_), channel_id=1, source_target_pairs={{8,16},{16,8},{9,17},{17,9},{10,18},{18,10},{11,19},{19,11},{12,20... | collective-permute-start | bytes 2654216 | tf_op jit(solution)/shard_map/ppermute | solution.py:643
  22.7 5.5 %collective-permute-start.2 = (f32[16,128]{1,0:T(8,128)S(1)}, f32[16,128]{1,0:T(8,128)S(1)}, u32[]{:S(2)}, u32[]{:S(2)}) collective-permute-start(f32[16,128]{1,0:T(8,128)S(1)} %get-tuple-element.18.a_2_), channel_id=1, source_target_pairs={{0,3},{1,2},{2,1},{3,0},{4,7},{5,6},{6,5},{7,4},{8,11},{9,10},{10,... | collective-permute-start | bytes 24584 | tf_op jit(solution)/shard_map/ppermute | solution.py:635
  26.4 4.5 %collective-permute-start.1 = (f32[16,128]{1,0:T(8,128)S(1)}, f32[16,128]{1,0:T(8,128)S(1)}, u32[]{:S(2)}, u32[]{:S(2)}) collective-permute-start(f32[16,128]{1,0:T(8,128)S(1)} %get-tuple-element.18.a_2_), channel_id=1, source_target_pairs={{0,2},{1,3},{2,0},{3,1},{4,6},{5,7},{6,4},{7,5},{8,10},{9,11},{10,... | collective-permute-start | bytes 24584 | tf_op jit(solution)/shard_map/ppermute | solution.py:635
  28.2 3.7 %collective-permute-start = (f32[16,128]{1,0:T(8,128)S(1)}, f32[16,128]{1,0:T(8,128)S(1)}, u32[]{:S(2)}, u32[]{:S(2)}) collective-permute-start(f32[16,128]{1,0:T(8,128)S(1)} %get-tuple-element.18.a_2_), channel_id=1, source_target_pairs={{0,1},{1,0},{2,3},{3,2},{4,5},{5,4},{6,7},{7,6},{8,9},{9,8},{10,11... | collective-permute-start | bytes 24584 | tf_op jit(solution)/shard_map/ppermute | solution.py:635
  52.4 16.1 %copy-start = (f32[8,16,27648]{2,1,0:T(8,128)}, f32[8,16,27648]{2,1,0:T(8,128)S(1)}, u32[]{:S(2)}) copy-start(f32[8,16,27648]{2,1,0:T(8,128)S(1)} %update.1.a_2_.a_6_) | copy-start | bytes 42467332
  56.2 21.5 %collective-permute-start.9 = (f32[12,8,2304]{2,1,0:T(8,128)S(1)}, f32[12,8,2304]{2,1,0:T(8,128)S(1)}, u32[]{:S(2)}, u32[]{:S(2)}) collective-permute-start(f32[12,8,2304]{2,1,0:T(8,128)S(1)} %get-tuple-element.24), channel_id=1, source_target_pairs={{0,4},{4,0},{1,5},{5,1},{2,6},{6,2},{3,7},{7,3},{8,12},{12,8},{9,1... | collective-permute-start | bytes 2654216 | tf_op jit(solution)/shard_map/ppermute | solution.py:639
  56.8 20.8 %collective-permute-start.10 = (f32[12,16,1152]{2,1,0:T(8,128)S(1)}, f32[12,16,1152]{2,1,0:T(8,128)S(1)}, u32[]{:S(2)}, u32[]{:S(2)}) collective-permute-start(f32[12,16,1152]{2,1,0:T(8,128)S(1)} %get-tuple-element.25), channel_id=1, source_target_pairs={{0,8},{8,0},{16,24},{24,16},{1,9},{9,1},{17,25},{25,17},{2,10},{10... | collective-permute-start | bytes 2654216 | tf_op jit(solution)/shard_map/ppermute | solution.py:641
  56.8 20.8 %collective-permute-start.11 = (f32[12,16,1152]{2,1,0:T(8,128)S(1)}, f32[12,16,1152]{2,1,0:T(8,128)S(1)}, u32[]{:S(2)}, u32[]{:S(2)}) collective-permute-start(f32[12,16,1152]{2,1,0:T(8,128)S(1)} %get-tuple-element.22.a_3_), channel_id=1, source_target_pairs={{8,16},{16,8},{9,17},{17,9},{10,18},{18,10},{11,19},{19,11},{12,20... | collective-permute-start | bytes 2654216 | tf_op jit(solution)/shard_map/ppermute | solution.py:643
  68.5 5.5 %collective-permute-start.8 = (f32[16,128]{1,0:T(8,128)S(1)}, f32[16,128]{1,0:T(8,128)S(1)}, u32[]{:S(2)}, u32[]{:S(2)}) collective-permute-start(f32[16,128]{1,0:T(8,128)S(1)} %get-tuple-element.23.a_2_), channel_id=1, source_target_pairs={{0,3},{1,2},{2,1},{3,0},{4,7},{5,6},{6,5},{7,4},{8,11},{9,10},{10,... | collective-permute-start | bytes 24584 | tf_op jit(solution)/shard_map/ppermute | solution.py:635
  72.1 4.5 %collective-permute-start.7 = (f32[16,128]{1,0:T(8,128)S(1)}, f32[16,128]{1,0:T(8,128)S(1)}, u32[]{:S(2)}, u32[]{:S(2)}) collective-permute-start(f32[16,128]{1,0:T(8,128)S(1)} %get-tuple-element.23.a_2_), channel_id=1, source_target_pairs={{0,2},{1,3},{2,0},{3,1},{4,6},{5,7},{6,4},{7,5},{8,10},{9,11},{10,... | collective-permute-start | bytes 24584 | tf_op jit(solution)/shard_map/ppermute | solution.py:635
  74.0 3.7 %collective-permute-start.6 = (f32[16,128]{1,0:T(8,128)S(1)}, f32[16,128]{1,0:T(8,128)S(1)}, u32[]{:S(2)}, u32[]{:S(2)}) collective-permute-start(f32[16,128]{1,0:T(8,128)S(1)} %get-tuple-element.23.a_2_), channel_id=1, source_target_pairs={{0,1},{1,0},{2,3},{3,2},{4,5},{5,4},{6,7},{7,6},{8,9},{9,8},{10,11... | collective-permute-start | bytes 24584 | tf_op jit(solution)/shard_map/ppermute | solution.py:635
  106.0 5.4 %collective-permute-start.14 = (f32[16,128]{1,0:T(8,128)S(1)}, f32[16,128]{1,0:T(8,128)S(1)}, u32[]{:S(2)}, u32[]{:S(2)}) collective-permute-start(f32[16,128]{1,0:T(8,128)S(1)} %get-tuple-element.28.a_1_), channel_id=1, source_target_pairs={{0,3},{1,2},{2,1},{3,0},{4,7},{5,6},{6,5},{7,4},{8,11},{9,10},{10,... | collective-permute-start | bytes 24584 | tf_op jit(solution)/shard_map/ppermute | solution.py:635
  109.7 4.5 %collective-permute-start.13 = (f32[16,128]{1,0:T(8,128)S(1)}, f32[16,128]{1,0:T(8,128)S(1)}, u32[]{:S(2)}, u32[]{:S(2)}) collective-permute-start(f32[16,128]{1,0:T(8,128)S(1)} %get-tuple-element.28.a_1_), channel_id=1, source_target_pairs={{0,2},{1,3},{2,0},{3,1},{4,6},{5,7},{6,4},{7,5},{8,10},{9,11},{10,... | collective-permute-start | bytes 24584 | tf_op jit(solution)/shard_map/ppermute | solution.py:635
  109.7 4.5 %collective-permute-start.12 = (f32[16,128]{1,0:T(8,128)S(1)}, f32[16,128]{1,0:T(8,128)S(1)}, u32[]{:S(2)}, u32[]{:S(2)}) collective-permute-start(f32[16,128]{1,0:T(8,128)S(1)} %get-tuple-element.28.a_1_), channel_id=1, source_target_pairs={{0,1},{1,0},{2,3},{3,2},{4,5},{5,4},{6,7},{7,6},{8,9},{9,8},{10,11... | collective-permute-start | bytes 24584 | tf_op jit(solution)/shard_map/ppermute | solution.py:635

commit v13 on v12

--- a/solution.py
+++ b/solution.py
@@ -116,13 +116,16 @@
     zout = np.block([[down, np.outer(LIFT_R, END_L)], [zero, DERIV]])
     axial = np.stack([np.kron(ident, zdown), np.kron(ident, zup), np.kron(ident, zout)])
     ghost_r = np.zeros((2, NODE_COUNT, 128))
-    ghost_z = np.zeros((2, LOCAL_Z, 128))
+    ghost_z = np.zeros((2, NODE_COUNT, 128))
     for r in range(NODES):
-        ghost_r[0, r * LOCAL_Z : (r + 1) * LOCAL_Z] = -LIFT_R[r]
-        ghost_r[1, r * LOCAL_Z : (r + 1) * LOCAL_Z] = LIFT_L[r]
-    for k in range(NODES):
-        ghost_z[0, NODES + k] = LIFT_R[k]
-        ghost_z[1, k] = LIFT_L[k]
+        for z in range(LOCAL_Z):
+            n = r * LOCAL_Z + z
+            ghost_r[0, n, z] = -LIFT_R[r]
+            ghost_r[1, n, z] = LIFT_L[r]
+            if z >= NODES:
+                ghost_z[0, n, LOCAL_Z + r] = LIFT_R[z - NODES]
+            else:
+                ghost_z[1, n, LOCAL_Z + r] = LIFT_L[z]
     trace = np.zeros((2, 2, GHOST_ROWS, NODE_COUNT))
     for side in range(2):
         radial_row = END_R if side == 1 else END_L
@@ -398,7 +401,7 @@
 
 
 def ghost_rows(
-    s, vz, row, place, in_axial_ref, in_near_ref, in_turned_ref, in_far_ref, rows_ref, wall_ref, radial_ref, axial_ref
+    s, vz, row, place, in_axial_ref, in_near_ref, in_turned_ref, in_far_ref, rows_ref, wall_ref, ghost_ref
 ):
     own = (place == 0) == (vz > 0)
     even = lax.rem(row, 2) == 0
@@ -410,10 +413,9 @@
         else:
             back = pl.ds(j * 128 - HALF, 128)
             radial = jnp.where(even, in_far_ref[s, :, back], in_near_ref[s, :, back]) + in_turned_ref[s, :, back]
-        radial_ref[s, :, at] = rows_ref[0:1, at] * radial
         axial = jnp.where(own, strength * rows_ref[2:3, at], in_axial_ref[s, :, at])
-        for r in range(NODES):
-            axial_ref[s, r, :, at] = jnp.broadcast_to(axial[r : r + 1], (NODES, 128))
+        rows = jnp.concatenate([rows_ref[0:1, at] * radial, axial, jnp.zeros((8, 128), F32)], axis=0)
+        ghost_ref[s * GHOST_ROWS : (s + 1) * GHOST_ROWS, at] = rows.astype(BF16)
 
 
 def outer_kernel(count, part_count, last, order, codes, *refs):
@@ -423,8 +425,8 @@
     refs = refs[14:]
     if last:
         (mom_ref, sums_ref), refs = refs[:2], refs[2:]
-    plane_ref, node_ref, wall_ref, slot_ref, lean_ref, radial_ref, axial_ref, table_ref = refs[:8]
-    inverse_ref, pad_ref, lhs_ref, work_ref = refs[8:]
+    plane_ref, node_ref, wall_ref, slot_ref, lift_ref, ghost_ref, table_ref = refs[:7]
+    inverse_ref, pad_ref, lhs_ref, work_ref = refs[7:]
     step = pl.program_id(0)
     row, place = places_of()
 
@@ -447,10 +449,12 @@
         vz = speeds[s]
         for k, value in enumerate(slot_factors(vz, node_ref)):
             slot_ref[s, k] = value
-        lean_ref[s] = jnp.abs(vz) * ghost_z_ref[jnp.where(vz > 0, 1, 0)]
+        lean = jnp.abs(vz) * ghost_z_ref[jnp.where(vz > 0, 1, 0)]
+        for side in range(2):
+            lift = ghost_r_ref[side] + lean
+            lift_ref[s, side] = (pltpu.roll(lift, s * GHOST_ROWS, 1) if s else lift).astype(BF16)
         ghost_rows(
-            s, vz, row, place, in_axial_ref, in_near_ref, in_turned_ref, in_far_ref, rows_ref, wall_ref,
-            radial_ref, axial_ref,
+            s, vz, row, place, in_axial_ref, in_near_ref, in_turned_ref, in_far_ref, rows_ref, wall_ref, ghost_ref
         )
 
     kind_out = jnp.where(jnp.logical_and(place == 1, codes[0, TOP] == 2), 2, 0)
@@ -463,26 +467,31 @@
             field = nodes_of(f_ref, s * PLANE + j * 128, 128)
             pad_ref[s, :, 128 + j * 128 : 256 + j * 128] = (field * inverse).astype(BF16)
 
-    for tile in range(PLANE // TILE):
+    held = count * GHOST_ROWS
+    lane = lax.broadcasted_iota(jnp.int32, (count * NODE_COUNT, 128), 1)
+    for first, lanes, side in PIECES:
+        tile = first // TILE
         start = tile * TILE
-        turned = dot(pad_ref[:, :, start : start + WINDOW].reshape(count * NODE_COUNT, WINDOW), rot_ref[tile])
-        for first, lanes, side in PIECES:
-            if first // TILE != tile:
-                continue
-            vr = rows_ref[0:1, first : first + lanes]
-            inside = first - start
-            for s in range(count):
-                field = nodes_of(f_ref, s * PLANE + first, lanes)
-                both = jnp.concatenate([(field * vr).astype(BF16), field.astype(BF16)], axis=0)
-                change = turned[s * NODE_COUNT : (s + 1) * NODE_COUNT, inside : inside + lanes]
-                work_ref[s, :, first : first + lanes] = change + dot(lhs_ref[s, side], both)
+        inside = first - start
+        lifts = lift_ref[:, side].reshape(count * NODE_COUNT, 128)
+        window = pad_ref[:, :, start : start + WINDOW].reshape(count * NODE_COUNT, WINDOW)
+        window = jnp.concatenate([jnp.where(lane < held, lifts, window[:, 0:128]), window[:, 128:]], axis=1)
+        turning = jnp.concatenate(
+            [ghost_ref[:, first : first + lanes], rot_ref[tile, held:, inside : inside + lanes]], axis=0
+        )
+        turned = dot(window, turning)
+        vr = rows_ref[0:1, first : first + lanes]
+        for s in range(count):
+            field = nodes_of(f_ref, s * PLANE + first, lanes)
+            both = jnp.concatenate([(field * vr).astype(BF16), field.astype(BF16)], axis=0)
+            work_ref[s, :, first : first + lanes] = turned[s * NODE_COUNT : (s + 1) * NODE_COUNT] + dot(
+                lhs_ref[s, side], both
+            )
 
     def update(r, carry):
         rows = pl.ds(pl.multiple_of(r * LOCAL_Z, LOCAL_Z), LOCAL_Z)
         keep = node_ref[5, rows, :]
-        lifts = [ghost_r_ref[side, rows, :] for side in range(2)]
         factor = [[slot_ref[s, k, rows, :] for k in range(3)] for s in range(count)]
-        lean = [lean_ref[s] for s in range(count)]
         for j in range(PLANE // 128):
             at = pl.ds(j * 128, 128)
             gauss, along, reach = (plane_ref[k, rows, at] for k in range(3))
@@ -490,10 +499,7 @@
                 sums = [sums_ref[k, r, :, at] for k in range(5)]
             for s in range(count):
                 here = pl.ds(s * PLANE + j * 128, 128)
-                across = axial_ref[s, r, :, at]
                 new = f_ref[r, :, here] * keep + work_ref[s, rows, at]
-                new = new + radial_ref[s, :, at] * lifts[1 if j * 128 >= HALF else 0]
-                new = new + jnp.concatenate([across, across], axis=0) * lean[s]
                 bend = (along + factor[s][1]) * (reach + factor[s][2]) + 1.0
                 new = new + (gauss * factor[s][0]) * bend
                 out_ref[r, :, here] = new
@@ -611,9 +617,8 @@
             pltpu.VMEM((10, NODE_COUNT, 128), F32),
             pltpu.VMEM((NODES, 128), F32),
             pltpu.VMEM((count, 3, NODE_COUNT, 128), F32),
-            pltpu.VMEM((count, LOCAL_Z, 128), F32),
-            pltpu.VMEM((count, LOCAL_Z, PLANE), F32),
-            pltpu.VMEM((count, NODES, NODES, PLANE), F32),
+            pltpu.VMEM((count, 2, NODE_COUNT, 128), BF16),
+            pltpu.VMEM((count * GHOST_ROWS, PLANE), BF16),
             square,
             square,
             pltpu.VMEM((count, NODE_COUNT, PLANE + 256), BF16),

time: 117 us -> 112 us (0.957)
  Pallas kernels: 76.9 us -> 71.9 us
    pallas_call x6, Pallas kernels: 74.7 us -> 69.8 us  [call(): pl.pallas_call(body, grid_spec=pltpu.PrefetchScalarGridSpec(num_scalar_pr...]
where the time goes in v13:
time: 112 us; the launch traced here: 111 us
  Pallas kernels  71.9 us (64%)
  starting transfers between devices  19 us (17%)
  waiting for transfers between devices  14.8 us (13%)
  local copies, waits for them, and re-layouts  5.03 us (4%)
    pallas_call x6, Pallas kernels, call(): pl.pallas_call(body, grid_spec=pltpu.PrefetchScalarGridSpec(num_scalar_pr...  69.8 us
    ppermute x9, waiting for transfers between devices, spread(): lax.ppermute(moments, 'vert', [(i, i ^ shift) for i in range(verts)])  14.7 us
    ppermute x9, starting transfers between devices, spread(): lax.ppermute(moments, 'vert', [(i, i ^ shift) for i in range(verts)])  11.7 us
    ppermute x2, starting transfers between devices, halo(): from_far = lax.ppermute(far, 'row', between + [(b, a) for a, b in between])  5.03 us
    unnamed x6, local copies, waits for them, and re-layouts  5.03 us
  transfers between devices with their start and end apart: 15, of which 8 were waited for; matrix products, arithmetic and copies ran while one was open for 0% of the time, Pallas kernels for 16%

profile of v13, /device:TPU:4, one launch (start us, length us, event | category | flops | bytes accessed | tf_op | source)
XLA Modules:
  0.0 111.4 jit_solution(7005156434645768997)
XLA Ops:
  0.6 0.0 copy-start.1
  0.6 5.0 %copy-done.1 = f32[8,16,27648]{2,1,0:T(8,128)S(1)} copy-done((f32[8,16,27648]{2,1,0:T(8,128)S(1)}, f32[8,16,27648]{2,1,0:T(8,128)}, u32[]{:S(2)}) %copy-start.1) | copy-done | bytes 14155800
  5.7 3.8 %traces.2 = (f32[12,16,1152]{2,1,0:T(8,128)S(1)}, f32[12,16,1152]{2,1,0:T(8,128)S(1)}, f32[12,8,2304]{2,1,0:T(8,128)S(1)}) custom-call(s32[12]{0:T(128)} %a_0_.11, s32[1,2]{1,0:T(1,128)} %bitcast.1, f32[8,16,27648]{2,1,0:T(8,128)S(1)} %copy-done.1, bf16[2,2,32,128]{3,2,1,0:T(8,128)(2,1)} %constant.27.clone.a_3_), custom_call_target="tpu_custom_call" | custom-call | tf_op jit(solution)/shard_map/traces/pallas_call | solution.py:578
  9.5 1.6 %collective-permute-start.3 = (f32[12,8,2304]{2,1,0:T(8,128)S(1)}, f32[12,8,2304]{2,1,0:T(8,128)S(1)}, u32[]{:S(2)}, u32[]{:S(2)}) collective-permute-start(f32[12,8,2304]{2,1,0:T(8,128)S(1)} %get-tuple-element.19), channel_id=1, source_target_pairs={{0,4},{4,0},{1,5},{5,1},{2,6},{6,2},{3,7},{7,3},{8,12},{12,8},{9,1... | collective-permute-start | bytes 2654216 | tf_op jit(solution)/shard_map/ppermute | solution.py:644
  11.1 2.5 %collective-permute-start.5 = (f32[12,16,1152]{2,1,0:T(8,128)S(1)}, f32[12,16,1152]{2,1,0:T(8,128)S(1)}, u32[]{:S(2)}, u32[]{:S(2)}) collective-permute-start(f32[12,16,1152]{2,1,0:T(8,128)S(1)} %get-tuple-element.17.a_3_), channel_id=1, source_target_pairs={{8,16},{16,8},{9,17},{17,9},{10,18},{18,10},{11,19},{19,11},{12,20... | collective-permute-start | bytes 2654216 | tf_op jit(solution)/shard_map/ppermute | solution.py:648
  13.6 9.1 %moments.2 = (f32[16,128]{1,0:T(8,128)S(1)}, f32[12,16,1152]{2,1,0:T(8,128)S(1)}) custom-call(s32[12]{0:T(128)} %a_0_.11, s32[1,2]{1,0:T(1,128)} %bitcast.2, f32[8,16,27648]{2,1,0:T(8,128)S(1)} %copy-done.1, f32[12,16,1152]{2,1,0:T(8,128)S(1)} %get-tuple-element.17.a_3_, f32[8,2304]{1,0:T(8,128)} %constant.20.clone.a_4_.a_11_, ...), custom_call_target="tpu_custom_call" | custom-call | tf_op jit(solution)/shard_map/moments/pallas_call | solution.py:578
  22.7 3.7 %collective-permute-start.2 = (f32[16,128]{1,0:T(8,128)S(1)}, f32[16,128]{1,0:T(8,128)S(1)}, u32[]{:S(2)}, u32[]{:S(2)}) collective-permute-start(f32[16,128]{1,0:T(8,128)S(1)} %get-tuple-element.18.a_2_), channel_id=1, source_target_pairs={{0,3},{1,2},{2,1},{3,0},{4,7},{5,6},{6,5},{7,4},{8,11},{9,10},{10,... | collective-permute-start | bytes 24584 | tf_op jit(solution)/shard_map/ppermute | solution.py:640
  26.4 0.0 collective-permute-start.1
  26.4 1.8 %collective-permute-done.2.a_5_ = f32[16,128]{1,0:T(8,128)S(1)} collective-permute-done((f32[16,128]{1,0:T(8,128)S(1)}, f32[16,128]{1,0:T(8,128)S(1)}, u32[]{:S(2)}, u32[]{:S(2)}) %collective-permute-start.2) | collective-permute-done | bytes 8224 | tf_op jit(solution)/shard_map/ppermute | solution.py:640
  28.2 0.0 collective-permute-start
  28.2 2.7 %collective-permute-done.1.a_4_ = f32[16,128]{1,0:T(8,128)S(1)} collective-permute-done((f32[16,128]{1,0:T(8,128)S(1)}, f32[16,128]{1,0:T(8,128)S(1)}, u32[]{:S(2)}, u32[]{:S(2)}) %collective-permute-start.1) | collective-permute-done | bytes 8224 | tf_op jit(solution)/shard_map/ppermute | solution.py:640
  30.9 0.9 collective-permute-done.a_3_
  31.9 18.3 %update.1.a_2_.a_6_ = f32[8,16,27648]{2,1,0:T(8,128)S(1)} custom-call(s32[12]{0:T(128)} %a_0_.11, s32[1,2]{1,0:T(1,128)} %bitcast.3, f32[16,128]{1,0:T(8,128)S(1)} %get-tuple-element.18.a_2_, f32[16,128]{1,0:T(8,128)S(1)} %collective-permute-done.a_3_, f32[16,128]{1,0:T(8,128)S(1)} %collective-permute-done.1.a_4_, ...), custom_call_target="tpu_custom_call" | custom-call | tf_op jit(solution)/shard_map/update/pallas_call | solution.py:578
  50.2 3.7 %traces.3 = (f32[12,16,1152]{2,1,0:T(8,128)S(1)}, f32[12,16,1152]{2,1,0:T(8,128)S(1)}, f32[12,8,2304]{2,1,0:T(8,128)S(1)}) custom-call(s32[12]{0:T(128)} %a_0_.11, s32[1,2]{1,0:T(1,128)} %bitcast.4, f32[8,16,27648]{2,1,0:T(8,128)S(1)} %update.1.a_2_.a_6_, bf16[2,2,32,128]{3,2,1,0:T(8,128)(2,1)} %constant.27.clone.a_3_), custom_call_target="tpu_custom_call" | custom-call | tf_op jit(solution)/shard_map/traces/pallas_call | solution.py:578
  54.0 0.6 collective-permute-start.9
  54.6 0.0 collective-permute-start.10
  54.6 2.5 %collective-permute-start.11 = (f32[12,16,1152]{2,1,0:T(8,128)S(1)}, f32[12,16,1152]{2,1,0:T(8,128)S(1)}, u32[]{:S(2)}, u32[]{:S(2)}) collective-permute-start(f32[12,16,1152]{2,1,0:T(8,128)S(1)} %get-tuple-element.22.a_3_), channel_id=1, source_target_pairs={{8,16},{16,8},{9,17},{17,9},{10,18},{18,10},{11,19},{19,11},{12,20... | collective-permute-start | bytes 2654216 | tf_op jit(solution)/shard_map/ppermute | solution.py:648
  57.1 9.1 %moments.3 = (f32[16,128]{1,0:T(8,128)S(1)}, f32[12,16,1152]{2,1,0:T(8,128)S(1)}) custom-call(s32[12]{0:T(128)} %a_0_.11, s32[1,2]{1,0:T(1,128)} %bitcast.5, f32[8,16,27648]{2,1,0:T(8,128)S(1)} %update.1.a_2_.a_6_, f32[12,16,1152]{2,1,0:T(8,128)S(1)} %get-tuple-element.22.a_3_, f32[8,2304]{1,0:T(8,128)} %constant.20.clone.a_4_.a_11_, ...), custom_call_target="tpu_custom_call" | custom-call | tf_op jit(solution)/shard_map/moments/pallas_call | solution.py:578
  66.3 3.7 %collective-permute-start.8 = (f32[16,128]{1,0:T(8,128)S(1)}, f32[16,128]{1,0:T(8,128)S(1)}, u32[]{:S(2)}, u32[]{:S(2)}) collective-permute-start(f32[16,128]{1,0:T(8,128)S(1)} %get-tuple-element.23.a_2_), channel_id=1, source_target_pairs={{0,3},{1,2},{2,1},{3,0},{4,7},{5,6},{6,5},{7,4},{8,11},{9,10},{10,... | collective-permute-start | bytes 24584 | tf_op jit(solution)/shard_map/ppermute | solution.py:640
  69.9 0.0 collective-permute-start.7
  69.9 1.8 %collective-permute-done.8.a_5_ = f32[16,128]{1,0:T(8,128)S(1)} collective-permute-done((f32[16,128]{1,0:T(8,128)S(1)}, f32[16,128]{1,0:T(8,128)S(1)}, u32[]{:S(2)}, u32[]{:S(2)}) %collective-permute-start.8) | collective-permute-done | bytes 8224 | tf_op jit(solution)/shard_map/ppermute | solution.py:640
  71.8 2.7 %collective-permute-done.7.a_4_ = f32[16,128]{1,0:T(8,128)S(1)} collective-permute-done((f32[16,128]{1,0:T(8,128)S(1)}, f32[16,128]{1,0:T(8,128)S(1)}, u32[]{:S(2)}, u32[]{:S(2)}) %collective-permute-start.7) | collective-permute-done | bytes 8224 | tf_op jit(solution)/shard_map/ppermute | solution.py:640
  74.5 1.0 collective-permute-done.6.a_3_
  75.4 0.0 collective-permute-done.10.a_8_
  75.4 0.0 collective-permute-done.11.a_10_
  75.4 25.7 %last_update.1 = (f32[8,16,27648]{2,1,0:T(8,128)}, f32[16,128]{1,0:T(8,128)S(1)}) custom-call(s32[12]{0:T(128)} %a_0_.11, s32[1,2]{1,0:T(1,128)} %bitcast.6, f32[16,128]{1,0:T(8,128)S(1)} %get-tuple-element.23.a_2_, f32[16,128]{1,0:T(8,128)S(1)} %collective-permute-done.6.a_3_, f32[16,128]{1,0:T(8,128)S(1)} %collective-permute-done.7.a_4_, ...), custom_call_target="tpu_custom_call" | custom-call | tf_op jit(solution)/shard_map/last_update/pallas_call | solution.py:578
  101.1 3.6 %collective-permute-start.14 = (f32[16,128]{1,0:T(8,128)S(1)}, f32[16,128]{1,0:T(8,128)S(1)}, u32[]{:S(2)}, u32[]{:S(2)}) collective-permute-start(f32[16,128]{1,0:T(8,128)S(1)} %get-tuple-element.28.a_1_), channel_id=1, source_target_pairs={{0,3},{1,2},{2,1},{3,0},{4,7},{5,6},{6,5},{7,4},{8,11},{9,10},{10,... | collective-permute-start | bytes 24584 | tf_op jit(solution)/shard_map/ppermute | solution.py:640
  104.7 0.8 collective-permute-start.12
  105.5 1.1 collective-permute-done.14.a_4_
  106.6 2.7 %collective-permute-done.13.a_3_ = f32[16,128]{1,0:T(8,128)S(1)} collective-permute-done((f32[16,128]{1,0:T(8,128)S(1)}, f32[16,128]{1,0:T(8,128)S(1)}, u32[]{:S(2)}, u32[]{:S(2)}) %collective-permute-start.13) | collective-permute-done | bytes 8224 | tf_op jit(solution)/shard_map/ppermute | solution.py:640
  109.3 0.0 collective-permute-done.12.a_2_
  109.3 2.1 %macroscopic.1 = (f32[8,8,16]{2,1,0:T(8,128)}, f32[1,8]{1,0:T(1,128)}) custom-call(s32[1,2]{1,0:T(1,128)} %bitcast.7, f32[16,128]{1,0:T(8,128)S(1)} %get-tuple-element.28.a_1_, f32[16,128]{1,0:T(8,128)S(1)} %collective-permute-done.12.a_2_, f32[16,128]{1,0:T(8,128)S(1)} %collective-permute-done.13.a_3_, f32[16,128]{1,0:T(8,128)S(1)} %collective-permute-done.14.a_4_, ...), custom_call_target="tpu_custom_call" | custom-call | tf_op jit(solution)/shard_map/macroscopic/pallas_call | solution.py:661
  (11 shorter events, 0.0 us)
Async XLA Ops:
  0.6 5.0 %copy-start.1 = (f32[8,16,27648]{2,1,0:T(8,128)S(1)}, f32[8,16,27648]{2,1,0:T(8,128)}, u32[]{:S(2)}) copy-start(f32[8,16,27648]{2,1,0:T(8,128)} %a_6_.1) | copy-start | bytes 42467332
  5.7 26.3 %copy-start.2 = (bf16[9,512,256]{2,1,0:T(8,128)(2,1)S(1)}, bf16[9,512,256]{2,1,0:T(8,128)(2,1)}, u32[]{:S(2)}) copy-start(bf16[9,512,256]{2,1,0:T(8,128)(2,1)} %constant.29.clone.a_18_) | copy-start | bytes 7077892
  9.5 22.4 %collective-permute-start.3 = (f32[12,8,2304]{2,1,0:T(8,128)S(1)}, f32[12,8,2304]{2,1,0:T(8,128)S(1)}, u32[]{:S(2)}, u32[]{:S(2)}) collective-permute-start(f32[12,8,2304]{2,1,0:T(8,128)S(1)} %get-tuple-element.19), channel_id=1, source_target_pairs={{0,4},{4,0},{1,5},{5,1},{2,6},{6,2},{3,7},{7,3},{8,12},{12,8},{9,1... | collective-permute-start | bytes 2654216 | tf_op jit(solution)/shard_map/ppermute | solution.py:644
  11.1 20.8 %collective-permute-start.4 = (f32[12,16,1152]{2,1,0:T(8,128)S(1)}, f32[12,16,1152]{2,1,0:T(8,128)S(1)}, u32[]{:S(2)}, u32[]{:S(2)}) collective-permute-start(f32[12,16,1152]{2,1,0:T(8,128)S(1)} %get-tuple-element.20), channel_id=1, source_target_pairs={{0,8},{8,0},{16,24},{24,16},{1,9},{9,1},{17,25},{25,17},{2,10},{10... | collective-permute-start | bytes 2654216 | tf_op jit(solution)/shard_map/ppermute | solution.py:646
  11.1 20.8 %collective-permute-start.5 = (f32[12,16,1152]{2,1,0:T(8,128)S(1)}, f32[12,16,1152]{2,1,0:T(8,128)S(1)}, u32[]{:S(2)}, u32[]{:S(2)}) collective-permute-start(f32[12,16,1152]{2,1,0:T(8,128)S(1)} %get-tuple-element.17.a_3_), channel_id=1, source_target_pairs={{8,16},{16,8},{9,17},{17,9},{10,18},{18,10},{11,19},{19,11},{12,20... | collective-permute-start | bytes 2654216 | tf_op jit(solution)/shard_map/ppermute | solution.py:648
  22.7 5.5 %collective-permute-start.2 = (f32[16,128]{1,0:T(8,128)S(1)}, f32[16,128]{1,0:T(8,128)S(1)}, u32[]{:S(2)}, u32[]{:S(2)}) collective-permute-start(f32[16,128]{1,0:T(8,128)S(1)} %get-tuple-element.18.a_2_), channel_id=1, source_target_pairs={{0,3},{1,2},{2,1},{3,0},{4,7},{5,6},{6,5},{7,4},{8,11},{9,10},{10,... | collective-permute-start | bytes 24584 | tf_op jit(solution)/shard_map/ppermute | solution.py:640
  26.4 4.5 %collective-permute-start.1 = (f32[16,128]{1,0:T(8,128)S(1)}, f32[16,128]{1,0:T(8,128)S(1)}, u32[]{:S(2)}, u32[]{:S(2)}) collective-permute-start(f32[16,128]{1,0:T(8,128)S(1)} %get-tuple-element.18.a_2_), channel_id=1, source_target_pairs={{0,2},{1,3},{2,0},{3,1},{4,6},{5,7},{6,4},{7,5},{8,10},{9,11},{10,... | collective-permute-start | bytes 24584 | tf_op jit(solution)/shard_map/ppermute | solution.py:640
  28.2 3.7 %collective-permute-start = (f32[16,128]{1,0:T(8,128)S(1)}, f32[16,128]{1,0:T(8,128)S(1)}, u32[]{:S(2)}, u32[]{:S(2)}) collective-permute-start(f32[16,128]{1,0:T(8,128)S(1)} %get-tuple-element.18.a_2_), channel_id=1, source_target_pairs={{0,1},{1,0},{2,3},{3,2},{4,5},{5,4},{6,7},{7,6},{8,9},{9,8},{10,11... | collective-permute-start | bytes 24584 | tf_op jit(solution)/shard_map/ppermute | solution.py:640
  50.2 16.1 %copy-start = (f32[8,16,27648]{2,1,0:T(8,128)}, f32[8,16,27648]{2,1,0:T(8,128)S(1)}, u32[]{:S(2)}) copy-start(f32[8,16,27648]{2,1,0:T(8,128)S(1)} %update.1.a_2_.a_6_) | copy-start | bytes 42467332
  54.0 21.5 %collective-permute-start.9 = (f32[12,8,2304]{2,1,0:T(8,128)S(1)}, f32[12,8,2304]{2,1,0:T(8,128)S(1)}, u32[]{:S(2)}, u32[]{:S(2)}) collective-permute-start(f32[12,8,2304]{2,1,0:T(8,128)S(1)} %get-tuple-element.24), channel_id=1, source_target_pairs={{0,4},{4,0},{1,5},{5,1},{2,6},{6,2},{3,7},{7,3},{8,12},{12,8},{9,1... | collective-permute-start | bytes 2654216 | tf_op jit(solution)/shard_map/ppermute | solution.py:644
  54.6 20.8 %collective-permute-start.10 = (f32[12,16,1152]{2,1,0:T(8,128)S(1)}, f32[12,16,1152]{2,1,0:T(8,128)S(1)}, u32[]{:S(2)}, u32[]{:S(2)}) collective-permute-start(f32[12,16,1152]{2,1,0:T(8,128)S(1)} %get-tuple-element.25), channel_id=1, source_target_pairs={{0,8},{8,0},{16,24},{24,16},{1,9},{9,1},{17,25},{25,17},{2,10},{10... | collective-permute-start | bytes 2654216 | tf_op jit(solution)/shard_map/ppermute | solution.py:646
  54.6 20.8 %collective-permute-start.11 = (f32[12,16,1152]{2,1,0:T(8,128)S(1)}, f32[12,16,1152]{2,1,0:T(8,128)S(1)}, u32[]{:S(2)}, u32[]{:S(2)}) collective-permute-start(f32[12,16,1152]{2,1,0:T(8,128)S(1)} %get-tuple-element.22.a_3_), channel_id=1, source_target_pairs={{8,16},{16,8},{9,17},{17,9},{10,18},{18,10},{11,19},{19,11},{12,20... | collective-permute-start | bytes 2654216 | tf_op jit(solution)/shard_map/ppermute | solution.py:648
  66.3 5.5 %collective-permute-start.8 = (f32[16,128]{1,0:T(8,128)S(1)}, f32[16,128]{1,0:T(8,128)S(1)}, u32[]{:S(2)}, u32[]{:S(2)}) collective-permute-start(f32[16,128]{1,0:T(8,128)S(1)} %get-tuple-element.23.a_2_), channel_id=1, source_target_pairs={{0,3},{1,2},{2,1},{3,0},{4,7},{5,6},{6,5},{7,4},{8,11},{9,10},{10,... | collective-permute-start | bytes 24584 | tf_op jit(solution)/shard_map/ppermute | solution.py:640
  69.9 4.5 %collective-permute-start.7 = (f32[16,128]{1,0:T(8,128)S(1)}, f32[16,128]{1,0:T(8,128)S(1)}, u32[]{:S(2)}, u32[]{:S(2)}) collective-permute-start(f32[16,128]{1,0:T(8,128)S(1)} %get-tuple-element.23.a_2_), channel_id=1, source_target_pairs={{0,2},{1,3},{2,0},{3,1},{4,6},{5,7},{6,4},{7,5},{8,10},{9,11},{10,... | collective-permute-start | bytes 24584 | tf_op jit(solution)/shard_map/ppermute | solution.py:640
  71.8 3.7 %collective-permute-start.6 = (f32[16,128]{1,0:T(8,128)S(1)}, f32[16,128]{1,0:T(8,128)S(1)}, u32[]{:S(2)}, u32[]{:S(2)}) collective-permute-start(f32[16,128]{1,0:T(8,128)S(1)} %get-tuple-element.23.a_2_), channel_id=1, source_target_pairs={{0,1},{1,0},{2,3},{3,2},{4,5},{5,4},{6,7},{7,6},{8,9},{9,8},{10,11... | collective-permute-start | bytes 24584 | tf_op jit(solution)/shard_map/ppermute | solution.py:640
  101.1 5.4 %collective-permute-start.14 = (f32[16,128]{1,0:T(8,128)S(1)}, f32[16,128]{1,0:T(8,128)S(1)}, u32[]{:S(2)}, u32[]{:S(2)}) collective-permute-start(f32[16,128]{1,0:T(8,128)S(1)} %get-tuple-element.28.a_1_), channel_id=1, source_target_pairs={{0,3},{1,2},{2,1},{3,0},{4,7},{5,6},{6,5},{7,4},{8,11},{9,10},{10,... | collective-permute-start | bytes 24584 | tf_op jit(solution)/shard_map/ppermute | solution.py:640
  104.7 4.5 %collective-permute-start.13 = (f32[16,128]{1,0:T(8,128)S(1)}, f32[16,128]{1,0:T(8,128)S(1)}, u32[]{:S(2)}, u32[]{:S(2)}) collective-permute-start(f32[16,128]{1,0:T(8,128)S(1)} %get-tuple-element.28.a_1_), channel_id=1, source_target_pairs={{0,2},{1,3},{2,0},{3,1},{4,6},{5,7},{6,4},{7,5},{8,10},{9,11},{10,... | collective-permute-start | bytes 24584 | tf_op jit(solution)/shard_map/ppermute | solution.py:640
  104.7 4.5 %collective-permute-start.12 = (f32[16,128]{1,0:T(8,128)S(1)}, f32[16,128]{1,0:T(8,128)S(1)}, u32[]{:S(2)}, u32[]{:S(2)}) collective-permute-start(f32[16,128]{1,0:T(8,128)S(1)} %get-tuple-element.28.a_1_), channel_id=1, source_target_pairs={{0,1},{1,0},{2,3},{3,2},{4,5},{5,4},{6,7},{7,6},{8,9},{9,8},{10,11... | collective-permute-start | bytes 24584 | tf_op jit(solution)/shard_map/ppermute | solution.py:640

commit v14 on v13

--- a/solution.py
+++ b/solution.py
@@ -123,9 +123,9 @@
             ghost_r[0, n, z] = -LIFT_R[r]
             ghost_r[1, n, z] = LIFT_L[r]
             if z >= NODES:
-                ghost_z[0, n, LOCAL_Z + r] = LIFT_R[z - NODES]
+                ghost_z[0, n, r] = LIFT_R[z - NODES]
             else:
-                ghost_z[1, n, LOCAL_Z + r] = LIFT_L[z]
+                ghost_z[1, n, r] = LIFT_L[z]
     trace = np.zeros((2, 2, GHOST_ROWS, NODE_COUNT))
     for side in range(2):
         radial_row = END_R if side == 1 else END_L
@@ -401,21 +401,26 @@
 
 
 def ghost_rows(
-    s, vz, row, place, in_axial_ref, in_near_ref, in_turned_ref, in_far_ref, rows_ref, wall_ref, ghost_ref
+    speeds, row, place, in_axial_ref, in_near_ref, in_turned_ref, in_far_ref, rows_ref, wall_ref, ghost_ref
 ):
-    own = (place == 0) == (vz > 0)
+    count = len(speeds)
     even = lax.rem(row, 2) == 0
-    strength = jnp.exp(-0.5 * vz * vz + jnp.zeros((NODES, 128), F32)) * wall_ref[...]
+    fill = ghost_ref.shape[0] - count * (LOCAL_Z + NODES)
+    strengths = [jnp.exp(-0.5 * vz * vz + jnp.zeros((NODES, 128), F32)) * wall_ref[...] for vz in speeds]
     for j in range(PLANE // 128):
         at = pl.ds(j * 128, 128)
-        if j * 128 < HALF:
-            radial = jnp.where(even, in_near_ref[s, :, at], in_far_ref[s, :, at])
-        else:
-            back = pl.ds(j * 128 - HALF, 128)
-            radial = jnp.where(even, in_far_ref[s, :, back], in_near_ref[s, :, back]) + in_turned_ref[s, :, back]
-        axial = jnp.where(own, strength * rows_ref[2:3, at], in_axial_ref[s, :, at])
-        rows = jnp.concatenate([rows_ref[0:1, at] * radial, axial, jnp.zeros((8, 128), F32)], axis=0)
-        ghost_ref[s * GHOST_ROWS : (s + 1) * GHOST_ROWS, at] = rows.astype(BF16)
+        radials, axials = [], []
+        for s in range(count):
+            if j * 128 < HALF:
+                radial = jnp.where(even, in_near_ref[s, :, at], in_far_ref[s, :, at])
+            else:
+                back = pl.ds(j * 128 - HALF, 128)
+                radial = jnp.where(even, in_far_ref[s, :, back], in_near_ref[s, :, back]) + in_turned_ref[s, :, back]
+            own = (place == 0) == (speeds[s] > 0)
+            radials.append(rows_ref[0:1, at] * radial)
+            axials.append(jnp.where(own, strengths[s] * rows_ref[2:3, at], in_axial_ref[s, :, at]))
+        zeros = [jnp.zeros((fill, 128), F32)] if fill else []
+        ghost_ref[:, at] = jnp.concatenate(radials + axials + zeros, axis=0).astype(BF16)
 
 
 def outer_kernel(count, part_count, last, order, codes, *refs):
@@ -450,12 +455,13 @@
         for k, value in enumerate(slot_factors(vz, node_ref)):
             slot_ref[s, k] = value
         lean = jnp.abs(vz) * ghost_z_ref[jnp.where(vz > 0, 1, 0)]
+        lean = pltpu.roll(lean, count * LOCAL_Z + s * NODES, 1)
         for side in range(2):
-            lift = ghost_r_ref[side] + lean
-            lift_ref[s, side] = (pltpu.roll(lift, s * GHOST_ROWS, 1) if s else lift).astype(BF16)
-        ghost_rows(
-            s, vz, row, place, in_axial_ref, in_near_ref, in_turned_ref, in_far_ref, rows_ref, wall_ref, ghost_ref
-        )
+            lift = ghost_r_ref[side]
+            lift_ref[s, side] = ((pltpu.roll(lift, s * LOCAL_Z, 1) if s else lift) + lean).astype(BF16)
+    ghost_rows(
+        speeds, row, place, in_axial_ref, in_near_ref, in_turned_ref, in_far_ref, rows_ref, wall_ref, ghost_ref
+    )
 
     kind_out = jnp.where(jnp.logical_and(place == 1, codes[0, TOP] == 2), 2, 0)
     inverse = inverse_ref[...]
@@ -467,7 +473,7 @@
             field = nodes_of(f_ref, s * PLANE + j * 128, 128)
             pad_ref[s, :, 128 + j * 128 : 256 + j * 128] = (field * inverse).astype(BF16)
 
-    held = count * GHOST_ROWS
+    held = ghost_ref.shape[0]
     lane = lax.broadcasted_iota(jnp.int32, (count * NODE_COUNT, 128), 1)
     for first, lanes, side in PIECES:
         tile = first // TILE
@@ -608,9 +614,8 @@
         )
 
     def outer(f, ghosts, parts, last):
-        count = math.gcd(slots, 2)
-        if last:
-            f = pltpu.with_memory_space_constraint(f, pltpu.HBM)
+        count = group
+        f = pltpu.with_memory_space_constraint(f, pltpu.HBM)
         tables = [rows, edge, ghost_r, ghost_z, pos, radial_m, axial_m, rot_m]
         scratch = [
             pltpu.VMEM((3, NODE_COUNT, PLANE), F32),
@@ -618,7 +623,7 @@
             pltpu.VMEM((NODES, 128), F32),
             pltpu.VMEM((count, 3, NODE_COUNT, 128), F32),
             pltpu.VMEM((count, 2, NODE_COUNT, 128), BF16),
-            pltpu.VMEM((count * GHOST_ROWS, PLANE), BF16),
+            pltpu.VMEM((-(-count * (LOCAL_Z + NODES) // 16) * 16, PLANE), BF16),
             square,
             square,
             pltpu.VMEM((count, NODE_COUNT, PLANE + 256), BF16),
@@ -626,7 +631,7 @@
             pltpu.VMEM((count, NODE_COUNT, PLANE), F32),
         ]
         return call(
-            lambda *a: outer_kernel(count, len(parts), last, *a), "last_update" if last else "update", count, 32 if last else 26,
+            lambda *a: outer_kernel(count, len(parts), last, *a), "last_update" if last else "update", count, 40 if last else 32,
             [mom_spec] * len(parts) + [slab(count), axial_spec(count)] + [radial_spec(count)] * 3
             + all_whole(tables),
             [slab(count)] + ([mom_spec] if last else []), [big_shape] + ([mom_shape] if last else []),

time: 112 us -> 112 us (level)
  no operation moved by 1% of the time
where the time goes in v14:
time: 112 us; the launch traced here: 111 us
  Pallas kernels  71.1 us (63%)
  starting transfers between devices  19.2 us (17%)
  waiting for transfers between devices  14.8 us (13%)
  local copies, waits for them, and re-layouts  5.03 us (4%)
    pallas_call x6, Pallas kernels, call(): pl.pallas_call(body, grid_spec=pltpu.PrefetchScalarGridSpec(num_scalar_pr...  69 us
    ppermute x9, waiting for transfers between devices, spread(): lax.ppermute(moments, 'vert', [(i, i ^ shift) for i in range(verts)])  14.7 us
    ppermute x9, starting transfers between devices, spread(): lax.ppermute(moments, 'vert', [(i, i ^ shift) for i in range(verts)])  11.7 us
    ppermute x2, starting transfers between devices, halo(): from_far = lax.ppermute(far, 'row', between + [(b, a) for a, b in between])  5.21 us
    unnamed x6, local copies, waits for them, and re-layouts  5.03 us
  transfers between devices with their start and end apart: 15, of which 8 were waited for; matrix products, arithmetic and copies ran while one was open for 0% of the time, Pallas kernels for 16%

profile of v14, /device:TPU:4, one launch (start us, length us, event | category | flops | bytes accessed | tf_op | source)
XLA Modules:
  0.0 110.8 jit_solution(18114974358321274284)
XLA Ops:
  0.6 0.0 copy-start.1
  0.6 5.0 %copy-done.1 = f32[8,16,27648]{2,1,0:T(8,128)S(1)} copy-done((f32[8,16,27648]{2,1,0:T(8,128)S(1)}, f32[8,16,27648]{2,1,0:T(8,128)}, u32[]{:S(2)}) %copy-start.1) | copy-done | bytes 14155800
  5.7 3.8 %traces.2 = (f32[12,16,1152]{2,1,0:T(8,128)S(1)}, f32[12,16,1152]{2,1,0:T(8,128)S(1)}, f32[12,8,2304]{2,1,0:T(8,128)S(1)}) custom-call(s32[12]{0:T(128)} %a_0_.11, s32[1,2]{1,0:T(1,128)} %bitcast.1, f32[8,16,27648]{2,1,0:T(8,128)S(1)} %copy-done.1, bf16[2,2,32,128]{3,2,1,0:T(8,128)(2,1)} %constant.27.clone.a_3_), custom_call_target="tpu_custom_call" | custom-call | tf_op jit(solution)/shard_map/traces/pallas_call | solution.py:584
  9.5 1.6 %collective-permute-start.3 = (f32[12,8,2304]{2,1,0:T(8,128)S(1)}, f32[12,8,2304]{2,1,0:T(8,128)S(1)}, u32[]{:S(2)}, u32[]{:S(2)}) collective-permute-start(f32[12,8,2304]{2,1,0:T(8,128)S(1)} %get-tuple-element.19), channel_id=1, source_target_pairs={{0,4},{4,0},{1,5},{5,1},{2,6},{6,2},{3,7},{7,3},{8,12},{12,8},{9,1... | collective-permute-start | bytes 2654216 | tf_op jit(solution)/shard_map/ppermute | solution.py:649
  11.1 2.5 %collective-permute-start.5 = (f32[12,16,1152]{2,1,0:T(8,128)S(1)}, f32[12,16,1152]{2,1,0:T(8,128)S(1)}, u32[]{:S(2)}, u32[]{:S(2)}) collective-permute-start(f32[12,16,1152]{2,1,0:T(8,128)S(1)} %get-tuple-element.17.a_3_), channel_id=1, source_target_pairs={{8,16},{16,8},{9,17},{17,9},{10,18},{18,10},{11,19},{19,11},{12,20... | collective-permute-start | bytes 2654216 | tf_op jit(solution)/shard_map/ppermute | solution.py:653
  13.6 9.1 %moments.2 = (f32[16,128]{1,0:T(8,128)S(1)}, f32[12,16,1152]{2,1,0:T(8,128)S(1)}) custom-call(s32[12]{0:T(128)} %a_0_.11, s32[1,2]{1,0:T(1,128)} %bitcast.2, f32[8,16,27648]{2,1,0:T(8,128)S(1)} %copy-done.1, f32[12,16,1152]{2,1,0:T(8,128)S(1)} %get-tuple-element.17.a_3_, f32[8,2304]{1,0:T(8,128)} %constant.20.clone.a_4_.a_11_, ...), custom_call_target="tpu_custom_call" | custom-call | tf_op jit(solution)/shard_map/moments/pallas_call | solution.py:584
  22.7 3.7 %collective-permute-start.2 = (f32[16,128]{1,0:T(8,128)S(1)}, f32[16,128]{1,0:T(8,128)S(1)}, u32[]{:S(2)}, u32[]{:S(2)}) collective-permute-start(f32[16,128]{1,0:T(8,128)S(1)} %get-tuple-element.18.a_2_), channel_id=1, source_target_pairs={{0,3},{1,2},{2,1},{3,0},{4,7},{5,6},{6,5},{7,4},{8,11},{9,10},{10,... | collective-permute-start | bytes 24584 | tf_op jit(solution)/shard_map/ppermute | solution.py:645
  26.4 0.0 collective-permute-start.1
  26.4 1.8 %collective-permute-done.2.a_5_ = f32[16,128]{1,0:T(8,128)S(1)} collective-permute-done((f32[16,128]{1,0:T(8,128)S(1)}, f32[16,128]{1,0:T(8,128)S(1)}, u32[]{:S(2)}, u32[]{:S(2)}) %collective-permute-start.2) | collective-permute-done | bytes 8224 | tf_op jit(solution)/shard_map/ppermute | solution.py:645
  28.2 0.0 collective-permute-start
  28.2 2.7 %collective-permute-done.1.a_4_ = f32[16,128]{1,0:T(8,128)S(1)} collective-permute-done((f32[16,128]{1,0:T(8,128)S(1)}, f32[16,128]{1,0:T(8,128)S(1)}, u32[]{:S(2)}, u32[]{:S(2)}) %collective-permute-start.1) | collective-permute-done | bytes 8224 | tf_op jit(solution)/shard_map/ppermute | solution.py:645
  30.9 0.9 collective-permute-done.a_3_
  31.9 0.0 collective-permute-done.3.a_7_
  31.9 0.0 collective-permute-done.4.a_8_
  31.9 0.0 collective-permute-done.5.a_10_
  31.9 17.8 %update.1.a_2_.a_6_ = f32[8,16,27648]{2,1,0:T(8,128)S(1)} custom-call(s32[12]{0:T(128)} %a_0_.11, s32[1,2]{1,0:T(1,128)} %bitcast.3, f32[16,128]{1,0:T(8,128)S(1)} %get-tuple-element.18.a_2_, f32[16,128]{1,0:T(8,128)S(1)} %collective-permute-done.a_3_, f32[16,128]{1,0:T(8,128)S(1)} %collective-permute-done.1.a_4_, ...), custom_call_target="tpu_custom_call" | custom-call | tf_op jit(solution)/shard_map/update/pallas_call | solution.py:584
  49.8 3.7 %traces.3 = (f32[12,16,1152]{2,1,0:T(8,128)S(1)}, f32[12,16,1152]{2,1,0:T(8,128)S(1)}, f32[12,8,2304]{2,1,0:T(8,128)S(1)}) custom-call(s32[12]{0:T(128)} %a_0_.11, s32[1,2]{1,0:T(1,128)} %bitcast.4, f32[8,16,27648]{2,1,0:T(8,128)S(1)} %update.1.a_2_.a_6_, bf16[2,2,32,128]{3,2,1,0:T(8,128)(2,1)} %constant.27.clone.a_3_), custom_call_target="tpu_custom_call" | custom-call | tf_op jit(solution)/shard_map/traces/pallas_call | solution.py:584
  53.5 0.6 collective-permute-start.9
  54.2 0.0 collective-permute-start.10
  54.2 2.7 %collective-permute-start.11 = (f32[12,16,1152]{2,1,0:T(8,128)S(1)}, f32[12,16,1152]{2,1,0:T(8,128)S(1)}, u32[]{:S(2)}, u32[]{:S(2)}) collective-permute-start(f32[12,16,1152]{2,1,0:T(8,128)S(1)} %get-tuple-element.22.a_3_), channel_id=1, source_target_pairs={{8,16},{16,8},{9,17},{17,9},{10,18},{18,10},{11,19},{19,11},{12,20... | collective-permute-start | bytes 2654216 | tf_op jit(solution)/shard_map/ppermute | solution.py:653
  56.9 9.1 %moments.3 = (f32[16,128]{1,0:T(8,128)S(1)}, f32[12,16,1152]{2,1,0:T(8,128)S(1)}) custom-call(s32[12]{0:T(128)} %a_0_.11, s32[1,2]{1,0:T(1,128)} %bitcast.5, f32[8,16,27648]{2,1,0:T(8,128)S(1)} %update.1.a_2_.a_6_, f32[12,16,1152]{2,1,0:T(8,128)S(1)} %get-tuple-element.22.a_3_, f32[8,2304]{1,0:T(8,128)} %constant.20.clone.a_4_.a_11_, ...), custom_call_target="tpu_custom_call" | custom-call | tf_op jit(solution)/shard_map/moments/pallas_call | solution.py:584
  66.0 3.7 %collective-permute-start.8 = (f32[16,128]{1,0:T(8,128)S(1)}, f32[16,128]{1,0:T(8,128)S(1)}, u32[]{:S(2)}, u32[]{:S(2)}) collective-permute-start(f32[16,128]{1,0:T(8,128)S(1)} %get-tuple-element.23.a_2_), channel_id=1, source_target_pairs={{0,3},{1,2},{2,1},{3,0},{4,7},{5,6},{6,5},{7,4},{8,11},{9,10},{10,... | collective-permute-start | bytes 24584 | tf_op jit(solution)/shard_map/ppermute | solution.py:645
  69.7 0.0 collective-permute-start.7
  69.7 1.8 %collective-permute-done.8.a_5_ = f32[16,128]{1,0:T(8,128)S(1)} collective-permute-done((f32[16,128]{1,0:T(8,128)S(1)}, f32[16,128]{1,0:T(8,128)S(1)}, u32[]{:S(2)}, u32[]{:S(2)}) %collective-permute-start.8) | collective-permute-done | bytes 8224 | tf_op jit(solution)/shard_map/ppermute | solution.py:645
  71.5 2.7 %collective-permute-done.7.a_4_ = f32[16,128]{1,0:T(8,128)S(1)} collective-permute-done((f32[16,128]{1,0:T(8,128)S(1)}, f32[16,128]{1,0:T(8,128)S(1)}, u32[]{:S(2)}, u32[]{:S(2)}) %collective-permute-start.7) | collective-permute-done | bytes 8224 | tf_op jit(solution)/shard_map/ppermute | solution.py:645
  74.2 0.9 collective-permute-done.6.a_3_
  75.2 25.3 %last_update.1 = (f32[8,16,27648]{2,1,0:T(8,128)}, f32[16,128]{1,0:T(8,128)S(1)}) custom-call(s32[12]{0:T(128)} %a_0_.11, s32[1,2]{1,0:T(1,128)} %bitcast.6, f32[16,128]{1,0:T(8,128)S(1)} %get-tuple-element.23.a_2_, f32[16,128]{1,0:T(8,128)S(1)} %collective-permute-done.6.a_3_, f32[16,128]{1,0:T(8,128)S(1)} %collective-permute-done.7.a_4_, ...), custom_call_target="tpu_custom_call" | custom-call | tf_op jit(solution)/shard_map/last_update/pallas_call | solution.py:584
  100.5 3.6 %collective-permute-start.14 = (f32[16,128]{1,0:T(8,128)S(1)}, f32[16,128]{1,0:T(8,128)S(1)}, u32[]{:S(2)}, u32[]{:S(2)}) collective-permute-start(f32[16,128]{1,0:T(8,128)S(1)} %get-tuple-element.28.a_1_), channel_id=1, source_target_pairs={{0,3},{1,2},{2,1},{3,0},{4,7},{5,6},{6,5},{7,4},{8,11},{9,10},{10,... | collective-permute-start | bytes 24584 | tf_op jit(solution)/shard_map/ppermute | solution.py:645
  104.1 0.8 collective-permute-start.12
  104.9 1.1 collective-permute-done.14.a_4_
  105.9 2.7 %collective-permute-done.13.a_3_ = f32[16,128]{1,0:T(8,128)S(1)} collective-permute-done((f32[16,128]{1,0:T(8,128)S(1)}, f32[16,128]{1,0:T(8,128)S(1)}, u32[]{:S(2)}, u32[]{:S(2)}) %collective-permute-start.13) | collective-permute-done | bytes 8224 | tf_op jit(solution)/shard_map/ppermute | solution.py:645
  108.7 2.1 %macroscopic.1 = (f32[8,8,16]{2,1,0:T(8,128)}, f32[1,8]{1,0:T(1,128)}) custom-call(s32[1,2]{1,0:T(1,128)} %bitcast.7, f32[16,128]{1,0:T(8,128)S(1)} %get-tuple-element.28.a_1_, f32[16,128]{1,0:T(8,128)S(1)} %collective-permute-done.12.a_2_, f32[16,128]{1,0:T(8,128)S(1)} %collective-permute-done.13.a_3_, f32[16,128]{1,0:T(8,128)S(1)} %collective-permute-done.14.a_4_, ...), custom_call_target="tpu_custom_call" | custom-call | tf_op jit(solution)/shard_map/macroscopic/pallas_call | solution.py:666
  (11 shorter events, 0.0 us)
Async XLA Ops:
  0.6 5.0 %copy-start.1 = (f32[8,16,27648]{2,1,0:T(8,128)S(1)}, f32[8,16,27648]{2,1,0:T(8,128)}, u32[]{:S(2)}) copy-start(f32[8,16,27648]{2,1,0:T(8,128)} %a_6_.1) | copy-start | bytes 42467332
  5.7 26.3 %copy-start.2 = (bf16[9,512,256]{2,1,0:T(8,128)(2,1)S(1)}, bf16[9,512,256]{2,1,0:T(8,128)(2,1)}, u32[]{:S(2)}) copy-start(bf16[9,512,256]{2,1,0:T(8,128)(2,1)} %constant.29.clone.a_18_) | copy-start | bytes 7077892
  9.5 22.4 %collective-permute-start.3 = (f32[12,8,2304]{2,1,0:T(8,128)S(1)}, f32[12,8,2304]{2,1,0:T(8,128)S(1)}, u32[]{:S(2)}, u32[]{:S(2)}) collective-permute-start(f32[12,8,2304]{2,1,0:T(8,128)S(1)} %get-tuple-element.19), channel_id=1, source_target_pairs={{0,4},{4,0},{1,5},{5,1},{2,6},{6,2},{3,7},{7,3},{8,12},{12,8},{9,1... | collective-permute-start | bytes 2654216 | tf_op jit(solution)/shard_map/ppermute | solution.py:649
  11.1 20.8 %collective-permute-start.4 = (f32[12,16,1152]{2,1,0:T(8,128)S(1)}, f32[12,16,1152]{2,1,0:T(8,128)S(1)}, u32[]{:S(2)}, u32[]{:S(2)}) collective-permute-start(f32[12,16,1152]{2,1,0:T(8,128)S(1)} %get-tuple-element.20), channel_id=1, source_target_pairs={{0,8},{8,0},{16,24},{24,16},{1,9},{9,1},{17,25},{25,17},{2,10},{10... | collective-permute-start | bytes 2654216 | tf_op jit(solution)/shard_map/ppermute | solution.py:651
  11.1 20.8 %collective-permute-start.5 = (f32[12,16,1152]{2,1,0:T(8,128)S(1)}, f32[12,16,1152]{2,1,0:T(8,128)S(1)}, u32[]{:S(2)}, u32[]{:S(2)}) collective-permute-start(f32[12,16,1152]{2,1,0:T(8,128)S(1)} %get-tuple-element.17.a_3_), channel_id=1, source_target_pairs={{8,16},{16,8},{9,17},{17,9},{10,18},{18,10},{11,19},{19,11},{12,20... | collective-permute-start | bytes 2654216 | tf_op jit(solution)/shard_map/ppermute | solution.py:653
  22.7 5.5 %collective-permute-start.2 = (f32[16,128]{1,0:T(8,128)S(1)}, f32[16,128]{1,0:T(8,128)S(1)}, u32[]{:S(2)}, u32[]{:S(2)}) collective-permute-start(f32[16,128]{1,0:T(8,128)S(1)} %get-tuple-element.18.a_2_), channel_id=1, source_target_pairs={{0,3},{1,2},{2,1},{3,0},{4,7},{5,6},{6,5},{7,4},{8,11},{9,10},{10,... | collective-permute-start | bytes 24584 | tf_op jit(solution)/shard_map/ppermute | solution.py:645
  26.4 4.5 %collective-permute-start.1 = (f32[16,128]{1,0:T(8,128)S(1)}, f32[16,128]{1,0:T(8,128)S(1)}, u32[]{:S(2)}, u32[]{:S(2)}) collective-permute-start(f32[16,128]{1,0:T(8,128)S(1)} %get-tuple-element.18.a_2_), channel_id=1, source_target_pairs={{0,2},{1,3},{2,0},{3,1},{4,6},{5,7},{6,4},{7,5},{8,10},{9,11},{10,... | collective-permute-start | bytes 24584 | tf_op jit(solution)/shard_map/ppermute | solution.py:645
  28.2 3.7 %collective-permute-start = (f32[16,128]{1,0:T(8,128)S(1)}, f32[16,128]{1,0:T(8,128)S(1)}, u32[]{:S(2)}, u32[]{:S(2)}) collective-permute-start(f32[16,128]{1,0:T(8,128)S(1)} %get-tuple-element.18.a_2_), channel_id=1, source_target_pairs={{0,1},{1,0},{2,3},{3,2},{4,5},{5,4},{6,7},{7,6},{8,9},{9,8},{10,11... | collective-permute-start | bytes 24584 | tf_op jit(solution)/shard_map/ppermute | solution.py:645
  49.8 16.2 %copy-start = (f32[8,16,27648]{2,1,0:T(8,128)}, f32[8,16,27648]{2,1,0:T(8,128)S(1)}, u32[]{:S(2)}) copy-start(f32[8,16,27648]{2,1,0:T(8,128)S(1)} %update.1.a_2_.a_6_) | copy-start | bytes 42467332
  53.5 21.6 %collective-permute-start.9 = (f32[12,8,2304]{2,1,0:T(8,128)S(1)}, f32[12,8,2304]{2,1,0:T(8,128)S(1)}, u32[]{:S(2)}, u32[]{:S(2)}) collective-permute-start(f32[12,8,2304]{2,1,0:T(8,128)S(1)} %get-tuple-element.24), channel_id=1, source_target_pairs={{0,4},{4,0},{1,5},{5,1},{2,6},{6,2},{3,7},{7,3},{8,12},{12,8},{9,1... | collective-permute-start | bytes 2654216 | tf_op jit(solution)/shard_map/ppermute | solution.py:649
  54.2 21.0 %collective-permute-start.10 = (f32[12,16,1152]{2,1,0:T(8,128)S(1)}, f32[12,16,1152]{2,1,0:T(8,128)S(1)}, u32[]{:S(2)}, u32[]{:S(2)}) collective-permute-start(f32[12,16,1152]{2,1,0:T(8,128)S(1)} %get-tuple-element.25), channel_id=1, source_target_pairs={{0,8},{8,0},{16,24},{24,16},{1,9},{9,1},{17,25},{25,17},{2,10},{10... | collective-permute-start | bytes 2654216 | tf_op jit(solution)/shard_map/ppermute | solution.py:651
  54.2 21.0 %collective-permute-start.11 = (f32[12,16,1152]{2,1,0:T(8,128)S(1)}, f32[12,16,1152]{2,1,0:T(8,128)S(1)}, u32[]{:S(2)}, u32[]{:S(2)}) collective-permute-start(f32[12,16,1152]{2,1,0:T(8,128)S(1)} %get-tuple-element.22.a_3_), channel_id=1, source_target_pairs={{8,16},{16,8},{9,17},{17,9},{10,18},{18,10},{11,19},{19,11},{12,20... | collective-permute-start | bytes 2654216 | tf_op jit(solution)/shard_map/ppermute | solution.py:653
  66.0 5.5 %collective-permute-start.8 = (f32[16,128]{1,0:T(8,128)S(1)}, f32[16,128]{1,0:T(8,128)S(1)}, u32[]{:S(2)}, u32[]{:S(2)}) collective-permute-start(f32[16,128]{1,0:T(8,128)S(1)} %get-tuple-element.23.a_2_), channel_id=1, source_target_pairs={{0,3},{1,2},{2,1},{3,0},{4,7},{5,6},{6,5},{7,4},{8,11},{9,10},{10,... | collective-permute-start | bytes 24584 | tf_op jit(solution)/shard_map/ppermute | solution.py:645
  69.7 4.5 %collective-permute-start.7 = (f32[16,128]{1,0:T(8,128)S(1)}, f32[16,128]{1,0:T(8,128)S(1)}, u32[]{:S(2)}, u32[]{:S(2)}) collective-permute-start(f32[16,128]{1,0:T(8,128)S(1)} %get-tuple-element.23.a_2_), channel_id=1, source_target_pairs={{0,2},{1,3},{2,0},{3,1},{4,6},{5,7},{6,4},{7,5},{8,10},{9,11},{10,... | collective-permute-start | bytes 24584 | tf_op jit(solution)/shard_map/ppermute | solution.py:645
  71.5 3.7 %collective-permute-start.6 = (f32[16,128]{1,0:T(8,128)S(1)}, f32[16,128]{1,0:T(8,128)S(1)}, u32[]{:S(2)}, u32[]{:S(2)}) collective-permute-start(f32[16,128]{1,0:T(8,128)S(1)} %get-tuple-element.23.a_2_), channel_id=1, source_target_pairs={{0,1},{1,0},{2,3},{3,2},{4,5},{5,4},{6,7},{7,6},{8,9},{9,8},{10,11... | collective-permute-start | bytes 24584 | tf_op jit(solution)/shard_map/ppermute | solution.py:645
  100.5 5.4 %collective-permute-start.14 = (f32[16,128]{1,0:T(8,128)S(1)}, f32[16,128]{1,0:T(8,128)S(1)}, u32[]{:S(2)}, u32[]{:S(2)}) collective-permute-start(f32[16,128]{1,0:T(8,128)S(1)} %get-tuple-element.28.a_1_), channel_id=1, source_target_pairs={{0,3},{1,2},{2,1},{3,0},{4,7},{5,6},{6,5},{7,4},{8,11},{9,10},{10,... | collective-permute-start | bytes 24584 | tf_op jit(solution)/shard_map/ppermute | solution.py:645
  104.1 4.5 %collective-permute-start.13 = (f32[16,128]{1,0:T(8,128)S(1)}, f32[16,128]{1,0:T(8,128)S(1)}, u32[]{:S(2)}, u32[]{:S(2)}) collective-permute-start(f32[16,128]{1,0:T(8,128)S(1)} %get-tuple-element.28.a_1_), channel_id=1, source_target_pairs={{0,2},{1,3},{2,0},{3,1},{4,6},{5,7},{6,4},{7,5},{8,10},{9,11},{10,... | collective-permute-start | bytes 24584 | tf_op jit(solution)/shard_map/ppermute | solution.py:645
  104.1 4.5 %collective-permute-start.12 = (f32[16,128]{1,0:T(8,128)S(1)}, f32[16,128]{1,0:T(8,128)S(1)}, u32[]{:S(2)}, u32[]{:S(2)}) collective-permute-start(f32[16,128]{1,0:T(8,128)S(1)} %get-tuple-element.28.a_1_), channel_id=1, source_target_pairs={{0,1},{1,0},{2,3},{3,2},{4,5},{5,4},{6,7},{7,6},{8,9},{9,8},{10,11... | collective-permute-start | bytes 24584 | tf_op jit(solution)/shard_map/ppermute | solution.py:645

commit v15 on v14

--- a/solution.py
+++ b/solution.py
@@ -598,7 +598,9 @@
     def all_whole(tables):
         return [whole(x.shape) for x in tables]
 
-    def traces_of(f):
+    def traces_of(f, first):
+        if first:
+            f = pltpu.with_memory_space_constraint(f, pltpu.HBM)
         return call(
             lambda *a: trace_kernel(group, *a), "traces", group, 20, [slab(group)] + all_whole([trace_m]),
             [radial_spec(group), radial_spec(group), axial_spec(group)], [radial_shape, radial_shape, axial_shape],
@@ -615,7 +617,8 @@
 
     def outer(f, ghosts, parts, last):
         count = group
-        f = pltpu.with_memory_space_constraint(f, pltpu.HBM)
+        if not last:
+            f = pltpu.with_memory_space_constraint(f, pltpu.HBM)
         tables = [rows, edge, ghost_r, ghost_z, pos, radial_m, axial_m, rot_m]
         scratch = [
             pltpu.VMEM((3, NODE_COUNT, PLANE), F32),
@@ -656,7 +659,7 @@
     current = distribution
     for number in range(STEPS):
         last = number == STEPS - 1
-        traces = traces_of(current)
+        traces = traces_of(current, number == 0)
         from_axial, from_near, from_far = halo(*traces)
         moments, turned = moments_of(current, traces[1])
         parts = spread(moments)

time: 112 us -> 113 us (level)
  Pallas kernels: 71.1 us -> 75.1 us
  local copies, waits for them, and re-layouts: 5.03 us -> 2.09 us
    pallas_call x6, Pallas kernels: 69 us -> 73 us  [call(): pl.pallas_call(body, grid_spec=pltpu.PrefetchScalarGridSpec(num_scalar_pr...]
    unnamed x6 -> x10, local copies, waits for them, and re-layouts: 5.03 us -> 2.09 us
where the time goes in v15:
time: 113 us; the launch traced here: 112 us
  Pallas kernels  75.1 us (66%)
  starting transfers between devices  19.1 us (17%)
  waiting for transfers between devices  14.8 us (13%)
  local copies, waits for them, and re-layouts  2.09 us (2%)
    pallas_call x6, Pallas kernels, call(): pl.pallas_call(body, grid_spec=pltpu.PrefetchScalarGridSpec(num_scalar_pr...  73 us
    ppermute x9, waiting for transfers between devices, spread(): lax.ppermute(moments, 'vert', [(i, i ^ shift) for i in range(verts)])  14.7 us
    ppermute x9, starting transfers between devices, spread(): lax.ppermute(moments, 'vert', [(i, i ^ shift) for i in range(verts)])  11.7 us
    ppermute x2, starting transfers between devices, halo(): from_far = lax.ppermute(far, 'row', between + [(b, a) for a, b in between])  5.22 us
  transfers between devices with their start and end apart: 15, of which 8 were waited for; matrix products, arithmetic and copies ran while one was open for 0% of the time, Pallas kernels for 16%

profile of v15, /device:TPU:4, one launch (start us, length us, event | category | flops | bytes accessed | tf_op | source)
XLA Modules:
  0.0 111.9 jit_solution(1441893428007310071)
XLA Ops:
  0.6 0.0 copy-start.1
  0.6 0.0 copy-start.2
  0.7 7.9 %traces.2 = (f32[12,16,1152]{2,1,0:T(8,128)S(1)}, f32[12,16,1152]{2,1,0:T(8,128)S(1)}, f32[12,8,2304]{2,1,0:T(8,128)S(1)}) custom-call(s32[12]{0:T(128)} %a_0_.11, s32[1,2]{1,0:T(1,128)} %bitcast.1, f32[8,16,27648]{2,1,0:T(8,128)} %a_6_.1, bf16[2,2,32,128]{3,2,1,0:T(8,128)(2,1)} %constant.27.clone.a_3_), custom_call_target="tpu_custom_call" | custom-call | tf_op jit(solution)/shard_map/traces/pallas_call | solution.py:584
  8.5 1.6 %collective-permute-start.3 = (f32[12,8,2304]{2,1,0:T(8,128)S(1)}, f32[12,8,2304]{2,1,0:T(8,128)S(1)}, u32[]{:S(2)}, u32[]{:S(2)}) collective-permute-start(f32[12,8,2304]{2,1,0:T(8,128)S(1)} %get-tuple-element.19), channel_id=1, source_target_pairs={{0,4},{4,0},{1,5},{5,1},{2,6},{6,2},{3,7},{7,3},{8,12},{12,8},{9,1... | collective-permute-start | bytes 2654216 | tf_op jit(solution)/shard_map/ppermute | solution.py:652
  10.1 0.0 collective-permute-start.4
  10.1 2.5 %collective-permute-start.5 = (f32[12,16,1152]{2,1,0:T(8,128)S(1)}, f32[12,16,1152]{2,1,0:T(8,128)S(1)}, u32[]{:S(2)}, u32[]{:S(2)}) collective-permute-start(f32[12,16,1152]{2,1,0:T(8,128)S(1)} %get-tuple-element.17.a_3_), channel_id=1, source_target_pairs={{8,16},{16,8},{9,17},{17,9},{10,18},{18,10},{11,19},{19,11},{12,20... | collective-permute-start | bytes 2654216 | tf_op jit(solution)/shard_map/ppermute | solution.py:656
  12.6 9.1 %moments.2 = (f32[16,128]{1,0:T(8,128)S(1)}, f32[12,16,1152]{2,1,0:T(8,128)S(1)}) custom-call(s32[12]{0:T(128)} %a_0_.11, s32[1,2]{1,0:T(1,128)} %bitcast.2, f32[8,16,27648]{2,1,0:T(8,128)S(1)} %copy-done.1, f32[12,16,1152]{2,1,0:T(8,128)S(1)} %get-tuple-element.17.a_3_, f32[8,2304]{1,0:T(8,128)} %constant.20.clone.a_4_.a_11_, ...), custom_call_target="tpu_custom_call" | custom-call | tf_op jit(solution)/shard_map/moments/pallas_call | solution.py:584
  21.8 3.7 %collective-permute-start.2 = (f32[16,128]{1,0:T(8,128)S(1)}, f32[16,128]{1,0:T(8,128)S(1)}, u32[]{:S(2)}, u32[]{:S(2)}) collective-permute-start(f32[16,128]{1,0:T(8,128)S(1)} %get-tuple-element.18.a_2_), channel_id=1, source_target_pairs={{0,3},{1,2},{2,1},{3,0},{4,7},{5,6},{6,5},{7,4},{8,11},{9,10},{10,... | collective-permute-start | bytes 24584 | tf_op jit(solution)/shard_map/ppermute | solution.py:648
  25.4 0.0 collective-permute-start.1
  25.4 1.8 %collective-permute-done.2.a_5_ = f32[16,128]{1,0:T(8,128)S(1)} collective-permute-done((f32[16,128]{1,0:T(8,128)S(1)}, f32[16,128]{1,0:T(8,128)S(1)}, u32[]{:S(2)}, u32[]{:S(2)}) %collective-permute-start.2) | collective-permute-done | bytes 8224 | tf_op jit(solution)/shard_map/ppermute | solution.py:648
  27.3 2.7 %collective-permute-done.1.a_4_ = f32[16,128]{1,0:T(8,128)S(1)} collective-permute-done((f32[16,128]{1,0:T(8,128)S(1)}, f32[16,128]{1,0:T(8,128)S(1)}, u32[]{:S(2)}, u32[]{:S(2)}) %collective-permute-start.1) | collective-permute-done | bytes 8224 | tf_op jit(solution)/shard_map/ppermute | solution.py:648
  30.0 0.9 collective-permute-done.a_3_
  30.9 0.0 collective-permute-done.5.a_10_
  30.9 0.0 copy-start.3
  30.9 0.9 copy-done.3
  31.8 1.2 %copy-done.4 = f32[12,16,1152]{2,1,0:T(8,128)S(1)} copy-done((f32[12,16,1152]{2,1,0:T(8,128)S(1)}, f32[12,16,1152]{2,1,0:T(8,128)}, u32[]{:S(2)}) %copy-start.4) | copy-done | bytes 884760
  33.0 17.8 %update.1.a_2_.a_6_ = f32[8,16,27648]{2,1,0:T(8,128)S(1)} custom-call(s32[12]{0:T(128)} %a_0_.11, s32[1,2]{1,0:T(1,128)} %bitcast.3, f32[16,128]{1,0:T(8,128)S(1)} %get-tuple-element.18.a_2_, f32[16,128]{1,0:T(8,128)S(1)} %collective-permute-done.a_3_, f32[16,128]{1,0:T(8,128)S(1)} %collective-permute-done.1.a_4_, ...), custom_call_target="tpu_custom_call" | custom-call | tf_op jit(solution)/shard_map/update/pallas_call | solution.py:584
  50.9 3.7 %traces.3 = (f32[12,16,1152]{2,1,0:T(8,128)S(1)}, f32[12,16,1152]{2,1,0:T(8,128)S(1)}, f32[12,8,2304]{2,1,0:T(8,128)S(1)}) custom-call(s32[12]{0:T(128)} %a_0_.11, s32[1,2]{1,0:T(1,128)} %bitcast.4, f32[8,16,27648]{2,1,0:T(8,128)S(1)} %update.1.a_2_.a_6_, bf16[2,2,32,128]{3,2,1,0:T(8,128)(2,1)} %constant.27.clone.a_3_), custom_call_target="tpu_custom_call" | custom-call | tf_op jit(solution)/shard_map/traces/pallas_call | solution.py:584
  54.6 0.6 collective-permute-start.9
  55.2 0.0 collective-permute-start.10
  55.2 2.7 %collective-permute-start.11 = (f32[12,16,1152]{2,1,0:T(8,128)S(1)}, f32[12,16,1152]{2,1,0:T(8,128)S(1)}, u32[]{:S(2)}, u32[]{:S(2)}) collective-permute-start(f32[12,16,1152]{2,1,0:T(8,128)S(1)} %get-tuple-element.22.a_3_), channel_id=1, source_target_pairs={{8,16},{16,8},{9,17},{17,9},{10,18},{18,10},{11,19},{19,11},{12,20... | collective-permute-start | bytes 2654216 | tf_op jit(solution)/shard_map/ppermute | solution.py:656
  57.9 9.1 %moments.3 = (f32[16,128]{1,0:T(8,128)S(1)}, f32[12,16,1152]{2,1,0:T(8,128)S(1)}) custom-call(s32[12]{0:T(128)} %a_0_.11, s32[1,2]{1,0:T(1,128)} %bitcast.5, f32[8,16,27648]{2,1,0:T(8,128)S(1)} %update.1.a_2_.a_6_, f32[12,16,1152]{2,1,0:T(8,128)S(1)} %get-tuple-element.22.a_3_, f32[8,2304]{1,0:T(8,128)} %constant.20.clone.a_4_.a_11_, ...), custom_call_target="tpu_custom_call" | custom-call | tf_op jit(solution)/shard_map/moments/pallas_call | solution.py:584
  67.1 3.7 %collective-permute-start.8 = (f32[16,128]{1,0:T(8,128)S(1)}, f32[16,128]{1,0:T(8,128)S(1)}, u32[]{:S(2)}, u32[]{:S(2)}) collective-permute-start(f32[16,128]{1,0:T(8,128)S(1)} %get-tuple-element.23.a_2_), channel_id=1, source_target_pairs={{0,3},{1,2},{2,1},{3,0},{4,7},{5,6},{6,5},{7,4},{8,11},{9,10},{10,... | collective-permute-start | bytes 24584 | tf_op jit(solution)/shard_map/ppermute | solution.py:648
  70.8 1.8 %collective-permute-done.8.a_5_ = f32[16,128]{1,0:T(8,128)S(1)} collective-permute-done((f32[16,128]{1,0:T(8,128)S(1)}, f32[16,128]{1,0:T(8,128)S(1)}, u32[]{:S(2)}, u32[]{:S(2)}) %collective-permute-start.8) | collective-permute-done | bytes 8224 | tf_op jit(solution)/shard_map/ppermute | solution.py:648
  72.6 2.7 %collective-permute-done.7.a_4_ = f32[16,128]{1,0:T(8,128)S(1)} collective-permute-done((f32[16,128]{1,0:T(8,128)S(1)}, f32[16,128]{1,0:T(8,128)S(1)}, u32[]{:S(2)}, u32[]{:S(2)}) %collective-permute-start.7) | collective-permute-done | bytes 8224 | tf_op jit(solution)/shard_map/ppermute | solution.py:648
  75.3 1.0 collective-permute-done.6.a_3_
  76.3 25.3 %last_update.1 = (f32[8,16,27648]{2,1,0:T(8,128)}, f32[16,128]{1,0:T(8,128)S(1)}) custom-call(s32[12]{0:T(128)} %a_0_.11, s32[1,2]{1,0:T(1,128)} %bitcast.6, f32[16,128]{1,0:T(8,128)S(1)} %get-tuple-element.23.a_2_, f32[16,128]{1,0:T(8,128)S(1)} %collective-permute-done.6.a_3_, f32[16,128]{1,0:T(8,128)S(1)} %collective-permute-done.7.a_4_, ...), custom_call_target="tpu_custom_call" | custom-call | tf_op jit(solution)/shard_map/last_update/pallas_call | solution.py:584
  101.6 3.6 %collective-permute-start.14 = (f32[16,128]{1,0:T(8,128)S(1)}, f32[16,128]{1,0:T(8,128)S(1)}, u32[]{:S(2)}, u32[]{:S(2)}) collective-permute-start(f32[16,128]{1,0:T(8,128)S(1)} %get-tuple-element.28.a_1_), channel_id=1, source_target_pairs={{0,3},{1,2},{2,1},{3,0},{4,7},{5,6},{6,5},{7,4},{8,11},{9,10},{10,... | collective-permute-start | bytes 24584 | tf_op jit(solution)/shard_map/ppermute | solution.py:648
  105.2 0.8 collective-permute-start.12
  106.0 1.1 collective-permute-done.14.a_4_
  107.0 2.7 %collective-permute-done.13.a_3_ = f32[16,128]{1,0:T(8,128)S(1)} collective-permute-done((f32[16,128]{1,0:T(8,128)S(1)}, f32[16,128]{1,0:T(8,128)S(1)}, u32[]{:S(2)}, u32[]{:S(2)}) %collective-permute-start.13) | collective-permute-done | bytes 8224 | tf_op jit(solution)/shard_map/ppermute | solution.py:648
  109.7 2.1 %macroscopic.1 = (f32[8,8,16]{2,1,0:T(8,128)}, f32[1,8]{1,0:T(1,128)}) custom-call(s32[1,2]{1,0:T(1,128)} %bitcast.7, f32[16,128]{1,0:T(8,128)S(1)} %get-tuple-element.28.a_1_, f32[16,128]{1,0:T(8,128)S(1)} %collective-permute-done.12.a_2_, f32[16,128]{1,0:T(8,128)S(1)} %collective-permute-done.13.a_3_, f32[16,128]{1,0:T(8,128)S(1)} %collective-permute-done.14.a_4_, ...), custom_call_target="tpu_custom_call" | custom-call | tf_op jit(solution)/shard_map/macroscopic/pallas_call | solution.py:669
  (15 shorter events, 0.0 us)
Async XLA Ops:
  0.6 12.0 %copy-start.1 = (f32[8,16,27648]{2,1,0:T(8,128)S(1)}, f32[8,16,27648]{2,1,0:T(8,128)}, u32[]{:S(2)}) copy-start(f32[8,16,27648]{2,1,0:T(8,128)} %a_6_.1) | copy-start | bytes 42467332
  0.6 31.2 %copy-start.2 = (bf16[9,512,256]{2,1,0:T(8,128)(2,1)S(1)}, bf16[9,512,256]{2,1,0:T(8,128)(2,1)}, u32[]{:S(2)}) copy-start(bf16[9,512,256]{2,1,0:T(8,128)(2,1)} %constant.29.clone.a_18_) | copy-start | bytes 7077892
  8.5 22.4 %collective-permute-start.3 = (f32[12,8,2304]{2,1,0:T(8,128)S(1)}, f32[12,8,2304]{2,1,0:T(8,128)S(1)}, u32[]{:S(2)}, u32[]{:S(2)}) collective-permute-start(f32[12,8,2304]{2,1,0:T(8,128)S(1)} %get-tuple-element.19), channel_id=1, source_target_pairs={{0,4},{4,0},{1,5},{5,1},{2,6},{6,2},{3,7},{7,3},{8,12},{12,8},{9,1... | collective-permute-start | bytes 2654216 | tf_op jit(solution)/shard_map/ppermute | solution.py:652
  10.1 20.8 %collective-permute-start.4 = (f32[12,16,1152]{2,1,0:T(8,128)S(1)}, f32[12,16,1152]{2,1,0:T(8,128)S(1)}, u32[]{:S(2)}, u32[]{:S(2)}) collective-permute-start(f32[12,16,1152]{2,1,0:T(8,128)S(1)} %get-tuple-element.20), channel_id=1, source_target_pairs={{0,8},{8,0},{16,24},{24,16},{1,9},{9,1},{17,25},{25,17},{2,10},{10... | collective-permute-start | bytes 2654216 | tf_op jit(solution)/shard_map/ppermute | solution.py:654
  10.1 20.8 %collective-permute-start.5 = (f32[12,16,1152]{2,1,0:T(8,128)S(1)}, f32[12,16,1152]{2,1,0:T(8,128)S(1)}, u32[]{:S(2)}, u32[]{:S(2)}) collective-permute-start(f32[12,16,1152]{2,1,0:T(8,128)S(1)} %get-tuple-element.17.a_3_), channel_id=1, source_target_pairs={{8,16},{16,8},{9,17},{17,9},{10,18},{18,10},{11,19},{19,11},{12,20... | collective-permute-start | bytes 2654216 | tf_op jit(solution)/shard_map/ppermute | solution.py:656
  21.8 5.5 %collective-permute-start.2 = (f32[16,128]{1,0:T(8,128)S(1)}, f32[16,128]{1,0:T(8,128)S(1)}, u32[]{:S(2)}, u32[]{:S(2)}) collective-permute-start(f32[16,128]{1,0:T(8,128)S(1)} %get-tuple-element.18.a_2_), channel_id=1, source_target_pairs={{0,3},{1,2},{2,1},{3,0},{4,7},{5,6},{6,5},{7,4},{8,11},{9,10},{10,... | collective-permute-start | bytes 24584 | tf_op jit(solution)/shard_map/ppermute | solution.py:648
  25.4 4.5 %collective-permute-start.1 = (f32[16,128]{1,0:T(8,128)S(1)}, f32[16,128]{1,0:T(8,128)S(1)}, u32[]{:S(2)}, u32[]{:S(2)}) collective-permute-start(f32[16,128]{1,0:T(8,128)S(1)} %get-tuple-element.18.a_2_), channel_id=1, source_target_pairs={{0,2},{1,3},{2,0},{3,1},{4,6},{5,7},{6,4},{7,5},{8,10},{9,11},{10,... | collective-permute-start | bytes 24584 | tf_op jit(solution)/shard_map/ppermute | solution.py:648
  27.3 3.7 %collective-permute-start = (f32[16,128]{1,0:T(8,128)S(1)}, f32[16,128]{1,0:T(8,128)S(1)}, u32[]{:S(2)}, u32[]{:S(2)}) collective-permute-start(f32[16,128]{1,0:T(8,128)S(1)} %get-tuple-element.18.a_2_), channel_id=1, source_target_pairs={{0,1},{1,0},{2,3},{3,2},{4,5},{5,4},{6,7},{7,6},{8,9},{9,8},{10,11... | collective-permute-start | bytes 24584 | tf_op jit(solution)/shard_map/ppermute | solution.py:648
  30.9 0.9 copy-start.3
  31.8 1.2 %copy-start.4 = (f32[12,16,1152]{2,1,0:T(8,128)S(1)}, f32[12,16,1152]{2,1,0:T(8,128)}, u32[]{:S(2)}) copy-start(f32[12,16,1152]{2,1,0:T(8,128)} %copy-done.3) | copy-start | bytes 2654212
  50.8 16.2 %copy-start = (f32[8,16,27648]{2,1,0:T(8,128)}, f32[8,16,27648]{2,1,0:T(8,128)S(1)}, u32[]{:S(2)}) copy-start(f32[8,16,27648]{2,1,0:T(8,128)S(1)} %update.1.a_2_.a_6_) | copy-start | bytes 42467332
  54.6 21.7 %collective-permute-start.9 = (f32[12,8,2304]{2,1,0:T(8,128)S(1)}, f32[12,8,2304]{2,1,0:T(8,128)S(1)}, u32[]{:S(2)}, u32[]{:S(2)}) collective-permute-start(f32[12,8,2304]{2,1,0:T(8,128)S(1)} %get-tuple-element.24), channel_id=1, source_target_pairs={{0,4},{4,0},{1,5},{5,1},{2,6},{6,2},{3,7},{7,3},{8,12},{12,8},{9,1... | collective-permute-start | bytes 2654216 | tf_op jit(solution)/shard_map/ppermute | solution.py:652
  55.2 21.0 %collective-permute-start.10 = (f32[12,16,1152]{2,1,0:T(8,128)S(1)}, f32[12,16,1152]{2,1,0:T(8,128)S(1)}, u32[]{:S(2)}, u32[]{:S(2)}) collective-permute-start(f32[12,16,1152]{2,1,0:T(8,128)S(1)} %get-tuple-element.25), channel_id=1, source_target_pairs={{0,8},{8,0},{16,24},{24,16},{1,9},{9,1},{17,25},{25,17},{2,10},{10... | collective-permute-start | bytes 2654216 | tf_op jit(solution)/shard_map/ppermute | solution.py:654
  55.2 21.0 %collective-permute-start.11 = (f32[12,16,1152]{2,1,0:T(8,128)S(1)}, f32[12,16,1152]{2,1,0:T(8,128)S(1)}, u32[]{:S(2)}, u32[]{:S(2)}) collective-permute-start(f32[12,16,1152]{2,1,0:T(8,128)S(1)} %get-tuple-element.22.a_3_), channel_id=1, source_target_pairs={{8,16},{16,8},{9,17},{17,9},{10,18},{18,10},{11,19},{19,11},{12,20... | collective-permute-start | bytes 2654216 | tf_op jit(solution)/shard_map/ppermute | solution.py:656
  67.1 5.5 %collective-permute-start.8 = (f32[16,128]{1,0:T(8,128)S(1)}, f32[16,128]{1,0:T(8,128)S(1)}, u32[]{:S(2)}, u32[]{:S(2)}) collective-permute-start(f32[16,128]{1,0:T(8,128)S(1)} %get-tuple-element.23.a_2_), channel_id=1, source_target_pairs={{0,3},{1,2},{2,1},{3,0},{4,7},{5,6},{6,5},{7,4},{8,11},{9,10},{10,... | collective-permute-start | bytes 24584 | tf_op jit(solution)/shard_map/ppermute | solution.py:648
  70.7 4.5 %collective-permute-start.7 = (f32[16,128]{1,0:T(8,128)S(1)}, f32[16,128]{1,0:T(8,128)S(1)}, u32[]{:S(2)}, u32[]{:S(2)}) collective-permute-start(f32[16,128]{1,0:T(8,128)S(1)} %get-tuple-element.23.a_2_), channel_id=1, source_target_pairs={{0,2},{1,3},{2,0},{3,1},{4,6},{5,7},{6,4},{7,5},{8,10},{9,11},{10,... | collective-permute-start | bytes 24584 | tf_op jit(solution)/shard_map/ppermute | solution.py:648
  72.6 3.7 %collective-permute-start.6 = (f32[16,128]{1,0:T(8,128)S(1)}, f32[16,128]{1,0:T(8,128)S(1)}, u32[]{:S(2)}, u32[]{:S(2)}) collective-permute-start(f32[16,128]{1,0:T(8,128)S(1)} %get-tuple-element.23.a_2_), channel_id=1, source_target_pairs={{0,1},{1,0},{2,3},{3,2},{4,5},{5,4},{6,7},{7,6},{8,9},{9,8},{10,11... | collective-permute-start | bytes 24584 | tf_op jit(solution)/shard_map/ppermute | solution.py:648
  101.6 5.4 %collective-permute-start.14 = (f32[16,128]{1,0:T(8,128)S(1)}, f32[16,128]{1,0:T(8,128)S(1)}, u32[]{:S(2)}, u32[]{:S(2)}) collective-permute-start(f32[16,128]{1,0:T(8,128)S(1)} %get-tuple-element.28.a_1_), channel_id=1, source_target_pairs={{0,3},{1,2},{2,1},{3,0},{4,7},{5,6},{6,5},{7,4},{8,11},{9,10},{10,... | collective-permute-start | bytes 24584 | tf_op jit(solution)/shard_map/ppermute | solution.py:648
  105.2 4.5 %collective-permute-start.13 = (f32[16,128]{1,0:T(8,128)S(1)}, f32[16,128]{1,0:T(8,128)S(1)}, u32[]{:S(2)}, u32[]{:S(2)}) collective-permute-start(f32[16,128]{1,0:T(8,128)S(1)} %get-tuple-element.28.a_1_), channel_id=1, source_target_pairs={{0,2},{1,3},{2,0},{3,1},{4,6},{5,7},{6,4},{7,5},{8,10},{9,11},{10,... | collective-permute-start | bytes 24584 | tf_op jit(solution)/shard_map/ppermute | solution.py:648
  105.2 4.5 %collective-permute-start.12 = (f32[16,128]{1,0:T(8,128)S(1)}, f32[16,128]{1,0:T(8,128)S(1)}, u32[]{:S(2)}, u32[]{:S(2)}) collective-permute-start(f32[16,128]{1,0:T(8,128)S(1)} %get-tuple-element.28.a_1_), channel_id=1, source_target_pairs={{0,1},{1,0},{2,3},{3,2},{4,5},{5,4},{6,7},{7,6},{8,9},{9,8},{10,11... | collective-permute-start | bytes 24584 | tf_op jit(solution)/shard_map/ppermute | solution.py:648
